TPU v7x, 32 devices: a whole 2x2x4 slice. The times are simulated.
32 devices in a mesh: groups: 2 (over y), frame: 4 (over z), strip: 2 (over x), slab: 2 (over core).
Axes of the slice: x: 2, y: 2, z: 4, core: 2. Of those that a mesh axis runs over, the one named last changes fastest.
Arguments:
- frames_in: bfloat16 [16, 8, 128, 192], P(('groups', 'frame'), 'strip', 'slab'), parts along dimension 0, may hold values from -6 to 6
- weight_first: bfloat16 [3, 3, 3, 192, 192], replicated, may hold values from -0.078125 to 0.078125
- scale_first: float32 [192], replicated, may hold values from 0.25 to 1.75
- weight_second: bfloat16 [3, 3, 3, 192, 192], replicated, may hold values from -0.078125 to 0.078125
- scale_second: float32 [192], replicated, may hold values from 0.25 to 1.75
Outputs:
- latents_out: bfloat16 [16, 8, 128, 192], P(('groups', 'frame'), 'strip', 'slab'), parts along dimension 0
There are 2 independent parts, one for each index of `groups`. A program takes and returns all parts, laid end to end along the dimension named above; an argument that names none is the same for every part. Nothing has to cross between parts.
All inputs are finite; a program needn't handle non-finite values.
Results may differ from a plain program's by a relative error of at most 0.0051.
Values may be sent and summed in bfloat16 or wider, within the bound.
No kernel may reach another device: no remote copies, remote signals or barrier semaphores. Data moves between devices by JAX's collectives and lax.ppermute only.
A program may use at most 64 MiB of HBM per device.

v0:
```python
import jax
import jax.numpy as jnp
from jax import lax
from jax.sharding import PartitionSpec as P


def from_behind(x, axis, by):
    size = lax.axis_size(axis)
    pairs = [(i, i + by) for i in range(size) if 0 <= i + by < size]
    return lax.ppermute(x, axis, pairs)


def with_halo(cells, sides, width):
    for axis, dim in sides:
        count = lax.axis_size(axis)
        ends = count - 1
        head = lax.slice_in_dim(cells, 0, width, axis=dim)
        tail = lax.slice_in_dim(cells, cells.shape[dim] - width, cells.shape[dim], axis=dim)
        cells = jnp.concatenate(
            [
                lax.ppermute(tail, axis, [(i, (i + 1) % count) for i in range(ends)]),
                cells,
                lax.ppermute(head, axis, [((i + 1) % count, i) for i in range(ends)]),
            ],
            axis=dim,
        )
    return cells


def tap_block(block, rows, cols):
    count = block.shape[0]
    pieces = [
        block[:, offset_y : offset_y + rows, offset_x : offset_x + cols]
        for offset_y in range(3)
        for offset_x in range(3)
    ]
    return jnp.concatenate(pieces, axis=-1).reshape(count * rows * cols, -1)


def finish(convolved, scales):
    mean_square = jnp.mean(convolved * convolved, axis=-1, keepdims=True)
    normed = convolved * lax.rsqrt(mean_square + 1e-06) * scales
    return jax.nn.silu(normed).astype(jnp.bfloat16)


def conv_layer(features, weight, scales):
    frames, rows, cols, channels = features.shape
    flat_weight = weight.reshape(3, 9 * channels, channels)
    cells = rows * cols
    earlier = from_behind(features, "frame", 1)
    extended = jnp.concatenate([earlier, features], axis=0)
    padded = with_halo(extended, (("strip", 1), ("slab", 2)), 1)
    accumulated = jnp.zeros((frames * cells, channels), jnp.float32)
    for offset_t in range(3):
        accumulated = accumulated + jnp.dot(
            tap_block(padded[offset_t : offset_t + frames], rows, cols),
            flat_weight[offset_t],
            preferred_element_type=jnp.float32,
        )
    accumulated = accumulated.reshape(frames, cells, channels)
    return finish(accumulated, scales).reshape(frames, rows, cols, channels)


def shards(frames_in, weight_first, scale_first, weight_second, scale_second):
    hidden = conv_layer(frames_in, weight_first, scale_first)
    return conv_layer(hidden, weight_second, scale_second)


def solution(mesh):
    return jax.shard_map(
        shards,
        mesh=mesh,
        in_specs=(P(("groups", "frame"), "strip", "slab", None), P(), P(), P(), P()),
        out_specs=P(("groups", "frame"), "strip", "slab", None),
        check_vma=False,
    )
```

profile of v0, /device:TPU:0, one launch (start us, length us, event | category | flops | bytes accessed | tf_op | source)
XLA Modules:
  0.0 92.0 jit_solution(4176239762942542063)
XLA Ops:
  0.0 4.9 %collective-permute-start = (bf16[2,4,64,192]{3,2,1,0:T(8,128)(2,1)}, bf16[2,4,64,192]{3,2,1,0:T(8,128)(2,1)S(1)}, u32[]{:S(2)}, u32[]{:S(2)}) collective-permute-start(bf16[2,4,64,192]{3,2,1,0:T(8,128)(2,1)} %param.5), channel_id=1, source_target_pairs={{0,4},{4,8},{8,12},{1,5},{5,9},{9,13},{2,6},{6,10},{10,14},{3,7},{... | collective-permute-start | bytes 589832 | tf_op jit(solution)/shard_map/ppermute | solution.py:10
  4.9 5.8 %collective-permute-done = bf16[2,4,64,192]{3,2,1,0:T(8,128)(2,1)S(1)} collective-permute-done((bf16[2,4,64,192]{3,2,1,0:T(8,128)(2,1)}, bf16[2,4,64,192]{3,2,1,0:T(8,128)(2,1)S(1)}, u32[]{:S(2)}, u32[]{:S(2)}) %collective-permute-start) | collective-permute-done | bytes 196640 | tf_op jit(solution)/shard_map/ppermute | solution.py:10
  10.8 0.0 copy-start.2
  10.8 1.1 %constant_dynamic-update-slice_fusion = bf16[4,4,64,192]{3,2,1,0:T(8,128)(2,1)S(1)} fusion(bf16[4,4,64,192]{3,2,1,0:T(8,128)(2,1)S(1)} %constant_dynamic-update-slice_fusion.1, bf16[2,4,64,192]{3,2,1,0:T(8,128)(2,1)} %param.5), kind=kLoop, calls=%fused_computation.38 | loop fusion | bytes 458752 | tf_op jit(solution)/shard_map/concatenate | solution.py:51
  11.9 3.4 %collective-permute-start.1 = (bf16[4,1,64,192]{3,2,1,0:T(8,128)(2,1)S(1)}, bf16[4,1,64,192]{3,2,1,0:T(8,128)(2,1)S(1)}, u32[]{:S(2)}, u32[]{:S(2)}) collective-permute-start(bf16[4,1,64,192]{3,2,1,0:T(8,128)(2,1)S(1)} %get-tuple-element.75), channel_id=1, source_target_pairs={{0,2},{1,3},{4,6},{5,7},{8,10},{9,11},{12,14},{13,15},{16,18},{17,... | collective-permute-start | bytes 294920 | tf_op jit(solution)/shard_map/ppermute | solution.py:21
  15.3 0.0 copy-done.2
  15.3 1.3 %collective-permute-start.2 = (bf16[4,1,64,192]{3,2,1,0:T(8,128)(2,1)S(1)}, bf16[4,1,64,192]{3,2,1,0:T(8,128)(2,1)S(1)}, u32[]{:S(2)}, u32[]{:S(2)}) collective-permute-start(bf16[4,1,64,192]{3,2,1,0:T(8,128)(2,1)S(1)} %get-tuple-element.76), channel_id=1, source_target_pairs={{2,0},{3,1},{6,4},{7,5},{10,8},{11,9},{14,12},{15,13},{18,16},{19,... | collective-permute-start | bytes 294920 | tf_op jit(solution)/shard_map/ppermute | solution.py:23
  16.6 3.2 %fusion.7 = (bf16[1,3,3,192,192]{4,3,2,1,0:T(8,128)(2,1)S(1)}, bf16[1,3,3,192,192]{4,3,2,1,0:T(8,128)(2,1)}, bf16[1,3,3,192,192]{4,3,2,1,0:T(8,128)(2,1)}) fusion(bf16[3,3,3,192,192]{4,3,2,1,0:T(8,128)(2,1)} %param.6), kind=kLoop, calls=%fused_computation.43 | loop fusion | bytes 3981312 | tf_op jit(solution)/shard_map/slice | solution.py:57
  19.8 0.0 collective-permute-done.1
  19.8 2.4 %collective-permute-done.2 = bf16[4,1,64,192]{3,2,1,0:T(8,128)(2,1)S(1)} collective-permute-done((bf16[4,1,64,192]{3,2,1,0:T(8,128)(2,1)S(1)}, bf16[4,1,64,192]{3,2,1,0:T(8,128)(2,1)S(1)}, u32[]{:S(2)}, u32[]{:S(2)}) %collective-permute-start.2) | collective-permute-done | bytes 98336 | tf_op jit(solution)/shard_map/ppermute | solution.py:23
  22.2 1.3 %collective-permute-start.3 = (bf16[4,6,1,192]{3,2,1,0:T(2,128)(2,1)S(1)}, bf16[4,6,1,192]{3,2,1,0:T(2,128)(2,1)S(1)}, u32[]{:S(2)}, u32[]{:S(2)}) collective-permute-start(bf16[4,6,1,192]{3,2,1,0:T(2,128)(2,1)S(1)} %get-tuple-element.54), channel_id=1, source_target_pairs={{0,1},{2,3},{4,5},{6,7},{8,9},{10,11},{12,13},{14,15},{16,17},{18,... | collective-permute-start | bytes 27656 | tf_op jit(solution)/shard_map/ppermute | solution.py:21
  23.5 1.3 %collective-permute-start.4 = (bf16[4,6,1,192]{3,2,1,0:T(2,128)(2,1)S(1)}, bf16[4,6,1,192]{3,2,1,0:T(2,128)(2,1)S(1)}, u32[]{:S(2)}, u32[]{:S(2)}) collective-permute-start(bf16[4,6,1,192]{3,2,1,0:T(2,128)(2,1)S(1)} %get-tuple-element.53), channel_id=1, source_target_pairs={{1,0},{3,2},{5,4},{7,6},{9,8},{11,10},{13,12},{15,14},{17,16},{19,... | collective-permute-start | bytes 27656 | tf_op jit(solution)/shard_map/ppermute | solution.py:23
  24.8 1.3 %fusion.3 = (bf16[2,4,64,192]{3,2,1,0:T(8,128)(2,1)}, bf16[2,4,64,192]{3,2,1,0:T(8,128)(2,1)}, bf16[2,4,64,192]{3,2,1,0:T(8,128)(2,1)}, bf16[2,4,64,192]{3,2,1,0...) fusion(bf16[4,4,64,192]{3,2,1,0:T(8,128)(2,1)S(1)} %constant_dy, ...), kind=kLoop, calls=%fused_computation.23 | loop fusion | flops 589824 | bytes 2424832 | tf_op jit(solution)/shard_map/concatenate | solution.py:19
  26.2 0.0 collective-permute-done.3
  26.2 0.5 collective-permute-done.4
  26.6 0.5 pad_maximum_fusion
  27.1 2.1 %fusion.10 = (bf16[2,4,64,192]{3,2,1,0:T(8,128)(2,1)}, bf16[2,4,64,192]{3,2,1,0:T(8,128)(2,1)S(1)}, bf16[2,4,64,192]{3,2,1,0:T(8,128)(2,1)}, bf16[2,4,64,192]{3,...) fusion(bf16[4,6,65,192]{3,2,1,0:T(8,128)(2,1)S(1)} %get-tuple-e, ...), kind=kLoop, calls=%fused_computation.46 | loop fusion | bytes 7077888 | tf_op jit(solution)/shard_map/slice | solution.py:33
  29.2 2.8 %concatenate.103 = bf16[2,4,64,1728]{3,2,1,0:T(8,128)(2,1)S(1)} concatenate(bf16[2,4,64,192]{3,2,1,0:T(8,128)(2,1)} %get-tuple-element.83, bf16[2,4,64,192]{3,2,1,0:T(8,128)(2,1)} %get-tuple-element.71, bf16[2,4,64,192]{3,2,1,0:T(8,128)(2,1)} %get-tuple-element.35, bf16[2,4,64,192]{3,2,1,0:T(8,128)(2,1)} %get-tuple-element.84, bf16[2,4,64,192]{3,2,1,0:T(8,128)(2,1)} %get-tuple-element.74, ...), dimensions={3} | concatenate | bytes 3538944 | tf_op jit(solution)/shard_map/concatenate | solution.py:37
  32.0 1.9 %fusion.15 = f32[512,192]{0,1:T(8,128)S(1)} fusion(bf16[512,1728]{1,0:T(8,128)(2,1)S(1)} %bitcast.28, bf16[1728,192]{1,0:T(8,128)(2,1)} %bitcast.37), kind=kOutput, calls=%fused_computation.51 | convolution fusion | flops 339738624 | bytes 2826240 | tf_op jit(solution)/shard_map/dot_general | solution.py:55
  33.9 2.8 %concatenate.104 = bf16[2,4,64,1728]{3,2,1,0:T(8,128)(2,1)S(1)} concatenate(bf16[2,4,64,192]{3,2,1,0:T(8,128)(2,1)} %get-tuple-element.86, bf16[2,4,64,192]{3,2,1,0:T(8,128)(2,1)} %get-tuple-element.72, bf16[2,4,64,192]{3,2,1,0:T(8,128)(2,1)} %get-tuple-element.32, bf16[2,4,64,192]{3,2,1,0:T(8,128)(2,1)} %get-tuple-element.87, bf16[2,4,64,192]{3,2,1,0:T(8,128)(2,1)} %param.5, ...), dimensions={3} | concatenate | bytes 3538944 | tf_op jit(solution)/shard_map/concatenate | solution.py:37
  36.7 1.9 %fusion.16 = f32[512,192]{0,1:T(8,128)S(1)} fusion(bf16[512,1728]{1,0:T(8,128)(2,1)S(1)} %bitcast.31, bf16[1728,192]{1,0:T(8,128)(2,1)} %bitcast.36), kind=kOutput, calls=%fused_computation.52 | convolution fusion | flops 339738624 | bytes 2826240 | tf_op jit(solution)/shard_map/dot_general | solution.py:55
  38.6 2.9 %concatenate.102 = bf16[2,4,64,1728]{3,2,1,0:T(8,128)(2,1)S(1)} concatenate(bf16[2,4,64,192]{3,2,1,0:T(8,128)(2,1)} %get-tuple-element.81, bf16[2,4,64,192]{3,2,1,0:T(8,128)(2,1)} %get-tuple-element.73, bf16[2,4,64,192]{3,2,1,0:T(8,128)(2,1)} %get-tuple-element.37, bf16[2,4,64,192]{3,2,1,0:T(8,128)(2,1)} %get-tuple-element.82, bf16[2,4,64,192]{3,2,1,0:T(8,128)(2,1)} %copy-done.2, ...), dimensions={3} | concatenate | bytes 3538944 | tf_op jit(solution)/shard_map/concatenate | solution.py:37
  41.5 0.0 copy-start.3
  41.5 1.5 %multiply_reduce_fusion.1 = (f32[512]{0:T(512)S(1)}, f32[512,192]{0,1:T(8,128)}) fusion(f32[512,192]{0,1:T(8,128)S(1)} %fusion.16, f32[512,192]{0,1:T(8,128)S(1)} %fusion.15, bf16[512,1728]{1,0:T(8,128)(2,1)S(1)} %bitcast.26, bf16[1728,192]{1,0:T(8,128)(2,1)S(1)} %bitcast.34), kind=kOutput, calls=%fused_computation.21 | convolution fusion | flops 340131328 | bytes 3614720 | tf_op jit(solution)/shard_map/dot_general | solution.py:55
  43.0 1.2 %copy.8 = f32[512,192]{1,0:T(8,128)S(1)} copy(f32[512,192]{0,1:T(8,128)} %get-tuple-element.78) | data formatting | bytes 786432 | tf_op jit(solution)/shard_map/add | solution.py:55
  44.2 0.1 rsqrt.23
  44.3 0.0 copy-done.3
  44.3 0.2 multiply_convert_fusion.1
  44.5 4.3 %collective-permute-start.5 = (bf16[2,4,64,192]{3,2,1,0:T(8,128)(2,1)S(1)}, bf16[2,4,64,192]{3,2,1,0:T(8,128)(2,1)S(1)}, u32[]{:S(2)}, u32[]{:S(2)}) collective-permute-start(bf16[2,4,64,192]{3,2,1,0:T(8,128)(2,1)S(1)} %multiply_convert_fusion.1), channel_id=1, source_target_pairs={{0,4},{4,8},{8,12},{1,5},{5,9},{9,13},{2,6},{6,10},{10,14},{3,7},{... | collective-permute-start | bytes 589832 | tf_op jit(solution)/shard_map/ppermute | solution.py:10
  48.8 3.2 %fusion.6 = (bf16[1,3,3,192,192]{4,3,2,1,0:T(8,128)(2,1)S(1)}, bf16[1,3,3,192,192]{4,3,2,1,0:T(8,128)(2,1)}, bf16[1,3,3,192,192]{4,3,2,1,0:T(8,128)(2,1)}) fusion(bf16[3,3,3,192,192]{4,3,2,1,0:T(8,128)(2,1)} %param.8), kind=kLoop, calls=%fused_computation.42 | loop fusion | bytes 3981312 | tf_op jit(solution)/shard_map/slice | solution.py:57
  52.0 3.2 %collective-permute-done.5 = bf16[2,4,64,192]{3,2,1,0:T(8,128)(2,1)S(1)} collective-permute-done((bf16[2,4,64,192]{3,2,1,0:T(8,128)(2,1)S(1)}, bf16[2,4,64,192]{3,2,1,0:T(8,128)(2,1)S(1)}, u32[]{:S(2)}, u32[]{:S(2)}) %collective-permute-start.5) | collective-permute-done | bytes 196640 | tf_op jit(solution)/shard_map/ppermute | solution.py:10
  55.3 2.2 %collective-permute-start.6 = (bf16[4,1,64,192]{3,2,1,0:T(8,128)(2,1)S(1)}, bf16[4,1,64,192]{3,2,1,0:T(8,128)(2,1)S(1)}, u32[]{:S(2)}, u32[]{:S(2)}) collective-permute-start(bf16[4,1,64,192]{3,2,1,0:T(8,128)(2,1)S(1)} %get-tuple-element.69), channel_id=1, source_target_pairs={{0,2},{1,3},{4,6},{5,7},{8,10},{9,11},{12,14},{13,15},{16,18},{17,... | collective-permute-start | bytes 294920 | tf_op jit(solution)/shard_map/ppermute | solution.py:21
  57.5 1.3 %collective-permute-start.7 = (bf16[4,1,64,192]{3,2,1,0:T(8,128)(2,1)S(1)}, bf16[4,1,64,192]{3,2,1,0:T(8,128)(2,1)S(1)}, u32[]{:S(2)}, u32[]{:S(2)}) collective-permute-start(bf16[4,1,64,192]{3,2,1,0:T(8,128)(2,1)S(1)} %get-tuple-element.70), channel_id=1, source_target_pairs={{2,0},{3,1},{6,4},{7,5},{10,8},{11,9},{14,12},{15,13},{18,16},{19,... | collective-permute-start | bytes 294920 | tf_op jit(solution)/shard_map/ppermute | solution.py:23
  58.8 1.4 %collective-permute-done.6 = bf16[4,1,64,192]{3,2,1,0:T(8,128)(2,1)S(1)} collective-permute-done((bf16[4,1,64,192]{3,2,1,0:T(8,128)(2,1)S(1)}, bf16[4,1,64,192]{3,2,1,0:T(8,128)(2,1)S(1)}, u32[]{:S(2)}, u32[]{:S(2)}) %collective-permute-start.6) | collective-permute-done | bytes 98336 | tf_op jit(solution)/shard_map/ppermute | solution.py:21
  60.2 4.1 %collective-permute-done.7 = bf16[4,1,64,192]{3,2,1,0:T(8,128)(2,1)S(1)} collective-permute-done((bf16[4,1,64,192]{3,2,1,0:T(8,128)(2,1)S(1)}, bf16[4,1,64,192]{3,2,1,0:T(8,128)(2,1)S(1)}, u32[]{:S(2)}, u32[]{:S(2)}) %collective-permute-start.7) | collective-permute-done | bytes 98336 | tf_op jit(solution)/shard_map/ppermute | solution.py:23
  64.3 0.2 pad_maximum_fusion.2
  64.6 0.9 %fusion.12 = (bf16[2,4,64,192]{3,2,1,0:T(8,128)(2,1)}, bf16[2,4,64,192]{3,2,1,0:T(8,128)(2,1)}, bf16[2,4,64,192]{3,2,1,0:T(8,128)(2,1)}) fusion(bf16[4,5,64,192]{3,2,1,0:T(8,128)(2,1)S(1)} %get-tuple-element.67), kind=kLoop, calls=%fused_computation.48 | loop fusion | bytes 1179648 | tf_op jit(solution)/shard_map/slice | solution.py:33
  65.6 1.3 %collective-permute-start.8 = (bf16[4,6,1,192]{3,2,1,0:T(2,128)(2,1)S(1)}, bf16[4,6,1,192]{3,2,1,0:T(2,128)(2,1)S(1)}, u32[]{:S(2)}, u32[]{:S(2)}) collective-permute-start(bf16[4,6,1,192]{3,2,1,0:T(2,128)(2,1)S(1)} %get-tuple-element.50), channel_id=1, source_target_pairs={{0,1},{2,3},{4,5},{6,7},{8,9},{10,11},{12,13},{14,15},{16,17},{18,... | collective-permute-start | bytes 27656 | tf_op jit(solution)/shard_map/ppermute | solution.py:21
  66.9 1.3 %collective-permute-start.9 = (bf16[4,6,1,192]{3,2,1,0:T(2,128)(2,1)S(1)}, bf16[4,6,1,192]{3,2,1,0:T(2,128)(2,1)S(1)}, u32[]{:S(2)}, u32[]{:S(2)}) collective-permute-start(bf16[4,6,1,192]{3,2,1,0:T(2,128)(2,1)S(1)} %get-tuple-element.49), channel_id=1, source_target_pairs={{1,0},{3,2},{5,4},{7,6},{9,8},{11,10},{13,12},{15,14},{17,16},{19,... | collective-permute-start | bytes 27656 | tf_op jit(solution)/shard_map/ppermute | solution.py:23
  68.2 0.9 fusion.13
  69.1 0.0 collective-permute-done.8
  69.1 0.9 collective-permute-done.9
  69.9 0.4 pad_maximum_fusion.1
  70.4 1.7 %fusion.8 = (bf16[2,4,64,192]{3,2,1,0:T(8,128)(2,1)}, bf16[2,4,64,192]{3,2,1,0:T(8,128)(2,1)}, bf16[2,4,64,192]{3,2,1,0:T(8,128)(2,1)}, bf16[2,4,64,192]{3,2,1,0...) fusion(bf16[4,6,65,192]{3,2,1,0:T(8,128)(2,1)S(1)} %get-tuple-e, ...), kind=kLoop, calls=%fused_computation.44 | loop fusion | bytes 3538944 | tf_op jit(solution)/shard_map/slice | solution.py:33
  72.1 1.4 %fusion.9 = (bf16[2,4,64,192]{3,2,1,0:T(8,128)(2,1)}, bf16[2,4,64,192]{3,2,1,0:T(8,128)(2,1)}, bf16[2,4,64,192]{3,2,1,0:T(8,128)(2,1)}, bf16[2,4,64,192]{3,2,1,0...) fusion(bf16[4,6,65,192]{3,2,1,0:T(8,128)(2,1)S(1)} %get-tuple-e, ...), kind=kLoop, calls=%fused_computation.45 | loop fusion | bytes 3538944 | tf_op jit(solution)/shard_map/slice | solution.py:33
  73.5 2.8 %concatenate.112 = bf16[2,4,64,1728]{3,2,1,0:T(8,128)(2,1)S(1)} concatenate(bf16[2,4,64,192]{3,2,1,0:T(8,128)(2,1)} %get-tuple-element.26, bf16[2,4,64,192]{3,2,1,0:T(8,128)(2,1)} %get-tuple-element.60, bf16[2,4,64,192]{3,2,1,0:T(8,128)(2,1)} %get-tuple-element.17, bf16[2,4,64,192]{3,2,1,0:T(8,128)(2,1)} %get-tuple-element.25, bf16[2,4,64,192]{3,2,1,0:T(8,128)(2,1)S(1)} %pad_maximum_fusion.3, ...), dimensions={3} | concatenate | bytes 3538944 | tf_op jit(solution)/shard_map/concatenate | solution.py:37
  76.3 0.0 copy-start.1
  76.3 2.7 %fusion.17 = f32[512,192]{0,1:T(8,128)} fusion(bf16[512,1728]{1,0:T(8,128)(2,1)S(1)} %bitcast.29, bf16[1728,192]{1,0:T(8,128)(2,1)} %bitcast.35), kind=kOutput, calls=%fused_computation.53 | convolution fusion | flops 339738624 | bytes 2826240 | tf_op jit(solution)/shard_map/dot_general | solution.py:55
  79.0 0.0 copy-done.1
  79.0 2.7 %concatenate.113 = bf16[2,4,64,1728]{3,2,1,0:T(8,128)(2,1)S(1)} concatenate(bf16[2,4,64,192]{3,2,1,0:T(8,128)(2,1)} %get-tuple-element.23, bf16[2,4,64,192]{3,2,1,0:T(8,128)(2,1)} %get-tuple-element.59, bf16[2,4,64,192]{3,2,1,0:T(8,128)(2,1)} %get-tuple-element.14, bf16[2,4,64,192]{3,2,1,0:T(8,128)(2,1)} %get-tuple-element.22, ...), dimensions={3} | concatenate | bytes 3538944 | tf_op jit(solution)/shard_map/concatenate | solution.py:37
  81.7 2.7 %fusion.18 = f32[512,192]{0,1:T(8,128)} fusion(bf16[512,1728]{1,0:T(8,128)(2,1)S(1)} %bitcast.30, bf16[1728,192]{1,0:T(8,128)(2,1)} %bitcast.33), kind=kOutput, calls=%fused_computation.54 | convolution fusion | flops 339738624 | bytes 2826240 | tf_op jit(solution)/shard_map/dot_general | solution.py:55
  84.4 0.0 copy-start
  84.4 2.8 %concatenate.111 = bf16[2,4,64,1728]{3,2,1,0:T(8,128)(2,1)S(1)} concatenate(bf16[2,4,64,192]{3,2,1,0:T(8,128)(2,1)} %get-tuple-element.28, bf16[2,4,64,192]{3,2,1,0:T(8,128)(2,1)} %get-tuple-element.58, bf16[2,4,64,192]{3,2,1,0:T(8,128)(2,1)} %get-tuple-element.19, bf16[2,4,64,192]{3,2,1,0:T(8,128)(2,1)} %get-tuple-element.27, ...), dimensions={3} | concatenate | bytes 3538944 | tf_op jit(solution)/shard_map/concatenate | solution.py:37
  87.3 0.0 copy-done
  87.3 0.0 copy-start.4
  87.3 2.5 %multiply_reduce_fusion = (f32[512]{0:T(512)S(1)}, f32[512,192]{0,1:T(8,128)}) fusion(f32[512,192]{0,1:T(8,128)} %fusion.18, f32[512,192]{0,1:T(8,128)S(1)} %copy-done, bf16[512,1728]{1,0:T(8,128)(2,1)S(1)} %bitcast.27, bf16[1728,192]{1,0:T(8,128)(2,1)S(1)} %bitcast.32), kind=kOutput, calls=%fused_computation.20 | convolution fusion | flops 340131328 | bytes 3614720 | tf_op jit(solution)/shard_map/dot_general | solution.py:55
  89.8 1.2 %copy.9 = f32[512,192]{1,0:T(8,128)S(1)} copy(f32[512,192]{0,1:T(8,128)} %get-tuple-element.80) | data formatting | bytes 786432 | tf_op jit(solution)/shard_map/add | solution.py:55
  91.0 0.1 rsqrt.25
  91.1 0.0 copy-done.4
  91.1 0.9 multiply_convert_fusion
  (8 shorter events, 0.2 us)
Async XLA Ops:
  0.0 10.8 %collective-permute-start = (bf16[2,4,64,192]{3,2,1,0:T(8,128)(2,1)}, bf16[2,4,64,192]{3,2,1,0:T(8,128)(2,1)S(1)}, u32[]{:S(2)}, u32[]{:S(2)}) collective-permute-start(bf16[2,4,64,192]{3,2,1,0:T(8,128)(2,1)} %param.5), channel_id=1, source_target_pairs={{0,4},{4,8},{8,12},{1,5},{5,9},{9,13},{2,6},{6,10},{10,14},{3,7},{... | collective-permute-start | bytes 589832 | tf_op jit(solution)/shard_map/ppermute | solution.py:10
  10.8 4.5 %copy-start.2 = (bf16[2,4,64,192]{3,2,1,0:T(8,128)(2,1)}, bf16[2,4,64,192]{3,2,1,0:T(8,128)(2,1)S(1)}, u32[]{:S(2)}) copy-start(bf16[2,4,64,192]{3,2,1,0:T(8,128)(2,1)S(1)} %collective-permute-done) | copy-start | bytes 589828
  11.9 7.9 %collective-permute-start.1 = (bf16[4,1,64,192]{3,2,1,0:T(8,128)(2,1)S(1)}, bf16[4,1,64,192]{3,2,1,0:T(8,128)(2,1)S(1)}, u32[]{:S(2)}, u32[]{:S(2)}) collective-permute-start(bf16[4,1,64,192]{3,2,1,0:T(8,128)(2,1)S(1)} %get-tuple-element.75), channel_id=1, source_target_pairs={{0,2},{1,3},{4,6},{5,7},{8,10},{9,11},{12,14},{13,15},{16,18},{17,... | collective-permute-start | bytes 294920 | tf_op jit(solution)/shard_map/ppermute | solution.py:21
  15.3 6.9 %collective-permute-start.2 = (bf16[4,1,64,192]{3,2,1,0:T(8,128)(2,1)S(1)}, bf16[4,1,64,192]{3,2,1,0:T(8,128)(2,1)S(1)}, u32[]{:S(2)}, u32[]{:S(2)}) collective-permute-start(bf16[4,1,64,192]{3,2,1,0:T(8,128)(2,1)S(1)} %get-tuple-element.76), channel_id=1, source_target_pairs={{2,0},{3,1},{6,4},{7,5},{10,8},{11,9},{14,12},{15,13},{18,16},{19,... | collective-permute-start | bytes 294920 | tf_op jit(solution)/shard_map/ppermute | solution.py:23
  22.2 3.9 %collective-permute-start.3 = (bf16[4,6,1,192]{3,2,1,0:T(2,128)(2,1)S(1)}, bf16[4,6,1,192]{3,2,1,0:T(2,128)(2,1)S(1)}, u32[]{:S(2)}, u32[]{:S(2)}) collective-permute-start(bf16[4,6,1,192]{3,2,1,0:T(2,128)(2,1)S(1)} %get-tuple-element.54), channel_id=1, source_target_pairs={{0,1},{2,3},{4,5},{6,7},{8,9},{10,11},{12,13},{14,15},{16,17},{18,... | collective-permute-start | bytes 27656 | tf_op jit(solution)/shard_map/ppermute | solution.py:21
  23.5 3.1 %collective-permute-start.4 = (bf16[4,6,1,192]{3,2,1,0:T(2,128)(2,1)S(1)}, bf16[4,6,1,192]{3,2,1,0:T(2,128)(2,1)S(1)}, u32[]{:S(2)}, u32[]{:S(2)}) collective-permute-start(bf16[4,6,1,192]{3,2,1,0:T(2,128)(2,1)S(1)} %get-tuple-element.53), channel_id=1, source_target_pairs={{1,0},{3,2},{5,4},{7,6},{9,8},{11,10},{13,12},{15,14},{17,16},{19,... | collective-permute-start | bytes 27656 | tf_op jit(solution)/shard_map/ppermute | solution.py:23
  41.5 2.8 %copy-start.3 = (f32[192]{0:T(256)S(1)}, f32[192]{0:T(256)}, u32[]{:S(2)}) copy-start(f32[192]{0:T(256)} %param.7) | copy-start | bytes 2308
  44.5 10.7 %collective-permute-start.5 = (bf16[2,4,64,192]{3,2,1,0:T(8,128)(2,1)S(1)}, bf16[2,4,64,192]{3,2,1,0:T(8,128)(2,1)S(1)}, u32[]{:S(2)}, u32[]{:S(2)}) collective-permute-start(bf16[2,4,64,192]{3,2,1,0:T(8,128)(2,1)S(1)} %multiply_convert_fusion.1), channel_id=1, source_target_pairs={{0,4},{4,8},{8,12},{1,5},{5,9},{9,13},{2,6},{6,10},{10,14},{3,7},{... | collective-permute-start | bytes 589832 | tf_op jit(solution)/shard_map/ppermute | solution.py:10
  55.3 4.9 %collective-permute-start.6 = (bf16[4,1,64,192]{3,2,1,0:T(8,128)(2,1)S(1)}, bf16[4,1,64,192]{3,2,1,0:T(8,128)(2,1)S(1)}, u32[]{:S(2)}, u32[]{:S(2)}) collective-permute-start(bf16[4,1,64,192]{3,2,1,0:T(8,128)(2,1)S(1)} %get-tuple-element.69), channel_id=1, source_target_pairs={{0,2},{1,3},{4,6},{5,7},{8,10},{9,11},{12,14},{13,15},{16,18},{17,... | collective-permute-start | bytes 294920 | tf_op jit(solution)/shard_map/ppermute | solution.py:21
  57.5 6.9 %collective-permute-start.7 = (bf16[4,1,64,192]{3,2,1,0:T(8,128)(2,1)S(1)}, bf16[4,1,64,192]{3,2,1,0:T(8,128)(2,1)S(1)}, u32[]{:S(2)}, u32[]{:S(2)}) collective-permute-start(bf16[4,1,64,192]{3,2,1,0:T(8,128)(2,1)S(1)} %get-tuple-element.70), channel_id=1, source_target_pairs={{2,0},{3,1},{6,4},{7,5},{10,8},{11,9},{14,12},{15,13},{18,16},{19,... | collective-permute-start | bytes 294920 | tf_op jit(solution)/shard_map/ppermute | solution.py:23
  65.6 3.5 %collective-permute-start.8 = (bf16[4,6,1,192]{3,2,1,0:T(2,128)(2,1)S(1)}, bf16[4,6,1,192]{3,2,1,0:T(2,128)(2,1)S(1)}, u32[]{:S(2)}, u32[]{:S(2)}) collective-permute-start(bf16[4,6,1,192]{3,2,1,0:T(2,128)(2,1)S(1)} %get-tuple-element.50), channel_id=1, source_target_pairs={{0,1},{2,3},{4,5},{6,7},{8,9},{10,11},{12,13},{14,15},{16,17},{18,... | collective-permute-start | bytes 27656 | tf_op jit(solution)/shard_map/ppermute | solution.py:21
  66.9 3.1 %collective-permute-start.9 = (bf16[4,6,1,192]{3,2,1,0:T(2,128)(2,1)S(1)}, bf16[4,6,1,192]{3,2,1,0:T(2,128)(2,1)S(1)}, u32[]{:S(2)}, u32[]{:S(2)}) collective-permute-start(bf16[4,6,1,192]{3,2,1,0:T(2,128)(2,1)S(1)} %get-tuple-element.49), channel_id=1, source_target_pairs={{1,0},{3,2},{5,4},{7,6},{9,8},{11,10},{13,12},{15,14},{17,16},{19,... | collective-permute-start | bytes 27656 | tf_op jit(solution)/shard_map/ppermute | solution.py:23
  76.3 2.7 %copy-start.1 = (bf16[2,4,64,192]{3,2,1,0:T(8,128)(2,1)S(1)}, bf16[2,4,64,192]{3,2,1,0:T(8,128)(2,1)}, u32[]{:S(2)}) copy-start(bf16[2,4,64,192]{3,2,1,0:T(8,128)(2,1)} %get-tuple-element.12) | copy-start | bytes 589828
  84.4 2.8 %copy-start = (f32[512,192]{0,1:T(8,128)S(1)}, f32[512,192]{0,1:T(8,128)}, u32[]{:S(2)}) copy-start(f32[512,192]{0,1:T(8,128)} %fusion.17) | copy-start | bytes 1179652
  87.3 3.8 %copy-start.4 = (f32[192]{0:T(256)S(1)}, f32[192]{0:T(256)}, u32[]{:S(2)}) copy-start(f32[192]{0:T(256)} %param.9) | copy-start | bytes 2308
where the time goes:
time: 93.4 us; the launch traced here: 92 us
  local copies, waits for them, and re-layouts  33.8 us (36%)
  starting transfers between devices  22.6 us (24%)
  waiting for transfers between devices  18.3 us (20%)
  matrix products  13.3 us (14%)
  other arithmetic  3.8 us (4%)
    concatenate x6, local copies, waits for them, and re-layouts, tap_block(): return jnp.concatenate(pieces, axis=-1).reshape(count * rows * cols, -1)  16.8 us
    dot_general x6, matrix products, conv_layer(): jnp.dot(tap_block(padded[offset_t:offset_t + frames], rows, cols), flat_w...  13.3 us
    ppermute x2, starting transfers between devices, from_behind(): return lax.ppermute(x, axis, pairs)  9.23 us
    ppermute x2, waiting for transfers between devices, from_behind(): return lax.ppermute(x, axis, pairs)  9.06 us
    ppermute x4, starting transfers between devices, with_halo(): lax.ppermute(tail, axis, [(i, (i + 1) % count) for i in range(ends)])  8.17 us
    ppermute x4, waiting for transfers between devices, with_halo(): lax.ppermute(head, axis, [((i + 1) % count, i) for i in range(ends)])  7.85 us
    slice x5, local copies, waits for them, and re-layouts, tap_block(): block[:, offset_y:offset_y + rows, offset_x:offset_x + cols]  7 us
    slice x2, local copies, waits for them, and re-layouts, conv_layer(): flat_weight[offset_t]  6.35 us
  transfers between devices with their start and end apart: 10, of which 7 were waited for; matrix products, arithmetic and copies ran while one was open for 9% of the time, Pallas kernels for 0%

commit v1 on v0

v1 whole, which is shorter than its diff:
```python
import functools

import jax
import jax.numpy as jnp
from jax import lax
from jax.experimental import pallas as pl
from jax.experimental.pallas import tpu as pltpu
from jax.sharding import PartitionSpec as P

LANES = 128
TILE = 16
EPS = 1e-06


def exchange(first, last, axis, offset=0):
    count = lax.axis_size(axis)
    steps = lax.axis_size("frame")

    def move(x, pairs):
        if offset == 0:
            return lax.ppermute(x, axis, pairs)
        both = [(f * count + i, (f + offset) * count + j) for f in range(steps - offset) for i, j in pairs]
        return lax.ppermute(x, ("frame", axis), both)

    if count == 2:
        facing = jnp.where(lax.axis_index(axis) == 0, last, first)
        return (move(facing, [(0, 1), (1, 0)]),)
    return (
        move(last, [(i, i + 1) for i in range(count - 1)]),
        move(first, [(i + 1, i) for i in range(count - 1)]),
    )


def fill(lo, pairs, stacked, frame, row, cols, cells):
    n_rows = cells.shape[0]
    at = pl.ds(row, n_rows)
    low, high = cells[:, :, :LANES], cells[:, :, LANES:]
    rest = high.shape[-1]
    lo[frame, at, cols, :] = low
    pairs[frame, pl.ds(row + 1, n_rows), cols, :rest] = high
    pairs[frame, at, cols, rest:] = high
    if frame < stacked.shape[0]:
        stacked[frame, at, cols, :rest] = high
    if frame > 0:
        stacked[frame - 1, at, cols, rest:] = high


def columns(taps, lo, pairs, stacked, row, rows):
    def flat(block):
        return block.reshape(-1, LANES)

    pieces = [flat(lo[f, pl.ds(row + b, rows)]) for f, _ in taps for b in range(3)]
    pieces += [flat(pairs[f, pl.ds(row + 1, rows)]) for f, _ in taps]
    for k in range(0, len(taps), 2):
        f = taps[k][0]
        if k + 1 < len(taps):
            pieces.append(flat(stacked[f, pl.ds(row + 2, rows)]))
        else:
            pieces.append(flat(pairs[f, pl.ds(row + 3, rows)]))
    return jnp.concatenate(pieces, axis=-1)


def planes(taps, weight, c):
    pieces = [weight[a, b, c, :LANES, :] for _, a in taps for b in range(3)]
    for _, a in taps:
        pieces += [weight[a, 0, c, LANES:, :], weight[a, 1, c, LANES:, :]]
    for _, a in taps:
        pieces.append(weight[a, 2, c, LANES:, :])
    if len(taps) % 2:
        pieces.append(jnp.zeros_like(weight[0, 0, 0, LANES:, :]))
    return jnp.concatenate(pieces, axis=0)


def convolve(taps, weight, lefts):
    return [
        jnp.dot(lefts, planes(taps, weight, c), preferred_element_type=jnp.float32)
        for c in range(3)
    ]


def join(products, start, width):
    before, middle, after = [p[start : start + width] for p in products]
    return pltpu.roll(before, 1, 0) + middle + pltpu.roll(after, width - 1, 0)


def activate(y, gains):
    mean_square = jnp.sum(y * y, axis=-1, keepdims=True) * (1.0 / y.shape[-1])
    v = y * lax.rsqrt(mean_square + EPS) * gains
    return v / (1.0 + jnp.exp(-v))


def keep_halo(cells, slabs, side):
    at = lax.broadcasted_iota(jnp.int32, cells.shape, cells.ndim - 2)
    if side is None:
        side = 1 - lax.axis_index("slab")
    begin, end = jnp.where(side == 1, 0, TILE - 2), jnp.where(side == 1, 2, TILE)
    wanted = (at >= begin) & (at < end)
    return jnp.where(wanted, cells.astype(jnp.float32), 0.0).astype(cells.dtype)


def first_kernel(strips, slabs, n_rows_h, *refs):
    n_strip = 1 if strips == 2 else 2
    n_slab = 1 if slabs == 2 else 2
    refs = list(refs)

    def take(n):
        got = refs[:n]
        del refs[:n]
        return got

    (own, prev) = take(2)
    own_rows, prev_rows = take(n_strip), take(n_strip)
    own_cols, prev_cols = take(n_slab), take(n_slab)
    w1, gains, w2 = take(3)
    h_lo, h_pairs, h_stacked, partial = take(4)
    lo, pairs, stacked = take(3)

    frames, rows, cols, channels = own.shape
    width = cols + TILE
    strip, slab = lax.axis_index("strip"), lax.axis_index("slab")

    for buffer in (lo, pairs, stacked):
        buffer[...] = jnp.zeros_like(buffer)

    def tiles(received, f, k):
        if slabs == 2:
            return keep_halo(received[0][f, k], slabs, None)
        return keep_halo(received[0][f, k], slabs, 0) + keep_halo(received[1][f, k], slabs, 1)

    every = slice(0, cols)
    edge = slice(cols, width)
    for source, source_rows, source_cols, base, skip in (
        (prev, prev_rows, prev_cols, 0, frames - 2),
        (own, own_rows, own_cols, 2, 0),
    ):
        for f in range(skip, frames):
            at = base + f - skip
            fill(lo, pairs, stacked, at, 2, every, source[f])
            fill(lo, pairs, stacked, at, 2, edge, tiles(source_cols, f, slice(None)))
            if strips == 2:
                places = [(source_rows[0], jnp.where(strip == 0, rows + 2, 0))]
            else:
                places = [(source_rows[0], 0), (source_rows[1], rows + 2)]
            for received, row in places:
                fill(lo, pairs, stacked, at, row, every, received[f, :, :cols])
                if slabs == 2:
                    corner = keep_halo(received[f, :, cols:], slabs, None)
                else:
                    corner = received[f, :, cols:]
                fill(lo, pairs, stacked, at, row, edge, corner)

    origin = jnp.where(strip == 0, 1, 0) if strips == 2 else 0
    lefts = jnp.concatenate(
        [
            columns([(t, 0), (t + 1, 1), (t + 2, 2)], lo, pairs, stacked, origin, n_rows_h)
            for t in range(frames)
        ],
        axis=0,
    )
    products = convolve([(0, 0), (1, 1), (2, 2)], w1, lefts)

    for buffer in (h_lo, h_pairs, h_stacked):
        buffer[...] = jnp.zeros_like(buffer)
    gain = gains[...]
    position = lax.broadcasted_iota(jnp.int32, (width, 1), 0)
    right, left = jnp.where(slab < slabs - 1, cols + 1, cols), jnp.where(slab > 0, width - 1, width)
    inside = (position < right) | (position >= left)
    for t in range(frames):
        for r in range(n_rows_h):
            h = activate(join(products, (t * n_rows_h + r) * width, width), gain)
            h = jnp.where(inside, h, 0.0)
            if strips != 2 and r == 0:
                h = h * jnp.where(strip > 0, 1.0, 0.0)
            if strips != 2 and r == n_rows_h - 1:
                h = h * jnp.where(strip < strips - 1, 1.0, 0.0)
            h = h.astype(jnp.bfloat16)
            fill(h_lo, h_pairs, h_stacked, t, origin + r, slice(0, width), h[None])

    last = frames - 1
    for t, taps in enumerate(([(last - 1, 0), (last, 1)], [(last, 0)])):
        lefts = columns(taps, h_lo, h_pairs, h_stacked, 0, rows)
        products = convolve(taps, w2, lefts)
        for r in range(rows):
            y = join(products, r * width, width)[:cols].astype(jnp.bfloat16)
            rest = channels - LANES
            partial[t, r] = y[:, :LANES]
            half = r % 2
            partial[t, rows + r // 2, :, half * rest : (half + 1) * rest] = y[:, LANES:]


def second_kernel(frames, rows, cols, h_lo, h_pairs, h_stacked, w2, out):
    width = cols + TILE
    for t in range(frames):
        taps = [(f, f - t + 2) for f in range(max(0, t - 2), t + 1)]
        products = convolve(taps, w2, columns(taps, h_lo, h_pairs, h_stacked, 0, rows))
        for r in range(rows):
            out[t, r] = join(products, r * width, width)[:cols]


def third_kernel(partial, own, gains, out):
    frames, rows, cols, channels = out.shape
    rest = channels - LANES
    gain = gains[...]
    for t in range(frames):
        for r in range(rows):
            y = own[t, r]
            if t < 2:
                half = r % 2
                high = partial[t, rows + r // 2, :, half * rest : (half + 1) * rest]
                sent = jnp.concatenate([partial[t, r], high], axis=-1)
                y = y + sent.astype(jnp.float32)
            out[t, r] = activate(y, gain).astype(jnp.bfloat16)


def in_vmem(n):
    return [pl.BlockSpec(memory_space=pltpu.VMEM)] * n


def forward(x):
    steps = lax.axis_size("frame")
    return lax.ppermute(x, "frame", [(i, i + 1) for i in range(steps - 1)])


def shards(frames_in, weight_first, scale_first, weight_second, scale_second):
    frames, rows, cols, channels = frames_in.shape
    strips, slabs = lax.axis_size("strip"), lax.axis_size("slab")
    width = cols + TILE
    n_rows_h = rows + 1 if strips == 2 else rows + 2
    gain_first, gain_second = scale_first[None], scale_second[None]
    weight_first = pltpu.with_memory_space_constraint(weight_first, pltpu.VMEM)
    weight_second = pltpu.with_memory_space_constraint(weight_second, pltpu.VMEM)

    def edge_cols(x):
        return exchange(x[:, :, :TILE], x[:, :, cols - TILE :], "slab")

    prev = forward(frames_in)
    own_cols = edge_cols(frames_in)

    def wide(rows_of, at):
        if slabs == 2:
            tile = own_cols[0][:, at]
        else:
            spot = lax.broadcasted_iota(jnp.int32, (1, 1, TILE, 1), 2)
            tile = jnp.where(spot < 2, own_cols[1][:, at], jnp.where(spot >= TILE - 2, own_cols[0][:, at], 0))
        return jnp.concatenate([rows_of[:, at], tile], axis=2)

    top, bottom = wide(frames_in, slice(0, 2)), wide(frames_in, slice(rows - 2, rows))
    own_rows = exchange(top, bottom, "strip")
    prev_rows = exchange(top, bottom, "strip", 1)
    prev_cols = edge_cols(prev)

    h_shapes = [
        jax.ShapeDtypeStruct((frames, rows + 2, width, LANES), jnp.bfloat16),
        jax.ShapeDtypeStruct((frames, rows + 3, width, LANES), jnp.bfloat16),
        jax.ShapeDtypeStruct((frames - 1, rows + 2, width, LANES), jnp.bfloat16),
    ]
    ins = [frames_in, prev, *own_rows, *prev_rows, *own_cols, *prev_cols, weight_first, gain_first, weight_second]
    h_lo, h_pairs, h_stacked, partial = pl.pallas_call(
        functools.partial(first_kernel, strips, slabs, n_rows_h),
        out_shape=h_shapes + [jax.ShapeDtypeStruct((2, rows + rows // 2, cols, LANES), jnp.bfloat16)],
        in_specs=in_vmem(len(ins)),
        out_specs=in_vmem(4),
        scratch_shapes=[
            pltpu.VMEM((frames + 2, rows + 4, width, LANES), jnp.bfloat16),
            pltpu.VMEM((frames + 2, rows + 5, width, LANES), jnp.bfloat16),
            pltpu.VMEM((frames + 1, rows + 4, width, LANES), jnp.bfloat16),
        ],
        compiler_params=pltpu.CompilerParams(vmem_limit_bytes=32 * 1024 * 1024),
        name="first_layer",
    )(*ins)
    sent = forward(partial)
    taps = frames * rows * cols * 27 * channels * channels
    own = pl.pallas_call(
        functools.partial(second_kernel, frames, rows, cols),
        out_shape=jax.ShapeDtypeStruct((frames, rows, cols, channels), jnp.float32),
        in_specs=in_vmem(4),
        out_specs=in_vmem(1)[0],
        compiler_params=pltpu.CompilerParams(vmem_limit_bytes=32 * 1024 * 1024),
        cost_estimate=pl.CostEstimate(flops=taps, bytes_accessed=4 * 1024 * 1024, transcendentals=0),
        name="second_layer",
    )(h_lo, h_pairs, h_stacked, weight_second)
    return pl.pallas_call(
        third_kernel,
        out_shape=jax.ShapeDtypeStruct((frames, rows, cols, channels), jnp.bfloat16),
        in_specs=in_vmem(3),
        out_specs=in_vmem(1)[0],
        compiler_params=pltpu.CompilerParams(vmem_limit_bytes=32 * 1024 * 1024),
        name="finish",
    )(sent, own, gain_second)


def solution(mesh):
    return jax.shard_map(
        shards,
        mesh=mesh,
        in_specs=(P(("groups", "frame"), "strip", "slab", None), P(), P(), P(), P()),
        out_specs=P(("groups", "frame"), "strip", "slab", None),
        check_vma=False,
    )
```

time: 93.4 us -> 40 us (0.43); the launches traced: 92 us -> 39.7 us
  local copies, waits for them, and re-layouts: 33.8 us -> 6.13 us
  matrix products: 13.3 us -> 0 us
  waiting for transfers between devices: 18.3 us -> 8.82 us
  Pallas kernels: 0 us -> 7.84 us
  starting transfers between devices: 22.6 us -> 15.8 us
  other arithmetic: 3.8 us -> 0.95 us
    concatenate x7 -> x0, local copies, waits for them, and re-layouts: 17.9 us -> none  [the longest x6 16.8 us: tap_block(): return jnp.concatenate(pieces, axis=-1).reshape(count * rows * cols, -1)]
    dot_general x6 -> x0, matrix products: 13.3 us -> none  [conv_layer(): jnp.dot(tap_block(padded[offset_t:offset_t + frames], rows, cols), flat_w...]
    slice x8 -> x2, local copies, waits for them, and re-layouts: 13.4 us -> 1 us  [the longest x1 0.99 us: wide(): return jnp.concatenate([rows_of[:, at], tile], axis=2)]
    ppermute x10 -> x6, waiting for transfers between devices: 18.3 us -> 8.82 us  [the longest x1 3.22 us: move(): return lax.ppermute(x, ('frame', axis), both)]
    pallas_call x0 -> x3, Pallas kernels: none -> 7.84 us  [the longest x1 5.57 us: shards(): pl.pallas_call(functools.partial(first_kernel, strips, slabs, n_rows_h),...]
    ppermute x10 -> x6, starting transfers between devices: 22.6 us -> 15.8 us  [the longest x2 10.7 us: forward(): return lax.ppermute(x, 'frame', [(i, i + 1) for i in range(steps - 1)])]
    unnamed x11 -> x12, local copies, waits for them, and re-layouts: 0.04 us -> 5.13 us
    concatenate x7 -> x0, other arithmetic: 2.6 us -> none  [the longest x6 2.56 us: with_halo(): jnp.concatenate([lax.ppermute(tail, axis, [(i, (i + 1) % count) for i in...]
  transfers between devices with their start and end apart: 10 -> 6, of which waited for: 7 -> 4; matrix products, arithmetic and copies ran while one was open for 9% -> 5% of each run, Pallas kernels for 0% -> 3%
where the time goes in v1:
time: 40 us; the launch traced here: 39.7 us
  starting transfers between devices  15.8 us (40%)
  waiting for transfers between devices  8.82 us (22%)
  Pallas kernels  7.84 us (20%)
  local copies, waits for them, and re-layouts  6.13 us (15%)
  other arithmetic  0.95 us (2%)
    ppermute x2, starting transfers between devices, forward(): return lax.ppermute(x, 'frame', [(i, i + 1) for i in range(steps - 1)])  10.7 us
    pallas_call x1, Pallas kernels, shards(): pl.pallas_call(functools.partial(first_kernel, strips, slabs, n_rows_h),...  5.57 us
    unnamed x12, local copies, waits for them, and re-layouts  5.13 us
    ppermute x1, starting transfers between devices, move(): return lax.ppermute(x, ('frame', axis), both)  4.41 us
    ppermute x1, waiting for transfers between devices, move(): return lax.ppermute(x, ('frame', axis), both)  3.22 us
    ppermute x2, waiting for transfers between devices, forward(): return lax.ppermute(x, 'frame', [(i, i + 1) for i in range(steps - 1)])  3.11 us
    ppermute x3, waiting for transfers between devices, move(): return lax.ppermute(x, axis, pairs)  2.49 us
    pallas_call x1, Pallas kernels, shards(): pl.pallas_call(functools.partial(second_kernel, frames, rows, cols), out_...  1.19 us
  transfers between devices with their start and end apart: 6, of which 4 were waited for; matrix products, arithmetic and copies ran while one was open for 5% of the time, Pallas kernels for 3%

profile of v1, /device:TPU:0, one launch (start us, length us, event | category | flops | bytes accessed | tf_op | source)
XLA Modules:
  0.0 39.7 jit_solution(15579066593127027014)
XLA Ops:
  0.0 4.9 %collective-permute-start = (bf16[2,4,64,192]{3,2,1,0:T(8,128)(2,1)}, bf16[2,4,64,192]{3,2,1,0:T(8,128)(2,1)S(1)}, u32[]{:S(2)}, u32[]{:S(2)}) collective-permute-start(bf16[2,4,64,192]{3,2,1,0:T(8,128)(2,1)} %refs_0_.1), channel_id=1, source_target_pairs={{0,4},{4,8},{8,12},{1,5},{5,9},{9,13},{2,6},{6,10},{10,14},{3,7},{... | collective-permute-start | bytes 589832 | tf_op jit(solution)/shard_map/ppermute | solution.py:221
  4.9 0.9 %slice_select_fusion.1 = bf16[2,4,16,192]{3,2,1,0:T(8,128)(2,1)S(1)} fusion(bf16[2,4,64,192]{3,2,1,0:T(8,128)(2,1)} %refs_0_.1, pred[]{:T(512)S(6)} %eq.9), kind=kLoop, calls=%fused_computation.2 | loop fusion | flops 24576 | bytes 147457 | tf_op jit(solution)/shard_map/jit(_where)/select_n | solution.py:26
  5.8 0.1 collective-permute-start.1
  5.9 1.0 %fusion = (bf16[2,2,64,192]{3,2,1,0:T(8,128)(2,1)S(1)}, bf16[2,2,64,192]{3,2,1,0:T(8,128)(2,1)S(1)}) fusion(bf16[2,4,64,192]{3,2,1,0:T(8,128)(2,1)} %refs_0_.1), kind=kLoop, calls=%fused_computation.3 | loop fusion | bytes 393216 | tf_op jit(solution)/shard_map/slice | solution.py:245
  6.9 0.2 collective-permute-done.1.refs_4_
  7.2 0.1 maximum_select_fusion
  7.2 4.4 %collective-permute-start.3 = (bf16[2,2,80,192]{3,2,1,0:T(8,128)(2,1)S(1)}, bf16[2,2,80,192]{3,2,1,0:T(8,128)(2,1)S(1)}, u32[]{:S(2)}, u32[]{:S(2)}) collective-permute-start(bf16[2,2,80,192]{3,2,1,0:T(8,128)(2,1)S(1)} %maximum_select_fusion), channel_id=1, source_target_pairs={{0,6},{2,4},{4,10},{6,8},{8,14},{10,12},{1,7},{3,5},{5,11},{7,9},{... | collective-permute-start | bytes 368648 | tf_op jit(solution)/shard_map/ppermute | solution.py:23
  11.6 0.6 %collective-permute-start.2 = (bf16[2,2,80,192]{3,2,1,0:T(8,128)(2,1)S(1)}, bf16[2,2,80,192]{3,2,1,0:T(8,128)(2,1)S(1)}, u32[]{:S(2)}, u32[]{:S(2)}) collective-permute-start(bf16[2,2,80,192]{3,2,1,0:T(8,128)(2,1)S(1)} %maximum_select_fusion), channel_id=1, source_target_pairs={{0,2},{2,0},{1,3},{3,1},{4,6},{6,4},{5,7},{7,5},{8,10},{10,8},{9,1... | collective-permute-start | bytes 368648 | tf_op jit(solution)/shard_map/ppermute | solution.py:21
  12.2 0.0 collective-permute-done.refs_1_
  12.3 0.1 collective-permute-start.4
  12.3 3.2 %collective-permute-done.3.refs_3_ = bf16[2,2,80,192]{3,2,1,0:T(8,128)(2,1)S(1)} collective-permute-done((bf16[2,2,80,192]{3,2,1,0:T(8,128)(2,1)S(1)}, bf16[2,2,80,192]{3,2,1,0:T(8,128)(2,1)S(1)}, u32[]{:S(2)}, u32[]{:S(2)}) %collective-permute-start.3) | collective-permute-done | bytes 122912 | tf_op jit(solution)/shard_map/ppermute | solution.py:23
  15.6 2.3 %collective-permute-done.2.refs_2_ = bf16[2,2,80,192]{3,2,1,0:T(8,128)(2,1)S(1)} collective-permute-done((bf16[2,2,80,192]{3,2,1,0:T(8,128)(2,1)S(1)}, bf16[2,2,80,192]{3,2,1,0:T(8,128)(2,1)S(1)}, u32[]{:S(2)}, u32[]{:S(2)}) %collective-permute-start.2) | collective-permute-done | bytes 122912 | tf_op jit(solution)/shard_map/ppermute | solution.py:21
  17.8 0.0 collective-permute-done.4.refs_5_
  17.8 0.0 copy-start
  17.8 1.7 %copy-done = bf16[3,3,3,192,192]{4,3,2,1,0:T(8,128)(2,1)S(1)} copy-done((bf16[3,3,3,192,192]{4,3,2,1,0:T(8,128)(2,1)S(1)}, bf16[3,3,3,192,192]{4,3,2,1,0:T(8,128)(2,1)}, u32[]{:S(2)}) %copy-start) | copy-done | bytes 1990680
  19.6 0.0 copy-start.2
  19.6 1.7 %copy-done.2 = bf16[3,3,3,192,192]{4,3,2,1,0:T(8,128)(2,1)S(1)} copy-done((bf16[3,3,3,192,192]{4,3,2,1,0:T(8,128)(2,1)S(1)}, bf16[3,3,3,192,192]{4,3,2,1,0:T(8,128)(2,1)}, u32[]{:S(2)}) %copy-start.2) | copy-done | bytes 1990680
  21.3 0.0 copy-start.3
  21.3 0.9 %copy-done.3 = bf16[2,4,64,192]{3,2,1,0:T(8,128)(2,1)S(1)} copy-done((bf16[2,4,64,192]{3,2,1,0:T(8,128)(2,1)S(1)}, bf16[2,4,64,192]{3,2,1,0:T(8,128)(2,1)}, u32[]{:S(2)}) %copy-start.3) | copy-done | bytes 196632
  22.3 0.0 copy-start.5
  22.3 0.7 %copy-done.5 = f32[192]{0:T(256)S(1)} copy-done((f32[192]{0:T(256)S(1)}, f32[192]{0:T(256)}, u32[]{:S(2)}) %copy-start.5) | copy-done | bytes 792
  22.9 0.0 copy-start.1
  22.9 5.6 %first_layer.1 = (bf16[2,6,80,128]{3,2,1,0:T(8,128)(2,1)S(1)}, bf16[2,7,80,128]{3,2,1,0:T(8,128)(2,1)S(1)}, bf16[1,6,80,128]{3,2,1,0:T(8,128)(2,1)S(1)}, bf16[2,6,64,128]{3,2,1,0:T(8,128)(2,1)S(1)}) custom-call(bf16[2,4,64,192]{3,2,1,0:T(8,128)(2,1)S(1)} %copy-done.3, bf16[2,4,64,192]{3,2,1,0:T(8,128)(2,1)S(1)} %collective-permute-done.refs_1_, ...), custom_call_target="tpu_custom_call" | custom-call | tf_op jit(solution)/shard_map/first_layer/pallas_call | solution.py:258
  28.5 0.0 copy-start.4
  28.5 5.7 %collective-permute-start.5 = (bf16[2,6,64,128]{3,2,1,0:T(8,128)(2,1)S(1)}, bf16[2,6,64,128]{3,2,1,0:T(8,128)(2,1)S(1)}, u32[]{:S(2)}, u32[]{:S(2)}) collective-permute-start(bf16[2,6,64,128]{3,2,1,0:T(8,128)(2,1)S(1)} %get-tuple-element.9), channel_id=1, source_target_pairs={{0,4},{4,8},{8,12},{1,5},{5,9},{9,13},{2,6},{6,10},{10,14},{3,7},{... | collective-permute-start | bytes 589832 | tf_op jit(solution)/shard_map/ppermute | solution.py:221
  34.3 0.0 copy-done.1
  34.3 1.2 %second_layer.1.own = f32[2,4,64,192]{3,2,1,0:T(8,128)S(1)} custom-call(bf16[2,6,80,128]{3,2,1,0:T(8,128)(2,1)S(1)} %get-tuple-element.10.h_lo, bf16[2,7,80,128]{3,2,1,0:T(8,128)(2,1)S(1)} %get-tuple-element.11.h_pairs, bf16[1,6,80,128]{3,2,1,0:T(8,128)(2,1)S(1)} %get-tuple-element.12.h_stacked, bf16[3,3,3,192,192]{4,3,2,1,0:T(8,128)(2,1)S(1)} %copy-done.1), custom_call_target="tpu_custom_call" | custom-call | flops 509607936 | bytes 4194304 | tf_op jit(solution)/shard_map/second_layer/pallas_call | solution.py:273
  35.5 3.1 %collective-permute-done.5.partial = bf16[2,6,64,128]{3,2,1,0:T(8,128)(2,1)S(1)} collective-permute-done((bf16[2,6,64,128]{3,2,1,0:T(8,128)(2,1)S(1)}, bf16[2,6,64,128]{3,2,1,0:T(8,128)(2,1)S(1)}, u32[]{:S(2)}, u32[]{:S(2)}) %collective-permute-start.5) | collective-permute-done | bytes 196640 | tf_op jit(solution)/shard_map/ppermute | solution.py:221
  38.6 0.0 copy-done.4
  38.6 1.1 %finish.1 = bf16[2,4,64,192]{3,2,1,0:T(8,128)(2,1)} custom-call(bf16[2,6,64,128]{3,2,1,0:T(8,128)(2,1)S(1)} %collective-permute-done.5.partial, f32[2,4,64,192]{3,2,1,0:T(8,128)S(1)} %second_layer.1.own, f32[1,192]{1,0:T(1,128)S(1)} %bitcast.2), custom_call_target="tpu_custom_call" | custom-call | tf_op jit(solution)/shard_map/finish/pallas_call | solution.py:282
  (2 shorter events, 0.0 us)
Async XLA Ops:
  0.0 12.2 %collective-permute-start = (bf16[2,4,64,192]{3,2,1,0:T(8,128)(2,1)}, bf16[2,4,64,192]{3,2,1,0:T(8,128)(2,1)S(1)}, u32[]{:S(2)}, u32[]{:S(2)}) collective-permute-start(bf16[2,4,64,192]{3,2,1,0:T(8,128)(2,1)} %refs_0_.1), channel_id=1, source_target_pairs={{0,4},{4,8},{8,12},{1,5},{5,9},{9,13},{2,6},{6,10},{10,14},{3,7},{... | collective-permute-start | bytes 589832 | tf_op jit(solution)/shard_map/ppermute | solution.py:221
  5.8 1.3 %collective-permute-start.1 = (bf16[2,4,16,192]{3,2,1,0:T(8,128)(2,1)S(1)}, bf16[2,4,16,192]{3,2,1,0:T(8,128)(2,1)S(1)}, u32[]{:S(2)}, u32[]{:S(2)}) collective-permute-start(bf16[2,4,16,192]{3,2,1,0:T(8,128)(2,1)S(1)} %slice_select_fusion.1), channel_id=1, source_target_pairs={{0,1},{1,0},{2,3},{3,2},{4,5},{5,4},{6,7},{7,6},{8,9},{9,8},{10,11... | collective-permute-start | bytes 147464 | tf_op jit(solution)/shard_map/ppermute | solution.py:21
  7.2 8.3 %collective-permute-start.3 = (bf16[2,2,80,192]{3,2,1,0:T(8,128)(2,1)S(1)}, bf16[2,2,80,192]{3,2,1,0:T(8,128)(2,1)S(1)}, u32[]{:S(2)}, u32[]{:S(2)}) collective-permute-start(bf16[2,2,80,192]{3,2,1,0:T(8,128)(2,1)S(1)} %maximum_select_fusion), channel_id=1, source_target_pairs={{0,6},{2,4},{4,10},{6,8},{8,14},{10,12},{1,7},{3,5},{5,11},{7,9},{... | collective-permute-start | bytes 368648 | tf_op jit(solution)/shard_map/ppermute | solution.py:23
  11.6 6.2 %collective-permute-start.2 = (bf16[2,2,80,192]{3,2,1,0:T(8,128)(2,1)S(1)}, bf16[2,2,80,192]{3,2,1,0:T(8,128)(2,1)S(1)}, u32[]{:S(2)}, u32[]{:S(2)}) collective-permute-start(bf16[2,2,80,192]{3,2,1,0:T(8,128)(2,1)S(1)} %maximum_select_fusion), channel_id=1, source_target_pairs={{0,2},{2,0},{1,3},{3,1},{4,6},{6,4},{5,7},{7,5},{8,10},{10,8},{9,1... | collective-permute-start | bytes 368648 | tf_op jit(solution)/shard_map/ppermute | solution.py:21
  12.3 5.5 %collective-permute-start.4 = (bf16[2,4,16,192]{3,2,1,0:T(8,128)(2,1)S(1)}, bf16[2,4,16,192]{3,2,1,0:T(8,128)(2,1)S(1)}, u32[]{:S(2)}, u32[]{:S(2)}) collective-permute-start(bf16[2,4,16,192]{3,2,1,0:T(8,128)(2,1)S(1)} %slice_select_fusion), channel_id=1, source_target_pairs={{0,1},{1,0},{2,3},{3,2},{4,5},{5,4},{6,7},{7,6},{8,9},{9,8},{10,11... | collective-permute-start | bytes 147464 | tf_op jit(solution)/shard_map/ppermute | solution.py:21
  17.8 1.8 %copy-start = (bf16[3,3,3,192,192]{4,3,2,1,0:T(8,128)(2,1)S(1)}, bf16[3,3,3,192,192]{4,3,2,1,0:T(8,128)(2,1)}, u32[]{:S(2)}) copy-start(bf16[3,3,3,192,192]{4,3,2,1,0:T(8,128)(2,1)} %w2.1) | copy-start | bytes 5971972
  19.6 1.7 %copy-start.2 = (bf16[3,3,3,192,192]{4,3,2,1,0:T(8,128)(2,1)S(1)}, bf16[3,3,3,192,192]{4,3,2,1,0:T(8,128)(2,1)}, u32[]{:S(2)}) copy-start(bf16[3,3,3,192,192]{4,3,2,1,0:T(8,128)(2,1)} %refs_6_.1) | copy-start | bytes 5971972
  21.3 0.9 %copy-start.3 = (bf16[2,4,64,192]{3,2,1,0:T(8,128)(2,1)S(1)}, bf16[2,4,64,192]{3,2,1,0:T(8,128)(2,1)}, u32[]{:S(2)}) copy-start(bf16[2,4,64,192]{3,2,1,0:T(8,128)(2,1)} %refs_0_.1) | copy-start | bytes 589828
  22.3 0.7 %copy-start.5 = (f32[192]{0:T(256)S(1)}, f32[192]{0:T(256)}, u32[]{:S(2)}) copy-start(f32[192]{0:T(256)} %param.7) | copy-start | bytes 2308
  22.9 11.3 %copy-start.1 = (bf16[3,3,3,192,192]{4,3,2,1,0:T(8,128)(2,1)S(1)}, bf16[3,3,3,192,192]{4,3,2,1,0:T(8,128)(2,1)}, u32[]{:S(2)}) copy-start(bf16[3,3,3,192,192]{4,3,2,1,0:T(8,128)(2,1)} %w2.1) | copy-start | bytes 5971972
  28.5 10.1 %copy-start.4 = (f32[192]{0:T(256)S(1)}, f32[192]{0:T(256)}, u32[]{:S(2)}) copy-start(f32[192]{0:T(256)} %param.9) | copy-start | bytes 2308
  28.5 10.1 %collective-permute-start.5 = (bf16[2,6,64,128]{3,2,1,0:T(8,128)(2,1)S(1)}, bf16[2,6,64,128]{3,2,1,0:T(8,128)(2,1)S(1)}, u32[]{:S(2)}, u32[]{:S(2)}) collective-permute-start(bf16[2,6,64,128]{3,2,1,0:T(8,128)(2,1)S(1)} %get-tuple-element.9), channel_id=1, source_target_pairs={{0,4},{4,8},{8,12},{1,5},{5,9},{9,13},{2,6},{6,10},{10,14},{3,7},{... | collective-permute-start | bytes 589832 | tf_op jit(solution)/shard_map/ppermute | solution.py:221

commit v2 on v0

v2 whole, which is shorter than its diff:
```python
import functools

import jax
import jax.numpy as jnp
from jax import lax
from jax.experimental import pallas as pl
from jax.experimental.pallas import tpu as pltpu
from jax.sharding import PartitionSpec as P

LANES = 128
TILE = 16
EPS = 1e-06


HALO = 2


def swap(x, axis, offset=0):
    return shift(x, axis, [(0, 1), (1, 0)], offset)


def shift(x, axis, pairs, offset=0):
    if offset == 0:
        return lax.ppermute(x, axis, pairs)
    count, steps = lax.axis_size(axis), lax.axis_size("frame")
    both = [(f * count + i, (f + offset) * count + j) for f in range(steps - offset) for i, j in pairs]
    return lax.ppermute(x, ("frame", axis), both)


def forward(x):
    steps = lax.axis_size("frame")
    return lax.ppermute(x, "frame", [(i, i + 1) for i in range(steps - 1)])


class Packed:
    def __init__(self, frames, rows, cols):
        self.frames, self.rows, self.cols = frames, rows, cols
        self.high = frames * rows * cols
        self.beside = self.high + frames * (rows // 2) * cols
        self.tiles = -(-frames * rows * HALO // TILE)
        self.shape = (self.beside + 2 * self.tiles * TILE, LANES)

    def low_at(self, f, r):
        return slice((f * self.rows + r) * self.cols, (f * self.rows + r + 1) * self.cols)

    def high_at(self, f, r):
        start = self.high + (f * (self.rows // 2) + r // 2) * self.cols
        return slice(start, start + self.cols)

    def spot(self, f, r):
        cell = (f * self.rows + r) * HALO
        return cell // TILE, cell % TILE

    def beside_at(self, tile, high):
        start = self.beside + (2 * tile + high) * TILE
        return slice(start, start + TILE)

    def write(self, out, cells, tile_of):
        slab = lax.axis_index("slab")
        at = lax.broadcasted_iota(jnp.int32, (TILE, 1), 0)
        sums = [None] * self.tiles
        for f in range(self.frames):
            for r in range(self.rows):
                row = cells(f, r)
                out[self.low_at(f, r), :] = row[:, :LANES]
                rest = row.shape[-1] - LANES
                half = slice((r % 2) * rest, (r % 2 + 1) * rest)
                out[self.high_at(f, r), half] = row[:, LANES:]
                tile, place = self.spot(f, r)
                moved = pltpu.roll(tile_of(f, r).astype(jnp.float32), lax.rem(place + HALO * slab, TILE), 0)
                moved = jnp.where((at >= place) & (at < place + HALO), moved, 0.0)
                sums[tile] = moved if sums[tile] is None else sums[tile] + moved
        for tile, cells_beside in enumerate(sums):
            cells_beside = cells_beside.astype(jnp.bfloat16)
            out[self.beside_at(tile, 0), :] = cells_beside[:, :LANES]
            out[self.beside_at(tile, 1), :rest] = cells_beside[:, LANES:]

    def read(self, ref, f, r, rest):
        half = slice((r % 2) * rest, (r % 2 + 1) * rest)
        return ref[self.low_at(f, r), :], ref[self.high_at(f, r), half]

    def read_beside(self, ref, f, r, rest):
        slab = lax.axis_index("slab")
        tile, place = self.spot(f, r)
        parts = []
        for high, lanes in ((0, LANES), (1, rest)):
            cells = ref[self.beside_at(tile, high), :].astype(jnp.float32)
            cells = pltpu.roll(cells, lax.rem(2 * TILE - place - HALO * slab, TILE), 0)
            parts.append(only_beside(cells).astype(jnp.bfloat16)[:, :lanes])
        return parts


def only_beside(tile):
    slab = lax.axis_index("slab")
    at = lax.broadcasted_iota(jnp.int32, tile.shape, 0)
    begin = slab * (TILE - HALO)
    return jnp.where((at >= begin) & (at < begin + HALO), tile, 0.0)


def fill(lo, pairs, stacked, frame, row, cols, low, high):
    rest = high.shape[-1]
    lo[frame, row, cols, :] = low
    pairs[frame, row + 1, cols, :rest] = high
    pairs[frame, row, cols, rest:] = high
    if frame < stacked.shape[0]:
        stacked[frame, row, cols, :rest] = high
    if frame > 0:
        stacked[frame - 1, row, cols, rest:] = high


def columns(taps, lo, pairs, stacked, row, rows):
    def flat(block):
        return block.reshape(-1, LANES)

    pieces = [flat(lo[f, pl.ds(row + b, rows)]) for f, _ in taps for b in range(3)]
    pieces += [flat(pairs[f, pl.ds(row + 1, rows)]) for f, _ in taps]
    for k in range(0, len(taps), 2):
        f = taps[k][0]
        if k + 1 < len(taps):
            pieces.append(flat(stacked[f, pl.ds(row + 2, rows)]))
        else:
            pieces.append(flat(pairs[f, pl.ds(row + 3, rows)]))
    return jnp.concatenate(pieces, axis=-1)


def planes(taps, weight, c):
    pieces = [weight[a, b, c, :LANES, :] for _, a in taps for b in range(3)]
    for _, a in taps:
        pieces += [weight[a, 0, c, LANES:, :], weight[a, 1, c, LANES:, :]]
    for _, a in taps:
        pieces.append(weight[a, 2, c, LANES:, :])
    if len(taps) % 2:
        pieces.append(jnp.zeros_like(weight[0, 0, 0, LANES:, :]))
    return jnp.concatenate(pieces, axis=0)


def convolve(taps, weight, lefts):
    return [
        jnp.dot(lefts, planes(taps, weight, c), preferred_element_type=jnp.float32)
        for c in range(3)
    ]


def join(products, start, width):
    before, middle, after = [p[start : start + width] for p in products]
    return pltpu.roll(before, 1, 0) + middle + pltpu.roll(after, width - 1, 0)


def activate(y, gains):
    mean_square = jnp.sum(y * y, axis=-1, keepdims=True) * (1.0 / y.shape[-1])
    v = y * lax.rsqrt(mean_square + EPS) * gains
    return v / (1.0 + jnp.exp(-v))


def fetch_planes(source, target, arrived):
    copies = [pltpu.make_async_copy(source.at[a], target.at[a], arrived.at[a]) for a in range(3)]
    for copy in copies[::-1]:
        copy.start()
    waited = set()

    def wait(a):
        if a not in waited:
            copies[a].wait()
            waited.add(a)

    return wait


def clear(buffers):
    for buffer in buffers:
        buffer[...] = jnp.zeros_like(buffer)


def facing(strips, rows):
    if strips == 2:
        return [jnp.where(lax.axis_index("strip") == 0, rows - HALO, 0)]
    return [rows - HALO, 0]


def beyond(strips, rows):
    if strips == 2:
        return [jnp.where(lax.axis_index("strip") == 0, rows + HALO, 0)]
    return [0, rows + HALO]


def first_row(strips):
    return 1 - lax.axis_index("strip") if strips == 2 else 0


def beside_of(neighbour, f, r, cols):
    start = pl.multiple_of(lax.axis_index("slab") * (cols - TILE), TILE)
    return neighbour[f, r, pl.ds(start, TILE), :]


def pack_kernel(strips, own, neighbour, block, *edges):
    frames, rows, cols, _ = own.shape
    whole = Packed(HALO, rows, cols)
    skip = frames - HALO
    whole.write(block, lambda f, r: own[f + skip, r], lambda f, r: beside_of(neighbour, f + skip, r, cols))
    for start, edge in zip(facing(strips, rows), edges):
        Packed(frames, HALO, cols).write(
            edge, lambda f, r: own[f, start + r], lambda f, r: beside_of(neighbour, f, start + r, cols)
        )


def own_kernel(strips, n_rows_h, *refs):
    own, neighbour, *edges, weight_far, out, weight, lo, pairs, stacked, arrived = refs
    frames, rows, cols, channels = own.shape
    fetch = fetch_planes(weight_far, weight, arrived)
    width, rest = cols + TILE, channels - LANES
    every, beside = slice(0, cols), slice(cols, width)
    clear((lo, pairs, stacked))
    strip_block = Packed(frames, HALO, cols)
    for f in range(frames):
        for r in range(rows):
            cells = own[f, r]
            fill(lo, pairs, stacked, f, r + HALO, every, cells[:, :LANES], cells[:, LANES:])
            tile = only_beside(beside_of(neighbour, f, r, cols).astype(jnp.float32)).astype(jnp.bfloat16)
            fill(lo, pairs, stacked, f, r + HALO, beside, tile[:, :LANES], tile[:, LANES:])
        for edge, row in zip(edges, beyond(strips, rows)):
            for r in range(HALO):
                fill(lo, pairs, stacked, f, row + r, every, *strip_block.read(edge, f, r, rest))
                fill(lo, pairs, stacked, f, row + r, beside, *strip_block.read_beside(edge, f, r, rest))
    for t in range(frames):
        taps = [(f, f - t + 2) for f in range(max(0, t - 2), t + 1)]
        for _, a in taps:
            fetch(a)
        products = convolve(taps, weight, columns(taps, lo, pairs, stacked, first_row(strips), n_rows_h))
        for r in range(n_rows_h):
            out[t, r] = join(products, r * width, width)
    for a in range(3):
        fetch(a)


def first_kernel(strips, n_rows_h, rows, cols, *refs):
    block, *edges, own, w1, gains, w2_far, h_lo, h_pairs, h_stacked, partial, w2, lo, pairs, stacked, arrived = refs
    fetch = fetch_planes(w2_far, w2, arrived)
    frames, channels = own.shape[0], own.shape[-1]
    width, rest = cols + TILE, channels - LANES
    every, beside = slice(0, cols), slice(cols, width)
    strip, slab = lax.axis_index("strip"), lax.axis_index("slab")
    clear((lo, pairs, stacked, h_lo, h_pairs, h_stacked))
    whole, strip_block = Packed(HALO, rows, cols), Packed(frames, HALO, cols)
    for f in range(HALO):
        for r in range(rows):
            fill(lo, pairs, stacked, f, r + HALO, every, *whole.read(block, f, r, rest))
            fill(lo, pairs, stacked, f, r + HALO, beside, *whole.read_beside(block, f, r, rest))
        for edge, row in zip(edges, beyond(strips, rows)):
            for r in range(HALO):
                sent = frames - HALO + f
                fill(lo, pairs, stacked, f, row + r, every, *strip_block.read(edge, sent, r, rest))
                fill(lo, pairs, stacked, f, row + r, beside, *strip_block.read_beside(edge, sent, r, rest))

    origin = first_row(strips)
    gain = gains[...]
    position = lax.broadcasted_iota(jnp.int32, (width, 1), 0)
    right = cols + (slab == 0).astype(jnp.int32)
    left = width - (slab == 1).astype(jnp.int32)
    inside = (position < right) | (position >= left)
    for t in range(frames):
        taps = [(f, f - t) for f in range(t, HALO)]
        products = convolve(taps, w1, columns(taps, lo, pairs, stacked, origin, n_rows_h)) if taps else None
        for r in range(n_rows_h):
            y = own[t, r]
            if taps:
                y = y + join(products, r * width, width)
            h = jnp.where(inside, activate(y, gain), 0.0)
            if strips != 2 and r == 0:
                h = h * jnp.where(strip > 0, 1.0, 0.0)
            if strips != 2 and r == n_rows_h - 1:
                h = h * jnp.where(strip < strips - 1, 1.0, 0.0)
            h = h.astype(jnp.bfloat16)
            fill(h_lo, h_pairs, h_stacked, t, origin + r, slice(0, width), h[:, :LANES], h[:, LANES:])

    for a in range(3):
        fetch(a)
    last = frames - 1
    for t, taps in enumerate(([(last - 1, 0), (last, 1)], [(last, 0)])):
        products = convolve(taps, w2, columns(taps, h_lo, h_pairs, h_stacked, 0, rows))
        for r in range(rows):
            y = join(products, r * width, width)[:cols].astype(jnp.bfloat16)
            partial[t, r] = y[:, :LANES]
            half = r % 2
            partial[t, rows + r // 2, :, half * rest : (half + 1) * rest] = y[:, LANES:]


def second_kernel(frames, rows, cols, h_lo, h_pairs, h_stacked, w2, out):
    width = cols + TILE
    for t in range(frames):
        taps = [(f, f - t + 2) for f in range(max(0, t - 2), t + 1)]
        products = convolve(taps, w2, columns(taps, h_lo, h_pairs, h_stacked, 0, rows))
        for r in range(rows):
            out[t, r] = join(products, r * width, width)[:cols]


def third_kernel(partial, own, gains, out):
    frames, rows, cols, channels = out.shape
    rest = channels - LANES
    gain = gains[...]
    for t in range(frames):
        for r in range(rows):
            y = own[t, r]
            if t < 2:
                half = r % 2
                high = partial[t, rows + r // 2, :, half * rest : (half + 1) * rest]
                sent = jnp.concatenate([partial[t, r], high], axis=-1)
                y = y + sent.astype(jnp.float32)
            out[t, r] = activate(y, gain).astype(jnp.bfloat16)


def in_vmem(n):
    return [pl.BlockSpec(memory_space=pltpu.VMEM)] * n


def call(kernel, name, ins, outs, scratch=(), flops=0, far=()):
    in_specs, ins = in_vmem(len(ins)), list(ins)
    for place in far:
        ins[place] = pltpu.with_memory_space_constraint(ins[place], pltpu.HBM)
        in_specs[place] = pl.BlockSpec(memory_space=pltpu.HBM)
    return pl.pallas_call(
        kernel,
        out_shape=outs,
        in_specs=in_specs,
        out_specs=in_vmem(len(outs)) if isinstance(outs, list) else in_vmem(1)[0],
        scratch_shapes=[pltpu.VMEM(shape, jnp.bfloat16) for shape in scratch]
        + [pltpu.SemaphoreType.DMA((3,))] * len(far),
        compiler_params=pltpu.CompilerParams(vmem_limit_bytes=24 * 1024 * 1024),
        cost_estimate=pl.CostEstimate(flops=flops, bytes_accessed=4 * 1024 * 1024, transcendentals=0),
        name=name,
    )(*ins)


def block_scratch(frames, rows, width):
    return [(frames, rows, width, LANES), (frames, rows + 1, width, LANES), (frames - 1, rows, width, LANES)]


def shards(frames_in, weight_first, scale_first, weight_second, scale_second):
    frames, rows, cols, channels = frames_in.shape
    strips = lax.axis_size("strip")
    width = cols + TILE
    n_rows_h = rows + 1 if strips == 2 else rows + 2
    flops = frames * rows * cols * 27 * channels * channels
    bf16 = functools.partial(jax.ShapeDtypeStruct, dtype=jnp.bfloat16)
    f32 = functools.partial(jax.ShapeDtypeStruct, dtype=jnp.float32)

    neighbour = swap(frames_in, "slab")
    edge_shape = bf16(Packed(frames, HALO, cols).shape)
    block, *edges = call(
        functools.partial(pack_kernel, strips),
        "pack",
        [frames_in, neighbour],
        [bf16(Packed(HALO, rows, cols).shape)] + [edge_shape] * (1 if strips == 2 else 2),
    )
    ups = [(i, i + 1) for i in range(strips - 1)]
    downs = [(i + 1, i) for i in range(strips - 1)]
    ways = [[(0, 1), (1, 0)]] if strips == 2 else [ups, downs]
    before = forward(block)
    own_edges = [shift(edge, "strip", way) for edge, way in zip(edges, ways)]
    before_edges = [shift(edge, "strip", way, 1) for edge, way in zip(edges, ways)]

    weight_shape = bf16(weight_first.shape)
    own, weight_first = call(
        functools.partial(own_kernel, strips, n_rows_h),
        "first_layer_own",
        [frames_in, neighbour, *own_edges, weight_first],
        [f32((frames, n_rows_h, width, channels)), weight_shape],
        block_scratch(frames, rows + 2 * HALO, width),
        flops,
        far=[-1],
    )
    h_shapes = [bf16(shape) for shape in block_scratch(frames, rows + 2, width)]
    h_lo, h_pairs, h_stacked, partial, weight_second = call(
        functools.partial(first_kernel, strips, n_rows_h, rows, cols),
        "first_layer",
        [before, *before_edges, own, weight_first, scale_first[None], weight_second],
        h_shapes + [bf16((HALO, rows + rows // 2, cols, LANES)), weight_shape],
        block_scratch(HALO, rows + 2 * HALO, width),
        flops,
        far=[-1],
    )
    sent = forward(partial)
    own = call(
        functools.partial(second_kernel, frames, rows, cols),
        "second_layer",
        [h_lo, h_pairs, h_stacked, weight_second],
        f32((frames, rows, cols, channels)),
        flops=flops,
    )
    return call(third_kernel, "finish", [sent, own, scale_second[None]], bf16((frames, rows, cols, channels)))


def solution(mesh):
    return jax.shard_map(
        shards,
        mesh=mesh,
        in_specs=(P(("groups", "frame"), "strip", "slab", None), P(), P(), P(), P()),
        out_specs=P(("groups", "frame"), "strip", "slab", None),
        check_vma=False,
    )
```

time: 93.4 us -> 29.8 us (0.32); the launches traced: 92 us -> 29.6 us
  local copies, waits for them, and re-layouts: 33.8 us -> 0.96 us
  waiting for transfers between devices: 18.3 us -> 3.33 us
  matrix products: 13.3 us -> 0 us
  Pallas kernels: 0 us -> 10.9 us
  starting transfers between devices: 22.6 us -> 14.3 us
  other arithmetic: 3.8 us -> 0 us
    concatenate x7 -> x0, local copies, waits for them, and re-layouts: 17.9 us -> none  [the longest x6 16.8 us: tap_block(): return jnp.concatenate(pieces, axis=-1).reshape(count * rows * cols, -1)]
    ppermute x10 -> x5, waiting for transfers between devices: 18.3 us -> 3.33 us  [the longest x2 1.95 us: forward(): return lax.ppermute(x, 'frame', [(i, i + 1) for i in range(steps - 1)])]
    slice x8 -> x0, local copies, waits for them, and re-layouts: 13.4 us -> none  [the longest x5 7 us: tap_block(): block[:, offset_y:offset_y + rows, offset_x:offset_x + cols]]
    dot_general x6 -> x0, matrix products: 13.3 us -> none  [conv_layer(): jnp.dot(tap_block(padded[offset_t:offset_t + frames], rows, cols), flat_w...]
    pallas_call x0 -> x5, Pallas kernels: none -> 10.9 us  [call(): pl.pallas_call(kernel, out_shape=outs, in_specs=in_specs, out_specs=in_vm...]
    ppermute x10 -> x5, starting transfers between devices: 22.6 us -> 14.3 us  [the longest x2 8.81 us: forward(): return lax.ppermute(x, 'frame', [(i, i + 1) for i in range(steps - 1)])]
    concatenate x7 -> x0, other arithmetic: 2.6 us -> none  [the longest x6 2.56 us: with_halo(): jnp.concatenate([lax.ppermute(tail, axis, [(i, (i + 1) % count) for i in...]
    add x2 -> x0, local copies, waits for them, and re-layouts: 2.38 us -> none  [conv_layer(): accumulated + jnp.dot(tap_block(padded[offset_t:offset_t + frames], rows,...]
  transfers between devices with their start and end apart: 10 -> 5, of which waited for: 7 -> 2; matrix products, arithmetic and copies ran while one was open for 9% -> 0% of each run, Pallas kernels for 0% -> 16%
where the time goes in v2:
time: 29.8 us; the launch traced here: 29.6 us
  starting transfers between devices  14.3 us (48%)
  Pallas kernels  10.9 us (37%)
  waiting for transfers between devices  3.33 us (11%)
  local copies, waits for them, and re-layouts  0.96 us (3%)
    pallas_call x5, Pallas kernels, call(): pl.pallas_call(kernel, out_shape=outs, in_specs=in_specs, out_specs=in_vm...  10.9 us
    ppermute x2, starting transfers between devices, forward(): return lax.ppermute(x, 'frame', [(i, i + 1) for i in range(steps - 1)])  8.81 us
    ppermute x1, starting transfers between devices, shift(): return lax.ppermute(x, ('frame', axis), both)  3.44 us
    ppermute x2, starting transfers between devices, shift(): return lax.ppermute(x, axis, pairs)  2.01 us
    ppermute x2, waiting for transfers between devices, forward(): return lax.ppermute(x, 'frame', [(i, i + 1) for i in range(steps - 1)])  1.95 us
    ppermute x2, waiting for transfers between devices, shift(): return lax.ppermute(x, axis, pairs)  1.38 us
    unnamed x6, local copies, waits for them, and re-layouts  0.96 us
  transfers between devices with their start and end apart: 5, of which 2 were waited for; matrix products, arithmetic and copies ran while one was open for 0% of the time, Pallas kernels for 16%

profile of v2, /device:TPU:0, one launch (start us, length us, event | category | flops | bytes accessed | tf_op | source)
XLA Modules:
  0.0 29.6 jit_solution(9528867066117150264)
XLA Ops:
  0.0 0.5 %collective-permute-start = (bf16[2,4,64,192]{3,2,1,0:T(8,128)(2,1)}, bf16[2,4,64,192]{3,2,1,0:T(8,128)(2,1)S(1)}, u32[]{:S(2)}, u32[]{:S(2)}) collective-permute-start(bf16[2,4,64,192]{3,2,1,0:T(8,128)(2,1)} %refs_0_.1), channel_id=1, source_target_pairs={{0,1},{1,0},{2,3},{3,2},{4,5},{5,4},{6,7},{7,6},{8,9},{9,8},{10,11... | collective-permute-start | bytes 589832 | tf_op jit(solution)/shard_map/ppermute | solution.py:24
  0.5 1.4 %collective-permute-done.neighbour.refs_1_ = bf16[2,4,64,192]{3,2,1,0:T(8,128)(2,1)S(1)} collective-permute-done((bf16[2,4,64,192]{3,2,1,0:T(8,128)(2,1)}, bf16[2,4,64,192]{3,2,1,0:T(8,128)(2,1)S(1)}, u32[]{:S(2)}, u32[]{:S(2)}) %collective-permute-start) | collective-permute-done | bytes 196640 | tf_op jit(solution)/shard_map/ppermute | solution.py:24
  1.8 0.0 copy-start
  1.8 0.9 %copy-done = bf16[2,4,64,192]{3,2,1,0:T(8,128)(2,1)S(1)} copy-done((bf16[2,4,64,192]{3,2,1,0:T(8,128)(2,1)S(1)}, bf16[2,4,64,192]{3,2,1,0:T(8,128)(2,1)}, u32[]{:S(2)}) %copy-start) | copy-done | bytes 196632
  2.8 0.0 copy-start.2
  2.8 0.1 pack.1
  2.9 4.9 %collective-permute-start.1 = (bf16[800,128]{1,0:T(8,128)(2,1)S(1)}, bf16[800,128]{1,0:T(8,128)(2,1)S(1)}, u32[]{:S(2)}, u32[]{:S(2)}) collective-permute-start(bf16[800,128]{1,0:T(8,128)(2,1)S(1)} %get-tuple-element.14), channel_id=1, source_target_pairs={{0,4},{4,8},{8,12},{1,5},{5,9},{9,13},{2,6},{6,10},{10,14},{3,7},{... | collective-permute-start | bytes 614408 | tf_op jit(solution)/shard_map/ppermute | solution.py:32
  7.8 1.6 %collective-permute-start.3 = (bf16[416,128]{1,0:T(8,128)(2,1)S(1)}, bf16[416,128]{1,0:T(8,128)(2,1)S(1)}, u32[]{:S(2)}, u32[]{:S(2)}) collective-permute-start(bf16[416,128]{1,0:T(8,128)(2,1)S(1)} %get-tuple-element.15), channel_id=1, source_target_pairs={{0,2},{2,0},{1,3},{3,1},{4,6},{6,4},{5,7},{7,5},{8,10},{10,8},{9,1... | collective-permute-start | bytes 319496 | tf_op jit(solution)/shard_map/ppermute | solution.py:24
  9.3 3.4 %collective-permute-start.2 = (bf16[416,128]{1,0:T(8,128)(2,1)S(1)}, bf16[416,128]{1,0:T(8,128)(2,1)S(1)}, u32[]{:S(2)}, u32[]{:S(2)}) collective-permute-start(bf16[416,128]{1,0:T(8,128)(2,1)S(1)} %get-tuple-element.15), channel_id=1, source_target_pairs={{0,6},{2,4},{4,10},{6,8},{8,14},{10,12},{1,7},{3,5},{5,11},{7,9},{... | collective-permute-start | bytes 319496 | tf_op jit(solution)/shard_map/ppermute | solution.py:27
  12.8 0.0 collective-permute-done.3.refs_2_
  12.8 3.5 %first_layer_own.1 = (f32[2,5,80,192]{3,2,1,0:T(8,128)S(1)}, bf16[3,3,3,192,192]{4,3,2,1,0:T(8,128)(2,1)S(1)}) custom-call(bf16[2,4,64,192]{3,2,1,0:T(8,128)(2,1)S(1)} %copy-done, bf16[2,4,64,192]{3,2,1,0:T(8,128)(2,1)S(1)} %collective-permute-done.neighbour.refs_1_, bf16[416,128]{1,0:T(8,128)(2,1)S(1)} %collective-permute-done.3.refs_2_, ...), custom_call_target="tpu_custom_call" | custom-call | flops 509607936 | bytes 4194304 | tf_op jit(solution)/shard_map/first_layer_own/pallas_call | solution.py:320
  16.3 0.0 collective-permute-done.2.refs_1_
  16.3 0.0 collective-permute-done.1.refs_0_
  16.3 0.0 copy-done.2
  16.4 5.0 %first_layer.1 = (bf16[2,6,80,128]{3,2,1,0:T(8,128)(2,1)S(1)}, bf16[2,7,80,128]{3,2,1,0:T(8,128)(2,1)S(1)}, bf16[1,6,80,128]{3,2,1,0:T(8,128)(2,1)S(1)}, bf16[2,...) custom-call(bf16[800,128]{1,0:T(8,128)(2,1)S(1)} %collective-permute-done.1.refs_0_, ...), custom_call_target="tpu_custom_call" | custom-call | flops 509607936 | bytes 4194304 | tf_op jit(solution)/shard_map/first_layer/pallas_call | solution.py:320
  21.3 0.0 copy-start.1
  21.4 4.0 %collective-permute-start.4 = (bf16[2,6,64,128]{3,2,1,0:T(8,128)(2,1)S(1)}, bf16[2,6,64,128]{3,2,1,0:T(8,128)(2,1)S(1)}, u32[]{:S(2)}, u32[]{:S(2)}) collective-permute-start(bf16[2,6,64,128]{3,2,1,0:T(8,128)(2,1)S(1)} %get-tuple-element.18), channel_id=1, source_target_pairs={{0,4},{4,8},{8,12},{1,5},{5,9},{9,13},{2,6},{6,10},{10,14},{3,7},{... | collective-permute-start | bytes 589832 | tf_op jit(solution)/shard_map/ppermute | solution.py:32
  25.3 1.2 %second_layer.1.own = f32[2,4,64,192]{3,2,1,0:T(8,128)S(1)} custom-call(bf16[2,6,80,128]{3,2,1,0:T(8,128)(2,1)S(1)} %get-tuple-element.19.h_lo, bf16[2,7,80,128]{3,2,1,0:T(8,128)(2,1)S(1)} %get-tuple-element.20.h_pairs, bf16[1,6,80,128]{3,2,1,0:T(8,128)(2,1)S(1)} %get-tuple-element.21.h_stacked, bf16[3,3,3,192,192]{4,3,2,1,0:T(8,128)(2,1)S(1)} %get-tuple-element.22.w2), custom_call_target="tpu_custom_call" | custom-call | flops 509607936 | bytes 4194304 | tf_op jit(solution)/shard_map/second_layer/pallas_call | solution.py:320
  26.5 1.9 %collective-permute-done.4.partial = bf16[2,6,64,128]{3,2,1,0:T(8,128)(2,1)S(1)} collective-permute-done((bf16[2,6,64,128]{3,2,1,0:T(8,128)(2,1)S(1)}, bf16[2,6,64,128]{3,2,1,0:T(8,128)(2,1)S(1)}, u32[]{:S(2)}, u32[]{:S(2)}) %collective-permute-start.4) | collective-permute-done | bytes 196640 | tf_op jit(solution)/shard_map/ppermute | solution.py:32
  28.5 0.0 copy-done.1
  28.5 1.1 %finish.1 = bf16[2,4,64,192]{3,2,1,0:T(8,128)(2,1)} custom-call(bf16[2,6,64,128]{3,2,1,0:T(8,128)(2,1)S(1)} %collective-permute-done.4.partial, f32[2,4,64,192]{3,2,1,0:T(8,128)S(1)} %second_layer.1.own, f32[1,192]{1,0:T(1,128)S(1)} %bitcast.2), custom_call_target="tpu_custom_call" | custom-call | bytes 4194304 | tf_op jit(solution)/shard_map/finish/pallas_call | solution.py:320
Async XLA Ops:
  0.0 1.8 %collective-permute-start = (bf16[2,4,64,192]{3,2,1,0:T(8,128)(2,1)}, bf16[2,4,64,192]{3,2,1,0:T(8,128)(2,1)S(1)}, u32[]{:S(2)}, u32[]{:S(2)}) collective-permute-start(bf16[2,4,64,192]{3,2,1,0:T(8,128)(2,1)} %refs_0_.1), channel_id=1, source_target_pairs={{0,1},{1,0},{2,3},{3,2},{4,5},{5,4},{6,7},{7,6},{8,9},{9,8},{10,11... | collective-permute-start | bytes 589832 | tf_op jit(solution)/shard_map/ppermute | solution.py:24
  1.8 0.9 %copy-start = (bf16[2,4,64,192]{3,2,1,0:T(8,128)(2,1)S(1)}, bf16[2,4,64,192]{3,2,1,0:T(8,128)(2,1)}, u32[]{:S(2)}) copy-start(bf16[2,4,64,192]{3,2,1,0:T(8,128)(2,1)} %refs_0_.1) | copy-start | bytes 589828
  2.8 13.6 %copy-start.2 = (f32[192]{0:T(256)S(1)}, f32[192]{0:T(256)}, u32[]{:S(2)}) copy-start(f32[192]{0:T(256)} %param.7) | copy-start | bytes 2308
  2.9 13.4 %collective-permute-start.1 = (bf16[800,128]{1,0:T(8,128)(2,1)S(1)}, bf16[800,128]{1,0:T(8,128)(2,1)S(1)}, u32[]{:S(2)}, u32[]{:S(2)}) collective-permute-start(bf16[800,128]{1,0:T(8,128)(2,1)S(1)} %get-tuple-element.14), channel_id=1, source_target_pairs={{0,4},{4,8},{8,12},{1,5},{5,9},{9,13},{2,6},{6,10},{10,14},{3,7},{... | collective-permute-start | bytes 614408 | tf_op jit(solution)/shard_map/ppermute | solution.py:32
  7.8 5.0 %collective-permute-start.3 = (bf16[416,128]{1,0:T(8,128)(2,1)S(1)}, bf16[416,128]{1,0:T(8,128)(2,1)S(1)}, u32[]{:S(2)}, u32[]{:S(2)}) collective-permute-start(bf16[416,128]{1,0:T(8,128)(2,1)S(1)} %get-tuple-element.15), channel_id=1, source_target_pairs={{0,2},{2,0},{1,3},{3,1},{4,6},{6,4},{5,7},{7,5},{8,10},{10,8},{9,1... | collective-permute-start | bytes 319496 | tf_op jit(solution)/shard_map/ppermute | solution.py:24
  9.3 7.0 %collective-permute-start.2 = (bf16[416,128]{1,0:T(8,128)(2,1)S(1)}, bf16[416,128]{1,0:T(8,128)(2,1)S(1)}, u32[]{:S(2)}, u32[]{:S(2)}) collective-permute-start(bf16[416,128]{1,0:T(8,128)(2,1)S(1)} %get-tuple-element.15), channel_id=1, source_target_pairs={{0,6},{2,4},{4,10},{6,8},{8,14},{10,12},{1,7},{3,5},{5,11},{7,9},{... | collective-permute-start | bytes 319496 | tf_op jit(solution)/shard_map/ppermute | solution.py:27
  21.3 7.1 %copy-start.1 = (f32[192]{0:T(256)S(1)}, f32[192]{0:T(256)}, u32[]{:S(2)}) copy-start(f32[192]{0:T(256)} %param.9) | copy-start | bytes 2308
  21.4 7.1 %collective-permute-start.4 = (bf16[2,6,64,128]{3,2,1,0:T(8,128)(2,1)S(1)}, bf16[2,6,64,128]{3,2,1,0:T(8,128)(2,1)S(1)}, u32[]{:S(2)}, u32[]{:S(2)}) collective-permute-start(bf16[2,6,64,128]{3,2,1,0:T(8,128)(2,1)S(1)} %get-tuple-element.18), channel_id=1, source_target_pairs={{0,4},{4,8},{8,12},{1,5},{5,9},{9,13},{2,6},{6,10},{10,14},{3,7},{... | collective-permute-start | bytes 589832 | tf_op jit(solution)/shard_map/ppermute | solution.py:32

commit v3 on v2

--- a/solution.py
+++ b/solution.py
@@ -15,21 +15,24 @@
 HALO = 2
 
 
-def swap(x, axis, offset=0):
-    return shift(x, axis, [(0, 1), (1, 0)], offset)
-
-
-def shift(x, axis, pairs, offset=0):
-    if offset == 0:
-        return lax.ppermute(x, axis, pairs)
-    count, steps = lax.axis_size(axis), lax.axis_size("frame")
-    both = [(f * count + i, (f + offset) * count + j) for f in range(steps - offset) for i, j in pairs]
-    return lax.ppermute(x, ("frame", axis), both)
-
-
-def forward(x):
-    steps = lax.axis_size("frame")
-    return lax.ppermute(x, "frame", [(i, i + 1) for i in range(steps - 1)])
+def swap(x, axis):
+    return lax.ppermute(x, axis, [(0, 1), (1, 0)])
+
+
+def forward(x, way=None):
+    steps, count = lax.axis_size("frame"), lax.axis_size("strip")
+    way = [(i, i) for i in range(count)] if way is None else way
+    received = []
+    for parity in range(2):
+        there = [(f * count + i, (f + 1) * count + j) for f in range(parity, steps - 1, 2) for i, j in way]
+        received.append(lax.ppermute(x, ("frame", "strip"), there + [(j, i) for i, j in there]))
+    return received
+
+
+def by_parity(build, first, second):
+    odd = lax.rem(lax.axis_index("frame"), 2) == 1
+    pl.when(odd)(lambda: build(first))
+    pl.when(jnp.logical_not(odd))(lambda: build(second))
 
 
 class Packed:
@@ -124,13 +127,13 @@
 
 
 def planes(taps, weight, c):
-    pieces = [weight[a, b, c, :LANES, :] for _, a in taps for b in range(3)]
+    pieces = [weight[a][b, c, :LANES, :] for _, a in taps for b in range(3)]
     for _, a in taps:
-        pieces += [weight[a, 0, c, LANES:, :], weight[a, 1, c, LANES:, :]]
+        pieces += [weight[a][0, c, LANES:, :], weight[a][1, c, LANES:, :]]
     for _, a in taps:
-        pieces.append(weight[a, 2, c, LANES:, :])
+        pieces.append(weight[a][2, c, LANES:, :])
     if len(taps) % 2:
-        pieces.append(jnp.zeros_like(weight[0, 0, 0, LANES:, :]))
+        pieces.append(jnp.zeros_like(weight[a][0, c, LANES:, :]))
     return jnp.concatenate(pieces, axis=0)
 
 
@@ -152,20 +155,6 @@
     return v / (1.0 + jnp.exp(-v))
 
 
-def fetch_planes(source, target, arrived):
-    copies = [pltpu.make_async_copy(source.at[a], target.at[a], arrived.at[a]) for a in range(3)]
-    for copy in copies[::-1]:
-        copy.start()
-    waited = set()
-
-    def wait(a):
-        if a not in waited:
-            copies[a].wait()
-            waited.add(a)
-
-    return wait
-
-
 def clear(buffers):
     for buffer in buffers:
         buffer[...] = jnp.zeros_like(buffer)
@@ -190,6 +179,18 @@
 def beside_of(neighbour, f, r, cols):
     start = pl.multiple_of(lax.axis_index("slab") * (cols - TILE), TILE)
     return neighbour[f, r, pl.ds(start, TILE), :]
+
+
+def stage_kernel(own_far, weight_far, own, middle, last, arrived):
+    copies = [
+        pltpu.make_async_copy(own_far, own, arrived.at[0]),
+        pltpu.make_async_copy(weight_far.at[2], last, arrived.at[1]),
+        pltpu.make_async_copy(weight_far.at[1], middle, arrived.at[2]),
+    ]
+    for copy in copies:
+        copy.start()
+    for copy in copies:
+        copy.wait()
 
 
 def pack_kernel(strips, own, neighbour, block, *edges):
@@ -204,9 +205,12 @@
 
 
 def own_kernel(strips, n_rows_h, *refs):
-    own, neighbour, *edges, weight_far, out, weight, lo, pairs, stacked, arrived = refs
+    own, neighbour, *edges, middle, last, weight_far, out, plane, lo, pairs, stacked, arrived = refs
     frames, rows, cols, channels = own.shape
-    fetch = fetch_planes(weight_far, weight, arrived)
+    copy = pltpu.make_async_copy(weight_far.at[0], plane, arrived.at[0])
+    copy.start()
+    if frames > 2:
+        copy.wait()
     width, rest = cols + TILE, channels - LANES
     every, beside = slice(0, cols), slice(cols, width)
     clear((lo, pairs, stacked))
@@ -223,33 +227,41 @@
                 fill(lo, pairs, stacked, f, row + r, beside, *strip_block.read_beside(edge, f, r, rest))
     for t in range(frames):
         taps = [(f, f - t + 2) for f in range(max(0, t - 2), t + 1)]
-        for _, a in taps:
-            fetch(a)
-        products = convolve(taps, weight, columns(taps, lo, pairs, stacked, first_row(strips), n_rows_h))
+        products = convolve(taps, [plane, middle, last], columns(taps, lo, pairs, stacked, first_row(strips), n_rows_h))
         for r in range(n_rows_h):
             out[t, r] = join(products, r * width, width)
-    for a in range(3):
-        fetch(a)
+    if frames <= 2:
+        copy.wait()
 
 
 def first_kernel(strips, n_rows_h, rows, cols, *refs):
-    block, *edges, own, w1, gains, w2_far, h_lo, h_pairs, h_stacked, partial, w2, lo, pairs, stacked, arrived = refs
-    fetch = fetch_planes(w2_far, w2, arrived)
+    *refs, lo, pairs, stacked, arrived = refs
+    *refs, h_lo, h_pairs, h_stacked, partial, w2_first, w2_middle, w2_last = refs
+    *received, own, plane, middle, gains, w2_far = refs
+    w2 = [w2_first, w2_middle, w2_last]
+    copies = [pltpu.make_async_copy(w2_far.at[a], w2[a], arrived.at[a]) for a in range(3)]
+    for copy in copies:
+        copy.start()
     frames, channels = own.shape[0], own.shape[-1]
     width, rest = cols + TILE, channels - LANES
     every, beside = slice(0, cols), slice(cols, width)
     strip, slab = lax.axis_index("strip"), lax.axis_index("slab")
     clear((lo, pairs, stacked, h_lo, h_pairs, h_stacked))
     whole, strip_block = Packed(HALO, rows, cols), Packed(frames, HALO, cols)
-    for f in range(HALO):
-        for r in range(rows):
-            fill(lo, pairs, stacked, f, r + HALO, every, *whole.read(block, f, r, rest))
-            fill(lo, pairs, stacked, f, r + HALO, beside, *whole.read_beside(block, f, r, rest))
-        for edge, row in zip(edges, beyond(strips, rows)):
-            for r in range(HALO):
-                sent = frames - HALO + f
-                fill(lo, pairs, stacked, f, row + r, every, *strip_block.read(edge, sent, r, rest))
-                fill(lo, pairs, stacked, f, row + r, beside, *strip_block.read_beside(edge, sent, r, rest))
+
+    def build(pieces):
+        block, *edges = pieces
+        for f in range(HALO):
+            for r in range(rows):
+                fill(lo, pairs, stacked, f, r + HALO, every, *whole.read(block, f, r, rest))
+                fill(lo, pairs, stacked, f, r + HALO, beside, *whole.read_beside(block, f, r, rest))
+            for edge, row in zip(edges, beyond(strips, rows)):
+                for r in range(HALO):
+                    sent = frames - HALO + f
+                    fill(lo, pairs, stacked, f, row + r, every, *strip_block.read(edge, sent, r, rest))
+                    fill(lo, pairs, stacked, f, row + r, beside, *strip_block.read_beside(edge, sent, r, rest))
+
+    by_parity(build, received[0::2], received[1::2])
 
     origin = first_row(strips)
     gain = gains[...]
@@ -259,7 +271,7 @@
     inside = (position < right) | (position >= left)
     for t in range(frames):
         taps = [(f, f - t) for f in range(t, HALO)]
-        products = convolve(taps, w1, columns(taps, lo, pairs, stacked, origin, n_rows_h)) if taps else None
+        products = convolve(taps, [plane, middle], columns(taps, lo, pairs, stacked, origin, n_rows_h)) if taps else None
         for r in range(n_rows_h):
             y = own[t, r]
             if taps:
@@ -272,8 +284,8 @@
             h = h.astype(jnp.bfloat16)
             fill(h_lo, h_pairs, h_stacked, t, origin + r, slice(0, width), h[:, :LANES], h[:, LANES:])
 
-    for a in range(3):
-        fetch(a)
+    for copy in copies:
+        copy.wait()
     last = frames - 1
     for t, taps in enumerate(([(last - 1, 0), (last, 1)], [(last, 0)])):
         products = convolve(taps, w2, columns(taps, h_lo, h_pairs, h_stacked, 0, rows))
@@ -284,7 +296,8 @@
             partial[t, rows + r // 2, :, half * rest : (half + 1) * rest] = y[:, LANES:]
 
 
-def second_kernel(frames, rows, cols, h_lo, h_pairs, h_stacked, w2, out):
+def second_kernel(frames, rows, cols, h_lo, h_pairs, h_stacked, *refs):
+    *w2, out = refs
     width = cols + TILE
     for t in range(frames):
         taps = [(f, f - t + 2) for f in range(max(0, t - 2), t + 1)]
@@ -293,37 +306,43 @@
             out[t, r] = join(products, r * width, width)[:cols]
 
 
-def third_kernel(partial, own, gains, out):
+def finish_kernel(first, second, own, gains, out_far, out, left):
     frames, rows, cols, channels = out.shape
     rest = channels - LANES
     gain = gains[...]
-    for t in range(frames):
-        for r in range(rows):
-            y = own[t, r]
-            if t < 2:
-                half = r % 2
-                high = partial[t, rows + r // 2, :, half * rest : (half + 1) * rest]
-                sent = jnp.concatenate([partial[t, r], high], axis=-1)
-                y = y + sent.astype(jnp.float32)
-            out[t, r] = activate(y, gain).astype(jnp.bfloat16)
-
-
-def in_vmem(n):
-    return [pl.BlockSpec(memory_space=pltpu.VMEM)] * n
-
-
-def call(kernel, name, ins, outs, scratch=(), flops=0, far=()):
-    in_specs, ins = in_vmem(len(ins)), list(ins)
+
+    def build(partial):
+        for t in range(frames):
+            for r in range(rows):
+                y = own[t, r]
+                if t < HALO:
+                    half = r % 2
+                    high = partial[t, rows + r // 2, :, half * rest : (half + 1) * rest]
+                    sent = jnp.concatenate([partial[t, r], high], axis=-1)
+                    y = y + sent.astype(jnp.float32)
+                out[t, r] = activate(y, gain).astype(jnp.bfloat16)
+            copies[t].start()
+
+    copies = [pltpu.make_async_copy(out.at[t], out_far.at[t], left.at[t]) for t in range(frames)]
+    by_parity(build, first, second)
+    for copy in copies:
+        copy.wait()
+
+
+def call(kernel, name, ins, outs, scratch=(), semaphores=0, flops=0, far=(), far_out=False):
+    near, away = pl.BlockSpec(memory_space=pltpu.VMEM), pl.BlockSpec(memory_space=pltpu.HBM)
+    in_specs, ins = [near] * len(ins), list(ins)
     for place in far:
         ins[place] = pltpu.with_memory_space_constraint(ins[place], pltpu.HBM)
-        in_specs[place] = pl.BlockSpec(memory_space=pltpu.HBM)
+        in_specs[place] = away
+    one = not isinstance(outs, list)
     return pl.pallas_call(
         kernel,
         out_shape=outs,
         in_specs=in_specs,
-        out_specs=in_vmem(len(outs)) if isinstance(outs, list) else in_vmem(1)[0],
+        out_specs=(away if far_out else near) if one else [near] * len(outs),
         scratch_shapes=[pltpu.VMEM(shape, jnp.bfloat16) for shape in scratch]
-        + [pltpu.SemaphoreType.DMA((3,))] * len(far),
+        + [pltpu.SemaphoreType.DMA((semaphores,))] * (semaphores > 0),
         compiler_params=pltpu.CompilerParams(vmem_limit_bytes=24 * 1024 * 1024),
         cost_estimate=pl.CostEstimate(flops=flops, bytes_accessed=4 * 1024 * 1024, transcendentals=0),
         name=name,
@@ -343,50 +362,70 @@
     bf16 = functools.partial(jax.ShapeDtypeStruct, dtype=jnp.bfloat16)
     f32 = functools.partial(jax.ShapeDtypeStruct, dtype=jnp.float32)
 
+    plane_shape = bf16(weight_first.shape[1:])
     neighbour = swap(frames_in, "slab")
+    own_in, middle, last = call(
+        stage_kernel,
+        "stage",
+        [frames_in, weight_first],
+        [bf16(frames_in.shape), plane_shape, plane_shape],
+        semaphores=3,
+        far=[0, 1],
+    )
     edge_shape = bf16(Packed(frames, HALO, cols).shape)
     block, *edges = call(
         functools.partial(pack_kernel, strips),
         "pack",
-        [frames_in, neighbour],
+        [own_in, neighbour],
         [bf16(Packed(HALO, rows, cols).shape)] + [edge_shape] * (1 if strips == 2 else 2),
     )
     ups = [(i, i + 1) for i in range(strips - 1)]
     downs = [(i + 1, i) for i in range(strips - 1)]
     ways = [[(0, 1), (1, 0)]] if strips == 2 else [ups, downs]
     before = forward(block)
-    own_edges = [shift(edge, "strip", way) for edge, way in zip(edges, ways)]
-    before_edges = [shift(edge, "strip", way, 1) for edge, way in zip(edges, ways)]
-
-    weight_shape = bf16(weight_first.shape)
-    own, weight_first = call(
+    own_edges = [lax.ppermute(edge, "strip", way) for edge, way in zip(edges, ways)]
+    for edge, way in zip(edges, ways):
+        before += forward(edge, way)
+
+    own, plane = call(
         functools.partial(own_kernel, strips, n_rows_h),
         "first_layer_own",
-        [frames_in, neighbour, *own_edges, weight_first],
-        [f32((frames, n_rows_h, width, channels)), weight_shape],
+        [own_in, neighbour, *own_edges, middle, last, weight_first],
+        [f32((frames, n_rows_h, width, channels)), plane_shape],
         block_scratch(frames, rows + 2 * HALO, width),
-        flops,
+        semaphores=1,
+        flops=flops,
         far=[-1],
     )
     h_shapes = [bf16(shape) for shape in block_scratch(frames, rows + 2, width)]
-    h_lo, h_pairs, h_stacked, partial, weight_second = call(
+    h_lo, h_pairs, h_stacked, partial, *w2 = call(
         functools.partial(first_kernel, strips, n_rows_h, rows, cols),
         "first_layer",
-        [before, *before_edges, own, weight_first, scale_first[None], weight_second],
-        h_shapes + [bf16((HALO, rows + rows // 2, cols, LANES)), weight_shape],
+        [*before, own, plane, middle, scale_first[None], weight_second],
+        h_shapes + [bf16((HALO, rows + rows // 2, cols, LANES))] + [plane_shape] * 3,
         block_scratch(HALO, rows + 2 * HALO, width),
-        flops,
+        semaphores=3,
+        flops=flops,
         far=[-1],
     )
     sent = forward(partial)
     own = call(
         functools.partial(second_kernel, frames, rows, cols),
         "second_layer",
-        [h_lo, h_pairs, h_stacked, weight_second],
+        [h_lo, h_pairs, h_stacked, *w2],
         f32((frames, rows, cols, channels)),
         flops=flops,
     )
-    return call(third_kernel, "finish", [sent, own, scale_second[None]], bf16((frames, rows, cols, channels)))
+    out = bf16(frames_in.shape)
+    return call(
+        finish_kernel,
+        "finish",
+        [*sent, own, scale_second[None]],
+        out,
+        [out.shape],
+        semaphores=frames,
+        far_out=True,
+    )
 
 
 def solution(mesh):

time: 29.8 us -> 31.7 us (1.064)
  starting transfers between devices: 14.3 us -> 17.7 us
  Pallas kernels: 10.9 us -> 9.95 us
  local copies, waits for them, and re-layouts: 0.96 us -> 0.01 us
  waiting for transfers between devices: 3.33 us -> 3.65 us
    ppermute x5 -> x8, starting transfers between devices: 14.3 us -> 17.7 us  [the longest x6 15.8 us: forward(): lax.ppermute(x, ('frame', 'strip'), there + [(j, i) for i, j in there])]
    pallas_call x5 -> x6, Pallas kernels: 10.9 us -> 9.95 us  [call(): pl.pallas_call(kernel, out_shape=outs, in_specs=in_specs, out_specs=(away...]
    unnamed x6 -> x4, local copies, waits for them, and re-layouts: 0.96 us -> 0.01 us
    ppermute x5 -> x8, waiting for transfers between devices: 3.33 us -> 3.65 us  [the longest x6 3.65 us: forward(): lax.ppermute(x, ('frame', 'strip'), there + [(j, i) for i, j in there])]
  transfers between devices with their start and end apart: 5 -> 8, of which waited for: 2 -> 2; matrix products, arithmetic and copies ran while one was open for 0% -> 0% of each run, Pallas kernels for 16% -> 16%
where the time goes in v3:
time: 31.7 us; the launch traced here: 31.4 us
  starting transfers between devices  17.7 us (56%)
  Pallas kernels  9.95 us (31%)
  waiting for transfers between devices  3.65 us (12%)
    ppermute x6, starting transfers between devices, forward(): lax.ppermute(x, ('frame', 'strip'), there + [(j, i) for i, j in there])  15.8 us
    pallas_call x6, Pallas kernels, call(): pl.pallas_call(kernel, out_shape=outs, in_specs=in_specs, out_specs=(away...  9.95 us
    ppermute x6, waiting for transfers between devices, forward(): lax.ppermute(x, ('frame', 'strip'), there + [(j, i) for i, j in there])  3.65 us
    ppermute x1, starting transfers between devices, shards(): lax.ppermute(edge, 'strip', way)  1.49 us
  transfers between devices with their start and end apart: 8, of which 2 were waited for; matrix products, arithmetic and copies ran while one was open for 0% of the time, Pallas kernels for 16%

profile of v3, /device:TPU:0, one launch (start us, length us, event | category | flops | bytes accessed | tf_op | source)
XLA Modules:
  0.0 31.4 jit_solution(1761039388236993258)
XLA Ops:
  0.0 0.5 %collective-permute-start = (bf16[2,4,64,192]{3,2,1,0:T(8,128)(2,1)}, bf16[2,4,64,192]{3,2,1,0:T(8,128)(2,1)S(1)}, u32[]{:S(2)}, u32[]{:S(2)}) collective-permute-start(bf16[2,4,64,192]{3,2,1,0:T(8,128)(2,1)} %own_far.1), channel_id=1, source_target_pairs={{0,1},{1,0},{2,3},{3,2},{4,5},{5,4},{6,7},{7,6},{8,9},{9,8},{10,11... | collective-permute-start | bytes 589832 | tf_op jit(solution)/shard_map/ppermute | solution.py:19
  0.5 1.5 %stage.1 = (bf16[2,4,64,192]{3,2,1,0:T(8,128)(2,1)S(1)}, bf16[3,3,192,192]{3,2,1,0:T(8,128)(2,1)S(1)}, bf16[3,3,192,192]{3,2,1,0:T(8,128)(2,1)S(1)}) custom-call(bf16[2,4,64,192]{3,2,1,0:T(8,128)(2,1)} %own_far.1, bf16[3,3,3,192,192]{4,3,2,1,0:T(8,128)(2,1)} %refs_5_.1), custom_call_target="tpu_custom_call" | custom-call | bytes 4194304 | tf_op jit(solution)/shard_map/stage/pallas_call | solution.py:339
  2.0 0.0 collective-permute-done.neighbour.refs_1_
  2.0 0.1 pack.1
  2.2 0.0 copy-start
  2.2 0.7 %collective-permute-start.2 = (bf16[800,128]{1,0:T(8,128)(2,1)S(1)}, bf16[800,128]{1,0:T(8,128)(2,1)S(1)}, u32[]{:S(2)}, u32[]{:S(2)}) collective-permute-start(bf16[800,128]{1,0:T(8,128)(2,1)S(1)} %get-tuple-element.20), channel_id=1, source_target_pairs={{4,8},{6,10},{8,4},{10,6},{5,9},{7,11},{9,5},{11,7},{20,24},{22,26... | collective-permute-start | bytes 614408 | tf_op jit(solution)/shard_map/ppermute | solution.py:28
  2.8 5.6 %collective-permute-start.1 = (bf16[800,128]{1,0:T(8,128)(2,1)S(1)}, bf16[800,128]{1,0:T(8,128)(2,1)S(1)}, u32[]{:S(2)}, u32[]{:S(2)}) collective-permute-start(bf16[800,128]{1,0:T(8,128)(2,1)S(1)} %get-tuple-element.20), channel_id=1, source_target_pairs={{0,4},{2,6},{8,12},{10,14},{4,0},{6,2},{12,8},{14,10},{1,5},{3,7},... | collective-permute-start | bytes 614408 | tf_op jit(solution)/shard_map/ppermute | solution.py:28
  8.5 1.5 %collective-permute-start.5 = (bf16[416,128]{1,0:T(8,128)(2,1)S(1)}, bf16[416,128]{1,0:T(8,128)(2,1)S(1)}, u32[]{:S(2)}, u32[]{:S(2)}) collective-permute-start(bf16[416,128]{1,0:T(8,128)(2,1)S(1)} %get-tuple-element.21), channel_id=1, source_target_pairs={{0,2},{2,0},{1,3},{3,1},{4,6},{6,4},{5,7},{7,5},{8,10},{10,8},{9,1... | collective-permute-start | bytes 319496 | tf_op jit(solution)/shard_map/ppermute | solution.py:386
  10.0 0.7 %collective-permute-start.4 = (bf16[416,128]{1,0:T(8,128)(2,1)S(1)}, bf16[416,128]{1,0:T(8,128)(2,1)S(1)}, u32[]{:S(2)}, u32[]{:S(2)}) collective-permute-start(bf16[416,128]{1,0:T(8,128)(2,1)S(1)} %get-tuple-element.21), channel_id=1, source_target_pairs={{4,10},{6,8},{10,4},{8,6},{5,11},{7,9},{11,5},{9,7},{20,26},{22,24... | collective-permute-start | bytes 319496 | tf_op jit(solution)/shard_map/ppermute | solution.py:28
  10.6 2.7 %collective-permute-start.3 = (bf16[416,128]{1,0:T(8,128)(2,1)S(1)}, bf16[416,128]{1,0:T(8,128)(2,1)S(1)}, u32[]{:S(2)}, u32[]{:S(2)}) collective-permute-start(bf16[416,128]{1,0:T(8,128)(2,1)S(1)} %get-tuple-element.21), channel_id=1, source_target_pairs={{0,6},{2,4},{8,14},{10,12},{6,0},{4,2},{14,8},{12,10},{1,7},{3,5},... | collective-permute-start | bytes 319496 | tf_op jit(solution)/shard_map/ppermute | solution.py:28
  13.4 0.0 collective-permute-done.5.refs_2_
  13.4 2.4 %first_layer_own.1 = (f32[2,5,80,192]{3,2,1,0:T(8,128)S(1)}, bf16[3,3,192,192]{3,2,1,0:T(8,128)(2,1)S(1)}) custom-call(bf16[2,4,64,192]{3,2,1,0:T(8,128)(2,1)S(1)} %get-tuple-element.19.own.refs_0_, bf16[2,4,64,192]{3,2,1,0:T(8,128)(2,1)S(1)} %collective-permute-done.neighbour.refs_1_, bf16[416,128]{1,0:T(8,128)(2,1)S(1)} %collective-permute-done.5.refs_2_, ...), custom_call_target="tpu_custom_call" | custom-call | flops 509607936 | bytes 4194304 | tf_op jit(solution)/shard_map/first_layer_own/pallas_call | solution.py:339
  15.8 0.0 collective-permute-done.4.refs_3_
  15.8 1.2 %collective-permute-done.3.refs_2_ = bf16[416,128]{1,0:T(8,128)(2,1)S(1)} collective-permute-done((bf16[416,128]{1,0:T(8,128)(2,1)S(1)}, bf16[416,128]{1,0:T(8,128)(2,1)S(1)}, u32[]{:S(2)}, u32[]{:S(2)}) %collective-permute-start.3) | collective-permute-done | bytes 106528 | tf_op jit(solution)/shard_map/ppermute | solution.py:28
  17.0 0.0 collective-permute-done.2.refs_1_
  17.0 0.0 collective-permute-done.1.refs_0_
  17.0 0.0 copy-done
  17.0 3.6 %first_layer.1 = (bf16[2,6,80,128]{3,2,1,0:T(8,128)(2,1)S(1)}, bf16[2,7,80,128]{3,2,1,0:T(8,128)(2,1)S(1)}, bf16[1,6,80,128]{3,2,1,0:T(8,128)(2,1)S(1)}, bf16[2,...) custom-call(bf16[800,128]{1,0:T(8,128)(2,1)S(1)} %collective-permute, ...), custom_call_target="tpu_custom_call" | custom-call | flops 509607936 | bytes 4194304 | tf_op jit(solution)/shard_map/first_layer/pallas_call | solution.py:339
  20.6 0.0 copy-start.1
  20.7 0.7 %collective-permute-start.7 = (bf16[2,6,64,128]{3,2,1,0:T(8,128)(2,1)S(1)}, bf16[2,6,64,128]{3,2,1,0:T(8,128)(2,1)S(1)}, u32[]{:S(2)}, u32[]{:S(2)}) collective-permute-start(bf16[2,6,64,128]{3,2,1,0:T(8,128)(2,1)S(1)} %get-tuple-element.26), channel_id=1, source_target_pairs={{4,8},{6,10},{8,4},{10,6},{5,9},{7,11},{9,5},{11,7},{20,24},{22,26... | collective-permute-start | bytes 589832 | tf_op jit(solution)/shard_map/ppermute | solution.py:28
  21.3 5.4 %collective-permute-start.6 = (bf16[2,6,64,128]{3,2,1,0:T(8,128)(2,1)S(1)}, bf16[2,6,64,128]{3,2,1,0:T(8,128)(2,1)S(1)}, u32[]{:S(2)}, u32[]{:S(2)}) collective-permute-start(bf16[2,6,64,128]{3,2,1,0:T(8,128)(2,1)S(1)} %get-tuple-element.26), channel_id=1, source_target_pairs={{0,4},{2,6},{8,12},{10,14},{4,0},{6,2},{12,8},{14,10},{1,5},{3,7},... | collective-permute-start | bytes 589832 | tf_op jit(solution)/shard_map/ppermute | solution.py:28
  26.7 1.2 %second_layer.1.own = f32[2,4,64,192]{3,2,1,0:T(8,128)S(1)} custom-call(bf16[2,6,80,128]{3,2,1,0:T(8,128)(2,1)S(1)} %get-tuple-element.27.h_lo, bf16[2,7,80,128]{3,2,1,0:T(8,128)(2,1)S(1)} %get-tuple-element.28.h_pairs, bf16[1,6,80,128]{3,2,1,0:T(8,128)(2,1)S(1)} %get-tuple-element.29.h_stacked, bf16[3,3,192,192]{3,2,1,0:T(8,128)(2,1)S(1)} %get-tuple-element.30.refs_0_, ...), custom_call_target="tpu_custom_call" | custom-call | flops 509607936 | bytes 4194304 | tf_op jit(solution)/shard_map/second_layer/pallas_call | solution.py:339
  27.9 0.0 collective-permute-done.7.second
  27.9 2.4 %collective-permute-done.6.first = bf16[2,6,64,128]{3,2,1,0:T(8,128)(2,1)S(1)} collective-permute-done((bf16[2,6,64,128]{3,2,1,0:T(8,128)(2,1)S(1)}, bf16[2,6,64,128]{3,2,1,0:T(8,128)(2,1)S(1)}, u32[]{:S(2)}, u32[]{:S(2)}) %collective-permute-start.6) | collective-permute-done | bytes 196640 | tf_op jit(solution)/shard_map/ppermute | solution.py:28
  30.4 0.0 copy-done.1
  30.4 1.0 %finish.1 = bf16[2,4,64,192]{3,2,1,0:T(8,128)(2,1)} custom-call(bf16[2,6,64,128]{3,2,1,0:T(8,128)(2,1)S(1)} %collective-permute-done.6.first, bf16[2,6,64,128]{3,2,1,0:T(8,128)(2,1)S(1)} %collective-permute-done.7.second, f32[2,4,64,192]{3,2,1,0:T(8,128)S(1)} %second_layer.1.own, f32[1,192]{1,0:T(1,128)S(1)} %bitcast.3), custom_call_target="tpu_custom_call" | custom-call | bytes 4194304 | tf_op jit(solution)/shard_map/finish/pallas_call | solution.py:339
Async XLA Ops:
  0.0 2.0 %collective-permute-start = (bf16[2,4,64,192]{3,2,1,0:T(8,128)(2,1)}, bf16[2,4,64,192]{3,2,1,0:T(8,128)(2,1)S(1)}, u32[]{:S(2)}, u32[]{:S(2)}) collective-permute-start(bf16[2,4,64,192]{3,2,1,0:T(8,128)(2,1)} %own_far.1), channel_id=1, source_target_pairs={{0,1},{1,0},{2,3},{3,2},{4,5},{5,4},{6,7},{7,6},{8,9},{9,8},{10,11... | collective-permute-start | bytes 589832 | tf_op jit(solution)/shard_map/ppermute | solution.py:19
  2.2 14.8 %copy-start = (f32[192]{0:T(256)S(1)}, f32[192]{0:T(256)}, u32[]{:S(2)}) copy-start(f32[192]{0:T(256)} %param.7) | copy-start | bytes 2308
  2.2 14.8 %collective-permute-start.2 = (bf16[800,128]{1,0:T(8,128)(2,1)S(1)}, bf16[800,128]{1,0:T(8,128)(2,1)S(1)}, u32[]{:S(2)}, u32[]{:S(2)}) collective-permute-start(bf16[800,128]{1,0:T(8,128)(2,1)S(1)} %get-tuple-element.20), channel_id=1, source_target_pairs={{4,8},{6,10},{8,4},{10,6},{5,9},{7,11},{9,5},{11,7},{20,24},{22,26... | collective-permute-start | bytes 614408 | tf_op jit(solution)/shard_map/ppermute | solution.py:28
  2.8 14.1 %collective-permute-start.1 = (bf16[800,128]{1,0:T(8,128)(2,1)S(1)}, bf16[800,128]{1,0:T(8,128)(2,1)S(1)}, u32[]{:S(2)}, u32[]{:S(2)}) collective-permute-start(bf16[800,128]{1,0:T(8,128)(2,1)S(1)} %get-tuple-element.20), channel_id=1, source_target_pairs={{0,4},{2,6},{8,12},{10,14},{4,0},{6,2},{12,8},{14,10},{1,5},{3,7},... | collective-permute-start | bytes 614408 | tf_op jit(solution)/shard_map/ppermute | solution.py:28
  8.5 4.9 %collective-permute-start.5 = (bf16[416,128]{1,0:T(8,128)(2,1)S(1)}, bf16[416,128]{1,0:T(8,128)(2,1)S(1)}, u32[]{:S(2)}, u32[]{:S(2)}) collective-permute-start(bf16[416,128]{1,0:T(8,128)(2,1)S(1)} %get-tuple-element.21), channel_id=1, source_target_pairs={{0,2},{2,0},{1,3},{3,1},{4,6},{6,4},{5,7},{7,5},{8,10},{10,8},{9,1... | collective-permute-start | bytes 319496 | tf_op jit(solution)/shard_map/ppermute | solution.py:386
  10.0 5.8 %collective-permute-start.4 = (bf16[416,128]{1,0:T(8,128)(2,1)S(1)}, bf16[416,128]{1,0:T(8,128)(2,1)S(1)}, u32[]{:S(2)}, u32[]{:S(2)}) collective-permute-start(bf16[416,128]{1,0:T(8,128)(2,1)S(1)} %get-tuple-element.21), channel_id=1, source_target_pairs={{4,10},{6,8},{10,4},{8,6},{5,11},{7,9},{11,5},{9,7},{20,26},{22,24... | collective-permute-start | bytes 319496 | tf_op jit(solution)/shard_map/ppermute | solution.py:28
  10.6 6.3 %collective-permute-start.3 = (bf16[416,128]{1,0:T(8,128)(2,1)S(1)}, bf16[416,128]{1,0:T(8,128)(2,1)S(1)}, u32[]{:S(2)}, u32[]{:S(2)}) collective-permute-start(bf16[416,128]{1,0:T(8,128)(2,1)S(1)} %get-tuple-element.21), channel_id=1, source_target_pairs={{0,6},{2,4},{8,14},{10,12},{6,0},{4,2},{14,8},{12,10},{1,7},{3,5},... | collective-permute-start | bytes 319496 | tf_op jit(solution)/shard_map/ppermute | solution.py:28
  20.6 9.8 %copy-start.1 = (f32[192]{0:T(256)S(1)}, f32[192]{0:T(256)}, u32[]{:S(2)}) copy-start(f32[192]{0:T(256)} %param.9) | copy-start | bytes 2308
  20.7 7.3 %collective-permute-start.7 = (bf16[2,6,64,128]{3,2,1,0:T(8,128)(2,1)S(1)}, bf16[2,6,64,128]{3,2,1,0:T(8,128)(2,1)S(1)}, u32[]{:S(2)}, u32[]{:S(2)}) collective-permute-start(bf16[2,6,64,128]{3,2,1,0:T(8,128)(2,1)S(1)} %get-tuple-element.26), channel_id=1, source_target_pairs={{4,8},{6,10},{8,4},{10,6},{5,9},{7,11},{9,5},{11,7},{20,24},{22,26... | collective-permute-start | bytes 589832 | tf_op jit(solution)/shard_map/ppermute | solution.py:28
  21.3 9.1 %collective-permute-start.6 = (bf16[2,6,64,128]{3,2,1,0:T(8,128)(2,1)S(1)}, bf16[2,6,64,128]{3,2,1,0:T(8,128)(2,1)S(1)}, u32[]{:S(2)}, u32[]{:S(2)}) collective-permute-start(bf16[2,6,64,128]{3,2,1,0:T(8,128)(2,1)S(1)} %get-tuple-element.26), channel_id=1, source_target_pairs={{0,4},{2,6},{8,12},{10,14},{4,0},{6,2},{12,8},{14,10},{1,5},{3,7},... | collective-permute-start | bytes 589832 | tf_op jit(solution)/shard_map/ppermute | solution.py:28

commit v4 on v3

--- a/solution.py
+++ b/solution.py
@@ -22,17 +22,12 @@
 def forward(x, way=None):
     steps, count = lax.axis_size("frame"), lax.axis_size("strip")
     way = [(i, i) for i in range(count)] if way is None else way
-    received = []
-    for parity in range(2):
-        there = [(f * count + i, (f + 1) * count + j) for f in range(parity, steps - 1, 2) for i, j in way]
-        received.append(lax.ppermute(x, ("frame", "strip"), there + [(j, i) for i, j in there]))
-    return received
-
-
-def by_parity(build, first, second):
-    odd = lax.rem(lax.axis_index("frame"), 2) == 1
-    pl.when(odd)(lambda: build(first))
-    pl.when(jnp.logical_not(odd))(lambda: build(second))
+    pairs = [(f * count + i, (f + 1) * count + j) for f in range(steps - 1) for i, j in way]
+    return lax.ppermute(x, ("frame", "strip"), pairs)
+
+
+def if_earlier(build):
+    pl.when(lax.axis_index("frame") > 0)(build)
 
 
 class Packed:
@@ -237,7 +232,7 @@
 def first_kernel(strips, n_rows_h, rows, cols, *refs):
     *refs, lo, pairs, stacked, arrived = refs
     *refs, h_lo, h_pairs, h_stacked, partial, w2_first, w2_middle, w2_last = refs
-    *received, own, plane, middle, gains, w2_far = refs
+    block, *edges, own, plane, middle, gains, w2_far = refs
     w2 = [w2_first, w2_middle, w2_last]
     copies = [pltpu.make_async_copy(w2_far.at[a], w2[a], arrived.at[a]) for a in range(3)]
     for copy in copies:
@@ -249,8 +244,8 @@
     clear((lo, pairs, stacked, h_lo, h_pairs, h_stacked))
     whole, strip_block = Packed(HALO, rows, cols), Packed(frames, HALO, cols)
 
-    def build(pieces):
-        block, *edges = pieces
+    @if_earlier
+    def build():
         for f in range(HALO):
             for r in range(rows):
                 fill(lo, pairs, stacked, f, r + HALO, every, *whole.read(block, f, r, rest))
@@ -261,7 +256,6 @@
                     fill(lo, pairs, stacked, f, row + r, every, *strip_block.read(edge, sent, r, rest))
                     fill(lo, pairs, stacked, f, row + r, beside, *strip_block.read_beside(edge, sent, r, rest))
 
-    by_parity(build, received[0::2], received[1::2])
 
     origin = first_row(strips)
     gain = gains[...]
@@ -306,25 +300,22 @@
             out[t, r] = join(products, r * width, width)[:cols]
 
 
-def finish_kernel(first, second, own, gains, out_far, out, left):
+def finish_kernel(partial, own, gains, out_far, out, left):
     frames, rows, cols, channels = out.shape
     rest = channels - LANES
     gain = gains[...]
 
-    def build(partial):
-        for t in range(frames):
-            for r in range(rows):
-                y = own[t, r]
-                if t < HALO:
-                    half = r % 2
-                    high = partial[t, rows + r // 2, :, half * rest : (half + 1) * rest]
-                    sent = jnp.concatenate([partial[t, r], high], axis=-1)
-                    y = y + sent.astype(jnp.float32)
-                out[t, r] = activate(y, gain).astype(jnp.bfloat16)
-            copies[t].start()
-
     copies = [pltpu.make_async_copy(out.at[t], out_far.at[t], left.at[t]) for t in range(frames)]
-    by_parity(build, first, second)
+    for t in range(frames):
+        for r in range(rows):
+            y = own[t, r]
+            if t < HALO:
+                half = r % 2
+                high = partial[t, rows + r // 2, :, half * rest : (half + 1) * rest]
+                sent = jnp.concatenate([partial[t, r], high], axis=-1)
+                y = y + sent.astype(jnp.float32)
+            out[t, r] = activate(y, gain).astype(jnp.bfloat16)
+        copies[t].start()
     for copy in copies:
         copy.wait()
 
@@ -382,10 +373,10 @@
     ups = [(i, i + 1) for i in range(strips - 1)]
     downs = [(i + 1, i) for i in range(strips - 1)]
     ways = [[(0, 1), (1, 0)]] if strips == 2 else [ups, downs]
-    before = forward(block)
+    before = [forward(block)]
     own_edges = [lax.ppermute(edge, "strip", way) for edge, way in zip(edges, ways)]
     for edge, way in zip(edges, ways):
-        before += forward(edge, way)
+        before.append(forward(edge, way))
 
     own, plane = call(
         functools.partial(own_kernel, strips, n_rows_h),
@@ -420,7 +411,7 @@
     return call(
         finish_kernel,
         "finish",
-        [*sent, own, scale_second[None]],
+        [sent, own, scale_second[None]],
         out,
         [out.shape],
         semaphores=frames,

time: 31.7 us -> 27.5 us (0.87)
  starting transfers between devices: 17.7 us -> 15.4 us
  waiting for transfers between devices: 3.65 us -> 1.97 us
    ppermute x6 -> x3, starting transfers between devices: 15.8 us -> 13.4 us  [forward(): return lax.ppermute(x, ('frame', 'strip'), pairs)]
    ppermute x6 -> x3, waiting for transfers between devices: 3.65 us -> 1.97 us  [forward(): return lax.ppermute(x, ('frame', 'strip'), pairs)]
  transfers between devices with their start and end apart: 8 -> 5, of which waited for: 2 -> 1; matrix products, arithmetic and copies ran while one was open for 0% -> 0% of each run, Pallas kernels for 16% -> 19%
where the time goes in v4:
time: 27.5 us; the launch traced here: 27.2 us
  starting transfers between devices  15.4 us (56%)
  Pallas kernels  9.74 us (35%)
  waiting for transfers between devices  1.97 us (7%)
    ppermute x3, starting transfers between devices, forward(): return lax.ppermute(x, ('frame', 'strip'), pairs)  13.4 us
    pallas_call x6, Pallas kernels, call(): pl.pallas_call(kernel, out_shape=outs, in_specs=in_specs, out_specs=(away...  9.74 us
    ppermute x3, waiting for transfers between devices, forward(): return lax.ppermute(x, ('frame', 'strip'), pairs)  1.97 us
    ppermute x1, starting transfers between devices, shards(): lax.ppermute(edge, 'strip', way)  1.56 us
  transfers between devices with their start and end apart: 5, of which 1 were waited for; matrix products, arithmetic and copies ran while one was open for 0% of the time, Pallas kernels for 19%

profile of v4, /device:TPU:0, one launch (start us, length us, event | category | flops | bytes accessed | tf_op | source)
XLA Modules:
  0.0 27.2 jit_solution(906181350243054186)
XLA Ops:
  0.0 0.5 %collective-permute-start = (bf16[2,4,64,192]{3,2,1,0:T(8,128)(2,1)}, bf16[2,4,64,192]{3,2,1,0:T(8,128)(2,1)S(1)}, u32[]{:S(2)}, u32[]{:S(2)}) collective-permute-start(bf16[2,4,64,192]{3,2,1,0:T(8,128)(2,1)} %own_far.1), channel_id=1, source_target_pairs={{0,1},{1,0},{2,3},{3,2},{4,5},{5,4},{6,7},{7,6},{8,9},{9,8},{10,11... | collective-permute-start | bytes 589832 | tf_op jit(solution)/shard_map/ppermute | solution.py:19
  0.5 1.5 %stage.1 = (bf16[2,4,64,192]{3,2,1,0:T(8,128)(2,1)S(1)}, bf16[3,3,192,192]{3,2,1,0:T(8,128)(2,1)S(1)}, bf16[3,3,192,192]{3,2,1,0:T(8,128)(2,1)S(1)}) custom-call(bf16[2,4,64,192]{3,2,1,0:T(8,128)(2,1)} %own_far.1, bf16[3,3,3,192,192]{4,3,2,1,0:T(8,128)(2,1)} %refs_5_.1), custom_call_target="tpu_custom_call" | custom-call | bytes 4194304 | tf_op jit(solution)/shard_map/stage/pallas_call | solution.py:330
  2.0 0.0 collective-permute-done.neighbour.refs_1_
  2.0 0.1 pack.1
  2.2 0.0 copy-start
  2.2 4.7 %collective-permute-start.1 = (bf16[800,128]{1,0:T(8,128)(2,1)S(1)}, bf16[800,128]{1,0:T(8,128)(2,1)S(1)}, u32[]{:S(2)}, u32[]{:S(2)}) collective-permute-start(bf16[800,128]{1,0:T(8,128)(2,1)S(1)} %get-tuple-element.20), channel_id=1, source_target_pairs={{0,4},{2,6},{4,8},{6,10},{8,12},{10,14},{1,5},{3,7},{5,9},{7,11},{... | collective-permute-start | bytes 614408 | tf_op jit(solution)/shard_map/ppermute | solution.py:26
  6.8 1.6 %collective-permute-start.3 = (bf16[416,128]{1,0:T(8,128)(2,1)S(1)}, bf16[416,128]{1,0:T(8,128)(2,1)S(1)}, u32[]{:S(2)}, u32[]{:S(2)}) collective-permute-start(bf16[416,128]{1,0:T(8,128)(2,1)S(1)} %get-tuple-element.21), channel_id=1, source_target_pairs={{0,2},{2,0},{1,3},{3,1},{4,6},{6,4},{5,7},{7,5},{8,10},{10,8},{9,1... | collective-permute-start | bytes 319496 | tf_op jit(solution)/shard_map/ppermute | solution.py:377
  8.4 3.4 %collective-permute-start.2 = (bf16[416,128]{1,0:T(8,128)(2,1)S(1)}, bf16[416,128]{1,0:T(8,128)(2,1)S(1)}, u32[]{:S(2)}, u32[]{:S(2)}) collective-permute-start(bf16[416,128]{1,0:T(8,128)(2,1)S(1)} %get-tuple-element.21), channel_id=1, source_target_pairs={{0,6},{2,4},{4,10},{6,8},{8,14},{10,12},{1,7},{3,5},{5,11},{7,9},{... | collective-permute-start | bytes 319496 | tf_op jit(solution)/shard_map/ppermute | solution.py:26
  11.8 0.0 collective-permute-done.3.refs_2_
  11.9 2.4 %first_layer_own.1 = (f32[2,5,80,192]{3,2,1,0:T(8,128)S(1)}, bf16[3,3,192,192]{3,2,1,0:T(8,128)(2,1)S(1)}) custom-call(bf16[2,4,64,192]{3,2,1,0:T(8,128)(2,1)S(1)} %get-tuple-element.19.own.refs_0_, bf16[2,4,64,192]{3,2,1,0:T(8,128)(2,1)S(1)} %collective-permute-done.neighbour.refs_1_, bf16[416,128]{1,0:T(8,128)(2,1)S(1)} %collective-permute-done.3.refs_2_, ...), custom_call_target="tpu_custom_call" | custom-call | flops 509607936 | bytes 4194304 | tf_op jit(solution)/shard_map/first_layer_own/pallas_call | solution.py:330
  14.3 0.0 collective-permute-done.2.refs_1_
  14.3 0.0 collective-permute-done.1.refs_0_
  14.3 0.0 copy-done
  14.3 3.4 %first_layer.1 = (bf16[2,6,80,128]{3,2,1,0:T(8,128)(2,1)S(1)}, bf16[2,7,80,128]{3,2,1,0:T(8,128)(2,1)S(1)}, bf16[1,6,80,128]{3,2,1,0:T(8,128)(2,1)S(1)}, bf16[2,...) custom-call(bf16[800,128]{1,0:T(8,128)(2,1)S(1)} %collective-permute, ...), custom_call_target="tpu_custom_call" | custom-call | flops 509607936 | bytes 4194304 | tf_op jit(solution)/shard_map/first_layer/pallas_call | solution.py:330
  17.7 0.0 copy-start.1
  17.7 5.3 %collective-permute-start.4 = (bf16[2,6,64,128]{3,2,1,0:T(8,128)(2,1)S(1)}, bf16[2,6,64,128]{3,2,1,0:T(8,128)(2,1)S(1)}, u32[]{:S(2)}, u32[]{:S(2)}) collective-permute-start(bf16[2,6,64,128]{3,2,1,0:T(8,128)(2,1)S(1)} %get-tuple-element.26), channel_id=1, source_target_pairs={{0,4},{2,6},{4,8},{6,10},{8,12},{10,14},{1,5},{3,7},{5,9},{7,11},{... | collective-permute-start | bytes 589832 | tf_op jit(solution)/shard_map/ppermute | solution.py:26
  23.0 1.2 %second_layer.1.own = f32[2,4,64,192]{3,2,1,0:T(8,128)S(1)} custom-call(bf16[2,6,80,128]{3,2,1,0:T(8,128)(2,1)S(1)} %get-tuple-element.27.h_lo, bf16[2,7,80,128]{3,2,1,0:T(8,128)(2,1)S(1)} %get-tuple-element.28.h_pairs, bf16[1,6,80,128]{3,2,1,0:T(8,128)(2,1)S(1)} %get-tuple-element.29.h_stacked, bf16[3,3,192,192]{3,2,1,0:T(8,128)(2,1)S(1)} %get-tuple-element.30.refs_0_, ...), custom_call_target="tpu_custom_call" | custom-call | flops 509607936 | bytes 4194304 | tf_op jit(solution)/shard_map/second_layer/pallas_call | solution.py:330
  24.2 2.0 %collective-permute-done.4.partial = bf16[2,6,64,128]{3,2,1,0:T(8,128)(2,1)S(1)} collective-permute-done((bf16[2,6,64,128]{3,2,1,0:T(8,128)(2,1)S(1)}, bf16[2,6,64,128]{3,2,1,0:T(8,128)(2,1)S(1)}, u32[]{:S(2)}, u32[]{:S(2)}) %collective-permute-start.4) | collective-permute-done | bytes 196640 | tf_op jit(solution)/shard_map/ppermute | solution.py:26
  26.2 0.0 copy-done.1
  26.2 1.0 %finish.1 = bf16[2,4,64,192]{3,2,1,0:T(8,128)(2,1)} custom-call(bf16[2,6,64,128]{3,2,1,0:T(8,128)(2,1)S(1)} %collective-permute-done.4.partial, f32[2,4,64,192]{3,2,1,0:T(8,128)S(1)} %second_layer.1.own, f32[1,192]{1,0:T(1,128)S(1)} %bitcast.3), custom_call_target="tpu_custom_call" | custom-call | bytes 4194304 | tf_op jit(solution)/shard_map/finish/pallas_call | solution.py:330
Async XLA Ops:
  0.0 2.0 %collective-permute-start = (bf16[2,4,64,192]{3,2,1,0:T(8,128)(2,1)}, bf16[2,4,64,192]{3,2,1,0:T(8,128)(2,1)S(1)}, u32[]{:S(2)}, u32[]{:S(2)}) collective-permute-start(bf16[2,4,64,192]{3,2,1,0:T(8,128)(2,1)} %own_far.1), channel_id=1, source_target_pairs={{0,1},{1,0},{2,3},{3,2},{4,5},{5,4},{6,7},{7,6},{8,9},{9,8},{10,11... | collective-permute-start | bytes 589832 | tf_op jit(solution)/shard_map/ppermute | solution.py:19
  2.2 12.1 %copy-start = (f32[192]{0:T(256)S(1)}, f32[192]{0:T(256)}, u32[]{:S(2)}) copy-start(f32[192]{0:T(256)} %param.7) | copy-start | bytes 2308
  2.2 12.1 %collective-permute-start.1 = (bf16[800,128]{1,0:T(8,128)(2,1)S(1)}, bf16[800,128]{1,0:T(8,128)(2,1)S(1)}, u32[]{:S(2)}, u32[]{:S(2)}) collective-permute-start(bf16[800,128]{1,0:T(8,128)(2,1)S(1)} %get-tuple-element.20), channel_id=1, source_target_pairs={{0,4},{2,6},{4,8},{6,10},{8,12},{10,14},{1,5},{3,7},{5,9},{7,11},{... | collective-permute-start | bytes 614408 | tf_op jit(solution)/shard_map/ppermute | solution.py:26
  6.8 5.0 %collective-permute-start.3 = (bf16[416,128]{1,0:T(8,128)(2,1)S(1)}, bf16[416,128]{1,0:T(8,128)(2,1)S(1)}, u32[]{:S(2)}, u32[]{:S(2)}) collective-permute-start(bf16[416,128]{1,0:T(8,128)(2,1)S(1)} %get-tuple-element.21), channel_id=1, source_target_pairs={{0,2},{2,0},{1,3},{3,1},{4,6},{6,4},{5,7},{7,5},{8,10},{10,8},{9,1... | collective-permute-start | bytes 319496 | tf_op jit(solution)/shard_map/ppermute | solution.py:377
  8.4 5.9 %collective-permute-start.2 = (bf16[416,128]{1,0:T(8,128)(2,1)S(1)}, bf16[416,128]{1,0:T(8,128)(2,1)S(1)}, u32[]{:S(2)}, u32[]{:S(2)}) collective-permute-start(bf16[416,128]{1,0:T(8,128)(2,1)S(1)} %get-tuple-element.21), channel_id=1, source_target_pairs={{0,6},{2,4},{4,10},{6,8},{8,14},{10,12},{1,7},{3,5},{5,11},{7,9},{... | collective-permute-start | bytes 319496 | tf_op jit(solution)/shard_map/ppermute | solution.py:26
  17.7 8.5 %copy-start.1 = (f32[192]{0:T(256)S(1)}, f32[192]{0:T(256)}, u32[]{:S(2)}) copy-start(f32[192]{0:T(256)} %param.9) | copy-start | bytes 2308
  17.7 8.5 %collective-permute-start.4 = (bf16[2,6,64,128]{3,2,1,0:T(8,128)(2,1)S(1)}, bf16[2,6,64,128]{3,2,1,0:T(8,128)(2,1)S(1)}, u32[]{:S(2)}, u32[]{:S(2)}) collective-permute-start(bf16[2,6,64,128]{3,2,1,0:T(8,128)(2,1)S(1)} %get-tuple-element.26), channel_id=1, source_target_pairs={{0,4},{2,6},{4,8},{6,10},{8,12},{10,14},{1,5},{3,7},{5,9},{7,11},{... | collective-permute-start | bytes 589832 | tf_op jit(solution)/shard_map/ppermute | solution.py:26

commit v5 on v4

--- a/solution.py
+++ b/solution.py
@@ -19,11 +19,9 @@
     return lax.ppermute(x, axis, [(0, 1), (1, 0)])
 
 
-def forward(x, way=None):
-    steps, count = lax.axis_size("frame"), lax.axis_size("strip")
-    way = [(i, i) for i in range(count)] if way is None else way
-    pairs = [(f * count + i, (f + 1) * count + j) for f in range(steps - 1) for i, j in way]
-    return lax.ppermute(x, ("frame", "strip"), pairs)
+def forward(x):
+    steps = lax.axis_size("frame")
+    return lax.ppermute(x, "frame", [(i, i + 1) for i in range(steps - 1)])
 
 
 def if_earlier(build):
@@ -78,14 +76,18 @@
         return ref[self.low_at(f, r), :], ref[self.high_at(f, r), half]
 
     def read_beside(self, ref, f, r, rest):
-        slab = lax.axis_index("slab")
-        tile, place = self.spot(f, r)
-        parts = []
-        for high, lanes in ((0, LANES), (1, rest)):
-            cells = ref[self.beside_at(tile, high), :].astype(jnp.float32)
-            cells = pltpu.roll(cells, lax.rem(2 * TILE - place - HALO * slab, TILE), 0)
-            parts.append(only_beside(cells).astype(jnp.bfloat16)[:, :lanes])
-        return parts
+        return beside_from(ref, self.beside, (f * self.rows + r) * HALO, rest)
+
+
+def beside_from(ref, start, cell, rest):
+    slab = lax.axis_index("slab")
+    parts = []
+    for high, lanes in ((0, LANES), (1, rest)):
+        at = start + (2 * (cell // TILE) + high) * TILE
+        cells = ref[pl.ds(pl.multiple_of(at, TILE), TILE), :].astype(jnp.float32)
+        cells = pltpu.roll(cells, lax.rem(2 * TILE - cell % TILE - HALO * slab, TILE), 0)
+        parts.append(only_beside(cells).astype(jnp.bfloat16)[:, :lanes])
+    return parts
 
 
 def only_beside(tile):
@@ -161,14 +163,12 @@
     return [rows - HALO, 0]
 
 
-def beyond(strips, rows):
-    if strips == 2:
-        return [jnp.where(lax.axis_index("strip") == 0, rows + HALO, 0)]
-    return [0, rows + HALO]
-
-
-def first_row(strips):
-    return 1 - lax.axis_index("strip") if strips == 2 else 0
+def at_top(strips):
+    return [lax.axis_index("strip")] if strips == 2 else [1, 0]
+
+
+def safe_rows(strips, rows):
+    return (1 + lax.axis_index("strip"), rows - 1) if strips == 2 else (2, rows - 2)
 
 
 def beside_of(neighbour, f, r, cols):
@@ -199,90 +199,181 @@
         )
 
 
-def own_kernel(strips, n_rows_h, *refs):
-    own, neighbour, *edges, middle, last, weight_far, out, plane, lo, pairs, stacked, arrived = refs
+def own_beside(neighbour, f, r, cols):
+    tile = only_beside(beside_of(neighbour, f, r, cols).astype(jnp.float32)).astype(jnp.bfloat16)
+    return tile[:, :LANES], tile[:, LANES:]
+
+
+def window(buffers, frames, top, rows, cols, own, halo):
+    every, beside = slice(0, cols), slice(cols, cols + TILE)
+    for f in range(frames):
+        for j in range(HALO):
+            for cells, row in ((own(f, (1 - top) * (rows - HALO) + j), HALO * top + j), (halo(f, j), HALO * (1 - top) + j)):
+                fill(*buffers, f, row, every, *cells[:2])
+                fill(*buffers, f, row, beside, *cells[2:])
+
+
+def safe_kernel(strips, own, neighbour, middle, last, weight_far, out, plane, lo, pairs, stacked, arrived):
     frames, rows, cols, channels = own.shape
+    width = cols + TILE
     copy = pltpu.make_async_copy(weight_far.at[0], plane, arrived.at[0])
     copy.start()
     if frames > 2:
         copy.wait()
-    width, rest = cols + TILE, channels - LANES
-    every, beside = slice(0, cols), slice(cols, width)
     clear((lo, pairs, stacked))
-    strip_block = Packed(frames, HALO, cols)
     for f in range(frames):
         for r in range(rows):
             cells = own[f, r]
-            fill(lo, pairs, stacked, f, r + HALO, every, cells[:, :LANES], cells[:, LANES:])
-            tile = only_beside(beside_of(neighbour, f, r, cols).astype(jnp.float32)).astype(jnp.bfloat16)
-            fill(lo, pairs, stacked, f, r + HALO, beside, tile[:, :LANES], tile[:, LANES:])
-        for edge, row in zip(edges, beyond(strips, rows)):
-            for r in range(HALO):
-                fill(lo, pairs, stacked, f, row + r, every, *strip_block.read(edge, f, r, rest))
-                fill(lo, pairs, stacked, f, row + r, beside, *strip_block.read_beside(edge, f, r, rest))
+            fill(lo, pairs, stacked, f, r + HALO, slice(0, cols), cells[:, :LANES], cells[:, LANES:])
+            fill(lo, pairs, stacked, f, r + HALO, slice(cols, width), *own_beside(neighbour, f, r, cols))
+    start, count = safe_rows(strips, rows)
     for t in range(frames):
-        taps = [(f, f - t + 2) for f in range(max(0, t - 2), t + 1)]
-        products = convolve(taps, [plane, middle, last], columns(taps, lo, pairs, stacked, first_row(strips), n_rows_h))
-        for r in range(n_rows_h):
+        taps = own_taps(t)
+        products = convolve(taps, [plane, middle, last], columns(taps, lo, pairs, stacked, start, count))
+        for r in range(count):
             out[t, r] = join(products, r * width, width)
     if frames <= 2:
         copy.wait()
 
 
-def first_kernel(strips, n_rows_h, rows, cols, *refs):
-    *refs, lo, pairs, stacked, arrived = refs
-    *refs, h_lo, h_pairs, h_stacked, partial, w2_first, w2_middle, w2_last = refs
-    block, *edges, own, plane, middle, gains, w2_far = refs
+def own_taps(t):
+    return [(f, f - t + 2) for f in range(max(0, t - 2), t + 1)]
+
+
+def earlier_taps(t):
+    return [(f, f - t) for f in range(t, HALO)]
+
+
+def hidden_row(y, gain, cols):
+    width, slab = y.shape[0], lax.axis_index("slab")
+    position = lax.broadcasted_iota(jnp.int32, (width, 1), 0)
+    right = cols + (slab == 0).astype(jnp.int32)
+    left = width - (slab == 1).astype(jnp.int32)
+    return jnp.where((position < right) | (position >= left), activate(y, gain), 0.0)
+
+
+def middle_kernel(strips, rows, cols, *refs):
+    *refs, lo, pairs, stacked, near_lo, near_pairs, near_stacked, arrived = refs
+    *refs, h_lo, h_pairs, h_stacked, edge_sums, w2_first, w2_middle, w2_last = refs
+    own, neighbour, *edges, block, sums, plane, middle, last, gains, w2_far = refs
+    frames, channels = own.shape[0], own.shape[-1]
+    width, rest = cols + TILE, channels - LANES
     w2 = [w2_first, w2_middle, w2_last]
     copies = [pltpu.make_async_copy(w2_far.at[a], w2[a], arrived.at[a]) for a in range(3)]
     for copy in copies:
         copy.start()
-    frames, channels = own.shape[0], own.shape[-1]
-    width, rest = cols + TILE, channels - LANES
-    every, beside = slice(0, cols), slice(cols, width)
-    strip, slab = lax.axis_index("strip"), lax.axis_index("slab")
-    clear((lo, pairs, stacked, h_lo, h_pairs, h_stacked))
+    clear((lo, pairs, stacked, h_lo, h_pairs, h_stacked, near_pairs))
     whole, strip_block = Packed(HALO, rows, cols), Packed(frames, HALO, cols)
 
     @if_earlier
     def build():
         for f in range(HALO):
             for r in range(rows):
-                fill(lo, pairs, stacked, f, r + HALO, every, *whole.read(block, f, r, rest))
-                fill(lo, pairs, stacked, f, r + HALO, beside, *whole.read_beside(block, f, r, rest))
-            for edge, row in zip(edges, beyond(strips, rows)):
-                for r in range(HALO):
-                    sent = frames - HALO + f
-                    fill(lo, pairs, stacked, f, row + r, every, *strip_block.read(edge, sent, r, rest))
-                    fill(lo, pairs, stacked, f, row + r, beside, *strip_block.read_beside(edge, sent, r, rest))
-
-
-    origin = first_row(strips)
+                fill(lo, pairs, stacked, f, r + HALO, slice(0, cols), *whole.read(block, f, r, rest))
+                fill(lo, pairs, stacked, f, r + HALO, slice(cols, width), *whole.read_beside(block, f, r, rest))
+
     gain = gains[...]
-    position = lax.broadcasted_iota(jnp.int32, (width, 1), 0)
-    right = cols + (slab == 0).astype(jnp.int32)
-    left = width - (slab == 1).astype(jnp.int32)
-    inside = (position < right) | (position >= left)
+    start, count = safe_rows(strips, rows)
     for t in range(frames):
-        taps = [(f, f - t) for f in range(t, HALO)]
-        products = convolve(taps, [plane, middle], columns(taps, lo, pairs, stacked, origin, n_rows_h)) if taps else None
-        for r in range(n_rows_h):
-            y = own[t, r]
+        taps = earlier_taps(t)
+        products = convolve(taps, [plane, middle], columns(taps, lo, pairs, stacked, start, count)) if taps else None
+        for r in range(count):
+            y = sums[t, r]
             if taps:
                 y = y + join(products, r * width, width)
-            h = jnp.where(inside, activate(y, gain), 0.0)
-            if strips != 2 and r == 0:
-                h = h * jnp.where(strip > 0, 1.0, 0.0)
-            if strips != 2 and r == n_rows_h - 1:
-                h = h * jnp.where(strip < strips - 1, 1.0, 0.0)
-            h = h.astype(jnp.bfloat16)
-            fill(h_lo, h_pairs, h_stacked, t, origin + r, slice(0, width), h[:, :LANES], h[:, LANES:])
-
+            h = hidden_row(y, gain, cols).astype(jnp.bfloat16)
+            fill(h_lo, h_pairs, h_stacked, t, start + r, slice(0, width), h[:, :LANES], h[:, LANES:])
+
+    near = (near_lo, near_pairs, near_stacked)
+    for group, (edge, top) in enumerate(zip(edges, at_top(strips))):
+
+        def own_row(f, r):
+            cells = own[f, r]
+            return cells[:, :LANES], cells[:, LANES:], *own_beside(neighbour, f, r, cols)
+
+        def halo_row(f, j):
+            return *strip_block.read(edge, f, j, rest), *strip_block.read_beside(edge, f, j, rest)
+
+        window(near, frames, top, rows, cols, own_row, halo_row)
+        for t in range(frames):
+            taps = own_taps(t)
+            products = convolve(taps, [plane, middle, last], columns(taps, *near, 0, HALO))
+            for r in range(HALO):
+                edge_sums[group, t, r] = join(products, r * width, width)
     for copy in copies:
         copy.wait()
+
+
+def pass_kernel(strips, rows, cols, block, _, *edges):
+    whole = Packed(HALO, rows, cols)
+    for start, edge in zip(facing(strips, rows), edges):
+        for f in range(HALO):
+            low = pl.multiple_of((f * rows + start) * cols, TILE)
+            edge[f * HALO * cols : (f + 1) * HALO * cols, :] = block[pl.ds(low, HALO * cols), :]
+            high = pl.multiple_of(whole.high + (f * (rows // 2) + start // 2) * cols, TILE)
+            at = HALO * HALO * cols + f * cols
+            edge[at : at + cols, :] = block[pl.ds(high, cols), :]
+        at = HALO * HALO * cols + HALO * cols
+        edge[at:, :] = block[whole.beside :, :]
+
+
+def edge_kernel(strips, rows, cols, *refs):
+    *refs, near_lo, near_pairs, near_stacked = refs
+    *refs, h_lo, h_pairs, h_stacked, partial = refs
+    *edges, block, edge_sums, safe_lo, safe_pairs, safe_stacked, plane, middle, gains, w2_first, w2_middle = refs
+    frames, channels = edge_sums.shape[1], edge_sums.shape[-1]
+    width, rest = cols + TILE, channels - LANES
+    strip = lax.axis_index("strip")
+    whole, strip_block = Packed(HALO, rows, cols), Packed(HALO, HALO, cols)
+    near = (near_lo, near_pairs, near_stacked)
+    clear(near)
+    for target, source in ((h_lo, safe_lo), (h_pairs, safe_pairs), (h_stacked, safe_stacked)):
+        target[...] = source[...]
+    gain = gains[...]
+    for group, (edge, top) in enumerate(zip(edges, at_top(strips))):
+
+        def own_row(f, r):
+            low = pl.multiple_of((f * rows + r) * cols, TILE)
+            high = pl.multiple_of(whole.high + (f * (rows // 2) + r // 2) * cols, TILE)
+            pair = block[pl.ds(high, cols), :]
+            return block[pl.ds(low, cols), :], pair, *beside_from(block, whole.beside, (f * rows + r) * HALO, rest)
+
+        def halo_row(f, j):
+            theirs = top * (rows - HALO) + j
+            cell = (f * rows + theirs) * HALO
+            return *strip_block.read(edge, f, j, rest), *beside_from(edge, strip_block.beside, cell, rest)
+
+        def own_half(f, r, j):
+            low, pair, *tile = own_row(f, r)
+            return low, pair[:, (j % 2) * rest : (j % 2 + 1) * rest], *tile
+
+        @if_earlier
+        def build():
+            every, beside = slice(0, cols), slice(cols, width)
+            for f in range(HALO):
+                for j in range(HALO):
+                    mine = own_half(f, (1 - top) * (rows - HALO) + j, j)
+                    for cells, row in ((mine, HALO * top + j), (halo_row(f, j), HALO * (1 - top) + j)):
+                        fill(*near, f, row, every, *cells[:2])
+                        fill(*near, f, row, beside, *cells[2:])
+
+        for t in range(frames):
+            taps = earlier_taps(t)
+            products = convolve(taps, [plane, middle], columns(taps, *near, 0, HALO)) if taps else None
+            for r in range(HALO):
+                y = edge_sums[group, t, r]
+                if taps:
+                    y = y + join(products, r * width, width)
+                h = hidden_row(y, gain, cols)
+                if strips != 2 and r == 1 - top:
+                    h = h * jnp.where(strip == (0 if top else strips - 1), 0.0, 1.0)
+                h = h.astype(jnp.bfloat16)
+                row = (1 - top) * rows + r
+                fill(h_lo, h_pairs, h_stacked, t, row, slice(0, width), h[:, :LANES], h[:, LANES:])
+
     last = frames - 1
     for t, taps in enumerate(([(last - 1, 0), (last, 1)], [(last, 0)])):
-        products = convolve(taps, w2, columns(taps, h_lo, h_pairs, h_stacked, 0, rows))
+        products = convolve(taps, [w2_first, w2_middle], columns(taps, h_lo, h_pairs, h_stacked, 0, rows))
         for r in range(rows):
             y = join(products, r * width, width)[:cols].astype(jnp.bfloat16)
             partial[t, r] = y[:, :LANES]
@@ -348,7 +439,6 @@
     frames, rows, cols, channels = frames_in.shape
     strips = lax.axis_size("strip")
     width = cols + TILE
-    n_rows_h = rows + 1 if strips == 2 else rows + 2
     flops = frames * rows * cols * 27 * channels * channels
     bf16 = functools.partial(jax.ShapeDtypeStruct, dtype=jnp.bfloat16)
     f32 = functools.partial(jax.ShapeDtypeStruct, dtype=jnp.float32)
@@ -373,32 +463,46 @@
     ups = [(i, i + 1) for i in range(strips - 1)]
     downs = [(i + 1, i) for i in range(strips - 1)]
     ways = [[(0, 1), (1, 0)]] if strips == 2 else [ups, downs]
-    before = [forward(block)]
+    before = forward(block)
     own_edges = [lax.ppermute(edge, "strip", way) for edge, way in zip(edges, ways)]
-    for edge, way in zip(edges, ways):
-        before.append(forward(edge, way))
-
-    own, plane = call(
-        functools.partial(own_kernel, strips, n_rows_h),
-        "first_layer_own",
-        [own_in, neighbour, *own_edges, middle, last, weight_first],
-        [f32((frames, n_rows_h, width, channels)), plane_shape],
+    sums, plane = call(
+        functools.partial(safe_kernel, strips),
+        "own_safe_rows",
+        [own_in, neighbour, middle, last, weight_first],
+        [f32((frames, safe_rows(strips, rows)[1], width, channels)), plane_shape],
         block_scratch(frames, rows + 2 * HALO, width),
         semaphores=1,
+        flops=flops // 2,
+        far=[-1],
+    )
+    passed = call(
+        functools.partial(pass_kernel, strips, rows, cols),
+        "pass_on",
+        [before, sums],
+        [bf16((Packed(HALO, HALO, cols).beside + 2 * TILE * Packed(HALO, rows, cols).tiles, LANES))] * len(ways),
+    )
+    before_edges = [lax.ppermute(edge, "strip", way) for edge, way in zip(passed, ways)]
+    h_shapes = [bf16(shape) for shape in block_scratch(frames, rows + 2, width)]
+    gain_first = scale_first[None]
+    *safe, edge_sums, w2_first, w2_middle, w2_last = call(
+        functools.partial(middle_kernel, strips, rows, cols),
+        "safe_rows",
+        [own_in, neighbour, *own_edges, before, sums, plane, middle, last, gain_first, weight_second],
+        h_shapes + [f32((len(ways), frames, HALO, width, channels))] + [plane_shape] * 3,
+        block_scratch(HALO, rows + 2 * HALO, width) + block_scratch(frames, 2 * HALO, width),
+        semaphores=3,
+        flops=flops // 2,
+        far=[-1],
+    )
+    h_lo, h_pairs, h_stacked, partial = call(
+        functools.partial(edge_kernel, strips, rows, cols),
+        "edge_rows",
+        [*before_edges, before, edge_sums, *safe, plane, middle, gain_first, w2_first, w2_middle],
+        h_shapes + [bf16((HALO, rows + rows // 2, cols, LANES))],
+        block_scratch(HALO, 2 * HALO, width),
         flops=flops,
-        far=[-1],
-    )
-    h_shapes = [bf16(shape) for shape in block_scratch(frames, rows + 2, width)]
-    h_lo, h_pairs, h_stacked, partial, *w2 = call(
-        functools.partial(first_kernel, strips, n_rows_h, rows, cols),
-        "first_layer",
-        [*before, own, plane, middle, scale_first[None], weight_second],
-        h_shapes + [bf16((HALO, rows + rows // 2, cols, LANES))] + [plane_shape] * 3,
-        block_scratch(HALO, rows + 2 * HALO, width),
-        semaphores=3,
-        flops=flops,
-        far=[-1],
-    )
+    )
+    w2 = [w2_first, w2_middle, w2_last]
     sent = forward(partial)
     own = call(
         functools.partial(second_kernel, frames, rows, cols),

time: 27.5 us -> 27.8 us (1.011)
  waiting for transfers between devices: 1.97 us -> 4.53 us
  starting transfers between devices: 15.4 us -> 12.9 us
    ppermute x3 -> x2, starting transfers between devices: 13.4 us -> 9.38 us  [forward(): return lax.ppermute(x, 'frame', [(i, i + 1) for i in range(steps - 1)])]
    ppermute x1 -> x2, starting transfers between devices: 1.56 us -> 3.11 us  [shards(): lax.ppermute(edge, 'strip', way)]
    ppermute x1 -> x2, waiting for transfers between devices: 0.01 us -> 1.41 us  [shards(): lax.ppermute(edge, 'strip', way)]
    ppermute x3 -> x2, waiting for transfers between devices: 1.97 us -> 3.11 us  [forward(): return lax.ppermute(x, 'frame', [(i, i + 1) for i in range(steps - 1)])]
    pallas_call x6 -> x8, Pallas kernels: 9.74 us -> 10 us  [call(): pl.pallas_call(kernel, out_shape=outs, in_specs=in_specs, out_specs=(away...]
  transfers between devices with their start and end apart: 5 -> 5, of which waited for: 1 -> 3; matrix products, arithmetic and copies ran while one was open for 0% -> 0% of each run, Pallas kernels for 19% -> 24%
where the time goes in v5:
time: 27.8 us; the launch traced here: 27.6 us
  starting transfers between devices  12.9 us (46%)
  Pallas kernels  10 us (36%)
  waiting for transfers between devices  4.53 us (16%)
    pallas_call x8, Pallas kernels, call(): pl.pallas_call(kernel, out_shape=outs, in_specs=in_specs, out_specs=(away...  10 us
    ppermute x2, starting transfers between devices, forward(): return lax.ppermute(x, 'frame', [(i, i + 1) for i in range(steps - 1)])  9.38 us
    ppermute x2, starting transfers between devices, shards(): lax.ppermute(edge, 'strip', way)  3.11 us
    ppermute x2, waiting for transfers between devices, forward(): return lax.ppermute(x, 'frame', [(i, i + 1) for i in range(steps - 1)])  3.11 us
    ppermute x2, waiting for transfers between devices, shards(): lax.ppermute(edge, 'strip', way)  1.41 us
  transfers between devices with their start and end apart: 5, of which 3 were waited for; matrix products, arithmetic and copies ran while one was open for 0% of the time, Pallas kernels for 24%

profile of v5, /device:TPU:0, one launch (start us, length us, event | category | flops | bytes accessed | tf_op | source)
XLA Modules:
  0.0 27.6 jit_solution(10757184491711721251)
XLA Ops:
  0.0 0.5 %collective-permute-start = (bf16[2,4,64,192]{3,2,1,0:T(8,128)(2,1)}, bf16[2,4,64,192]{3,2,1,0:T(8,128)(2,1)S(1)}, u32[]{:S(2)}, u32[]{:S(2)}) collective-permute-start(bf16[2,4,64,192]{3,2,1,0:T(8,128)(2,1)} %own_far.1), channel_id=1, source_target_pairs={{0,1},{1,0},{2,3},{3,2},{4,5},{5,4},{6,7},{7,6},{8,9},{9,8},{10,11... | collective-permute-start | bytes 589832 | tf_op jit(solution)/shard_map/ppermute | solution.py:19
  0.5 1.5 %stage.1 = (bf16[2,4,64,192]{3,2,1,0:T(8,128)(2,1)S(1)}, bf16[3,3,192,192]{3,2,1,0:T(8,128)(2,1)S(1)}, bf16[3,3,192,192]{3,2,1,0:T(8,128)(2,1)S(1)}) custom-call(bf16[2,4,64,192]{3,2,1,0:T(8,128)(2,1)} %own_far.1, bf16[3,3,3,192,192]{4,3,2,1,0:T(8,128)(2,1)} %weight_far.3), custom_call_target="tpu_custom_call" | custom-call | bytes 4194304 | tf_op jit(solution)/shard_map/stage/pallas_call | solution.py:421
  2.0 0.0 collective-permute-done.neighbour.refs_1_
  2.0 0.1 pack.1
  2.2 4.7 %collective-permute-start.1 = (bf16[800,128]{1,0:T(8,128)(2,1)S(1)}, bf16[800,128]{1,0:T(8,128)(2,1)S(1)}, u32[]{:S(2)}, u32[]{:S(2)}) collective-permute-start(bf16[800,128]{1,0:T(8,128)(2,1)S(1)} %get-tuple-element.24), channel_id=1, source_target_pairs={{0,4},{4,8},{8,12},{1,5},{5,9},{9,13},{2,6},{6,10},{10,14},{3,7},{... | collective-permute-start | bytes 614408 | tf_op jit(solution)/shard_map/ppermute | solution.py:24
  6.8 1.6 %collective-permute-start.3 = (bf16[416,128]{1,0:T(8,128)(2,1)S(1)}, bf16[416,128]{1,0:T(8,128)(2,1)S(1)}, u32[]{:S(2)}, u32[]{:S(2)}) collective-permute-start(bf16[416,128]{1,0:T(8,128)(2,1)S(1)} %get-tuple-element.28), channel_id=1, source_target_pairs={{0,2},{2,0},{1,3},{3,1},{4,6},{6,4},{5,7},{7,5},{8,10},{10,8},{9,1... | collective-permute-start | bytes 319496 | tf_op jit(solution)/shard_map/ppermute | solution.py:467
  8.4 0.0 copy-start
  8.4 2.1 %own_safe_rows.1 = (f32[2,3,80,192]{3,2,1,0:T(8,128)S(1)}, bf16[3,3,192,192]{3,2,1,0:T(8,128)(2,1)S(1)}) custom-call(bf16[2,4,64,192]{3,2,1,0:T(8,128)(2,1)S(1)} %get-tuple-element.23.own.refs_0_, bf16[2,4,64,192]{3,2,1,0:T(8,128)(2,1)S(1)} %collective-permute-done.neighbour.refs_1_, bf16[3,3,192,192]{3,2,1,0:T(8,128)(2,1)S(1)} %get-tuple-element.25.middle.refs_6_.refs_7_, ...), custom_call_target="tpu_custom_call" | custom-call | flops 254803968 | bytes 4194304 | tf_op jit(solution)/shard_map/own_safe_rows/pallas_call | solution.py:421
  10.5 1.2 %collective-permute-done.1.block.refs_3_.refs_1_ = bf16[800,128]{1,0:T(8,128)(2,1)S(1)} collective-permute-done((bf16[800,128]{1,0:T(8,128)(2,1)S(1)}, bf16[800,128]{1,0:T(8,128)(2,1)S(1)}, u32[]{:S(2)}, u32[]{:S(2)}) %collective-permute-start.1) | collective-permute-done | bytes 204832 | tf_op jit(solution)/shard_map/ppermute | solution.py:24
  11.6 1.6 %collective-permute-start.2 = (bf16[416,128]{1,0:T(8,128)(2,1)S(1)}, bf16[416,128]{1,0:T(8,128)(2,1)S(1)}, u32[]{:S(2)}, u32[]{:S(2)}) collective-permute-start(bf16[416,128]{1,0:T(8,128)(2,1)S(1)} %pass_on.1), channel_id=1, source_target_pairs={{0,2},{2,0},{1,3},{3,1},{4,6},{6,4},{5,7},{7,5},{8,10},{10,8},{9,1... | collective-permute-start | bytes 319496 | tf_op jit(solution)/shard_map/ppermute | solution.py:484
  13.2 0.0 collective-permute-done.3.refs_2_
  13.2 0.0 copy-done
  13.2 1.8 %safe_rows.1 = (bf16[2,6,80,128]{3,2,1,0:T(8,128)(2,1)S(1)}, bf16[2,7,80,128]{3,2,1,0:T(8,128)(2,1)S(1)}, bf16[1,6,80,128]{3,2,1,0:T(8,128)(2,1)S(1)}, f32[1,2,2...) custom-call(bf16[2,4,64,192]{3,2,1,0:T(8,128)(2,1)S(1)} %get-tuple-e, ...), custom_call_target="tpu_custom_call" | custom-call | flops 254803968 | bytes 4194304 | tf_op jit(solution)/shard_map/safe_rows/pallas_call | solution.py:421
  15.0 1.4 %collective-permute-done.2.refs_0_ = bf16[416,128]{1,0:T(8,128)(2,1)S(1)} collective-permute-done((bf16[416,128]{1,0:T(8,128)(2,1)S(1)}, bf16[416,128]{1,0:T(8,128)(2,1)S(1)}, u32[]{:S(2)}, u32[]{:S(2)}) %collective-permute-start.2) | collective-permute-done | bytes 106528 | tf_op jit(solution)/shard_map/ppermute | solution.py:484
  16.4 2.2 %edge_rows.1 = (bf16[2,6,80,128]{3,2,1,0:T(8,128)(2,1)S(1)}, bf16[2,7,80,128]{3,2,1,0:T(8,128)(2,1)S(1)}, bf16[1,6,80,128]{3,2,1,0:T(8,128)(2,1)S(1)}, bf16[2,6,64,128]{3,2,1,0:T(8,128)(2,1)S(1)}) custom-call(bf16[416,128]{1,0:T(8,128)(2,1)S(1)} %collective-permute-done.2.refs_0_, bf16[800,128]{1,0:T(8,128)(2,1)S(1)} %collective-permute-done.1.block.refs_3_.refs_1_, ...), custom_call_target="tpu_custom_call" | custom-call | flops 509607936 | bytes 4194304 | tf_op jit(solution)/shard_map/edge_rows/pallas_call | solution.py:421
  18.7 0.0 copy-start.1
  18.7 4.7 %collective-permute-start.4 = (bf16[2,6,64,128]{3,2,1,0:T(8,128)(2,1)S(1)}, bf16[2,6,64,128]{3,2,1,0:T(8,128)(2,1)S(1)}, u32[]{:S(2)}, u32[]{:S(2)}) collective-permute-start(bf16[2,6,64,128]{3,2,1,0:T(8,128)(2,1)S(1)} %get-tuple-element.36), channel_id=1, source_target_pairs={{0,4},{4,8},{8,12},{1,5},{5,9},{9,13},{2,6},{6,10},{10,14},{3,7},{... | collective-permute-start | bytes 589832 | tf_op jit(solution)/shard_map/ppermute | solution.py:24
  23.4 1.2 %second_layer.1.own = f32[2,4,64,192]{3,2,1,0:T(8,128)S(1)} custom-call(bf16[2,6,80,128]{3,2,1,0:T(8,128)(2,1)S(1)} %get-tuple-element.37.h_lo, bf16[2,7,80,128]{3,2,1,0:T(8,128)(2,1)S(1)} %get-tuple-element.38.h_pairs, bf16[1,6,80,128]{3,2,1,0:T(8,128)(2,1)S(1)} %get-tuple-element.39.h_stacked, ...), custom_call_target="tpu_custom_call" | custom-call | flops 509607936 | bytes 4194304 | tf_op jit(solution)/shard_map/second_layer/pallas_call | solution.py:421
  24.6 2.0 %collective-permute-done.4.partial = bf16[2,6,64,128]{3,2,1,0:T(8,128)(2,1)S(1)} collective-permute-done((bf16[2,6,64,128]{3,2,1,0:T(8,128)(2,1)S(1)}, bf16[2,6,64,128]{3,2,1,0:T(8,128)(2,1)S(1)}, u32[]{:S(2)}, u32[]{:S(2)}) %collective-permute-start.4) | collective-permute-done | bytes 196640 | tf_op jit(solution)/shard_map/ppermute | solution.py:24
  26.5 0.0 copy-done.1
  26.5 1.0 %finish.1 = bf16[2,4,64,192]{3,2,1,0:T(8,128)(2,1)} custom-call(bf16[2,6,64,128]{3,2,1,0:T(8,128)(2,1)S(1)} %collective-permute-done.4.partial, f32[2,4,64,192]{3,2,1,0:T(8,128)S(1)} %second_layer.1.own, f32[1,192]{1,0:T(1,128)S(1)} %bitcast.4), custom_call_target="tpu_custom_call" | custom-call | bytes 4194304 | tf_op jit(solution)/shard_map/finish/pallas_call | solution.py:421
  (1 shorter events, 0.0 us)
Async XLA Ops:
  0.0 2.0 %collective-permute-start = (bf16[2,4,64,192]{3,2,1,0:T(8,128)(2,1)}, bf16[2,4,64,192]{3,2,1,0:T(8,128)(2,1)S(1)}, u32[]{:S(2)}, u32[]{:S(2)}) collective-permute-start(bf16[2,4,64,192]{3,2,1,0:T(8,128)(2,1)} %own_far.1), channel_id=1, source_target_pairs={{0,1},{1,0},{2,3},{3,2},{4,5},{5,4},{6,7},{7,6},{8,9},{9,8},{10,11... | collective-permute-start | bytes 589832 | tf_op jit(solution)/shard_map/ppermute | solution.py:19
  2.2 9.5 %collective-permute-start.1 = (bf16[800,128]{1,0:T(8,128)(2,1)S(1)}, bf16[800,128]{1,0:T(8,128)(2,1)S(1)}, u32[]{:S(2)}, u32[]{:S(2)}) collective-permute-start(bf16[800,128]{1,0:T(8,128)(2,1)S(1)} %get-tuple-element.24), channel_id=1, source_target_pairs={{0,4},{4,8},{8,12},{1,5},{5,9},{9,13},{2,6},{6,10},{10,14},{3,7},{... | collective-permute-start | bytes 614408 | tf_op jit(solution)/shard_map/ppermute | solution.py:24
  6.8 6.4 %collective-permute-start.3 = (bf16[416,128]{1,0:T(8,128)(2,1)S(1)}, bf16[416,128]{1,0:T(8,128)(2,1)S(1)}, u32[]{:S(2)}, u32[]{:S(2)}) collective-permute-start(bf16[416,128]{1,0:T(8,128)(2,1)S(1)} %get-tuple-element.28), channel_id=1, source_target_pairs={{0,2},{2,0},{1,3},{3,1},{4,6},{6,4},{5,7},{7,5},{8,10},{10,8},{9,1... | collective-permute-start | bytes 319496 | tf_op jit(solution)/shard_map/ppermute | solution.py:467
  8.4 4.8 %copy-start = (f32[192]{0:T(256)S(1)}, f32[192]{0:T(256)}, u32[]{:S(2)}) copy-start(f32[192]{0:T(256)} %param.7) | copy-start | bytes 2308
  11.6 4.8 %collective-permute-start.2 = (bf16[416,128]{1,0:T(8,128)(2,1)S(1)}, bf16[416,128]{1,0:T(8,128)(2,1)S(1)}, u32[]{:S(2)}, u32[]{:S(2)}) collective-permute-start(bf16[416,128]{1,0:T(8,128)(2,1)S(1)} %pass_on.1), channel_id=1, source_target_pairs={{0,2},{2,0},{1,3},{3,1},{4,6},{6,4},{5,7},{7,5},{8,10},{10,8},{9,1... | collective-permute-start | bytes 319496 | tf_op jit(solution)/shard_map/ppermute | solution.py:484
  18.7 7.9 %copy-start.1 = (f32[192]{0:T(256)S(1)}, f32[192]{0:T(256)}, u32[]{:S(2)}) copy-start(f32[192]{0:T(256)} %param.9) | copy-start | bytes 2308
  18.7 7.9 %collective-permute-start.4 = (bf16[2,6,64,128]{3,2,1,0:T(8,128)(2,1)S(1)}, bf16[2,6,64,128]{3,2,1,0:T(8,128)(2,1)S(1)}, u32[]{:S(2)}, u32[]{:S(2)}) collective-permute-start(bf16[2,6,64,128]{3,2,1,0:T(8,128)(2,1)S(1)} %get-tuple-element.36), channel_id=1, source_target_pairs={{0,4},{4,8},{8,12},{1,5},{5,9},{9,13},{2,6},{6,10},{10,14},{3,7},{... | collective-permute-start | bytes 589832 | tf_op jit(solution)/shard_map/ppermute | solution.py:24

commit v6 on v5

--- a/solution.py
+++ b/solution.py
@@ -19,9 +19,11 @@
     return lax.ppermute(x, axis, [(0, 1), (1, 0)])
 
 
-def forward(x):
-    steps = lax.axis_size("frame")
-    return lax.ppermute(x, "frame", [(i, i + 1) for i in range(steps - 1)])
+def forward(x, way=None):
+    steps, count = lax.axis_size("frame"), lax.axis_size("strip")
+    way = [(i, i) for i in range(count)] if way is None else way
+    pairs = [(f * count + i, (f + 1) * count + j) for f in range(steps - 1) for i, j in way]
+    return lax.ppermute(x, ("frame", "strip"), pairs)
 
 
 def if_earlier(build):
@@ -304,19 +306,6 @@
         copy.wait()
 
 
-def pass_kernel(strips, rows, cols, block, _, *edges):
-    whole = Packed(HALO, rows, cols)
-    for start, edge in zip(facing(strips, rows), edges):
-        for f in range(HALO):
-            low = pl.multiple_of((f * rows + start) * cols, TILE)
-            edge[f * HALO * cols : (f + 1) * HALO * cols, :] = block[pl.ds(low, HALO * cols), :]
-            high = pl.multiple_of(whole.high + (f * (rows // 2) + start // 2) * cols, TILE)
-            at = HALO * HALO * cols + f * cols
-            edge[at : at + cols, :] = block[pl.ds(high, cols), :]
-        at = HALO * HALO * cols + HALO * cols
-        edge[at:, :] = block[whole.beside :, :]
-
-
 def edge_kernel(strips, rows, cols, *refs):
     *refs, near_lo, near_pairs, near_stacked = refs
     *refs, h_lo, h_pairs, h_stacked, partial = refs
@@ -324,7 +313,7 @@
     frames, channels = edge_sums.shape[1], edge_sums.shape[-1]
     width, rest = cols + TILE, channels - LANES
     strip = lax.axis_index("strip")
-    whole, strip_block = Packed(HALO, rows, cols), Packed(HALO, HALO, cols)
+    whole, strip_block = Packed(HALO, rows, cols), Packed(frames, HALO, cols)
     near = (near_lo, near_pairs, near_stacked)
     clear(near)
     for target, source in ((h_lo, safe_lo), (h_pairs, safe_pairs), (h_stacked, safe_stacked)):
@@ -339,9 +328,8 @@
             return block[pl.ds(low, cols), :], pair, *beside_from(block, whole.beside, (f * rows + r) * HALO, rest)
 
         def halo_row(f, j):
-            theirs = top * (rows - HALO) + j
-            cell = (f * rows + theirs) * HALO
-            return *strip_block.read(edge, f, j, rest), *beside_from(edge, strip_block.beside, cell, rest)
+            sent = frames - HALO + f
+            return *strip_block.read(edge, sent, j, rest), *strip_block.read_beside(edge, sent, j, rest)
 
         def own_half(f, r, j):
             low, pair, *tile = own_row(f, r)
@@ -465,6 +453,7 @@
     ways = [[(0, 1), (1, 0)]] if strips == 2 else [ups, downs]
     before = forward(block)
     own_edges = [lax.ppermute(edge, "strip", way) for edge, way in zip(edges, ways)]
+    before_edges = [forward(edge, way) for edge, way in zip(edges, ways)]
     sums, plane = call(
         functools.partial(safe_kernel, strips),
         "own_safe_rows",
@@ -475,13 +464,6 @@
         flops=flops // 2,
         far=[-1],
     )
-    passed = call(
-        functools.partial(pass_kernel, strips, rows, cols),
-        "pass_on",
-        [before, sums],
-        [bf16((Packed(HALO, HALO, cols).beside + 2 * TILE * Packed(HALO, rows, cols).tiles, LANES))] * len(ways),
-    )
-    before_edges = [lax.ppermute(edge, "strip", way) for edge, way in zip(passed, ways)]
     h_shapes = [bf16(shape) for shape in block_scratch(frames, rows + 2, width)]
     gain_first = scale_first[None]
     *safe, edge_sums, w2_first, w2_middle, w2_last = call(

time: 27.8 us -> 27.1 us (0.975)
  waiting for transfers between devices: 4.53 us -> 2.58 us
  starting transfers between devices: 12.9 us -> 14.1 us
    ppermute x2 -> x3, starting transfers between devices: 9.38 us -> 12.1 us  [forward(): return lax.ppermute(x, ('frame', 'strip'), pairs)]
    ppermute x2 -> x1, starting transfers between devices: 3.11 us -> 1.56 us  [shards(): lax.ppermute(edge, 'strip', way)]
    ppermute x2 -> x1, waiting for transfers between devices: 1.41 us -> 0.01 us  [shards(): lax.ppermute(edge, 'strip', way)]
    ppermute x2 -> x3, waiting for transfers between devices: 3.11 us -> 2.57 us  [forward(): return lax.ppermute(x, ('frame', 'strip'), pairs)]
    pallas_call x8 -> x7, Pallas kernels: 10 us -> 10.1 us  [call(): pl.pallas_call(kernel, out_shape=outs, in_specs=in_specs, out_specs=(away...]
  transfers between devices with their start and end apart: 5 -> 5, of which waited for: 3 -> 1; matrix products, arithmetic and copies ran while one was open for 0% -> 0% of each run, Pallas kernels for 24% -> 25%
where the time goes in v6:
time: 27.1 us; the launch traced here: 26.9 us
  starting transfers between devices  14.1 us (52%)
  Pallas kernels  10.1 us (37%)
  waiting for transfers between devices  2.58 us (10%)
    ppermute x3, starting transfers between devices, forward(): return lax.ppermute(x, ('frame', 'strip'), pairs)  12.1 us
    pallas_call x7, Pallas kernels, call(): pl.pallas_call(kernel, out_shape=outs, in_specs=in_specs, out_specs=(away...  10.1 us
    ppermute x3, waiting for transfers between devices, forward(): return lax.ppermute(x, ('frame', 'strip'), pairs)  2.57 us
    ppermute x1, starting transfers between devices, shards(): lax.ppermute(edge, 'strip', way)  1.56 us
  transfers between devices with their start and end apart: 5, of which 1 were waited for; matrix products, arithmetic and copies ran while one was open for 0% of the time, Pallas kernels for 25%

profile of v6, /device:TPU:0, one launch (start us, length us, event | category | flops | bytes accessed | tf_op | source)
XLA Modules:
  0.0 26.9 jit_solution(5448244131132979646)
XLA Ops:
  0.0 0.5 %collective-permute-start = (bf16[2,4,64,192]{3,2,1,0:T(8,128)(2,1)}, bf16[2,4,64,192]{3,2,1,0:T(8,128)(2,1)S(1)}, u32[]{:S(2)}, u32[]{:S(2)}) collective-permute-start(bf16[2,4,64,192]{3,2,1,0:T(8,128)(2,1)} %own_far.1), channel_id=1, source_target_pairs={{0,1},{1,0},{2,3},{3,2},{4,5},{5,4},{6,7},{7,6},{8,9},{9,8},{10,11... | collective-permute-start | bytes 589832 | tf_op jit(solution)/shard_map/ppermute | solution.py:19
  0.5 1.5 %stage.1 = (bf16[2,4,64,192]{3,2,1,0:T(8,128)(2,1)S(1)}, bf16[3,3,192,192]{3,2,1,0:T(8,128)(2,1)S(1)}, bf16[3,3,192,192]{3,2,1,0:T(8,128)(2,1)S(1)}) custom-call(bf16[2,4,64,192]{3,2,1,0:T(8,128)(2,1)} %own_far.1, bf16[3,3,3,192,192]{4,3,2,1,0:T(8,128)(2,1)} %weight_far.3), custom_call_target="tpu_custom_call" | custom-call | bytes 4194304 | tf_op jit(solution)/shard_map/stage/pallas_call | solution.py:409
  2.0 0.0 collective-permute-done.neighbour.refs_1_
  2.0 0.0 copy-start
  2.0 0.1 pack.1
  2.2 4.7 %collective-permute-start.2 = (bf16[800,128]{1,0:T(8,128)(2,1)S(1)}, bf16[800,128]{1,0:T(8,128)(2,1)S(1)}, u32[]{:S(2)}, u32[]{:S(2)}) collective-permute-start(bf16[800,128]{1,0:T(8,128)(2,1)S(1)} %get-tuple-element.25), channel_id=1, source_target_pairs={{0,4},{2,6},{4,8},{6,10},{8,12},{10,14},{1,5},{3,7},{5,9},{7,11},{... | collective-permute-start | bytes 614408 | tf_op jit(solution)/shard_map/ppermute | solution.py:26
  6.8 1.6 %collective-permute-start.3 = (bf16[416,128]{1,0:T(8,128)(2,1)S(1)}, bf16[416,128]{1,0:T(8,128)(2,1)S(1)}, u32[]{:S(2)}, u32[]{:S(2)}) collective-permute-start(bf16[416,128]{1,0:T(8,128)(2,1)S(1)} %get-tuple-element.24), channel_id=1, source_target_pairs={{0,2},{2,0},{1,3},{3,1},{4,6},{6,4},{5,7},{7,5},{8,10},{10,8},{9,1... | collective-permute-start | bytes 319496 | tf_op jit(solution)/shard_map/ppermute | solution.py:455
  8.4 3.4 %collective-permute-start.1 = (bf16[416,128]{1,0:T(8,128)(2,1)S(1)}, bf16[416,128]{1,0:T(8,128)(2,1)S(1)}, u32[]{:S(2)}, u32[]{:S(2)}) collective-permute-start(bf16[416,128]{1,0:T(8,128)(2,1)S(1)} %get-tuple-element.24), channel_id=1, source_target_pairs={{0,6},{2,4},{4,10},{6,8},{8,14},{10,12},{1,7},{3,5},{5,11},{7,9},{... | collective-permute-start | bytes 319496 | tf_op jit(solution)/shard_map/ppermute | solution.py:26
  11.8 2.1 %own_safe_rows.1 = (f32[2,3,80,192]{3,2,1,0:T(8,128)S(1)}, bf16[3,3,192,192]{3,2,1,0:T(8,128)(2,1)S(1)}) custom-call(bf16[2,4,64,192]{3,2,1,0:T(8,128)(2,1)S(1)} %get-tuple-element.23.own.refs_0_, bf16[2,4,64,192]{3,2,1,0:T(8,128)(2,1)S(1)} %collective-permute-done.neighbour.refs_1_, bf16[3,3,192,192]{3,2,1,0:T(8,128)(2,1)S(1)} %get-tuple-element.26.middle.refs_6_.refs_7_, ...), custom_call_target="tpu_custom_call" | custom-call | flops 254803968 | bytes 4194304 | tf_op jit(solution)/shard_map/own_safe_rows/pallas_call | solution.py:409
  13.9 0.0 collective-permute-done.3.refs_2_
  13.9 0.0 collective-permute-done.2.refs_3_.refs_1_
  13.9 0.0 copy-done
  14.0 1.8 %safe_rows.1 = (bf16[2,6,80,128]{3,2,1,0:T(8,128)(2,1)S(1)}, bf16[2,7,80,128]{3,2,1,0:T(8,128)(2,1)S(1)}, bf16[1,6,80,128]{3,2,1,0:T(8,128)(2,1)S(1)}, f32[1,2,2...) custom-call(bf16[2,4,64,192]{3,2,1,0:T(8,128)(2,1)S(1)} %get-tuple-e, ...), custom_call_target="tpu_custom_call" | custom-call | flops 254803968 | bytes 4194304 | tf_op jit(solution)/shard_map/safe_rows/pallas_call | solution.py:409
  15.8 0.0 collective-permute-done.1.refs_0_
  15.8 2.3 %edge_rows.1 = (bf16[2,6,80,128]{3,2,1,0:T(8,128)(2,1)S(1)}, bf16[2,7,80,128]{3,2,1,0:T(8,128)(2,1)S(1)}, bf16[1,6,80,128]{3,2,1,0:T(8,128)(2,1)S(1)}, bf16[2,6,64,128]{3,2,1,0:T(8,128)(2,1)S(1)}) custom-call(bf16[416,128]{1,0:T(8,128)(2,1)S(1)} %collective-permute-done.1.refs_0_, bf16[800,128]{1,0:T(8,128)(2,1)S(1)} %collective-permute-done.2.refs_3_.refs_1_, ...), custom_call_target="tpu_custom_call" | custom-call | flops 509607936 | bytes 4194304 | tf_op jit(solution)/shard_map/edge_rows/pallas_call | solution.py:409
  18.0 0.0 copy-start.1
  18.0 4.0 %collective-permute-start.4 = (bf16[2,6,64,128]{3,2,1,0:T(8,128)(2,1)S(1)}, bf16[2,6,64,128]{3,2,1,0:T(8,128)(2,1)S(1)}, u32[]{:S(2)}, u32[]{:S(2)}) collective-permute-start(bf16[2,6,64,128]{3,2,1,0:T(8,128)(2,1)S(1)} %get-tuple-element.36), channel_id=1, source_target_pairs={{0,4},{2,6},{4,8},{6,10},{8,12},{10,14},{1,5},{3,7},{5,9},{7,11},{... | collective-permute-start | bytes 589832 | tf_op jit(solution)/shard_map/ppermute | solution.py:26
  22.0 1.2 %second_layer.1.own = f32[2,4,64,192]{3,2,1,0:T(8,128)S(1)} custom-call(bf16[2,6,80,128]{3,2,1,0:T(8,128)(2,1)S(1)} %get-tuple-element.37.h_lo, bf16[2,7,80,128]{3,2,1,0:T(8,128)(2,1)S(1)} %get-tuple-element.38.h_pairs, bf16[1,6,80,128]{3,2,1,0:T(8,128)(2,1)S(1)} %get-tuple-element.39.h_stacked, ...), custom_call_target="tpu_custom_call" | custom-call | flops 509607936 | bytes 4194304 | tf_op jit(solution)/shard_map/second_layer/pallas_call | solution.py:409
  23.2 2.6 %collective-permute-done.4.partial = bf16[2,6,64,128]{3,2,1,0:T(8,128)(2,1)S(1)} collective-permute-done((bf16[2,6,64,128]{3,2,1,0:T(8,128)(2,1)S(1)}, bf16[2,6,64,128]{3,2,1,0:T(8,128)(2,1)S(1)}, u32[]{:S(2)}, u32[]{:S(2)}) %collective-permute-start.4) | collective-permute-done | bytes 196640 | tf_op jit(solution)/shard_map/ppermute | solution.py:26
  25.8 0.0 copy-done.1
  25.8 1.0 %finish.1 = bf16[2,4,64,192]{3,2,1,0:T(8,128)(2,1)} custom-call(bf16[2,6,64,128]{3,2,1,0:T(8,128)(2,1)S(1)} %collective-permute-done.4.partial, f32[2,4,64,192]{3,2,1,0:T(8,128)S(1)} %second_layer.1.own, f32[1,192]{1,0:T(1,128)S(1)} %bitcast.4), custom_call_target="tpu_custom_call" | custom-call | bytes 4194304 | tf_op jit(solution)/shard_map/finish/pallas_call | solution.py:409
Async XLA Ops:
  0.0 2.0 %collective-permute-start = (bf16[2,4,64,192]{3,2,1,0:T(8,128)(2,1)}, bf16[2,4,64,192]{3,2,1,0:T(8,128)(2,1)S(1)}, u32[]{:S(2)}, u32[]{:S(2)}) collective-permute-start(bf16[2,4,64,192]{3,2,1,0:T(8,128)(2,1)} %own_far.1), channel_id=1, source_target_pairs={{0,1},{1,0},{2,3},{3,2},{4,5},{5,4},{6,7},{7,6},{8,9},{9,8},{10,11... | collective-permute-start | bytes 589832 | tf_op jit(solution)/shard_map/ppermute | solution.py:19
  2.0 11.9 %copy-start = (f32[192]{0:T(256)S(1)}, f32[192]{0:T(256)}, u32[]{:S(2)}) copy-start(f32[192]{0:T(256)} %param.7) | copy-start | bytes 2308
  2.2 11.8 %collective-permute-start.2 = (bf16[800,128]{1,0:T(8,128)(2,1)S(1)}, bf16[800,128]{1,0:T(8,128)(2,1)S(1)}, u32[]{:S(2)}, u32[]{:S(2)}) collective-permute-start(bf16[800,128]{1,0:T(8,128)(2,1)S(1)} %get-tuple-element.25), channel_id=1, source_target_pairs={{0,4},{2,6},{4,8},{6,10},{8,12},{10,14},{1,5},{3,7},{5,9},{7,11},{... | collective-permute-start | bytes 614408 | tf_op jit(solution)/shard_map/ppermute | solution.py:26
  6.8 7.1 %collective-permute-start.3 = (bf16[416,128]{1,0:T(8,128)(2,1)S(1)}, bf16[416,128]{1,0:T(8,128)(2,1)S(1)}, u32[]{:S(2)}, u32[]{:S(2)}) collective-permute-start(bf16[416,128]{1,0:T(8,128)(2,1)S(1)} %get-tuple-element.24), channel_id=1, source_target_pairs={{0,2},{2,0},{1,3},{3,1},{4,6},{6,4},{5,7},{7,5},{8,10},{10,8},{9,1... | collective-permute-start | bytes 319496 | tf_op jit(solution)/shard_map/ppermute | solution.py:455
  8.4 7.4 %collective-permute-start.1 = (bf16[416,128]{1,0:T(8,128)(2,1)S(1)}, bf16[416,128]{1,0:T(8,128)(2,1)S(1)}, u32[]{:S(2)}, u32[]{:S(2)}) collective-permute-start(bf16[416,128]{1,0:T(8,128)(2,1)S(1)} %get-tuple-element.24), channel_id=1, source_target_pairs={{0,6},{2,4},{4,10},{6,8},{8,14},{10,12},{1,7},{3,5},{5,11},{7,9},{... | collective-permute-start | bytes 319496 | tf_op jit(solution)/shard_map/ppermute | solution.py:26
  18.0 7.8 %copy-start.1 = (f32[192]{0:T(256)S(1)}, f32[192]{0:T(256)}, u32[]{:S(2)}) copy-start(f32[192]{0:T(256)} %param.9) | copy-start | bytes 2308
  18.0 7.8 %collective-permute-start.4 = (bf16[2,6,64,128]{3,2,1,0:T(8,128)(2,1)S(1)}, bf16[2,6,64,128]{3,2,1,0:T(8,128)(2,1)S(1)}, u32[]{:S(2)}, u32[]{:S(2)}) collective-permute-start(bf16[2,6,64,128]{3,2,1,0:T(8,128)(2,1)S(1)} %get-tuple-element.36), channel_id=1, source_target_pairs={{0,4},{2,6},{4,8},{6,10},{8,12},{10,14},{1,5},{3,7},{5,9},{7,11},{... | collective-permute-start | bytes 589832 | tf_op jit(solution)/shard_map/ppermute | solution.py:26

commit v7 on v6

--- a/solution.py
+++ b/solution.py
@@ -10,6 +10,7 @@
 LANES = 128
 TILE = 16
 EPS = 1e-06
+MOVED = 64
 
 
 HALO = 2
@@ -178,11 +179,10 @@
     return neighbour[f, r, pl.ds(start, TILE), :]
 
 
-def stage_kernel(own_far, weight_far, own, middle, last, arrived):
+def stage_kernel(own_far, weight_far, own, weight, arrived):
     copies = [
         pltpu.make_async_copy(own_far, own, arrived.at[0]),
-        pltpu.make_async_copy(weight_far.at[2], last, arrived.at[1]),
-        pltpu.make_async_copy(weight_far.at[1], middle, arrived.at[2]),
+        pltpu.make_async_copy(weight_far, weight, arrived.at[1]),
     ]
     for copy in copies:
         copy.start()
@@ -206,44 +206,12 @@
     return tile[:, :LANES], tile[:, LANES:]
 
 
-def window(buffers, frames, top, rows, cols, own, halo):
-    every, beside = slice(0, cols), slice(cols, cols + TILE)
-    for f in range(frames):
-        for j in range(HALO):
-            for cells, row in ((own(f, (1 - top) * (rows - HALO) + j), HALO * top + j), (halo(f, j), HALO * (1 - top) + j)):
-                fill(*buffers, f, row, every, *cells[:2])
-                fill(*buffers, f, row, beside, *cells[2:])
-
-
-def safe_kernel(strips, own, neighbour, middle, last, weight_far, out, plane, lo, pairs, stacked, arrived):
-    frames, rows, cols, channels = own.shape
-    width = cols + TILE
-    copy = pltpu.make_async_copy(weight_far.at[0], plane, arrived.at[0])
-    copy.start()
-    if frames > 2:
-        copy.wait()
-    clear((lo, pairs, stacked))
-    for f in range(frames):
-        for r in range(rows):
-            cells = own[f, r]
-            fill(lo, pairs, stacked, f, r + HALO, slice(0, cols), cells[:, :LANES], cells[:, LANES:])
-            fill(lo, pairs, stacked, f, r + HALO, slice(cols, width), *own_beside(neighbour, f, r, cols))
-    start, count = safe_rows(strips, rows)
-    for t in range(frames):
-        taps = own_taps(t)
-        products = convolve(taps, [plane, middle, last], columns(taps, lo, pairs, stacked, start, count))
-        for r in range(count):
-            out[t, r] = join(products, r * width, width)
-    if frames <= 2:
-        copy.wait()
-
-
-def own_taps(t):
-    return [(f, f - t + 2) for f in range(max(0, t - 2), t + 1)]
-
-
-def earlier_taps(t):
-    return [(f, f - t) for f in range(t, HALO)]
+def split(weight):
+    return [weight.at[a] for a in range(3)]
+
+
+def all_taps(t):
+    return [(t, 0), (t + 1, 1), (t + 2, 2)]
 
 
 def hidden_row(y, gain, cols):
@@ -254,114 +222,94 @@
     return jnp.where((position < right) | (position >= left), activate(y, gain), 0.0)
 
 
-def middle_kernel(strips, rows, cols, *refs):
-    *refs, lo, pairs, stacked, near_lo, near_pairs, near_stacked, arrived = refs
-    *refs, h_lo, h_pairs, h_stacked, edge_sums, w2_first, w2_middle, w2_last = refs
-    own, neighbour, *edges, block, sums, plane, middle, last, gains, w2_far = refs
-    frames, channels = own.shape[0], own.shape[-1]
+def hidden_rows(strips, frames, buffers, start, count, weight, gain, cols):
+    lefts = jnp.concatenate([columns(all_taps(t), *buffers, start, count) for t in range(frames)], axis=0)
+    products = convolve(all_taps(0), split(weight), lefts)
+    width = cols + TILE
+    for t in range(frames):
+        for r in range(count):
+            yield t, r, hidden_row(join(products, (t * count + r) * width, width), gain, cols)
+
+
+def safe_kernel(strips, own, neighbour, block, weight, gains, h_lo, h_pairs, h_stacked, lo, pairs, stacked):
+    frames, rows, cols, channels = own.shape
     width, rest = cols + TILE, channels - LANES
-    w2 = [w2_first, w2_middle, w2_last]
-    copies = [pltpu.make_async_copy(w2_far.at[a], w2[a], arrived.at[a]) for a in range(3)]
-    for copy in copies:
-        copy.start()
-    clear((lo, pairs, stacked, h_lo, h_pairs, h_stacked, near_pairs))
-    whole, strip_block = Packed(HALO, rows, cols), Packed(frames, HALO, cols)
+    every, beside = slice(0, cols), slice(cols, width)
+    clear((lo, pairs, stacked, h_lo, h_pairs, h_stacked))
+    whole = Packed(HALO, rows, cols)
 
     @if_earlier
     def build():
         for f in range(HALO):
             for r in range(rows):
-                fill(lo, pairs, stacked, f, r + HALO, slice(0, cols), *whole.read(block, f, r, rest))
-                fill(lo, pairs, stacked, f, r + HALO, slice(cols, width), *whole.read_beside(block, f, r, rest))
-
-    gain = gains[...]
+                fill(lo, pairs, stacked, f, r + HALO, every, *whole.read(block, f, r, rest))
+                fill(lo, pairs, stacked, f, r + HALO, beside, *whole.read_beside(block, f, r, rest))
+
+    for f in range(frames):
+        for r in range(rows):
+            cells = own[f, r]
+            fill(lo, pairs, stacked, HALO + f, r + HALO, every, cells[:, :LANES], cells[:, LANES:])
+            fill(lo, pairs, stacked, HALO + f, r + HALO, beside, *own_beside(neighbour, f, r, cols))
     start, count = safe_rows(strips, rows)
-    for t in range(frames):
-        taps = earlier_taps(t)
-        products = convolve(taps, [plane, middle], columns(taps, lo, pairs, stacked, start, count)) if taps else None
-        for r in range(count):
-            y = sums[t, r]
-            if taps:
-                y = y + join(products, r * width, width)
-            h = hidden_row(y, gain, cols).astype(jnp.bfloat16)
-            fill(h_lo, h_pairs, h_stacked, t, start + r, slice(0, width), h[:, :LANES], h[:, LANES:])
-
-    near = (near_lo, near_pairs, near_stacked)
-    for group, (edge, top) in enumerate(zip(edges, at_top(strips))):
-
-        def own_row(f, r):
-            cells = own[f, r]
-            return cells[:, :LANES], cells[:, LANES:], *own_beside(neighbour, f, r, cols)
-
-        def halo_row(f, j):
-            return *strip_block.read(edge, f, j, rest), *strip_block.read_beside(edge, f, j, rest)
-
-        window(near, frames, top, rows, cols, own_row, halo_row)
-        for t in range(frames):
-            taps = own_taps(t)
-            products = convolve(taps, [plane, middle, last], columns(taps, *near, 0, HALO))
-            for r in range(HALO):
-                edge_sums[group, t, r] = join(products, r * width, width)
-    for copy in copies:
-        copy.wait()
-
-
-def edge_kernel(strips, rows, cols, *refs):
+    for t, r, h in hidden_rows(strips, frames, (lo, pairs, stacked), start, count, weight, gains[...], cols):
+        h = h.astype(jnp.bfloat16)
+        fill(h_lo, h_pairs, h_stacked, t, start + r, slice(0, width), h[:, :LANES], h[:, LANES:])
+
+
+def edge_kernel(strips, *refs):
     *refs, near_lo, near_pairs, near_stacked = refs
     *refs, h_lo, h_pairs, h_stacked, partial = refs
-    *edges, block, edge_sums, safe_lo, safe_pairs, safe_stacked, plane, middle, gains, w2_first, w2_middle = refs
-    frames, channels = edge_sums.shape[1], edge_sums.shape[-1]
+    *edges, own, neighbour, block, safe_lo, safe_pairs, safe_stacked, w1, gains, w2 = refs
+    frames, rows, cols, channels = own.shape
     width, rest = cols + TILE, channels - LANES
+    every, beside = slice(0, cols), slice(cols, width)
     strip = lax.axis_index("strip")
     whole, strip_block = Packed(HALO, rows, cols), Packed(frames, HALO, cols)
     near = (near_lo, near_pairs, near_stacked)
     clear(near)
     for target, source in ((h_lo, safe_lo), (h_pairs, safe_pairs), (h_stacked, safe_stacked)):
         target[...] = source[...]
-    gain = gains[...]
-    for group, (edge, top) in enumerate(zip(edges, at_top(strips))):
-
-        def own_row(f, r):
-            low = pl.multiple_of((f * rows + r) * cols, TILE)
-            high = pl.multiple_of(whole.high + (f * (rows // 2) + r // 2) * cols, TILE)
-            pair = block[pl.ds(high, cols), :]
-            return block[pl.ds(low, cols), :], pair, *beside_from(block, whole.beside, (f * rows + r) * HALO, rest)
-
-        def halo_row(f, j):
-            sent = frames - HALO + f
-            return *strip_block.read(edge, sent, j, rest), *strip_block.read_beside(edge, sent, j, rest)
-
-        def own_half(f, r, j):
-            low, pair, *tile = own_row(f, r)
-            return low, pair[:, (j % 2) * rest : (j % 2 + 1) * rest], *tile
+    tops = at_top(strips)
+    for own_edge, earlier_edge, top in zip(edges, edges[len(tops) :], tops):
+        first, mine, theirs = (1 - top) * (rows - HALO), HALO * top, HALO * (1 - top)
+
+        def put(frame, row, *cells):
+            fill(*near, frame, row, every, *cells[:2])
+            fill(*near, frame, row, beside, *cells[2:])
+
+        def put_halo(frame, j, edge, f):
+            cells = *strip_block.read(edge, f, j, rest), *strip_block.read_beside(edge, f, j, rest)
+            put(frame, theirs + j, *cells)
 
         @if_earlier
         def build():
-            every, beside = slice(0, cols), slice(cols, width)
             for f in range(HALO):
                 for j in range(HALO):
-                    mine = own_half(f, (1 - top) * (rows - HALO) + j, j)
-                    for cells, row in ((mine, HALO * top + j), (halo_row(f, j), HALO * (1 - top) + j)):
-                        fill(*near, f, row, every, *cells[:2])
-                        fill(*near, f, row, beside, *cells[2:])
-
-        for t in range(frames):
-            taps = earlier_taps(t)
-            products = convolve(taps, [plane, middle], columns(taps, *near, 0, HALO)) if taps else None
-            for r in range(HALO):
-                y = edge_sums[group, t, r]
-                if taps:
-                    y = y + join(products, r * width, width)
-                h = hidden_row(y, gain, cols)
-                if strips != 2 and r == 1 - top:
-                    h = h * jnp.where(strip == (0 if top else strips - 1), 0.0, 1.0)
-                h = h.astype(jnp.bfloat16)
-                row = (1 - top) * rows + r
-                fill(h_lo, h_pairs, h_stacked, t, row, slice(0, width), h[:, :LANES], h[:, LANES:])
+                    r = first + j
+                    low = pl.multiple_of((f * rows + r) * cols, TILE)
+                    high = pl.multiple_of(whole.high + (f * (rows // 2) + r // 2) * cols, TILE)
+                    half = block[pl.ds(high, cols), :][:, (j % 2) * rest : (j % 2 + 1) * rest]
+                    tile = beside_from(block, whole.beside, (f * rows + r) * HALO, rest)
+                    put(f, mine + j, block[pl.ds(low, cols), :], half, *tile)
+                    put_halo(f, j, earlier_edge, frames - HALO + f)
+
+        for f in range(frames):
+            for j in range(HALO):
+                cells = own[f, first + j]
+                tile = own_beside(neighbour, f, first + j, cols)
+                put(HALO + f, mine + j, cells[:, :LANES], cells[:, LANES:], *tile)
+                put_halo(HALO + f, j, own_edge, f)
+
+        for t, r, h in hidden_rows(strips, frames, near, 0, HALO, w1, gains[...], cols):
+            if strips != 2 and r == 1 - top:
+                h = h * jnp.where(strip == (0 if top else strips - 1), 0.0, 1.0)
+            h = h.astype(jnp.bfloat16)
+            row = (1 - top) * rows + r
+            fill(h_lo, h_pairs, h_stacked, t, row, slice(0, width), h[:, :LANES], h[:, LANES:])
 
     last = frames - 1
     for t, taps in enumerate(([(last - 1, 0), (last, 1)], [(last, 0)])):
-        products = convolve(taps, [w2_first, w2_middle], columns(taps, h_lo, h_pairs, h_stacked, 0, rows))
+        products = convolve(taps, split(w2), columns(taps, h_lo, h_pairs, h_stacked, 0, rows))
         for r in range(rows):
             y = join(products, r * width, width)[:cols].astype(jnp.bfloat16)
             partial[t, r] = y[:, :LANES]
@@ -369,12 +317,11 @@
             partial[t, rows + r // 2, :, half * rest : (half + 1) * rest] = y[:, LANES:]
 
 
-def second_kernel(frames, rows, cols, h_lo, h_pairs, h_stacked, *refs):
-    *w2, out = refs
+def second_kernel(frames, rows, cols, h_lo, h_pairs, h_stacked, w2, out):
     width = cols + TILE
     for t in range(frames):
         taps = [(f, f - t + 2) for f in range(max(0, t - 2), t + 1)]
-        products = convolve(taps, w2, columns(taps, h_lo, h_pairs, h_stacked, 0, rows))
+        products = convolve(taps, split(w2), columns(taps, h_lo, h_pairs, h_stacked, 0, rows))
         for r in range(rows):
             out[t, r] = join(products, r * width, width)[:cols]
 
@@ -399,7 +346,7 @@
         copy.wait()
 
 
-def call(kernel, name, ins, outs, scratch=(), semaphores=0, flops=0, far=(), far_out=False):
+def call(kernel, name, ins, outs, scratch=(), semaphores=0, flops=0, moved=4, far=(), far_out=False):
     near, away = pl.BlockSpec(memory_space=pltpu.VMEM), pl.BlockSpec(memory_space=pltpu.HBM)
     in_specs, ins = [near] * len(ins), list(ins)
     for place in far:
@@ -414,7 +361,7 @@
         scratch_shapes=[pltpu.VMEM(shape, jnp.bfloat16) for shape in scratch]
         + [pltpu.SemaphoreType.DMA((semaphores,))] * (semaphores > 0),
         compiler_params=pltpu.CompilerParams(vmem_limit_bytes=24 * 1024 * 1024),
-        cost_estimate=pl.CostEstimate(flops=flops, bytes_accessed=4 * 1024 * 1024, transcendentals=0),
+        cost_estimate=pl.CostEstimate(flops=flops, bytes_accessed=moved * 1024 * 1024, transcendentals=0),
         name=name,
     )(*ins)
 
@@ -431,22 +378,22 @@
     bf16 = functools.partial(jax.ShapeDtypeStruct, dtype=jnp.bfloat16)
     f32 = functools.partial(jax.ShapeDtypeStruct, dtype=jnp.float32)
 
-    plane_shape = bf16(weight_first.shape[1:])
     neighbour = swap(frames_in, "slab")
-    own_in, middle, last = call(
+    own, weight_first = call(
         stage_kernel,
         "stage",
         [frames_in, weight_first],
-        [bf16(frames_in.shape), plane_shape, plane_shape],
-        semaphores=3,
+        [bf16(frames_in.shape), bf16(weight_first.shape)],
+        semaphores=2,
         far=[0, 1],
     )
     edge_shape = bf16(Packed(frames, HALO, cols).shape)
     block, *edges = call(
         functools.partial(pack_kernel, strips),
         "pack",
-        [own_in, neighbour],
+        [own, neighbour],
         [bf16(Packed(HALO, rows, cols).shape)] + [edge_shape] * (1 if strips == 2 else 2),
+        moved=MOVED,
     )
     ups = [(i, i + 1) for i in range(strips - 1)]
     downs = [(i + 1, i) for i in range(strips - 1)]
@@ -454,42 +401,29 @@
     before = forward(block)
     own_edges = [lax.ppermute(edge, "strip", way) for edge, way in zip(edges, ways)]
     before_edges = [forward(edge, way) for edge, way in zip(edges, ways)]
-    sums, plane = call(
+    gain_first = scale_first[None]
+    h_shapes = [bf16(shape) for shape in block_scratch(frames, rows + 2, width)]
+    safe = call(
         functools.partial(safe_kernel, strips),
-        "own_safe_rows",
-        [own_in, neighbour, middle, last, weight_first],
-        [f32((frames, safe_rows(strips, rows)[1], width, channels)), plane_shape],
-        block_scratch(frames, rows + 2 * HALO, width),
-        semaphores=1,
-        flops=flops // 2,
-        far=[-1],
-    )
-    h_shapes = [bf16(shape) for shape in block_scratch(frames, rows + 2, width)]
-    gain_first = scale_first[None]
-    *safe, edge_sums, w2_first, w2_middle, w2_last = call(
-        functools.partial(middle_kernel, strips, rows, cols),
         "safe_rows",
-        [own_in, neighbour, *own_edges, before, sums, plane, middle, last, gain_first, weight_second],
-        h_shapes + [f32((len(ways), frames, HALO, width, channels))] + [plane_shape] * 3,
-        block_scratch(HALO, rows + 2 * HALO, width) + block_scratch(frames, 2 * HALO, width),
-        semaphores=3,
-        flops=flops // 2,
-        far=[-1],
+        [own, neighbour, before, weight_first, gain_first],
+        h_shapes,
+        block_scratch(HALO + frames, rows + 2 * HALO, width),
+        flops=flops,
     )
     h_lo, h_pairs, h_stacked, partial = call(
-        functools.partial(edge_kernel, strips, rows, cols),
+        functools.partial(edge_kernel, strips),
         "edge_rows",
-        [*before_edges, before, edge_sums, *safe, plane, middle, gain_first, w2_first, w2_middle],
+        [*own_edges, *before_edges, own, neighbour, before, *safe, weight_first, gain_first, weight_second],
         h_shapes + [bf16((HALO, rows + rows // 2, cols, LANES))],
-        block_scratch(HALO, 2 * HALO, width),
+        block_scratch(HALO + frames, 2 * HALO, width),
         flops=flops,
     )
-    w2 = [w2_first, w2_middle, w2_last]
     sent = forward(partial)
     own = call(
         functools.partial(second_kernel, frames, rows, cols),
         "second_layer",
-        [h_lo, h_pairs, h_stacked, *w2],
+        [h_lo, h_pairs, h_stacked, weight_second],
         f32((frames, rows, cols, channels)),
         flops=flops,
     )

time: 27.1 us -> 30.9 us (1.14)
  waiting for transfers between devices: 2.58 us -> 5.11 us
  starting transfers between devices: 14.1 us -> 15.9 us
  Pallas kernels: 10.1 us -> 9.68 us
    ppermute x3, starting transfers between devices: 12.1 us -> 14.8 us  [forward(): return lax.ppermute(x, ('frame', 'strip'), pairs)]
    ppermute x1, waiting for transfers between devices: 0.01 us -> 1.95 us  [shards(): lax.ppermute(edge, 'strip', way)]
    ppermute x1, starting transfers between devices: 1.56 us -> 0.6 us  [shards(): lax.ppermute(edge, 'strip', way)]
    ppermute x3, waiting for transfers between devices: 2.57 us -> 3.16 us  [forward(): return lax.ppermute(x, ('frame', 'strip'), pairs)]
    pallas_call x7 -> x6, Pallas kernels: 10.1 us -> 9.68 us  [call(): pl.pallas_call(kernel, out_shape=outs, in_specs=in_specs, out_specs=(away...]
  transfers between devices with their start and end apart: 5 -> 5, of which waited for: 1 -> 3; matrix products, arithmetic and copies ran while one was open for 0% -> 0% of each run, Pallas kernels for 25% -> 17%
where the time goes in v7:
time: 30.9 us; the launch traced here: 30.7 us
  starting transfers between devices  15.9 us (51%)
  Pallas kernels  9.68 us (31%)
  waiting for transfers between devices  5.11 us (17%)
    ppermute x3, starting transfers between devices, forward(): return lax.ppermute(x, ('frame', 'strip'), pairs)  14.8 us
    pallas_call x6, Pallas kernels, call(): pl.pallas_call(kernel, out_shape=outs, in_specs=in_specs, out_specs=(away...  9.68 us
    ppermute x3, waiting for transfers between devices, forward(): return lax.ppermute(x, ('frame', 'strip'), pairs)  3.16 us
    ppermute x1, waiting for transfers between devices, shards(): lax.ppermute(edge, 'strip', way)  1.95 us
  transfers between devices with their start and end apart: 5, of which 3 were waited for; matrix products, arithmetic and copies ran while one was open for 0% of the time, Pallas kernels for 17%

profile of v7, /device:TPU:0, one launch (start us, length us, event | category | flops | bytes accessed | tf_op | source)
XLA Modules:
  0.0 30.7 jit_solution(9450536102732255727)
XLA Ops:
  0.0 0.0 copy-start.1
  0.0 0.5 %collective-permute-start = (bf16[2,4,64,192]{3,2,1,0:T(8,128)(2,1)}, bf16[2,4,64,192]{3,2,1,0:T(8,128)(2,1)S(1)}, u32[]{:S(2)}, u32[]{:S(2)}) collective-permute-start(bf16[2,4,64,192]{3,2,1,0:T(8,128)(2,1)} %own_far.1), channel_id=1, source_target_pairs={{0,1},{1,0},{2,3},{3,2},{4,5},{5,4},{6,7},{7,6},{8,9},{9,8},{10,11... | collective-permute-start | bytes 589832 | tf_op jit(solution)/shard_map/ppermute | solution.py:20
  0.5 1.9 %stage.1 = (bf16[2,4,64,192]{3,2,1,0:T(8,128)(2,1)S(1)}, bf16[3,3,3,192,192]{4,3,2,1,0:T(8,128)(2,1)S(1)}) custom-call(bf16[2,4,64,192]{3,2,1,0:T(8,128)(2,1)} %own_far.1, bf16[3,3,3,192,192]{4,3,2,1,0:T(8,128)(2,1)} %weight_far.1), custom_call_target="tpu_custom_call" | custom-call | bytes 4194304 | tf_op jit(solution)/shard_map/stage/pallas_call | solution.py:356
  2.3 0.0 copy-start
  2.3 0.0 collective-permute-done.neighbour.refs_3_
  2.4 0.1 pack.1
  2.5 4.6 %collective-permute-start.3 = (bf16[800,128]{1,0:T(8,128)(2,1)S(1)}, bf16[800,128]{1,0:T(8,128)(2,1)S(1)}, u32[]{:S(2)}, u32[]{:S(2)}) collective-permute-start(bf16[800,128]{1,0:T(8,128)(2,1)S(1)} %get-tuple-element.18), channel_id=1, source_target_pairs={{0,4},{2,6},{4,8},{6,10},{8,12},{10,14},{1,5},{3,7},{5,9},{7,11},{... | collective-permute-start | bytes 614408 | tf_op jit(solution)/shard_map/ppermute | solution.py:27
  7.1 4.4 %collective-permute-start.2 = (bf16[416,128]{1,0:T(8,128)(2,1)S(1)}, bf16[416,128]{1,0:T(8,128)(2,1)S(1)}, u32[]{:S(2)}, u32[]{:S(2)}) collective-permute-start(bf16[416,128]{1,0:T(8,128)(2,1)S(1)} %get-tuple-element.17), channel_id=1, source_target_pairs={{0,6},{2,4},{4,10},{6,8},{8,14},{10,12},{1,7},{3,5},{5,11},{7,9},{... | collective-permute-start | bytes 319496 | tf_op jit(solution)/shard_map/ppermute | solution.py:27
  11.5 0.6 %collective-permute-start.1 = (bf16[416,128]{1,0:T(8,128)(2,1)S(1)}, bf16[416,128]{1,0:T(8,128)(2,1)S(1)}, u32[]{:S(2)}, u32[]{:S(2)}) collective-permute-start(bf16[416,128]{1,0:T(8,128)(2,1)S(1)} %get-tuple-element.17), channel_id=1, source_target_pairs={{0,2},{2,0},{1,3},{3,1},{4,6},{6,4},{5,7},{7,5},{8,10},{10,8},{9,1... | collective-permute-start | bytes 319496 | tf_op jit(solution)/shard_map/ppermute | solution.py:402
  12.1 0.1 collective-permute-done.3.block.refs_4_
  12.3 0.0 copy-done.1
  12.3 2.2 %safe_rows.1 = (bf16[2,6,80,128]{3,2,1,0:T(8,128)(2,1)S(1)}, bf16[2,7,80,128]{3,2,1,0:T(8,128)(2,1)S(1)}, bf16[1,6,80,128]{3,2,1,0:T(8,128)(2,1)S(1)}) custom-call(bf16[2,4,64,192]{3,2,1,0:T(8,128)(2,1)S(1)} %get-tuple-element.16.own.refs_2_, bf16[2,4,64,192]{3,2,1,0:T(8,128)(2,1)S(1)} %collective-permute-done.neighbour.refs_3_, ...), custom_call_target="tpu_custom_call" | custom-call | flops 509607936 | bytes 4194304 | tf_op jit(solution)/shard_map/safe_rows/pallas_call | solution.py:356
  14.5 0.0 collective-permute-done.2.refs_1_
  14.5 1.9 %collective-permute-done.1.refs_0_ = bf16[416,128]{1,0:T(8,128)(2,1)S(1)} collective-permute-done((bf16[416,128]{1,0:T(8,128)(2,1)S(1)}, bf16[416,128]{1,0:T(8,128)(2,1)S(1)}, u32[]{:S(2)}, u32[]{:S(2)}) %collective-permute-start.1) | collective-permute-done | bytes 106528 | tf_op jit(solution)/shard_map/ppermute | solution.py:402
  16.4 0.0 copy-done
  16.4 3.2 %edge_rows.1 = (bf16[2,6,80,128]{3,2,1,0:T(8,128)(2,1)S(1)}, bf16[2,7,80,128]{3,2,1,0:T(8,128)(2,1)S(1)}, bf16[1,6,80,128]{3,2,1,0:T(8,128)(2,1)S(1)}, bf16[2,6,64,128]{3,2,1,0:T(8,128)(2,1)S(1)}) custom-call(bf16[416,128]{1,0:T(8,128)(2,1)S(1)} %collective-permute-done.1.refs_0_, bf16[416,128]{1,0:T(8,128)(2,1)S(1)} %collective-permute-done.2.refs_1_, ...), custom_call_target="tpu_custom_call" | custom-call | flops 509607936 | bytes 4194304 | tf_op jit(solution)/shard_map/edge_rows/pallas_call | solution.py:356
  19.7 0.0 copy-start.2
  19.7 5.8 %collective-permute-start.4 = (bf16[2,6,64,128]{3,2,1,0:T(8,128)(2,1)S(1)}, bf16[2,6,64,128]{3,2,1,0:T(8,128)(2,1)S(1)}, u32[]{:S(2)}, u32[]{:S(2)}) collective-permute-start(bf16[2,6,64,128]{3,2,1,0:T(8,128)(2,1)S(1)} %get-tuple-element.23), channel_id=1, source_target_pairs={{0,4},{2,6},{4,8},{6,10},{8,12},{10,14},{1,5},{3,7},{5,9},{7,11},{... | collective-permute-start | bytes 589832 | tf_op jit(solution)/shard_map/ppermute | solution.py:27
  25.4 1.2 %second_layer.1.own = f32[2,4,64,192]{3,2,1,0:T(8,128)S(1)} custom-call(bf16[2,6,80,128]{3,2,1,0:T(8,128)(2,1)S(1)} %get-tuple-element.24.h_lo, bf16[2,7,80,128]{3,2,1,0:T(8,128)(2,1)S(1)} %get-tuple-element.25.h_pairs, bf16[1,6,80,128]{3,2,1,0:T(8,128)(2,1)S(1)} %get-tuple-element.26.h_stacked, bf16[3,3,3,192,192]{4,3,2,1,0:T(8,128)(2,1)S(1)} %copy-done), custom_call_target="tpu_custom_call" | custom-call | flops 509607936 | bytes 4194304 | tf_op jit(solution)/shard_map/second_layer/pallas_call | solution.py:356
  26.7 3.0 %collective-permute-done.4.partial = bf16[2,6,64,128]{3,2,1,0:T(8,128)(2,1)S(1)} collective-permute-done((bf16[2,6,64,128]{3,2,1,0:T(8,128)(2,1)S(1)}, bf16[2,6,64,128]{3,2,1,0:T(8,128)(2,1)S(1)}, u32[]{:S(2)}, u32[]{:S(2)}) %collective-permute-start.4) | collective-permute-done | bytes 196640 | tf_op jit(solution)/shard_map/ppermute | solution.py:27
  29.7 0.0 copy-done.2
  29.7 1.0 %finish.1 = bf16[2,4,64,192]{3,2,1,0:T(8,128)(2,1)} custom-call(bf16[2,6,64,128]{3,2,1,0:T(8,128)(2,1)S(1)} %collective-permute-done.4.partial, f32[2,4,64,192]{3,2,1,0:T(8,128)S(1)} %second_layer.1.own, f32[1,192]{1,0:T(1,128)S(1)} %bitcast.4), custom_call_target="tpu_custom_call" | custom-call | bytes 4194304 | tf_op jit(solution)/shard_map/finish/pallas_call | solution.py:356
Async XLA Ops:
  0.0 12.3 %copy-start.1 = (f32[192]{0:T(256)S(1)}, f32[192]{0:T(256)}, u32[]{:S(2)}) copy-start(f32[192]{0:T(256)} %param.7) | copy-start | bytes 2308
  0.0 2.3 %collective-permute-start = (bf16[2,4,64,192]{3,2,1,0:T(8,128)(2,1)}, bf16[2,4,64,192]{3,2,1,0:T(8,128)(2,1)S(1)}, u32[]{:S(2)}, u32[]{:S(2)}) collective-permute-start(bf16[2,4,64,192]{3,2,1,0:T(8,128)(2,1)} %own_far.1), channel_id=1, source_target_pairs={{0,1},{1,0},{2,3},{3,2},{4,5},{5,4},{6,7},{7,6},{8,9},{9,8},{10,11... | collective-permute-start | bytes 589832 | tf_op jit(solution)/shard_map/ppermute | solution.py:20
  2.3 14.1 %copy-start = (bf16[3,3,3,192,192]{4,3,2,1,0:T(8,128)(2,1)S(1)}, bf16[3,3,3,192,192]{4,3,2,1,0:T(8,128)(2,1)}, u32[]{:S(2)}) copy-start(bf16[3,3,3,192,192]{4,3,2,1,0:T(8,128)(2,1)} %w2.1) | copy-start | bytes 5971972
  2.5 9.8 %collective-permute-start.3 = (bf16[800,128]{1,0:T(8,128)(2,1)S(1)}, bf16[800,128]{1,0:T(8,128)(2,1)S(1)}, u32[]{:S(2)}, u32[]{:S(2)}) collective-permute-start(bf16[800,128]{1,0:T(8,128)(2,1)S(1)} %get-tuple-element.18), channel_id=1, source_target_pairs={{0,4},{2,6},{4,8},{6,10},{8,12},{10,14},{1,5},{3,7},{5,9},{7,11},{... | collective-permute-start | bytes 614408 | tf_op jit(solution)/shard_map/ppermute | solution.py:27
  7.1 7.3 %collective-permute-start.2 = (bf16[416,128]{1,0:T(8,128)(2,1)S(1)}, bf16[416,128]{1,0:T(8,128)(2,1)S(1)}, u32[]{:S(2)}, u32[]{:S(2)}) collective-permute-start(bf16[416,128]{1,0:T(8,128)(2,1)S(1)} %get-tuple-element.17), channel_id=1, source_target_pairs={{0,6},{2,4},{4,10},{6,8},{8,14},{10,12},{1,7},{3,5},{5,11},{7,9},{... | collective-permute-start | bytes 319496 | tf_op jit(solution)/shard_map/ppermute | solution.py:27
  11.5 4.9 %collective-permute-start.1 = (bf16[416,128]{1,0:T(8,128)(2,1)S(1)}, bf16[416,128]{1,0:T(8,128)(2,1)S(1)}, u32[]{:S(2)}, u32[]{:S(2)}) collective-permute-start(bf16[416,128]{1,0:T(8,128)(2,1)S(1)} %get-tuple-element.17), channel_id=1, source_target_pairs={{0,2},{2,0},{1,3},{3,1},{4,6},{6,4},{5,7},{7,5},{8,10},{10,8},{9,1... | collective-permute-start | bytes 319496 | tf_op jit(solution)/shard_map/ppermute | solution.py:402
  19.7 10.0 %copy-start.2 = (f32[192]{0:T(256)S(1)}, f32[192]{0:T(256)}, u32[]{:S(2)}) copy-start(f32[192]{0:T(256)} %param.9) | copy-start | bytes 2308
  19.7 10.0 %collective-permute-start.4 = (bf16[2,6,64,128]{3,2,1,0:T(8,128)(2,1)S(1)}, bf16[2,6,64,128]{3,2,1,0:T(8,128)(2,1)S(1)}, u32[]{:S(2)}, u32[]{:S(2)}) collective-permute-start(bf16[2,6,64,128]{3,2,1,0:T(8,128)(2,1)S(1)} %get-tuple-element.23), channel_id=1, source_target_pairs={{0,4},{2,6},{4,8},{6,10},{8,12},{10,14},{1,5},{3,7},{5,9},{7,11},{... | collective-permute-start | bytes 589832 | tf_op jit(solution)/shard_map/ppermute | solution.py:27

commit v8 on v6

--- a/solution.py
+++ b/solution.py
@@ -215,25 +215,33 @@
                 fill(*buffers, f, row, beside, *cells[2:])
 
 
-def safe_kernel(strips, own, neighbour, middle, last, weight_far, out, plane, lo, pairs, stacked, arrived):
+def edge_own_kernel(strips, *refs):
+    *refs, near_lo, near_pairs, near_stacked, arrived = refs
+    own, neighbour, *edges, middle, last, weight_far, edge_sums, plane = refs
     frames, rows, cols, channels = own.shape
-    width = cols + TILE
+    width, rest = cols + TILE, channels - LANES
     copy = pltpu.make_async_copy(weight_far.at[0], plane, arrived.at[0])
     copy.start()
     if frames > 2:
         copy.wait()
-    clear((lo, pairs, stacked))
-    for f in range(frames):
-        for r in range(rows):
+    strip_block = Packed(frames, HALO, cols)
+    near = (near_lo, near_pairs, near_stacked)
+    clear((near_pairs,))
+    for group, (edge, top) in enumerate(zip(edges, at_top(strips))):
+
+        def own_row(f, r):
             cells = own[f, r]
-            fill(lo, pairs, stacked, f, r + HALO, slice(0, cols), cells[:, :LANES], cells[:, LANES:])
-            fill(lo, pairs, stacked, f, r + HALO, slice(cols, width), *own_beside(neighbour, f, r, cols))
-    start, count = safe_rows(strips, rows)
-    for t in range(frames):
-        taps = own_taps(t)
-        products = convolve(taps, [plane, middle, last], columns(taps, lo, pairs, stacked, start, count))
-        for r in range(count):
-            out[t, r] = join(products, r * width, width)
+            return cells[:, :LANES], cells[:, LANES:], *own_beside(neighbour, f, r, cols)
+
+        def halo_row(f, j):
+            return *strip_block.read(edge, f, j, rest), *strip_block.read_beside(edge, f, j, rest)
+
+        window(near, frames, top, rows, cols, own_row, halo_row)
+        for t in range(frames):
+            taps = own_taps(t)
+            products = convolve(taps, [plane, middle, last], columns(taps, *near, 0, HALO))
+            for r in range(HALO):
+                edge_sums[group, t, r] = join(products, r * width, width)
     if frames <= 2:
         copy.wait()
 
@@ -254,69 +262,74 @@
     return jnp.where((position < right) | (position >= left), activate(y, gain), 0.0)
 
 
-def middle_kernel(strips, rows, cols, *refs):
-    *refs, lo, pairs, stacked, near_lo, near_pairs, near_stacked, arrived = refs
-    *refs, h_lo, h_pairs, h_stacked, edge_sums, w2_first, w2_middle, w2_last = refs
-    own, neighbour, *edges, block, sums, plane, middle, last, gains, w2_far = refs
-    frames, channels = own.shape[0], own.shape[-1]
+def all_taps(t):
+    return [(t, 0), (t + 1, 1), (t + 2, 2)]
+
+
+def safe_sums(strips, rows):
+    if strips == 2:
+        strip = lax.axis_index("strip")
+        return (HALO * strip, rows - HALO), ((1 - strip) * (rows - HALO), HALO)
+    return (0, 0), (0, rows)
+
+
+def partial_sums(frames, hidden, w2, start, count, rows, cols, partial):
+    width, last = cols + TILE, frames - 1
+    for t, taps in enumerate(([(last - 1, 0), (last, 1)], [(last, 0)])):
+        products = convolve(taps, [w2.at[0], w2.at[1]], columns(taps, *hidden, start, count))
+        for r in range(count):
+            y = join(products, r * width, width)[:cols].astype(jnp.bfloat16)
+            rest = y.shape[-1] - LANES
+            partial[t, start + r] = y[:, :LANES]
+            half = slice((r % 2) * rest, (r % 2 + 1) * rest)
+            partial[t, rows + start // 2 + r // 2, :, half] = y[:, LANES:]
+
+
+def safe_kernel(strips, *refs):
+    *refs, lo, pairs, stacked = refs
+    own, neighbour, block, plane, middle, last, gains, w2, h_lo, h_pairs, h_stacked, partial = refs
+    frames, rows, cols, channels = own.shape
     width, rest = cols + TILE, channels - LANES
-    w2 = [w2_first, w2_middle, w2_last]
-    copies = [pltpu.make_async_copy(w2_far.at[a], w2[a], arrived.at[a]) for a in range(3)]
-    for copy in copies:
-        copy.start()
-    clear((lo, pairs, stacked, h_lo, h_pairs, h_stacked, near_pairs))
-    whole, strip_block = Packed(HALO, rows, cols), Packed(frames, HALO, cols)
+    every, beside = slice(0, cols), slice(cols, width)
+    clear((lo, pairs, stacked, h_lo, h_pairs, h_stacked))
+    whole = Packed(HALO, rows, cols)
 
     @if_earlier
     def build():
         for f in range(HALO):
             for r in range(rows):
-                fill(lo, pairs, stacked, f, r + HALO, slice(0, cols), *whole.read(block, f, r, rest))
-                fill(lo, pairs, stacked, f, r + HALO, slice(cols, width), *whole.read_beside(block, f, r, rest))
-
+                fill(lo, pairs, stacked, f, r + HALO, every, *whole.read(block, f, r, rest))
+                fill(lo, pairs, stacked, f, r + HALO, beside, *whole.read_beside(block, f, r, rest))
+
+    for f in range(frames):
+        for r in range(rows):
+            cells = own[f, r]
+            fill(lo, pairs, stacked, HALO + f, r + HALO, every, cells[:, :LANES], cells[:, LANES:])
+            fill(lo, pairs, stacked, HALO + f, r + HALO, beside, *own_beside(neighbour, f, r, cols))
+    start, count = safe_rows(strips, rows)
+    lefts = jnp.concatenate([columns(all_taps(t), lo, pairs, stacked, start, count) for t in range(frames)], axis=0)
+    products = convolve(all_taps(0), [plane, middle, last], lefts)
     gain = gains[...]
-    start, count = safe_rows(strips, rows)
     for t in range(frames):
-        taps = earlier_taps(t)
-        products = convolve(taps, [plane, middle], columns(taps, lo, pairs, stacked, start, count)) if taps else None
         for r in range(count):
-            y = sums[t, r]
-            if taps:
-                y = y + join(products, r * width, width)
-            h = hidden_row(y, gain, cols).astype(jnp.bfloat16)
+            h = hidden_row(join(products, (t * count + r) * width, width), gain, cols).astype(jnp.bfloat16)
             fill(h_lo, h_pairs, h_stacked, t, start + r, slice(0, width), h[:, :LANES], h[:, LANES:])
-
-    near = (near_lo, near_pairs, near_stacked)
-    for group, (edge, top) in enumerate(zip(edges, at_top(strips))):
-
-        def own_row(f, r):
-            cells = own[f, r]
-            return cells[:, :LANES], cells[:, LANES:], *own_beside(neighbour, f, r, cols)
-
-        def halo_row(f, j):
-            return *strip_block.read(edge, f, j, rest), *strip_block.read_beside(edge, f, j, rest)
-
-        window(near, frames, top, rows, cols, own_row, halo_row)
-        for t in range(frames):
-            taps = own_taps(t)
-            products = convolve(taps, [plane, middle, last], columns(taps, *near, 0, HALO))
-            for r in range(HALO):
-                edge_sums[group, t, r] = join(products, r * width, width)
-    for copy in copies:
-        copy.wait()
+    (start, count), _ = safe_sums(strips, rows)
+    if count:
+        partial_sums(frames, (h_lo, h_pairs, h_stacked), w2, start, count, rows, cols, partial)
 
 
 def edge_kernel(strips, rows, cols, *refs):
     *refs, near_lo, near_pairs, near_stacked = refs
     *refs, h_lo, h_pairs, h_stacked, partial = refs
-    *edges, block, edge_sums, safe_lo, safe_pairs, safe_stacked, plane, middle, gains, w2_first, w2_middle = refs
+    *edges, block, edge_sums, safe_lo, safe_pairs, safe_stacked, safe_partial, plane, middle, gains, w2 = refs
     frames, channels = edge_sums.shape[1], edge_sums.shape[-1]
     width, rest = cols + TILE, channels - LANES
     strip = lax.axis_index("strip")
     whole, strip_block = Packed(HALO, rows, cols), Packed(frames, HALO, cols)
     near = (near_lo, near_pairs, near_stacked)
     clear(near)
-    for target, source in ((h_lo, safe_lo), (h_pairs, safe_pairs), (h_stacked, safe_stacked)):
+    for target, source in zip((h_lo, h_pairs, h_stacked, partial), (safe_lo, safe_pairs, safe_stacked, safe_partial)):
         target[...] = source[...]
     gain = gains[...]
     for group, (edge, top) in enumerate(zip(edges, at_top(strips))):
@@ -359,22 +372,15 @@
                 row = (1 - top) * rows + r
                 fill(h_lo, h_pairs, h_stacked, t, row, slice(0, width), h[:, :LANES], h[:, LANES:])
 
-    last = frames - 1
-    for t, taps in enumerate(([(last - 1, 0), (last, 1)], [(last, 0)])):
-        products = convolve(taps, [w2_first, w2_middle], columns(taps, h_lo, h_pairs, h_stacked, 0, rows))
-        for r in range(rows):
-            y = join(products, r * width, width)[:cols].astype(jnp.bfloat16)
-            partial[t, r] = y[:, :LANES]
-            half = r % 2
-            partial[t, rows + r // 2, :, half * rest : (half + 1) * rest] = y[:, LANES:]
-
-
-def second_kernel(frames, rows, cols, h_lo, h_pairs, h_stacked, *refs):
-    *w2, out = refs
+    _, (start, count) = safe_sums(strips, rows)
+    partial_sums(frames, (h_lo, h_pairs, h_stacked), w2, start, count, rows, cols, partial)
+
+
+def second_kernel(frames, rows, cols, h_lo, h_pairs, h_stacked, w2, out):
     width = cols + TILE
     for t in range(frames):
         taps = [(f, f - t + 2) for f in range(max(0, t - 2), t + 1)]
-        products = convolve(taps, w2, columns(taps, h_lo, h_pairs, h_stacked, 0, rows))
+        products = convolve(taps, [w2.at[a] for a in range(3)], columns(taps, h_lo, h_pairs, h_stacked, 0, rows))
         for r in range(rows):
             out[t, r] = join(products, r * width, width)[:cols]
 
@@ -454,42 +460,40 @@
     before = forward(block)
     own_edges = [lax.ppermute(edge, "strip", way) for edge, way in zip(edges, ways)]
     before_edges = [forward(edge, way) for edge, way in zip(edges, ways)]
-    sums, plane = call(
+    edge_sums, plane = call(
+        functools.partial(edge_own_kernel, strips),
+        "edge_rows_own",
+        [own_in, neighbour, *own_edges, middle, last, weight_first],
+        [f32((len(ways), frames, HALO, width, channels)), plane_shape],
+        block_scratch(frames, 2 * HALO, width),
+        semaphores=1,
+        flops=flops // 4,
+        far=[-1],
+    )
+    gain_first = scale_first[None]
+    h_shapes = [bf16(shape) for shape in block_scratch(frames, rows + 2, width)]
+    partial_shape = bf16((HALO, rows + rows // 2, cols, LANES))
+    safe = call(
         functools.partial(safe_kernel, strips),
-        "own_safe_rows",
-        [own_in, neighbour, middle, last, weight_first],
-        [f32((frames, safe_rows(strips, rows)[1], width, channels)), plane_shape],
-        block_scratch(frames, rows + 2 * HALO, width),
-        semaphores=1,
-        flops=flops // 2,
-        far=[-1],
-    )
-    h_shapes = [bf16(shape) for shape in block_scratch(frames, rows + 2, width)]
-    gain_first = scale_first[None]
-    *safe, edge_sums, w2_first, w2_middle, w2_last = call(
-        functools.partial(middle_kernel, strips, rows, cols),
         "safe_rows",
-        [own_in, neighbour, *own_edges, before, sums, plane, middle, last, gain_first, weight_second],
-        h_shapes + [f32((len(ways), frames, HALO, width, channels))] + [plane_shape] * 3,
-        block_scratch(HALO, rows + 2 * HALO, width) + block_scratch(frames, 2 * HALO, width),
-        semaphores=3,
-        flops=flops // 2,
-        far=[-1],
+        [own_in, neighbour, before, plane, middle, last, gain_first, weight_second],
+        h_shapes + [partial_shape],
+        block_scratch(HALO + frames, rows + 2 * HALO, width),
+        flops=flops,
     )
     h_lo, h_pairs, h_stacked, partial = call(
         functools.partial(edge_kernel, strips, rows, cols),
         "edge_rows",
-        [*before_edges, before, edge_sums, *safe, plane, middle, gain_first, w2_first, w2_middle],
-        h_shapes + [bf16((HALO, rows + rows // 2, cols, LANES))],
+        [*before_edges, before, edge_sums, *safe, plane, middle, gain_first, weight_second],
+        h_shapes + [partial_shape],
         block_scratch(HALO, 2 * HALO, width),
         flops=flops,
     )
-    w2 = [w2_first, w2_middle, w2_last]
     sent = forward(partial)
     own = call(
         functools.partial(second_kernel, frames, rows, cols),
         "second_layer",
-        [h_lo, h_pairs, h_stacked, *w2],
+        [h_lo, h_pairs, h_stacked, weight_second],
         f32((frames, rows, cols, channels)),
         flops=flops,
     )

time: 27.1 us -> 27.9 us (1.030)
  Pallas kernels: 10.1 us -> 10.6 us
    pallas_call x7, Pallas kernels: 10.1 us -> 10.6 us  [call(): pl.pallas_call(kernel, out_shape=outs, in_specs=in_specs, out_specs=(away...]
  transfers between devices with their start and end apart: 5 -> 5, of which waited for: 1 -> 1; matrix products, arithmetic and copies ran while one was open for 0% -> 0% of each run, Pallas kernels for 25% -> 28%
where the time goes in v8:
time: 27.9 us; the launch traced here: 27.6 us
  starting transfers between devices  14.3 us (51%)
  Pallas kernels  10.6 us (38%)
  waiting for transfers between devices  2.58 us (9%)
    ppermute x3, starting transfers between devices, forward(): return lax.ppermute(x, ('frame', 'strip'), pairs)  12.3 us
    pallas_call x7, Pallas kernels, call(): pl.pallas_call(kernel, out_shape=outs, in_specs=in_specs, out_specs=(away...  10.6 us
    ppermute x3, waiting for transfers between devices, forward(): return lax.ppermute(x, ('frame', 'strip'), pairs)  2.57 us
    ppermute x1, starting transfers between devices, shards(): lax.ppermute(edge, 'strip', way)  1.56 us
  transfers between devices with their start and end apart: 5, of which 1 were waited for; matrix products, arithmetic and copies ran while one was open for 0% of the time, Pallas kernels for 28%

profile of v8, /device:TPU:0, one launch (start us, length us, event | category | flops | bytes accessed | tf_op | source)
XLA Modules:
  0.0 27.6 jit_solution(5048616792450943429)
XLA Ops:
  0.0 0.5 %collective-permute-start = (bf16[2,4,64,192]{3,2,1,0:T(8,128)(2,1)}, bf16[2,4,64,192]{3,2,1,0:T(8,128)(2,1)S(1)}, u32[]{:S(2)}, u32[]{:S(2)}) collective-permute-start(bf16[2,4,64,192]{3,2,1,0:T(8,128)(2,1)} %own_far.1), channel_id=1, source_target_pairs={{0,1},{1,0},{2,3},{3,2},{4,5},{5,4},{6,7},{7,6},{8,9},{9,8},{10,11... | collective-permute-start | bytes 589832 | tf_op jit(solution)/shard_map/ppermute | solution.py:19
  0.5 1.5 %stage.1 = (bf16[2,4,64,192]{3,2,1,0:T(8,128)(2,1)S(1)}, bf16[3,3,192,192]{3,2,1,0:T(8,128)(2,1)S(1)}, bf16[3,3,192,192]{3,2,1,0:T(8,128)(2,1)S(1)}) custom-call(bf16[2,4,64,192]{3,2,1,0:T(8,128)(2,1)} %own_far.1, bf16[3,3,3,192,192]{4,3,2,1,0:T(8,128)(2,1)} %refs_5_.1), custom_call_target="tpu_custom_call" | custom-call | bytes 4194304 | tf_op jit(solution)/shard_map/stage/pallas_call | solution.py:415
  2.0 0.0 collective-permute-done.neighbour.refs_1_
  2.0 0.1 pack.1
  2.2 0.0 copy-start
  2.2 0.0 copy-start.1
  2.2 4.9 %collective-permute-start.2 = (bf16[800,128]{1,0:T(8,128)(2,1)S(1)}, bf16[800,128]{1,0:T(8,128)(2,1)S(1)}, u32[]{:S(2)}, u32[]{:S(2)}) collective-permute-start(bf16[800,128]{1,0:T(8,128)(2,1)S(1)} %get-tuple-element.22), channel_id=1, source_target_pairs={{0,4},{2,6},{4,8},{6,10},{8,12},{10,14},{1,5},{3,7},{5,9},{7,11},{... | collective-permute-start | bytes 614408 | tf_op jit(solution)/shard_map/ppermute | solution.py:26
  7.1 1.6 %collective-permute-start.3 = (bf16[416,128]{1,0:T(8,128)(2,1)S(1)}, bf16[416,128]{1,0:T(8,128)(2,1)S(1)}, u32[]{:S(2)}, u32[]{:S(2)}) collective-permute-start(bf16[416,128]{1,0:T(8,128)(2,1)S(1)} %get-tuple-element.21), channel_id=1, source_target_pairs={{0,2},{2,0},{1,3},{3,1},{4,6},{6,4},{5,7},{7,5},{8,10},{10,8},{9,1... | collective-permute-start | bytes 319496 | tf_op jit(solution)/shard_map/ppermute | solution.py:461
  8.7 3.4 %collective-permute-start.1 = (bf16[416,128]{1,0:T(8,128)(2,1)S(1)}, bf16[416,128]{1,0:T(8,128)(2,1)S(1)}, u32[]{:S(2)}, u32[]{:S(2)}) collective-permute-start(bf16[416,128]{1,0:T(8,128)(2,1)S(1)} %get-tuple-element.21), channel_id=1, source_target_pairs={{0,6},{2,4},{4,10},{6,8},{8,14},{10,12},{1,7},{3,5},{5,11},{7,9},{... | collective-permute-start | bytes 319496 | tf_op jit(solution)/shard_map/ppermute | solution.py:26
  12.1 0.0 collective-permute-done.3.refs_2_
  12.1 1.4 %edge_rows_own.1 = (f32[1,2,2,80,192]{4,3,2,1,0:T(8,128)S(1)}, bf16[3,3,192,192]{3,2,1,0:T(8,128)(2,1)S(1)}) custom-call(bf16[2,4,64,192]{3,2,1,0:T(8,128)(2,1)S(1)} %get-tuple-element.20.own.refs_0_, bf16[2,4,64,192]{3,2,1,0:T(8,128)(2,1)S(1)} %collective-permute-done.neighbour.refs_1_, bf16[416,128]{1,0:T(8,128)(2,1)S(1)} %collective-permute-done.3.refs_2_, ...), custom_call_target="tpu_custom_call" | custom-call | flops 127401984 | bytes 4194304 | tf_op jit(solution)/shard_map/edge_rows_own/pallas_call | solution.py:415
  13.6 0.0 collective-permute-done.2.refs_2_.refs_1_
  13.6 0.0 copy-done
  13.6 0.0 copy-done.1
  13.6 3.5 %safe_rows.1 = (bf16[2,6,80,128]{3,2,1,0:T(8,128)(2,1)S(1)}, bf16[2,7,80,128]{3,2,1,0:T(8,128)(2,1)S(1)}, bf16[1,6,80,128]{3,2,1,0:T(8,128)(2,1)S(1)}, bf16[2,6,64,128]{3,2,1,0:T(8,128)(2,1)S(1)}) custom-call(bf16[2,4,64,192]{3,2,1,0:T(8,128)(2,1)S(1)} %get-tuple-element.20.own.refs_0_, bf16[2,4,64,192]{3,2,1,0:T(8,128)(2,1)S(1)} %collective-permute-done.neighbour.refs_1_, ...), custom_call_target="tpu_custom_call" | custom-call | flops 509607936 | bytes 4194304 | tf_op jit(solution)/shard_map/safe_rows/pallas_call | solution.py:415
  17.1 0.0 collective-permute-done.1.refs_0_
  17.1 1.7 %edge_rows.1 = (bf16[2,6,80,128]{3,2,1,0:T(8,128)(2,1)S(1)}, bf16[2,7,80,128]{3,2,1,0:T(8,128)(2,1)S(1)}, bf16[1,6,80,128]{3,2,1,0:T(8,128)(2,1)S(1)}, bf16[2,6,64,128]{3,2,1,0:T(8,128)(2,1)S(1)}) custom-call(bf16[416,128]{1,0:T(8,128)(2,1)S(1)} %collective-permute-done.1.refs_0_, bf16[800,128]{1,0:T(8,128)(2,1)S(1)} %collective-permute-done.2.refs_2_.refs_1_, ...), custom_call_target="tpu_custom_call" | custom-call | flops 509607936 | bytes 4194304 | tf_op jit(solution)/shard_map/edge_rows/pallas_call | solution.py:415
  18.8 0.0 copy-start.2
  18.8 4.0 %collective-permute-start.4 = (bf16[2,6,64,128]{3,2,1,0:T(8,128)(2,1)S(1)}, bf16[2,6,64,128]{3,2,1,0:T(8,128)(2,1)S(1)}, u32[]{:S(2)}, u32[]{:S(2)}) collective-permute-start(bf16[2,6,64,128]{3,2,1,0:T(8,128)(2,1)S(1)} %get-tuple-element.31), channel_id=1, source_target_pairs={{0,4},{2,6},{4,8},{6,10},{8,12},{10,14},{1,5},{3,7},{5,9},{7,11},{... | collective-permute-start | bytes 589832 | tf_op jit(solution)/shard_map/ppermute | solution.py:26
  22.8 1.2 %second_layer.1.own = f32[2,4,64,192]{3,2,1,0:T(8,128)S(1)} custom-call(bf16[2,6,80,128]{3,2,1,0:T(8,128)(2,1)S(1)} %get-tuple-element.32.h_lo, bf16[2,7,80,128]{3,2,1,0:T(8,128)(2,1)S(1)} %get-tuple-element.33.h_pairs, bf16[1,6,80,128]{3,2,1,0:T(8,128)(2,1)S(1)} %get-tuple-element.34.h_stacked, bf16[3,3,3,192,192]{4,3,2,1,0:T(8,128)(2,1)S(1)} %copy-done), custom_call_target="tpu_custom_call" | custom-call | flops 509607936 | bytes 4194304 | tf_op jit(solution)/shard_map/second_layer/pallas_call | solution.py:415
  24.0 2.6 %collective-permute-done.4.partial = bf16[2,6,64,128]{3,2,1,0:T(8,128)(2,1)S(1)} collective-permute-done((bf16[2,6,64,128]{3,2,1,0:T(8,128)(2,1)S(1)}, bf16[2,6,64,128]{3,2,1,0:T(8,128)(2,1)S(1)}, u32[]{:S(2)}, u32[]{:S(2)}) %collective-permute-start.4) | collective-permute-done | bytes 196640 | tf_op jit(solution)/shard_map/ppermute | solution.py:26
  26.6 0.0 copy-done.2
  26.6 1.0 %finish.1 = bf16[2,4,64,192]{3,2,1,0:T(8,128)(2,1)} custom-call(bf16[2,6,64,128]{3,2,1,0:T(8,128)(2,1)S(1)} %collective-permute-done.4.partial, f32[2,4,64,192]{3,2,1,0:T(8,128)S(1)} %second_layer.1.own, f32[1,192]{1,0:T(1,128)S(1)} %bitcast.4), custom_call_target="tpu_custom_call" | custom-call | bytes 4194304 | tf_op jit(solution)/shard_map/finish/pallas_call | solution.py:415
Async XLA Ops:
  0.0 2.0 %collective-permute-start = (bf16[2,4,64,192]{3,2,1,0:T(8,128)(2,1)}, bf16[2,4,64,192]{3,2,1,0:T(8,128)(2,1)S(1)}, u32[]{:S(2)}, u32[]{:S(2)}) collective-permute-start(bf16[2,4,64,192]{3,2,1,0:T(8,128)(2,1)} %own_far.1), channel_id=1, source_target_pairs={{0,1},{1,0},{2,3},{3,2},{4,5},{5,4},{6,7},{7,6},{8,9},{9,8},{10,11... | collective-permute-start | bytes 589832 | tf_op jit(solution)/shard_map/ppermute | solution.py:19
  2.2 11.4 %copy-start = (bf16[3,3,3,192,192]{4,3,2,1,0:T(8,128)(2,1)S(1)}, bf16[3,3,3,192,192]{4,3,2,1,0:T(8,128)(2,1)}, u32[]{:S(2)}) copy-start(bf16[3,3,3,192,192]{4,3,2,1,0:T(8,128)(2,1)} %w2.1) | copy-start | bytes 5971972
  2.2 11.4 %copy-start.1 = (f32[192]{0:T(256)S(1)}, f32[192]{0:T(256)}, u32[]{:S(2)}) copy-start(f32[192]{0:T(256)} %param.7) | copy-start | bytes 2308
  2.2 11.4 %collective-permute-start.2 = (bf16[800,128]{1,0:T(8,128)(2,1)S(1)}, bf16[800,128]{1,0:T(8,128)(2,1)S(1)}, u32[]{:S(2)}, u32[]{:S(2)}) collective-permute-start(bf16[800,128]{1,0:T(8,128)(2,1)S(1)} %get-tuple-element.22), channel_id=1, source_target_pairs={{0,4},{2,6},{4,8},{6,10},{8,12},{10,14},{1,5},{3,7},{5,9},{7,11},{... | collective-permute-start | bytes 614408 | tf_op jit(solution)/shard_map/ppermute | solution.py:26
  7.1 5.0 %collective-permute-start.3 = (bf16[416,128]{1,0:T(8,128)(2,1)S(1)}, bf16[416,128]{1,0:T(8,128)(2,1)S(1)}, u32[]{:S(2)}, u32[]{:S(2)}) collective-permute-start(bf16[416,128]{1,0:T(8,128)(2,1)S(1)} %get-tuple-element.21), channel_id=1, source_target_pairs={{0,2},{2,0},{1,3},{3,1},{4,6},{6,4},{5,7},{7,5},{8,10},{10,8},{9,1... | collective-permute-start | bytes 319496 | tf_op jit(solution)/shard_map/ppermute | solution.py:461
  8.7 8.4 %collective-permute-start.1 = (bf16[416,128]{1,0:T(8,128)(2,1)S(1)}, bf16[416,128]{1,0:T(8,128)(2,1)S(1)}, u32[]{:S(2)}, u32[]{:S(2)}) collective-permute-start(bf16[416,128]{1,0:T(8,128)(2,1)S(1)} %get-tuple-element.21), channel_id=1, source_target_pairs={{0,6},{2,4},{4,10},{6,8},{8,14},{10,12},{1,7},{3,5},{5,11},{7,9},{... | collective-permute-start | bytes 319496 | tf_op jit(solution)/shard_map/ppermute | solution.py:26
  18.8 7.7 %copy-start.2 = (f32[192]{0:T(256)S(1)}, f32[192]{0:T(256)}, u32[]{:S(2)}) copy-start(f32[192]{0:T(256)} %param.9) | copy-start | bytes 2308
  18.8 7.7 %collective-permute-start.4 = (bf16[2,6,64,128]{3,2,1,0:T(8,128)(2,1)S(1)}, bf16[2,6,64,128]{3,2,1,0:T(8,128)(2,1)S(1)}, u32[]{:S(2)}, u32[]{:S(2)}) collective-permute-start(bf16[2,6,64,128]{3,2,1,0:T(8,128)(2,1)S(1)} %get-tuple-element.31), channel_id=1, source_target_pairs={{0,4},{2,6},{4,8},{6,10},{8,12},{10,14},{1,5},{3,7},{5,9},{7,11},{... | collective-permute-start | bytes 589832 | tf_op jit(solution)/shard_map/ppermute | solution.py:26

commit v9 on v8

--- a/solution.py
+++ b/solution.py
@@ -159,6 +159,13 @@
         buffer[...] = jnp.zeros_like(buffer)
 
 
+def clear_rows(buffers, above, below):
+    lo, pairs, stacked = buffers
+    for buffer, rows in ((lo, (above, below)), (pairs, (above, above + 1, below, below + 1)), (stacked, (above, below))):
+        for row in rows:
+            buffer[:, row] = jnp.zeros(buffer.shape[:1] + buffer.shape[2:], buffer.dtype)
+
+
 def facing(strips, rows):
     if strips == 2:
         return [jnp.where(lax.axis_index("strip") == 0, rows - HALO, 0)]
@@ -266,33 +273,35 @@
     return [(t, 0), (t + 1, 1), (t + 2, 2)]
 
 
-def safe_sums(strips, rows):
-    if strips == 2:
-        strip = lax.axis_index("strip")
-        return (HALO * strip, rows - HALO), ((1 - strip) * (rows - HALO), HALO)
-    return (0, 0), (0, rows)
-
-
-def partial_sums(frames, hidden, w2, start, count, rows, cols, partial):
+def partial_sums(frames, hidden, w2, rows, cols, partial):
     width, last = cols + TILE, frames - 1
     for t, taps in enumerate(([(last - 1, 0), (last, 1)], [(last, 0)])):
-        products = convolve(taps, [w2.at[0], w2.at[1]], columns(taps, *hidden, start, count))
-        for r in range(count):
+        products = convolve(taps, w2, columns(taps, *hidden, 0, rows))
+        for r in range(rows):
             y = join(products, r * width, width)[:cols].astype(jnp.bfloat16)
             rest = y.shape[-1] - LANES
-            partial[t, start + r] = y[:, :LANES]
+            partial[t, r] = y[:, :LANES]
             half = slice((r % 2) * rest, (r % 2 + 1) * rest)
-            partial[t, rows + start // 2 + r // 2, :, half] = y[:, LANES:]
+            partial[t, rows + r // 2, :, half] = y[:, LANES:]
 
 
 def safe_kernel(strips, *refs):
-    *refs, lo, pairs, stacked = refs
-    own, neighbour, block, plane, middle, last, gains, w2, h_lo, h_pairs, h_stacked, partial = refs
+    *refs, lo, pairs, stacked, arrived = refs
+    own, neighbour, block, plane, middle, last, gains, w2_far, h_lo, h_pairs, h_stacked, *w2 = refs
+    copies = [pltpu.make_async_copy(w2_far.at[a], w2[a], arrived.at[a]) for a in range(3)]
+    for copy in copies:
+        copy.start()
     frames, rows, cols, channels = own.shape
     width, rest = cols + TILE, channels - LANES
     every, beside = slice(0, cols), slice(cols, width)
-    clear((lo, pairs, stacked, h_lo, h_pairs, h_stacked))
+    clear_rows((lo, pairs, stacked), HALO - 1, HALO + rows)
+    clear_rows((h_lo, h_pairs, h_stacked), 0, rows + 1)
     whole = Packed(HALO, rows, cols)
+
+    @pl.when(lax.axis_index("frame") == 0)
+    def none_earlier():
+        for buffer in (lo, pairs, stacked):
+            buffer[:HALO] = jnp.zeros((HALO,) + buffer.shape[1:], buffer.dtype)
 
     @if_earlier
     def build():
@@ -314,22 +323,21 @@
         for r in range(count):
             h = hidden_row(join(products, (t * count + r) * width, width), gain, cols).astype(jnp.bfloat16)
             fill(h_lo, h_pairs, h_stacked, t, start + r, slice(0, width), h[:, :LANES], h[:, LANES:])
-    (start, count), _ = safe_sums(strips, rows)
-    if count:
-        partial_sums(frames, (h_lo, h_pairs, h_stacked), w2, start, count, rows, cols, partial)
+    for copy in copies:
+        copy.wait()
 
 
 def edge_kernel(strips, rows, cols, *refs):
     *refs, near_lo, near_pairs, near_stacked = refs
     *refs, h_lo, h_pairs, h_stacked, partial = refs
-    *edges, block, edge_sums, safe_lo, safe_pairs, safe_stacked, safe_partial, plane, middle, gains, w2 = refs
+    *edges, block, edge_sums, safe_lo, safe_pairs, safe_stacked, plane, middle, gains, w2_first, w2_middle = refs
     frames, channels = edge_sums.shape[1], edge_sums.shape[-1]
     width, rest = cols + TILE, channels - LANES
     strip = lax.axis_index("strip")
     whole, strip_block = Packed(HALO, rows, cols), Packed(frames, HALO, cols)
     near = (near_lo, near_pairs, near_stacked)
     clear(near)
-    for target, source in zip((h_lo, h_pairs, h_stacked, partial), (safe_lo, safe_pairs, safe_stacked, safe_partial)):
+    for target, source in zip((h_lo, h_pairs, h_stacked), (safe_lo, safe_pairs, safe_stacked)):
         target[...] = source[...]
     gain = gains[...]
     for group, (edge, top) in enumerate(zip(edges, at_top(strips))):
@@ -372,15 +380,15 @@
                 row = (1 - top) * rows + r
                 fill(h_lo, h_pairs, h_stacked, t, row, slice(0, width), h[:, :LANES], h[:, LANES:])
 
-    _, (start, count) = safe_sums(strips, rows)
-    partial_sums(frames, (h_lo, h_pairs, h_stacked), w2, start, count, rows, cols, partial)
-
-
-def second_kernel(frames, rows, cols, h_lo, h_pairs, h_stacked, w2, out):
+    partial_sums(frames, (h_lo, h_pairs, h_stacked), [w2_first, w2_middle], rows, cols, partial)
+
+
+def second_kernel(frames, rows, cols, h_lo, h_pairs, h_stacked, *refs):
+    *w2, out = refs
     width = cols + TILE
     for t in range(frames):
         taps = [(f, f - t + 2) for f in range(max(0, t - 2), t + 1)]
-        products = convolve(taps, [w2.at[a] for a in range(3)], columns(taps, h_lo, h_pairs, h_stacked, 0, rows))
+        products = convolve(taps, w2, columns(taps, h_lo, h_pairs, h_stacked, 0, rows))
         for r in range(rows):
             out[t, r] = join(products, r * width, width)[:cols]
 
@@ -473,18 +481,20 @@
     gain_first = scale_first[None]
     h_shapes = [bf16(shape) for shape in block_scratch(frames, rows + 2, width)]
     partial_shape = bf16((HALO, rows + rows // 2, cols, LANES))
-    safe = call(
+    *safe, w2_first, w2_middle, w2_last = call(
         functools.partial(safe_kernel, strips),
         "safe_rows",
         [own_in, neighbour, before, plane, middle, last, gain_first, weight_second],
-        h_shapes + [partial_shape],
+        h_shapes + [plane_shape] * 3,
         block_scratch(HALO + frames, rows + 2 * HALO, width),
+        semaphores=3,
         flops=flops,
+        far=[-1],
     )
     h_lo, h_pairs, h_stacked, partial = call(
         functools.partial(edge_kernel, strips, rows, cols),
         "edge_rows",
-        [*before_edges, before, edge_sums, *safe, plane, middle, gain_first, weight_second],
+        [*before_edges, before, edge_sums, *safe, plane, middle, gain_first, w2_first, w2_middle],
         h_shapes + [partial_shape],
         block_scratch(HALO, 2 * HALO, width),
         flops=flops,
@@ -493,7 +503,7 @@
     own = call(
         functools.partial(second_kernel, frames, rows, cols),
         "second_layer",
-        [h_lo, h_pairs, h_stacked, weight_second],
+        [h_lo, h_pairs, h_stacked, w2_first, w2_middle, w2_last],
         f32((frames, rows, cols, channels)),
         flops=flops,
     )

time: 27.9 us -> 26.7 us (0.957)
  Pallas kernels: 10.6 us -> 9.81 us
  waiting for transfers between devices: 2.58 us -> 2.25 us
    pallas_call x7, Pallas kernels: 10.6 us -> 9.81 us  [call(): pl.pallas_call(kernel, out_shape=outs, in_specs=in_specs, out_specs=(away...]
    ppermute x3, waiting for transfers between devices: 2.57 us -> 2.24 us  [forward(): return lax.ppermute(x, ('frame', 'strip'), pairs)]
  transfers between devices with their start and end apart: 5 -> 5, of which waited for: 1 -> 1; matrix products, arithmetic and copies ran while one was open for 0% -> 0% of each run, Pallas kernels for 28% -> 24%
where the time goes in v9:
time: 26.7 us; the launch traced here: 26.5 us
  starting transfers between devices  14.3 us (54%)
  Pallas kernels  9.81 us (37%)
  waiting for transfers between devices  2.25 us (8%)
    ppermute x3, starting transfers between devices, forward(): return lax.ppermute(x, ('frame', 'strip'), pairs)  12.3 us
    pallas_call x7, Pallas kernels, call(): pl.pallas_call(kernel, out_shape=outs, in_specs=in_specs, out_specs=(away...  9.81 us
    ppermute x3, waiting for transfers between devices, forward(): return lax.ppermute(x, ('frame', 'strip'), pairs)  2.24 us
    ppermute x1, starting transfers between devices, shards(): lax.ppermute(edge, 'strip', way)  1.56 us
  transfers between devices with their start and end apart: 5, of which 1 were waited for; matrix products, arithmetic and copies ran while one was open for 0% of the time, Pallas kernels for 24%

profile of v9, /device:TPU:0, one launch (start us, length us, event | category | flops | bytes accessed | tf_op | source)
XLA Modules:
  0.0 26.5 jit_solution(17664969148508033171)
XLA Ops:
  0.0 0.5 %collective-permute-start = (bf16[2,4,64,192]{3,2,1,0:T(8,128)(2,1)}, bf16[2,4,64,192]{3,2,1,0:T(8,128)(2,1)S(1)}, u32[]{:S(2)}, u32[]{:S(2)}) collective-permute-start(bf16[2,4,64,192]{3,2,1,0:T(8,128)(2,1)} %own_far.1), channel_id=1, source_target_pairs={{0,1},{1,0},{2,3},{3,2},{4,5},{5,4},{6,7},{7,6},{8,9},{9,8},{10,11... | collective-permute-start | bytes 589832 | tf_op jit(solution)/shard_map/ppermute | solution.py:19
  0.5 1.5 %stage.1 = (bf16[2,4,64,192]{3,2,1,0:T(8,128)(2,1)S(1)}, bf16[3,3,192,192]{3,2,1,0:T(8,128)(2,1)S(1)}, bf16[3,3,192,192]{3,2,1,0:T(8,128)(2,1)S(1)}) custom-call(bf16[2,4,64,192]{3,2,1,0:T(8,128)(2,1)} %own_far.1, bf16[3,3,3,192,192]{4,3,2,1,0:T(8,128)(2,1)} %refs_5_.1), custom_call_target="tpu_custom_call" | custom-call | bytes 4194304 | tf_op jit(solution)/shard_map/stage/pallas_call | solution.py:423
  2.0 0.0 collective-permute-done.neighbour.refs_1_
  2.0 0.1 pack.1
  2.2 0.0 copy-start
  2.2 4.7 %collective-permute-start.2 = (bf16[800,128]{1,0:T(8,128)(2,1)S(1)}, bf16[800,128]{1,0:T(8,128)(2,1)S(1)}, u32[]{:S(2)}, u32[]{:S(2)}) collective-permute-start(bf16[800,128]{1,0:T(8,128)(2,1)S(1)} %get-tuple-element.24), channel_id=1, source_target_pairs={{0,4},{2,6},{4,8},{6,10},{8,12},{10,14},{1,5},{3,7},{5,9},{7,11},{... | collective-permute-start | bytes 614408 | tf_op jit(solution)/shard_map/ppermute | solution.py:26
  6.8 1.6 %collective-permute-start.3 = (bf16[416,128]{1,0:T(8,128)(2,1)S(1)}, bf16[416,128]{1,0:T(8,128)(2,1)S(1)}, u32[]{:S(2)}, u32[]{:S(2)}) collective-permute-start(bf16[416,128]{1,0:T(8,128)(2,1)S(1)} %get-tuple-element.23), channel_id=1, source_target_pairs={{0,2},{2,0},{1,3},{3,1},{4,6},{6,4},{5,7},{7,5},{8,10},{10,8},{9,1... | collective-permute-start | bytes 319496 | tf_op jit(solution)/shard_map/ppermute | solution.py:469
  8.4 3.4 %collective-permute-start.1 = (bf16[416,128]{1,0:T(8,128)(2,1)S(1)}, bf16[416,128]{1,0:T(8,128)(2,1)S(1)}, u32[]{:S(2)}, u32[]{:S(2)}) collective-permute-start(bf16[416,128]{1,0:T(8,128)(2,1)S(1)} %get-tuple-element.23), channel_id=1, source_target_pairs={{0,6},{2,4},{4,10},{6,8},{8,14},{10,12},{1,7},{3,5},{5,11},{7,9},{... | collective-permute-start | bytes 319496 | tf_op jit(solution)/shard_map/ppermute | solution.py:26
  11.8 0.0 collective-permute-done.3.refs_2_
  11.9 1.4 %edge_rows_own.1 = (f32[1,2,2,80,192]{4,3,2,1,0:T(8,128)S(1)}, bf16[3,3,192,192]{3,2,1,0:T(8,128)(2,1)S(1)}) custom-call(bf16[2,4,64,192]{3,2,1,0:T(8,128)(2,1)S(1)} %get-tuple-element.22.own.refs_0_, bf16[2,4,64,192]{3,2,1,0:T(8,128)(2,1)S(1)} %collective-permute-done.neighbour.refs_1_, bf16[416,128]{1,0:T(8,128)(2,1)S(1)} %collective-permute-done.3.refs_2_, ...), custom_call_target="tpu_custom_call" | custom-call | flops 127401984 | bytes 4194304 | tf_op jit(solution)/shard_map/edge_rows_own/pallas_call | solution.py:423
  13.3 0.0 collective-permute-done.2.refs_2_.refs_1_
  13.3 0.0 copy-done
  13.3 2.2 %safe_rows.1 = (bf16[2,6,80,128]{3,2,1,0:T(8,128)(2,1)S(1)}, bf16[2,7,80,128]{3,2,1,0:T(8,128)(2,1)S(1)}, bf16[1,6,80,128]{3,2,1,0:T(8,128)(2,1)S(1)}, bf16[3,3,...) custom-call(bf16[2,4,64,192]{3,2,1,0:T(8,128)(2,1)S(1)} %get-tuple-element.22, ...), custom_call_target="tpu_custom_call" | custom-call | flops 509607936 | bytes 4194304 | tf_op jit(solution)/shard_map/safe_rows/pallas_call | solution.py:423
  15.5 0.0 collective-permute-done.1.refs_0_
  15.5 2.3 %edge_rows.1 = (bf16[2,6,80,128]{3,2,1,0:T(8,128)(2,1)S(1)}, bf16[2,7,80,128]{3,2,1,0:T(8,128)(2,1)S(1)}, bf16[1,6,80,128]{3,2,1,0:T(8,128)(2,1)S(1)}, bf16[2,6,64,128]{3,2,1,0:T(8,128)(2,1)S(1)}) custom-call(bf16[416,128]{1,0:T(8,128)(2,1)S(1)} %collective-permute-done.1.refs_0_, bf16[800,128]{1,0:T(8,128)(2,1)S(1)} %collective-permute-done.2.refs_2_.refs_1_, ...), custom_call_target="tpu_custom_call" | custom-call | flops 509607936 | bytes 4194304 | tf_op jit(solution)/shard_map/edge_rows/pallas_call | solution.py:423
  17.8 0.0 copy-start.1
  17.8 4.2 %collective-permute-start.4 = (bf16[2,6,64,128]{3,2,1,0:T(8,128)(2,1)S(1)}, bf16[2,6,64,128]{3,2,1,0:T(8,128)(2,1)S(1)}, u32[]{:S(2)}, u32[]{:S(2)}) collective-permute-start(bf16[2,6,64,128]{3,2,1,0:T(8,128)(2,1)S(1)} %get-tuple-element.34), channel_id=1, source_target_pairs={{0,4},{2,6},{4,8},{6,10},{8,12},{10,14},{1,5},{3,7},{5,9},{7,11},{... | collective-permute-start | bytes 589832 | tf_op jit(solution)/shard_map/ppermute | solution.py:26
  22.0 1.2 %second_layer.1.own = f32[2,4,64,192]{3,2,1,0:T(8,128)S(1)} custom-call(bf16[2,6,80,128]{3,2,1,0:T(8,128)(2,1)S(1)} %get-tuple-element.35.h_lo, bf16[2,7,80,128]{3,2,1,0:T(8,128)(2,1)S(1)} %get-tuple-element.36.h_pairs, bf16[1,6,80,128]{3,2,1,0:T(8,128)(2,1)S(1)} %get-tuple-element.37.h_stacked, ...), custom_call_target="tpu_custom_call" | custom-call | flops 509607936 | bytes 4194304 | tf_op jit(solution)/shard_map/second_layer/pallas_call | solution.py:423
  23.2 2.2 %collective-permute-done.4.partial = bf16[2,6,64,128]{3,2,1,0:T(8,128)(2,1)S(1)} collective-permute-done((bf16[2,6,64,128]{3,2,1,0:T(8,128)(2,1)S(1)}, bf16[2,6,64,128]{3,2,1,0:T(8,128)(2,1)S(1)}, u32[]{:S(2)}, u32[]{:S(2)}) %collective-permute-start.4) | collective-permute-done | bytes 196640 | tf_op jit(solution)/shard_map/ppermute | solution.py:26
  25.4 0.0 copy-done.1
  25.4 1.0 %finish.1 = bf16[2,4,64,192]{3,2,1,0:T(8,128)(2,1)} custom-call(bf16[2,6,64,128]{3,2,1,0:T(8,128)(2,1)S(1)} %collective-permute-done.4.partial, f32[2,4,64,192]{3,2,1,0:T(8,128)S(1)} %second_layer.1.own, f32[1,192]{1,0:T(1,128)S(1)} %bitcast.4), custom_call_target="tpu_custom_call" | custom-call | bytes 4194304 | tf_op jit(solution)/shard_map/finish/pallas_call | solution.py:423
Async XLA Ops:
  0.0 2.0 %collective-permute-start = (bf16[2,4,64,192]{3,2,1,0:T(8,128)(2,1)}, bf16[2,4,64,192]{3,2,1,0:T(8,128)(2,1)S(1)}, u32[]{:S(2)}, u32[]{:S(2)}) collective-permute-start(bf16[2,4,64,192]{3,2,1,0:T(8,128)(2,1)} %own_far.1), channel_id=1, source_target_pairs={{0,1},{1,0},{2,3},{3,2},{4,5},{5,4},{6,7},{7,6},{8,9},{9,8},{10,11... | collective-permute-start | bytes 589832 | tf_op jit(solution)/shard_map/ppermute | solution.py:19
  2.2 11.2 %copy-start = (f32[192]{0:T(256)S(1)}, f32[192]{0:T(256)}, u32[]{:S(2)}) copy-start(f32[192]{0:T(256)} %param.7) | copy-start | bytes 2308
  2.2 11.1 %collective-permute-start.2 = (bf16[800,128]{1,0:T(8,128)(2,1)S(1)}, bf16[800,128]{1,0:T(8,128)(2,1)S(1)}, u32[]{:S(2)}, u32[]{:S(2)}) collective-permute-start(bf16[800,128]{1,0:T(8,128)(2,1)S(1)} %get-tuple-element.24), channel_id=1, source_target_pairs={{0,4},{2,6},{4,8},{6,10},{8,12},{10,14},{1,5},{3,7},{5,9},{7,11},{... | collective-permute-start | bytes 614408 | tf_op jit(solution)/shard_map/ppermute | solution.py:26
  6.8 5.0 %collective-permute-start.3 = (bf16[416,128]{1,0:T(8,128)(2,1)S(1)}, bf16[416,128]{1,0:T(8,128)(2,1)S(1)}, u32[]{:S(2)}, u32[]{:S(2)}) collective-permute-start(bf16[416,128]{1,0:T(8,128)(2,1)S(1)} %get-tuple-element.23), channel_id=1, source_target_pairs={{0,2},{2,0},{1,3},{3,1},{4,6},{6,4},{5,7},{7,5},{8,10},{10,8},{9,1... | collective-permute-start | bytes 319496 | tf_op jit(solution)/shard_map/ppermute | solution.py:469
  8.4 7.1 %collective-permute-start.1 = (bf16[416,128]{1,0:T(8,128)(2,1)S(1)}, bf16[416,128]{1,0:T(8,128)(2,1)S(1)}, u32[]{:S(2)}, u32[]{:S(2)}) collective-permute-start(bf16[416,128]{1,0:T(8,128)(2,1)S(1)} %get-tuple-element.23), channel_id=1, source_target_pairs={{0,6},{2,4},{4,10},{6,8},{8,14},{10,12},{1,7},{3,5},{5,11},{7,9},{... | collective-permute-start | bytes 319496 | tf_op jit(solution)/shard_map/ppermute | solution.py:26
  17.8 7.6 %copy-start.1 = (f32[192]{0:T(256)S(1)}, f32[192]{0:T(256)}, u32[]{:S(2)}) copy-start(f32[192]{0:T(256)} %param.9) | copy-start | bytes 2308
  17.8 7.6 %collective-permute-start.4 = (bf16[2,6,64,128]{3,2,1,0:T(8,128)(2,1)S(1)}, bf16[2,6,64,128]{3,2,1,0:T(8,128)(2,1)S(1)}, u32[]{:S(2)}, u32[]{:S(2)}) collective-permute-start(bf16[2,6,64,128]{3,2,1,0:T(8,128)(2,1)S(1)} %get-tuple-element.34), channel_id=1, source_target_pairs={{0,4},{2,6},{4,8},{6,10},{8,12},{10,14},{1,5},{3,7},{5,9},{7,11},{... | collective-permute-start | bytes 589832 | tf_op jit(solution)/shard_map/ppermute | solution.py:26

commit v10 on v9

--- a/solution.py
+++ b/solution.py
@@ -216,10 +216,13 @@
 def window(buffers, frames, top, rows, cols, own, halo):
     every, beside = slice(0, cols), slice(cols, cols + TILE)
     for f in range(frames):
+        found = []
         for j in range(HALO):
-            for cells, row in ((own(f, (1 - top) * (rows - HALO) + j), HALO * top + j), (halo(f, j), HALO * (1 - top) + j)):
-                fill(*buffers, f, row, every, *cells[:2])
-                fill(*buffers, f, row, beside, *cells[2:])
+            found.append((HALO * top + j, own(f, (1 - top) * (rows - HALO) + j)))
+            found.append((HALO * (1 - top) + j, halo(f, j)))
+        for row, cells in found:
+            fill(*buffers, f, row, every, *cells[:2])
+            fill(*buffers, f, row, beside, *cells[2:])
 
 
 def edge_own_kernel(strips, *refs):
@@ -303,18 +306,20 @@
         for buffer in (lo, pairs, stacked):
             buffer[:HALO] = jnp.zeros((HALO,) + buffer.shape[1:], buffer.dtype)
 
+    def put(frame, rows_of):
+        for r, cells in enumerate(rows_of):
+            fill(lo, pairs, stacked, frame, r + HALO, every, *cells[:2])
+            fill(lo, pairs, stacked, frame, r + HALO, beside, *cells[2:])
+
     @if_earlier
     def build():
         for f in range(HALO):
-            for r in range(rows):
-                fill(lo, pairs, stacked, f, r + HALO, every, *whole.read(block, f, r, rest))
-                fill(lo, pairs, stacked, f, r + HALO, beside, *whole.read_beside(block, f, r, rest))
+            put(f, [(*whole.read(block, f, r, rest), *whole.read_beside(block, f, r, rest)) for r in range(rows)])
 
     for f in range(frames):
-        for r in range(rows):
-            cells = own[f, r]
-            fill(lo, pairs, stacked, HALO + f, r + HALO, every, cells[:, :LANES], cells[:, LANES:])
-            fill(lo, pairs, stacked, HALO + f, r + HALO, beside, *own_beside(neighbour, f, r, cols))
+        cells = [own[f, r] for r in range(rows)]
+        tiles = [own_beside(neighbour, f, r, cols) for r in range(rows)]
+        put(HALO + f, [(c[:, :LANES], c[:, LANES:], *tile) for c, tile in zip(cells, tiles)])
     start, count = safe_rows(strips, rows)
     lefts = jnp.concatenate([columns(all_taps(t), lo, pairs, stacked, start, count) for t in range(frames)], axis=0)
     products = convolve(all_taps(0), [plane, middle, last], lefts)
@@ -359,26 +364,30 @@
         @if_earlier
         def build():
             every, beside = slice(0, cols), slice(cols, width)
+            found = []
             for f in range(HALO):
                 for j in range(HALO):
                     mine = own_half(f, (1 - top) * (rows - HALO) + j, j)
-                    for cells, row in ((mine, HALO * top + j), (halo_row(f, j), HALO * (1 - top) + j)):
-                        fill(*near, f, row, every, *cells[:2])
-                        fill(*near, f, row, beside, *cells[2:])
-
+                    found += [(f, HALO * top + j, mine), (f, HALO * (1 - top) + j, halo_row(f, j))]
+            for f, row, cells in found:
+                fill(*near, f, row, every, *cells[:2])
+                fill(*near, f, row, beside, *cells[2:])
+
+        sums = [[edge_sums[group, t, r] for r in range(HALO)] for t in range(frames)]
+        found = []
         for t in range(frames):
             taps = earlier_taps(t)
             products = convolve(taps, [plane, middle], columns(taps, *near, 0, HALO)) if taps else None
             for r in range(HALO):
-                y = edge_sums[group, t, r]
+                y = sums[t][r]
                 if taps:
                     y = y + join(products, r * width, width)
                 h = hidden_row(y, gain, cols)
                 if strips != 2 and r == 1 - top:
                     h = h * jnp.where(strip == (0 if top else strips - 1), 0.0, 1.0)
-                h = h.astype(jnp.bfloat16)
-                row = (1 - top) * rows + r
-                fill(h_lo, h_pairs, h_stacked, t, row, slice(0, width), h[:, :LANES], h[:, LANES:])
+                found.append((t, (1 - top) * rows + r, h.astype(jnp.bfloat16)))
+        for t, row, h in found:
+            fill(h_lo, h_pairs, h_stacked, t, row, slice(0, width), h[:, :LANES], h[:, LANES:])
 
     partial_sums(frames, (h_lo, h_pairs, h_stacked), [w2_first, w2_middle], rows, cols, partial)
 
@@ -398,16 +407,18 @@
     rest = channels - LANES
     gain = gains[...]
 
+    sums = []
+    for t in range(frames):
+        y = own[t]
+        if t < HALO:
+            halves = [partial[t, rows + r // 2, :, (r % 2) * rest : (r % 2 + 1) * rest] for r in range(rows)]
+            sent = [jnp.concatenate([partial[t, r], halves[r]], axis=-1) for r in range(rows)]
+            y = y + jnp.stack(sent).astype(jnp.float32)
+        sums.append(y.reshape(rows * cols, channels))
+    results = [activate(y, gain).astype(jnp.bfloat16) for y in sums]
     copies = [pltpu.make_async_copy(out.at[t], out_far.at[t], left.at[t]) for t in range(frames)]
     for t in range(frames):
-        for r in range(rows):
-            y = own[t, r]
-            if t < HALO:
-                half = r % 2
-                high = partial[t, rows + r // 2, :, half * rest : (half + 1) * rest]
-                sent = jnp.concatenate([partial[t, r], high], axis=-1)
-                y = y + sent.astype(jnp.float32)
-            out[t, r] = activate(y, gain).astype(jnp.bfloat16)
+        out[t] = results[t].reshape(rows, cols, channels)
         copies[t].start()
     for copy in copies:
         copy.wait()

time: 26.7 us -> 26.5 us (level)
  no operation moved by 1% of the time
where the time goes in v10:
time: 26.5 us; the launch traced here: 26.3 us
  starting transfers between devices  14.3 us (54%)
  Pallas kernels  9.67 us (36%)
  waiting for transfers between devices  2.14 us (8%)
    ppermute x3, starting transfers between devices, forward(): return lax.ppermute(x, ('frame', 'strip'), pairs)  12.3 us
    pallas_call x7, Pallas kernels, call(): pl.pallas_call(kernel, out_shape=outs, in_specs=in_specs, out_specs=(away...  9.67 us
    ppermute x3, waiting for transfers between devices, forward(): return lax.ppermute(x, ('frame', 'strip'), pairs)  2.13 us
    ppermute x1, starting transfers between devices, shards(): lax.ppermute(edge, 'strip', way)  1.56 us
  transfers between devices with their start and end apart: 5, of which 1 were waited for; matrix products, arithmetic and copies ran while one was open for 0% of the time, Pallas kernels for 24%

profile of v10, /device:TPU:0, one launch (start us, length us, event | category | flops | bytes accessed | tf_op | source)
XLA Modules:
  0.0 26.3 jit_solution(6093091702207479738)
XLA Ops:
  0.0 0.5 %collective-permute-start = (bf16[2,4,64,192]{3,2,1,0:T(8,128)(2,1)}, bf16[2,4,64,192]{3,2,1,0:T(8,128)(2,1)S(1)}, u32[]{:S(2)}, u32[]{:S(2)}) collective-permute-start(bf16[2,4,64,192]{3,2,1,0:T(8,128)(2,1)} %own_far.1), channel_id=1, source_target_pairs={{0,1},{1,0},{2,3},{3,2},{4,5},{5,4},{6,7},{7,6},{8,9},{9,8},{10,11... | collective-permute-start | bytes 589832 | tf_op jit(solution)/shard_map/ppermute | solution.py:19
  0.5 1.5 %stage.1 = (bf16[2,4,64,192]{3,2,1,0:T(8,128)(2,1)S(1)}, bf16[3,3,192,192]{3,2,1,0:T(8,128)(2,1)S(1)}, bf16[3,3,192,192]{3,2,1,0:T(8,128)(2,1)S(1)}) custom-call(bf16[2,4,64,192]{3,2,1,0:T(8,128)(2,1)} %own_far.1, bf16[3,3,3,192,192]{4,3,2,1,0:T(8,128)(2,1)} %refs_5_.1), custom_call_target="tpu_custom_call" | custom-call | bytes 4194304 | tf_op jit(solution)/shard_map/stage/pallas_call | solution.py:434
  2.0 0.0 collective-permute-done.neighbour.refs_1_
  2.0 0.1 pack.1
  2.2 0.0 copy-start
  2.2 4.7 %collective-permute-start.2 = (bf16[800,128]{1,0:T(8,128)(2,1)S(1)}, bf16[800,128]{1,0:T(8,128)(2,1)S(1)}, u32[]{:S(2)}, u32[]{:S(2)}) collective-permute-start(bf16[800,128]{1,0:T(8,128)(2,1)S(1)} %get-tuple-element.24), channel_id=1, source_target_pairs={{0,4},{2,6},{4,8},{6,10},{8,12},{10,14},{1,5},{3,7},{5,9},{7,11},{... | collective-permute-start | bytes 614408 | tf_op jit(solution)/shard_map/ppermute | solution.py:26
  6.8 1.6 %collective-permute-start.3 = (bf16[416,128]{1,0:T(8,128)(2,1)S(1)}, bf16[416,128]{1,0:T(8,128)(2,1)S(1)}, u32[]{:S(2)}, u32[]{:S(2)}) collective-permute-start(bf16[416,128]{1,0:T(8,128)(2,1)S(1)} %get-tuple-element.23), channel_id=1, source_target_pairs={{0,2},{2,0},{1,3},{3,1},{4,6},{6,4},{5,7},{7,5},{8,10},{10,8},{9,1... | collective-permute-start | bytes 319496 | tf_op jit(solution)/shard_map/ppermute | solution.py:480
  8.4 3.4 %collective-permute-start.1 = (bf16[416,128]{1,0:T(8,128)(2,1)S(1)}, bf16[416,128]{1,0:T(8,128)(2,1)S(1)}, u32[]{:S(2)}, u32[]{:S(2)}) collective-permute-start(bf16[416,128]{1,0:T(8,128)(2,1)S(1)} %get-tuple-element.23), channel_id=1, source_target_pairs={{0,6},{2,4},{4,10},{6,8},{8,14},{10,12},{1,7},{3,5},{5,11},{7,9},{... | collective-permute-start | bytes 319496 | tf_op jit(solution)/shard_map/ppermute | solution.py:26
  11.8 0.0 collective-permute-done.3.refs_2_
  11.9 1.4 %edge_rows_own.1 = (f32[1,2,2,80,192]{4,3,2,1,0:T(8,128)S(1)}, bf16[3,3,192,192]{3,2,1,0:T(8,128)(2,1)S(1)}) custom-call(bf16[2,4,64,192]{3,2,1,0:T(8,128)(2,1)S(1)} %get-tuple-element.22.own.refs_0_, bf16[2,4,64,192]{3,2,1,0:T(8,128)(2,1)S(1)} %collective-permute-done.neighbour.refs_1_, bf16[416,128]{1,0:T(8,128)(2,1)S(1)} %collective-permute-done.3.refs_2_, ...), custom_call_target="tpu_custom_call" | custom-call | flops 127401984 | bytes 4194304 | tf_op jit(solution)/shard_map/edge_rows_own/pallas_call | solution.py:434
  13.2 0.0 collective-permute-done.2.refs_2_.refs_1_
  13.3 0.0 copy-done
  13.3 2.2 %safe_rows.1 = (bf16[2,6,80,128]{3,2,1,0:T(8,128)(2,1)S(1)}, bf16[2,7,80,128]{3,2,1,0:T(8,128)(2,1)S(1)}, bf16[1,6,80,128]{3,2,1,0:T(8,128)(2,1)S(1)}, bf16[3,3,...) custom-call(bf16[2,4,64,192]{3,2,1,0:T(8,128)(2,1)S(1)} %get-tuple-element.22, ...), custom_call_target="tpu_custom_call" | custom-call | flops 509607936 | bytes 4194304 | tf_op jit(solution)/shard_map/safe_rows/pallas_call | solution.py:434
  15.4 0.0 collective-permute-done.1.refs_0_
  15.4 2.3 %edge_rows.1 = (bf16[2,6,80,128]{3,2,1,0:T(8,128)(2,1)S(1)}, bf16[2,7,80,128]{3,2,1,0:T(8,128)(2,1)S(1)}, bf16[1,6,80,128]{3,2,1,0:T(8,128)(2,1)S(1)}, bf16[2,6,64,128]{3,2,1,0:T(8,128)(2,1)S(1)}) custom-call(bf16[416,128]{1,0:T(8,128)(2,1)S(1)} %collective-permute-done.1.refs_0_, bf16[800,128]{1,0:T(8,128)(2,1)S(1)} %collective-permute-done.2.refs_2_.refs_1_, ...), custom_call_target="tpu_custom_call" | custom-call | flops 509607936 | bytes 4194304 | tf_op jit(solution)/shard_map/edge_rows/pallas_call | solution.py:434
  17.7 0.0 copy-start.1
  17.7 4.2 %collective-permute-start.4 = (bf16[2,6,64,128]{3,2,1,0:T(8,128)(2,1)S(1)}, bf16[2,6,64,128]{3,2,1,0:T(8,128)(2,1)S(1)}, u32[]{:S(2)}, u32[]{:S(2)}) collective-permute-start(bf16[2,6,64,128]{3,2,1,0:T(8,128)(2,1)S(1)} %get-tuple-element.34), channel_id=1, source_target_pairs={{0,4},{2,6},{4,8},{6,10},{8,12},{10,14},{1,5},{3,7},{5,9},{7,11},{... | collective-permute-start | bytes 589832 | tf_op jit(solution)/shard_map/ppermute | solution.py:26
  21.9 1.2 %second_layer.1.own = f32[2,4,64,192]{3,2,1,0:T(8,128)S(1)} custom-call(bf16[2,6,80,128]{3,2,1,0:T(8,128)(2,1)S(1)} %get-tuple-element.35.h_lo, bf16[2,7,80,128]{3,2,1,0:T(8,128)(2,1)S(1)} %get-tuple-element.36.h_pairs, bf16[1,6,80,128]{3,2,1,0:T(8,128)(2,1)S(1)} %get-tuple-element.37.h_stacked, ...), custom_call_target="tpu_custom_call" | custom-call | flops 509607936 | bytes 4194304 | tf_op jit(solution)/shard_map/second_layer/pallas_call | solution.py:434
  23.1 2.1 %collective-permute-done.4.partial = bf16[2,6,64,128]{3,2,1,0:T(8,128)(2,1)S(1)} collective-permute-done((bf16[2,6,64,128]{3,2,1,0:T(8,128)(2,1)S(1)}, bf16[2,6,64,128]{3,2,1,0:T(8,128)(2,1)S(1)}, u32[]{:S(2)}, u32[]{:S(2)}) %collective-permute-start.4) | collective-permute-done | bytes 196640 | tf_op jit(solution)/shard_map/ppermute | solution.py:26
  25.3 0.0 copy-done.1
  25.3 1.0 %finish.1 = bf16[2,4,64,192]{3,2,1,0:T(8,128)(2,1)} custom-call(bf16[2,6,64,128]{3,2,1,0:T(8,128)(2,1)S(1)} %collective-permute-done.4.partial, f32[2,4,64,192]{3,2,1,0:T(8,128)S(1)} %second_layer.1.own, f32[1,192]{1,0:T(1,128)S(1)} %bitcast.4), custom_call_target="tpu_custom_call" | custom-call | bytes 4194304 | tf_op jit(solution)/shard_map/finish/pallas_call | solution.py:434
Async XLA Ops:
  0.0 2.0 %collective-permute-start = (bf16[2,4,64,192]{3,2,1,0:T(8,128)(2,1)}, bf16[2,4,64,192]{3,2,1,0:T(8,128)(2,1)S(1)}, u32[]{:S(2)}, u32[]{:S(2)}) collective-permute-start(bf16[2,4,64,192]{3,2,1,0:T(8,128)(2,1)} %own_far.1), channel_id=1, source_target_pairs={{0,1},{1,0},{2,3},{3,2},{4,5},{5,4},{6,7},{7,6},{8,9},{9,8},{10,11... | collective-permute-start | bytes 589832 | tf_op jit(solution)/shard_map/ppermute | solution.py:19
  2.2 11.1 %copy-start = (f32[192]{0:T(256)S(1)}, f32[192]{0:T(256)}, u32[]{:S(2)}) copy-start(f32[192]{0:T(256)} %param.7) | copy-start | bytes 2308
  2.2 11.1 %collective-permute-start.2 = (bf16[800,128]{1,0:T(8,128)(2,1)S(1)}, bf16[800,128]{1,0:T(8,128)(2,1)S(1)}, u32[]{:S(2)}, u32[]{:S(2)}) collective-permute-start(bf16[800,128]{1,0:T(8,128)(2,1)S(1)} %get-tuple-element.24), channel_id=1, source_target_pairs={{0,4},{2,6},{4,8},{6,10},{8,12},{10,14},{1,5},{3,7},{5,9},{7,11},{... | collective-permute-start | bytes 614408 | tf_op jit(solution)/shard_map/ppermute | solution.py:26
  6.8 5.0 %collective-permute-start.3 = (bf16[416,128]{1,0:T(8,128)(2,1)S(1)}, bf16[416,128]{1,0:T(8,128)(2,1)S(1)}, u32[]{:S(2)}, u32[]{:S(2)}) collective-permute-start(bf16[416,128]{1,0:T(8,128)(2,1)S(1)} %get-tuple-element.23), channel_id=1, source_target_pairs={{0,2},{2,0},{1,3},{3,1},{4,6},{6,4},{5,7},{7,5},{8,10},{10,8},{9,1... | collective-permute-start | bytes 319496 | tf_op jit(solution)/shard_map/ppermute | solution.py:480
  8.4 7.0 %collective-permute-start.1 = (bf16[416,128]{1,0:T(8,128)(2,1)S(1)}, bf16[416,128]{1,0:T(8,128)(2,1)S(1)}, u32[]{:S(2)}, u32[]{:S(2)}) collective-permute-start(bf16[416,128]{1,0:T(8,128)(2,1)S(1)} %get-tuple-element.23), channel_id=1, source_target_pairs={{0,6},{2,4},{4,10},{6,8},{8,14},{10,12},{1,7},{3,5},{5,11},{7,9},{... | collective-permute-start | bytes 319496 | tf_op jit(solution)/shard_map/ppermute | solution.py:26
  17.7 7.6 %copy-start.1 = (f32[192]{0:T(256)S(1)}, f32[192]{0:T(256)}, u32[]{:S(2)}) copy-start(f32[192]{0:T(256)} %param.9) | copy-start | bytes 2308
  17.7 7.6 %collective-permute-start.4 = (bf16[2,6,64,128]{3,2,1,0:T(8,128)(2,1)S(1)}, bf16[2,6,64,128]{3,2,1,0:T(8,128)(2,1)S(1)}, u32[]{:S(2)}, u32[]{:S(2)}) collective-permute-start(bf16[2,6,64,128]{3,2,1,0:T(8,128)(2,1)S(1)} %get-tuple-element.34), channel_id=1, source_target_pairs={{0,4},{2,6},{4,8},{6,10},{8,12},{10,14},{1,5},{3,7},{5,9},{7,11},{... | collective-permute-start | bytes 589832 | tf_op jit(solution)/shard_map/ppermute | solution.py:26

commit v11 on v10

--- a/solution.py
+++ b/solution.py
@@ -226,8 +226,16 @@
 
 
 def edge_own_kernel(strips, *refs):
-    *refs, near_lo, near_pairs, near_stacked, arrived = refs
-    own, neighbour, *edges, middle, last, weight_far, edge_sums, plane = refs
+    *refs, arrived = refs
+    if strips == 2:
+        *refs, edge = refs
+        own, neighbour, gathered, middle, last, weight_far, edge_sums, plane, *near = refs
+        landed = pltpu.make_async_copy(gathered.at[1 - lax.axis_index("strip")], edge, arrived.at[1])
+        landed.start()
+        edges = [edge]
+    else:
+        own, neighbour, *edges, middle, last, weight_far, edge_sums, plane, near_lo, near_pairs, near_stacked = refs
+        near = [near_lo, near_pairs, near_stacked]
     frames, rows, cols, channels = own.shape
     width, rest = cols + TILE, channels - LANES
     copy = pltpu.make_async_copy(weight_far.at[0], plane, arrived.at[0])
@@ -235,8 +243,9 @@
     if frames > 2:
         copy.wait()
     strip_block = Packed(frames, HALO, cols)
-    near = (near_lo, near_pairs, near_stacked)
-    clear((near_pairs,))
+    clear((near[1],))
+    if strips == 2:
+        landed.wait()
     for group, (edge, top) in enumerate(zip(edges, at_top(strips))):
 
         def own_row(f, r):
@@ -477,17 +486,20 @@
     downs = [(i + 1, i) for i in range(strips - 1)]
     ways = [[(0, 1), (1, 0)]] if strips == 2 else [ups, downs]
     before = forward(block)
-    own_edges = [lax.ppermute(edge, "strip", way) for edge, way in zip(edges, ways)]
+    if strips == 2:
+        own_edges = [lax.all_gather(edges[0], "strip")]
+    else:
+        own_edges = [lax.ppermute(edge, "strip", way) for edge, way in zip(edges, ways)]
     before_edges = [forward(edge, way) for edge, way in zip(edges, ways)]
     edge_sums, plane = call(
         functools.partial(edge_own_kernel, strips),
         "edge_rows_own",
         [own_in, neighbour, *own_edges, middle, last, weight_first],
         [f32((len(ways), frames, HALO, width, channels)), plane_shape],
-        block_scratch(frames, 2 * HALO, width),
-        semaphores=1,
+        block_scratch(frames, 2 * HALO, width) + [edge_shape.shape] * (strips == 2),
+        semaphores=2,
         flops=flops // 4,
-        far=[-1],
+        far=[2, -1] if strips == 2 else [-1],
     )
     gain_first = scale_first[None]
     h_shapes = [bf16(shape) for shape in block_scratch(frames, rows + 2, width)]

time: 26.5 us -> 33.6 us (1.27)
  blocking collectives: 0 us -> 5.49 us
  waiting for transfers between devices: 2.14 us -> 3.11 us
  starting transfers between devices: 14.3 us -> 14.7 us
    all_gather x0 -> x1, blocking collectives: none -> 5.49 us  [shards(): own_edges = [lax.all_gather(edges[0], 'strip')]]
    ppermute x3, starting transfers between devices: 12.3 us -> 14.3 us  [forward(): return lax.ppermute(x, ('frame', 'strip'), pairs)]
    ppermute x1 -> x0, starting transfers between devices: 1.56 us -> none  [shards(): lax.ppermute(edge, 'strip', way)]
    ppermute x3, waiting for transfers between devices: 2.13 us -> 3.11 us  [forward(): return lax.ppermute(x, ('frame', 'strip'), pairs)]
  transfers between devices with their start and end apart: 5 -> 4, of which waited for: 1 -> 1; matrix products, arithmetic and copies ran while one was open for 0% -> 0% of each run, Pallas kernels for 24% -> 20%
where the time goes in v11:
time: 33.6 us; the launch traced here: 33.4 us
  starting transfers between devices  14.7 us (44%)
  Pallas kernels  9.99 us (30%)
  blocking collectives  5.49 us (16%)
  waiting for transfers between devices  3.11 us (9%)
    ppermute x3, starting transfers between devices, forward(): return lax.ppermute(x, ('frame', 'strip'), pairs)  14.3 us
    pallas_call x7, Pallas kernels, call(): pl.pallas_call(kernel, out_shape=outs, in_specs=in_specs, out_specs=(away...  9.99 us
    all_gather x1, blocking collectives, shards(): own_edges = [lax.all_gather(edges[0], 'strip')]  5.49 us
    ppermute x3, waiting for transfers between devices, forward(): return lax.ppermute(x, ('frame', 'strip'), pairs)  3.11 us
  transfers between devices with their start and end apart: 4, of which 1 were waited for; matrix products, arithmetic and copies ran while one was open for 0% of the time, Pallas kernels for 20%

profile of v11, /device:TPU:0, one launch (start us, length us, event | category | flops | bytes accessed | tf_op | source)
XLA Modules:
  0.0 33.4 jit_solution(18111472983349275456)
XLA Ops:
  0.0 0.5 %collective-permute-start = (bf16[2,4,64,192]{3,2,1,0:T(8,128)(2,1)}, bf16[2,4,64,192]{3,2,1,0:T(8,128)(2,1)S(1)}, u32[]{:S(2)}, u32[]{:S(2)}) collective-permute-start(bf16[2,4,64,192]{3,2,1,0:T(8,128)(2,1)} %own_far.1), channel_id=1, source_target_pairs={{0,1},{1,0},{2,3},{3,2},{4,5},{5,4},{6,7},{7,6},{8,9},{9,8},{10,11... | collective-permute-start | bytes 589832 | tf_op jit(solution)/shard_map/ppermute | solution.py:19
  0.5 1.5 %stage.1 = (bf16[2,4,64,192]{3,2,1,0:T(8,128)(2,1)S(1)}, bf16[3,3,192,192]{3,2,1,0:T(8,128)(2,1)S(1)}, bf16[3,3,192,192]{3,2,1,0:T(8,128)(2,1)S(1)}) custom-call(bf16[2,4,64,192]{3,2,1,0:T(8,128)(2,1)} %own_far.1, bf16[3,3,3,192,192]{4,3,2,1,0:T(8,128)(2,1)} %refs_5_.1), custom_call_target="tpu_custom_call" | custom-call | bytes 4194304 | tf_op jit(solution)/shard_map/stage/pallas_call | solution.py:443
  2.0 0.0 collective-permute-done.neighbour.refs_1_
  2.0 0.1 pack.1
  2.2 4.7 %collective-permute-start.2 = (bf16[800,128]{1,0:T(8,128)(2,1)S(1)}, bf16[800,128]{1,0:T(8,128)(2,1)S(1)}, u32[]{:S(2)}, u32[]{:S(2)}) collective-permute-start(bf16[800,128]{1,0:T(8,128)(2,1)S(1)} %get-tuple-element.24), channel_id=1, source_target_pairs={{0,4},{2,6},{4,8},{6,10},{8,12},{10,14},{1,5},{3,7},{5,9},{7,11},{... | collective-permute-start | bytes 614408 | tf_op jit(solution)/shard_map/ppermute | solution.py:26
  6.8 4.4 %collective-permute-start.1 = (bf16[416,128]{1,0:T(8,128)(2,1)S(1)}, bf16[416,128]{1,0:T(8,128)(2,1)S(1)}, u32[]{:S(2)}, u32[]{:S(2)}) collective-permute-start(bf16[416,128]{1,0:T(8,128)(2,1)S(1)} %get-tuple-element.23), channel_id=1, source_target_pairs={{0,6},{2,4},{4,10},{6,8},{8,14},{10,12},{1,7},{3,5},{5,11},{7,9},{... | collective-permute-start | bytes 319496 | tf_op jit(solution)/shard_map/ppermute | solution.py:26
  11.2 5.5 %all-gather = bf16[832,128]{1,0:T(8,128)(2,1)} all-gather(bf16[416,128]{1,0:T(8,128)(2,1)S(1)} %get-tuple-element.23), channel_id=2, replica_groups=mesh['groups'=2,'frame'=4,'strip'=2,'slab'=2] {'strip'}, dimensions={0}, use_global_device_ids=true | all-gather | bytes 319488 | tf_op jit(solution)/shard_map/all_gather | solution.py:490
  16.7 0.0 copy-start
  16.7 1.7 %edge_rows_own.1 = (f32[1,2,2,80,192]{4,3,2,1,0:T(8,128)S(1)}, bf16[3,3,192,192]{3,2,1,0:T(8,128)(2,1)S(1)}) custom-call(bf16[2,4,64,192]{3,2,1,0:T(8,128)(2,1)S(1)} %get-tuple-element.22.own.refs_0_, bf16[2,4,64,192]{3,2,1,0:T(8,128)(2,1)S(1)} %collective-permute-done.neighbour.refs_1_, bf16[2,416,128]{2,1,0:T(8,128)(2,1)} %bitcast.6, ...), custom_call_target="tpu_custom_call" | custom-call | flops 127401984 | bytes 4194304 | tf_op jit(solution)/shard_map/edge_rows_own/pallas_call | solution.py:443
  18.5 0.0 collective-permute-done.2.refs_2_.refs_1_
  18.5 0.0 copy-done
  18.5 2.2 %safe_rows.1 = (bf16[2,6,80,128]{3,2,1,0:T(8,128)(2,1)S(1)}, bf16[2,7,80,128]{3,2,1,0:T(8,128)(2,1)S(1)}, bf16[1,6,80,128]{3,2,1,0:T(8,128)(2,1)S(1)}, bf16[3,3,...) custom-call(bf16[2,4,64,192]{3,2,1,0:T(8,128)(2,1)S(1)} %get-tuple-element.22, ...), custom_call_target="tpu_custom_call" | custom-call | flops 509607936 | bytes 4194304 | tf_op jit(solution)/shard_map/safe_rows/pallas_call | solution.py:443
  20.6 0.0 collective-permute-done.1.refs_0_
  20.7 2.2 %edge_rows.1 = (bf16[2,6,80,128]{3,2,1,0:T(8,128)(2,1)S(1)}, bf16[2,7,80,128]{3,2,1,0:T(8,128)(2,1)S(1)}, bf16[1,6,80,128]{3,2,1,0:T(8,128)(2,1)S(1)}, bf16[2,6,64,128]{3,2,1,0:T(8,128)(2,1)S(1)}) custom-call(bf16[416,128]{1,0:T(8,128)(2,1)S(1)} %collective-permute-done.1.refs_0_, bf16[800,128]{1,0:T(8,128)(2,1)S(1)} %collective-permute-done.2.refs_2_.refs_1_, ...), custom_call_target="tpu_custom_call" | custom-call | flops 509607936 | bytes 4194304 | tf_op jit(solution)/shard_map/edge_rows/pallas_call | solution.py:443
  22.9 0.0 copy-start.1
  22.9 5.2 %collective-permute-start.3 = (bf16[2,6,64,128]{3,2,1,0:T(8,128)(2,1)S(1)}, bf16[2,6,64,128]{3,2,1,0:T(8,128)(2,1)S(1)}, u32[]{:S(2)}, u32[]{:S(2)}) collective-permute-start(bf16[2,6,64,128]{3,2,1,0:T(8,128)(2,1)S(1)} %get-tuple-element.34), channel_id=1, source_target_pairs={{0,4},{2,6},{4,8},{6,10},{8,12},{10,14},{1,5},{3,7},{5,9},{7,11},{... | collective-permute-start | bytes 589832 | tf_op jit(solution)/shard_map/ppermute | solution.py:26
  28.1 1.2 %second_layer.1.own = f32[2,4,64,192]{3,2,1,0:T(8,128)S(1)} custom-call(bf16[2,6,80,128]{3,2,1,0:T(8,128)(2,1)S(1)} %get-tuple-element.35.h_lo, bf16[2,7,80,128]{3,2,1,0:T(8,128)(2,1)S(1)} %get-tuple-element.36.h_pairs, bf16[1,6,80,128]{3,2,1,0:T(8,128)(2,1)S(1)} %get-tuple-element.37.h_stacked, ...), custom_call_target="tpu_custom_call" | custom-call | flops 509607936 | bytes 4194304 | tf_op jit(solution)/shard_map/second_layer/pallas_call | solution.py:443
  29.3 3.1 %collective-permute-done.3.partial = bf16[2,6,64,128]{3,2,1,0:T(8,128)(2,1)S(1)} collective-permute-done((bf16[2,6,64,128]{3,2,1,0:T(8,128)(2,1)S(1)}, bf16[2,6,64,128]{3,2,1,0:T(8,128)(2,1)S(1)}, u32[]{:S(2)}, u32[]{:S(2)}) %collective-permute-start.3) | collective-permute-done | bytes 196640 | tf_op jit(solution)/shard_map/ppermute | solution.py:26
  32.4 0.0 copy-done.1
  32.4 1.0 %finish.1 = bf16[2,4,64,192]{3,2,1,0:T(8,128)(2,1)} custom-call(bf16[2,6,64,128]{3,2,1,0:T(8,128)(2,1)S(1)} %collective-permute-done.3.partial, f32[2,4,64,192]{3,2,1,0:T(8,128)S(1)} %second_layer.1.own, f32[1,192]{1,0:T(1,128)S(1)} %bitcast.5), custom_call_target="tpu_custom_call" | custom-call | bytes 4194304 | tf_op jit(solution)/shard_map/finish/pallas_call | solution.py:443
Async XLA Ops:
  0.0 2.0 %collective-permute-start = (bf16[2,4,64,192]{3,2,1,0:T(8,128)(2,1)}, bf16[2,4,64,192]{3,2,1,0:T(8,128)(2,1)S(1)}, u32[]{:S(2)}, u32[]{:S(2)}) collective-permute-start(bf16[2,4,64,192]{3,2,1,0:T(8,128)(2,1)} %own_far.1), channel_id=1, source_target_pairs={{0,1},{1,0},{2,3},{3,2},{4,5},{5,4},{6,7},{7,6},{8,9},{9,8},{10,11... | collective-permute-start | bytes 589832 | tf_op jit(solution)/shard_map/ppermute | solution.py:19
  2.2 16.3 %collective-permute-start.2 = (bf16[800,128]{1,0:T(8,128)(2,1)S(1)}, bf16[800,128]{1,0:T(8,128)(2,1)S(1)}, u32[]{:S(2)}, u32[]{:S(2)}) collective-permute-start(bf16[800,128]{1,0:T(8,128)(2,1)S(1)} %get-tuple-element.24), channel_id=1, source_target_pairs={{0,4},{2,6},{4,8},{6,10},{8,12},{10,14},{1,5},{3,7},{5,9},{7,11},{... | collective-permute-start | bytes 614408 | tf_op jit(solution)/shard_map/ppermute | solution.py:26
  6.8 13.8 %collective-permute-start.1 = (bf16[416,128]{1,0:T(8,128)(2,1)S(1)}, bf16[416,128]{1,0:T(8,128)(2,1)S(1)}, u32[]{:S(2)}, u32[]{:S(2)}) collective-permute-start(bf16[416,128]{1,0:T(8,128)(2,1)S(1)} %get-tuple-element.23), channel_id=1, source_target_pairs={{0,6},{2,4},{4,10},{6,8},{8,14},{10,12},{1,7},{3,5},{5,11},{7,9},{... | collective-permute-start | bytes 319496 | tf_op jit(solution)/shard_map/ppermute | solution.py:26
  16.7 1.7 %copy-start = (f32[192]{0:T(256)S(1)}, f32[192]{0:T(256)}, u32[]{:S(2)}) copy-start(f32[192]{0:T(256)} %param.7) | copy-start | bytes 2308
  22.9 9.5 %copy-start.1 = (f32[192]{0:T(256)S(1)}, f32[192]{0:T(256)}, u32[]{:S(2)}) copy-start(f32[192]{0:T(256)} %param.9) | copy-start | bytes 2308
  22.9 9.5 %collective-permute-start.3 = (bf16[2,6,64,128]{3,2,1,0:T(8,128)(2,1)S(1)}, bf16[2,6,64,128]{3,2,1,0:T(8,128)(2,1)S(1)}, u32[]{:S(2)}, u32[]{:S(2)}) collective-permute-start(bf16[2,6,64,128]{3,2,1,0:T(8,128)(2,1)S(1)} %get-tuple-element.34), channel_id=1, source_target_pairs={{0,4},{2,6},{4,8},{6,10},{8,12},{10,14},{1,5},{3,7},{5,9},{7,11},{... | collective-permute-start | bytes 589832 | tf_op jit(solution)/shard_map/ppermute | solution.py:26

commit v12 on v10

--- a/solution.py
+++ b/solution.py
@@ -213,7 +213,7 @@
     return tile[:, :LANES], tile[:, LANES:]
 
 
-def window(buffers, frames, top, rows, cols, own, halo):
+def window(buffers, skip, frames, top, rows, cols, own, halo):
     every, beside = slice(0, cols), slice(cols, cols + TILE)
     for f in range(frames):
         found = []
@@ -221,8 +221,8 @@
             found.append((HALO * top + j, own(f, (1 - top) * (rows - HALO) + j)))
             found.append((HALO * (1 - top) + j, halo(f, j)))
         for row, cells in found:
-            fill(*buffers, f, row, every, *cells[:2])
-            fill(*buffers, f, row, beside, *cells[2:])
+            fill(*buffers, skip + f, row, every, *cells[:2])
+            fill(*buffers, skip + f, row, beside, *cells[2:])
 
 
 def edge_own_kernel(strips, *refs):
@@ -236,7 +236,11 @@
         copy.wait()
     strip_block = Packed(frames, HALO, cols)
     near = (near_lo, near_pairs, near_stacked)
+    span = min(frames, 3)
+    zeros = span - 1
     clear((near_pairs,))
+    for buffer in (near_lo, near_stacked):
+        buffer[:zeros] = jnp.zeros((zeros,) + buffer.shape[1:], buffer.dtype)
     for group, (edge, top) in enumerate(zip(edges, at_top(strips))):
 
         def own_row(f, r):
@@ -246,12 +250,13 @@
         def halo_row(f, j):
             return *strip_block.read(edge, f, j, rest), *strip_block.read_beside(edge, f, j, rest)
 
-        window(near, frames, top, rows, cols, own_row, halo_row)
+        window(near, zeros, frames, top, rows, cols, own_row, halo_row)
+        lefts = [columns([(t + k, 3 - span + k) for k in range(span)], *near, 0, HALO) for t in range(frames)]
+        taps = [(k, 3 - span + k) for k in range(span)]
+        products = convolve(taps, [plane, middle, last], jnp.concatenate(lefts, axis=0))
         for t in range(frames):
-            taps = own_taps(t)
-            products = convolve(taps, [plane, middle, last], columns(taps, *near, 0, HALO))
             for r in range(HALO):
-                edge_sums[group, t, r] = join(products, r * width, width)
+                edge_sums[group, t, r] = join(products, (t * HALO + r) * width, width)
     if frames <= 2:
         copy.wait()
 
@@ -341,9 +346,15 @@
     strip = lax.axis_index("strip")
     whole, strip_block = Packed(HALO, rows, cols), Packed(frames, HALO, cols)
     near = (near_lo, near_pairs, near_stacked)
-    clear(near)
-    for target, source in zip((h_lo, h_pairs, h_stacked), (safe_lo, safe_pairs, safe_stacked)):
-        target[...] = source[...]
+    none = jnp.zeros(near_lo.shape[1:], near_lo.dtype)
+    near_lo[HALO] = none
+    near_stacked[HALO - 1] = none
+    clear((near_pairs,))
+
+    @pl.when(lax.axis_index("frame") == 0)
+    def none_earlier():
+        clear((near_lo, near_stacked))
+
     gain = gains[...]
     for group, (edge, top) in enumerate(zip(edges, at_top(strips))):
 
@@ -375,13 +386,13 @@
 
         sums = [[edge_sums[group, t, r] for r in range(HALO)] for t in range(frames)]
         found = []
+        lefts = [columns([(t, 0), (t + 1, 1)], *near, 0, HALO) for t in range(HALO)]
+        products = convolve([(0, 0), (1, 1)], [plane, middle], jnp.concatenate(lefts, axis=0))
         for t in range(frames):
-            taps = earlier_taps(t)
-            products = convolve(taps, [plane, middle], columns(taps, *near, 0, HALO)) if taps else None
             for r in range(HALO):
                 y = sums[t][r]
-                if taps:
-                    y = y + join(products, r * width, width)
+                if t < HALO:
+                    y = y + join(products, (t * HALO + r) * width, width)
                 h = hidden_row(y, gain, cols)
                 if strips != 2 and r == 1 - top:
                     h = h * jnp.where(strip == (0 if top else strips - 1), 0.0, 1.0)
@@ -424,7 +435,7 @@
         copy.wait()
 
 
-def call(kernel, name, ins, outs, scratch=(), semaphores=0, flops=0, far=(), far_out=False):
+def call(kernel, name, ins, outs, scratch=(), semaphores=0, flops=0, far=(), far_out=False, alias=None):
     near, away = pl.BlockSpec(memory_space=pltpu.VMEM), pl.BlockSpec(memory_space=pltpu.HBM)
     in_specs, ins = [near] * len(ins), list(ins)
     for place in far:
@@ -438,6 +449,7 @@
         out_specs=(away if far_out else near) if one else [near] * len(outs),
         scratch_shapes=[pltpu.VMEM(shape, jnp.bfloat16) for shape in scratch]
         + [pltpu.SemaphoreType.DMA((semaphores,))] * (semaphores > 0),
+        input_output_aliases=alias or {},
         compiler_params=pltpu.CompilerParams(vmem_limit_bytes=24 * 1024 * 1024),
         cost_estimate=pl.CostEstimate(flops=flops, bytes_accessed=4 * 1024 * 1024, transcendentals=0),
         name=name,
@@ -484,7 +496,7 @@
         "edge_rows_own",
         [own_in, neighbour, *own_edges, middle, last, weight_first],
         [f32((len(ways), frames, HALO, width, channels)), plane_shape],
-        block_scratch(frames, 2 * HALO, width),
+        block_scratch(frames + min(frames, 3) - 1, 2 * HALO, width),
         semaphores=1,
         flops=flops // 4,
         far=[-1],
@@ -507,8 +519,9 @@
         "edge_rows",
         [*before_edges, before, edge_sums, *safe, plane, middle, gain_first, w2_first, w2_middle],
         h_shapes + [partial_shape],
-        block_scratch(HALO, 2 * HALO, width),
+        block_scratch(HALO + 1, 2 * HALO, width),
         flops=flops,
+        alias={len(before_edges) + 2 + k: k for k in range(3)},
     )
     sent = forward(partial)
     own = call(

time: 26.5 us -> 26.5 us (level)
  no operation moved by 1% of the time
where the time goes in v12:
time: 26.5 us; the launch traced here: 26.2 us
  starting transfers between devices  14.4 us (54%)
  Pallas kernels  9.68 us (37%)
  waiting for transfers between devices  2 us (8%)
    ppermute x3, starting transfers between devices, forward(): return lax.ppermute(x, ('frame', 'strip'), pairs)  12.4 us
    pallas_call x7, Pallas kernels, call(): pl.pallas_call(kernel, out_shape=outs, in_specs=in_specs, out_specs=(away...  9.68 us
    ppermute x3, waiting for transfers between devices, forward(): return lax.ppermute(x, ('frame', 'strip'), pairs)  2 us
    ppermute x1, starting transfers between devices, shards(): lax.ppermute(edge, 'strip', way)  1.56 us
  transfers between devices with their start and end apart: 5, of which 1 were waited for; matrix products, arithmetic and copies ran while one was open for 0% of the time, Pallas kernels for 24%

profile of v12, /device:TPU:0, one launch (start us, length us, event | category | flops | bytes accessed | tf_op | source)
XLA Modules:
  0.0 26.2 jit_solution(8214729098079113148)
XLA Ops:
  0.0 0.5 %collective-permute-start = (bf16[2,4,64,192]{3,2,1,0:T(8,128)(2,1)}, bf16[2,4,64,192]{3,2,1,0:T(8,128)(2,1)S(1)}, u32[]{:S(2)}, u32[]{:S(2)}) collective-permute-start(bf16[2,4,64,192]{3,2,1,0:T(8,128)(2,1)} %own_far.1), channel_id=1, source_target_pairs={{0,1},{1,0},{2,3},{3,2},{4,5},{5,4},{6,7},{7,6},{8,9},{9,8},{10,11... | collective-permute-start | bytes 589832 | tf_op jit(solution)/shard_map/ppermute | solution.py:19
  0.5 1.5 %stage.1 = (bf16[2,4,64,192]{3,2,1,0:T(8,128)(2,1)S(1)}, bf16[3,3,192,192]{3,2,1,0:T(8,128)(2,1)S(1)}, bf16[3,3,192,192]{3,2,1,0:T(8,128)(2,1)S(1)}) custom-call(bf16[2,4,64,192]{3,2,1,0:T(8,128)(2,1)} %own_far.1, bf16[3,3,3,192,192]{4,3,2,1,0:T(8,128)(2,1)} %refs_5_.1), custom_call_target="tpu_custom_call" | custom-call | bytes 4194304 | tf_op jit(solution)/shard_map/stage/pallas_call | solution.py:445
  2.0 0.0 collective-permute-done.neighbour.refs_1_
  2.0 0.1 pack.1
  2.2 0.0 copy-start
  2.2 4.7 %collective-permute-start.2 = (bf16[800,128]{1,0:T(8,128)(2,1)S(1)}, bf16[800,128]{1,0:T(8,128)(2,1)S(1)}, u32[]{:S(2)}, u32[]{:S(2)}) collective-permute-start(bf16[800,128]{1,0:T(8,128)(2,1)S(1)} %get-tuple-element.24), channel_id=1, source_target_pairs={{0,4},{2,6},{4,8},{6,10},{8,12},{10,14},{1,5},{3,7},{5,9},{7,11},{... | collective-permute-start | bytes 614408 | tf_op jit(solution)/shard_map/ppermute | solution.py:26
  6.8 1.6 %collective-permute-start.3 = (bf16[416,128]{1,0:T(8,128)(2,1)S(1)}, bf16[416,128]{1,0:T(8,128)(2,1)S(1)}, u32[]{:S(2)}, u32[]{:S(2)}) collective-permute-start(bf16[416,128]{1,0:T(8,128)(2,1)S(1)} %get-tuple-element.23), channel_id=1, source_target_pairs={{0,2},{2,0},{1,3},{3,1},{4,6},{6,4},{5,7},{7,5},{8,10},{10,8},{9,1... | collective-permute-start | bytes 319496 | tf_op jit(solution)/shard_map/ppermute | solution.py:492
  8.4 3.4 %collective-permute-start.1 = (bf16[416,128]{1,0:T(8,128)(2,1)S(1)}, bf16[416,128]{1,0:T(8,128)(2,1)S(1)}, u32[]{:S(2)}, u32[]{:S(2)}) collective-permute-start(bf16[416,128]{1,0:T(8,128)(2,1)S(1)} %get-tuple-element.23), channel_id=1, source_target_pairs={{0,6},{2,4},{4,10},{6,8},{8,14},{10,12},{1,7},{3,5},{5,11},{7,9},{... | collective-permute-start | bytes 319496 | tf_op jit(solution)/shard_map/ppermute | solution.py:26
  11.8 0.0 collective-permute-done.3.refs_2_
  11.9 1.2 %edge_rows_own.1 = (f32[1,2,2,80,192]{4,3,2,1,0:T(8,128)S(1)}, bf16[3,3,192,192]{3,2,1,0:T(8,128)(2,1)S(1)}) custom-call(bf16[2,4,64,192]{3,2,1,0:T(8,128)(2,1)S(1)} %get-tuple-element.22.own.refs_0_, bf16[2,4,64,192]{3,2,1,0:T(8,128)(2,1)S(1)} %collective-permute-done.neighbour.refs_1_, bf16[416,128]{1,0:T(8,128)(2,1)S(1)} %collective-permute-done.3.refs_2_, ...), custom_call_target="tpu_custom_call" | custom-call | flops 127401984 | bytes 4194304 | tf_op jit(solution)/shard_map/edge_rows_own/pallas_call | solution.py:445
  13.1 0.0 collective-permute-done.2.refs_2_.refs_1_
  13.1 0.0 copy-done
  13.1 2.2 %safe_rows.1 = (bf16[2,6,80,128]{3,2,1,0:T(8,128)(2,1)S(1)}, bf16[2,7,80,128]{3,2,1,0:T(8,128)(2,1)S(1)}, bf16[1,6,80,128]{3,2,1,0:T(8,128)(2,1)S(1)}, bf16[3,3,...) custom-call(bf16[2,4,64,192]{3,2,1,0:T(8,128)(2,1)S(1)} %get-tuple-element.22, ...), custom_call_target="tpu_custom_call" | custom-call | flops 509607936 | bytes 4194304 | tf_op jit(solution)/shard_map/safe_rows/pallas_call | solution.py:445
  15.3 0.0 collective-permute-done.1.refs_0_
  15.3 2.4 %edge_rows.1 = (bf16[2,6,80,128]{3,2,1,0:T(8,128)(2,1)S(1)}, bf16[2,7,80,128]{3,2,1,0:T(8,128)(2,1)S(1)}, bf16[1,6,80,128]{3,2,1,0:T(8,128)(2,1)S(1)}, bf16[2,6,64,128]{3,2,1,0:T(8,128)(2,1)S(1)}) custom-call(bf16[416,128]{1,0:T(8,128)(2,1)S(1)} %collective-permute-done.1.refs_0_, ...), custom_call_target="tpu_custom_call", output_to_operand_aliasing={{0}: (3, {}), {1}: (4, {}), {2}: (5, {})} | custom-call | flops 509607936 | bytes 4194304 | tf_op jit(solution)/shard_map/edge_rows/pallas_call | solution.py:445
  17.7 0.0 copy-start.1
  17.7 4.3 %collective-permute-start.4 = (bf16[2,6,64,128]{3,2,1,0:T(8,128)(2,1)S(1)}, bf16[2,6,64,128]{3,2,1,0:T(8,128)(2,1)S(1)}, u32[]{:S(2)}, u32[]{:S(2)}) collective-permute-start(bf16[2,6,64,128]{3,2,1,0:T(8,128)(2,1)S(1)} %get-tuple-element.34), channel_id=1, source_target_pairs={{0,4},{2,6},{4,8},{6,10},{8,12},{10,14},{1,5},{3,7},{5,9},{7,11},{... | collective-permute-start | bytes 589832 | tf_op jit(solution)/shard_map/ppermute | solution.py:26
  22.0 1.2 %second_layer.1.own = f32[2,4,64,192]{3,2,1,0:T(8,128)S(1)} custom-call(bf16[2,6,80,128]{3,2,1,0:T(8,128)(2,1)S(1)} %get-tuple-element.35.h_lo, bf16[2,7,80,128]{3,2,1,0:T(8,128)(2,1)S(1)} %get-tuple-element.36.h_pairs, bf16[1,6,80,128]{3,2,1,0:T(8,128)(2,1)S(1)} %get-tuple-element.37.h_stacked, ...), custom_call_target="tpu_custom_call" | custom-call | flops 509607936 | bytes 4194304 | tf_op jit(solution)/shard_map/second_layer/pallas_call | solution.py:445
  23.2 2.0 %collective-permute-done.4.partial = bf16[2,6,64,128]{3,2,1,0:T(8,128)(2,1)S(1)} collective-permute-done((bf16[2,6,64,128]{3,2,1,0:T(8,128)(2,1)S(1)}, bf16[2,6,64,128]{3,2,1,0:T(8,128)(2,1)S(1)}, u32[]{:S(2)}, u32[]{:S(2)}) %collective-permute-start.4) | collective-permute-done | bytes 196640 | tf_op jit(solution)/shard_map/ppermute | solution.py:26
  25.2 0.0 copy-done.1
  25.2 1.0 %finish.1 = bf16[2,4,64,192]{3,2,1,0:T(8,128)(2,1)} custom-call(bf16[2,6,64,128]{3,2,1,0:T(8,128)(2,1)S(1)} %collective-permute-done.4.partial, f32[2,4,64,192]{3,2,1,0:T(8,128)S(1)} %second_layer.1.own, f32[1,192]{1,0:T(1,128)S(1)} %bitcast.4), custom_call_target="tpu_custom_call" | custom-call | bytes 4194304 | tf_op jit(solution)/shard_map/finish/pallas_call | solution.py:445
Async XLA Ops:
  0.0 2.0 %collective-permute-start = (bf16[2,4,64,192]{3,2,1,0:T(8,128)(2,1)}, bf16[2,4,64,192]{3,2,1,0:T(8,128)(2,1)S(1)}, u32[]{:S(2)}, u32[]{:S(2)}) collective-permute-start(bf16[2,4,64,192]{3,2,1,0:T(8,128)(2,1)} %own_far.1), channel_id=1, source_target_pairs={{0,1},{1,0},{2,3},{3,2},{4,5},{5,4},{6,7},{7,6},{8,9},{9,8},{10,11... | collective-permute-start | bytes 589832 | tf_op jit(solution)/shard_map/ppermute | solution.py:19
  2.2 11.0 %copy-start = (f32[192]{0:T(256)S(1)}, f32[192]{0:T(256)}, u32[]{:S(2)}) copy-start(f32[192]{0:T(256)} %param.7) | copy-start | bytes 2308
  2.2 10.9 %collective-permute-start.2 = (bf16[800,128]{1,0:T(8,128)(2,1)S(1)}, bf16[800,128]{1,0:T(8,128)(2,1)S(1)}, u32[]{:S(2)}, u32[]{:S(2)}) collective-permute-start(bf16[800,128]{1,0:T(8,128)(2,1)S(1)} %get-tuple-element.24), channel_id=1, source_target_pairs={{0,4},{2,6},{4,8},{6,10},{8,12},{10,14},{1,5},{3,7},{5,9},{7,11},{... | collective-permute-start | bytes 614408 | tf_op jit(solution)/shard_map/ppermute | solution.py:26
  6.8 5.0 %collective-permute-start.3 = (bf16[416,128]{1,0:T(8,128)(2,1)S(1)}, bf16[416,128]{1,0:T(8,128)(2,1)S(1)}, u32[]{:S(2)}, u32[]{:S(2)}) collective-permute-start(bf16[416,128]{1,0:T(8,128)(2,1)S(1)} %get-tuple-element.23), channel_id=1, source_target_pairs={{0,2},{2,0},{1,3},{3,1},{4,6},{6,4},{5,7},{7,5},{8,10},{10,8},{9,1... | collective-permute-start | bytes 319496 | tf_op jit(solution)/shard_map/ppermute | solution.py:492
  8.4 6.9 %collective-permute-start.1 = (bf16[416,128]{1,0:T(8,128)(2,1)S(1)}, bf16[416,128]{1,0:T(8,128)(2,1)S(1)}, u32[]{:S(2)}, u32[]{:S(2)}) collective-permute-start(bf16[416,128]{1,0:T(8,128)(2,1)S(1)} %get-tuple-element.23), channel_id=1, source_target_pairs={{0,6},{2,4},{4,10},{6,8},{8,14},{10,12},{1,7},{3,5},{5,11},{7,9},{... | collective-permute-start | bytes 319496 | tf_op jit(solution)/shard_map/ppermute | solution.py:26
  17.7 7.5 %copy-start.1 = (f32[192]{0:T(256)S(1)}, f32[192]{0:T(256)}, u32[]{:S(2)}) copy-start(f32[192]{0:T(256)} %param.9) | copy-start | bytes 2308
  17.7 7.5 %collective-permute-start.4 = (bf16[2,6,64,128]{3,2,1,0:T(8,128)(2,1)S(1)}, bf16[2,6,64,128]{3,2,1,0:T(8,128)(2,1)S(1)}, u32[]{:S(2)}, u32[]{:S(2)}) collective-permute-start(bf16[2,6,64,128]{3,2,1,0:T(8,128)(2,1)S(1)} %get-tuple-element.34), channel_id=1, source_target_pairs={{0,4},{2,6},{4,8},{6,10},{8,12},{10,14},{1,5},{3,7},{5,9},{7,11},{... | collective-permute-start | bytes 589832 | tf_op jit(solution)/shard_map/ppermute | solution.py:26

commit v13 on v12

--- a/solution.py
+++ b/solution.py
@@ -346,14 +346,11 @@
     strip = lax.axis_index("strip")
     whole, strip_block = Packed(HALO, rows, cols), Packed(frames, HALO, cols)
     near = (near_lo, near_pairs, near_stacked)
-    none = jnp.zeros(near_lo.shape[1:], near_lo.dtype)
-    near_lo[HALO] = none
-    near_stacked[HALO - 1] = none
-    clear((near_pairs,))
+    near_pairs[:, 2 * HALO] = jnp.zeros(near_pairs.shape[:1] + near_pairs.shape[2:], near_pairs.dtype)
 
     @pl.when(lax.axis_index("frame") == 0)
     def none_earlier():
-        clear((near_lo, near_stacked))
+        clear(near)
 
     gain = gains[...]
     for group, (edge, top) in enumerate(zip(edges, at_top(strips))):
@@ -386,13 +383,13 @@
 
         sums = [[edge_sums[group, t, r] for r in range(HALO)] for t in range(frames)]
         found = []
-        lefts = [columns([(t, 0), (t + 1, 1)], *near, 0, HALO) for t in range(HALO)]
-        products = convolve([(0, 0), (1, 1)], [plane, middle], jnp.concatenate(lefts, axis=0))
         for t in range(frames):
+            taps = earlier_taps(t)
+            products = convolve(taps, [plane, middle], columns(taps, *near, 0, HALO)) if taps else None
             for r in range(HALO):
                 y = sums[t][r]
-                if t < HALO:
-                    y = y + join(products, (t * HALO + r) * width, width)
+                if taps:
+                    y = y + join(products, r * width, width)
                 h = hidden_row(y, gain, cols)
                 if strips != 2 and r == 1 - top:
                     h = h * jnp.where(strip == (0 if top else strips - 1), 0.0, 1.0)
@@ -519,7 +516,7 @@
         "edge_rows",
         [*before_edges, before, edge_sums, *safe, plane, middle, gain_first, w2_first, w2_middle],
         h_shapes + [partial_shape],
-        block_scratch(HALO + 1, 2 * HALO, width),
+        block_scratch(HALO, 2 * HALO, width),
         flops=flops,
         alias={len(before_edges) + 2 + k: k for k in range(3)},
     )

time: 26.5 us -> 26.3 us (level)
  no operation moved by 1% of the time
where the time goes in v13:
time: 26.3 us; the launch traced here: 26.1 us
  starting transfers between devices  14.4 us (55%)
  Pallas kernels  9.52 us (36%)
  waiting for transfers between devices  2 us (8%)
    ppermute x3, starting transfers between devices, forward(): return lax.ppermute(x, ('frame', 'strip'), pairs)  12.4 us
    pallas_call x7, Pallas kernels, call(): pl.pallas_call(kernel, out_shape=outs, in_specs=in_specs, out_specs=(away...  9.52 us
    ppermute x3, waiting for transfers between devices, forward(): return lax.ppermute(x, ('frame', 'strip'), pairs)  2 us
    ppermute x1, starting transfers between devices, shards(): lax.ppermute(edge, 'strip', way)  1.56 us
  transfers between devices with their start and end apart: 5, of which 1 were waited for; matrix products, arithmetic and copies ran while one was open for 0% of the time, Pallas kernels for 24%

profile of v13, /device:TPU:0, one launch (start us, length us, event | category | flops | bytes accessed | tf_op | source)
XLA Modules:
  0.0 26.1 jit_solution(10900891149100113784)
XLA Ops:
  0.0 0.5 %collective-permute-start = (bf16[2,4,64,192]{3,2,1,0:T(8,128)(2,1)}, bf16[2,4,64,192]{3,2,1,0:T(8,128)(2,1)S(1)}, u32[]{:S(2)}, u32[]{:S(2)}) collective-permute-start(bf16[2,4,64,192]{3,2,1,0:T(8,128)(2,1)} %own_far.1), channel_id=1, source_target_pairs={{0,1},{1,0},{2,3},{3,2},{4,5},{5,4},{6,7},{7,6},{8,9},{9,8},{10,11... | collective-permute-start | bytes 589832 | tf_op jit(solution)/shard_map/ppermute | solution.py:19
  0.5 1.5 %stage.1 = (bf16[2,4,64,192]{3,2,1,0:T(8,128)(2,1)S(1)}, bf16[3,3,192,192]{3,2,1,0:T(8,128)(2,1)S(1)}, bf16[3,3,192,192]{3,2,1,0:T(8,128)(2,1)S(1)}) custom-call(bf16[2,4,64,192]{3,2,1,0:T(8,128)(2,1)} %own_far.1, bf16[3,3,3,192,192]{4,3,2,1,0:T(8,128)(2,1)} %refs_5_.1), custom_call_target="tpu_custom_call" | custom-call | bytes 4194304 | tf_op jit(solution)/shard_map/stage/pallas_call | solution.py:442
  2.0 0.0 collective-permute-done.neighbour.refs_1_
  2.0 0.1 pack.1
  2.2 0.0 copy-start
  2.2 4.7 %collective-permute-start.2 = (bf16[800,128]{1,0:T(8,128)(2,1)S(1)}, bf16[800,128]{1,0:T(8,128)(2,1)S(1)}, u32[]{:S(2)}, u32[]{:S(2)}) collective-permute-start(bf16[800,128]{1,0:T(8,128)(2,1)S(1)} %get-tuple-element.24), channel_id=1, source_target_pairs={{0,4},{2,6},{4,8},{6,10},{8,12},{10,14},{1,5},{3,7},{5,9},{7,11},{... | collective-permute-start | bytes 614408 | tf_op jit(solution)/shard_map/ppermute | solution.py:26
  6.8 1.6 %collective-permute-start.3 = (bf16[416,128]{1,0:T(8,128)(2,1)S(1)}, bf16[416,128]{1,0:T(8,128)(2,1)S(1)}, u32[]{:S(2)}, u32[]{:S(2)}) collective-permute-start(bf16[416,128]{1,0:T(8,128)(2,1)S(1)} %get-tuple-element.23), channel_id=1, source_target_pairs={{0,2},{2,0},{1,3},{3,1},{4,6},{6,4},{5,7},{7,5},{8,10},{10,8},{9,1... | collective-permute-start | bytes 319496 | tf_op jit(solution)/shard_map/ppermute | solution.py:489
  8.4 3.4 %collective-permute-start.1 = (bf16[416,128]{1,0:T(8,128)(2,1)S(1)}, bf16[416,128]{1,0:T(8,128)(2,1)S(1)}, u32[]{:S(2)}, u32[]{:S(2)}) collective-permute-start(bf16[416,128]{1,0:T(8,128)(2,1)S(1)} %get-tuple-element.23), channel_id=1, source_target_pairs={{0,6},{2,4},{4,10},{6,8},{8,14},{10,12},{1,7},{3,5},{5,11},{7,9},{... | collective-permute-start | bytes 319496 | tf_op jit(solution)/shard_map/ppermute | solution.py:26
  11.8 0.0 collective-permute-done.3.refs_2_
  11.9 1.2 %edge_rows_own.1 = (f32[1,2,2,80,192]{4,3,2,1,0:T(8,128)S(1)}, bf16[3,3,192,192]{3,2,1,0:T(8,128)(2,1)S(1)}) custom-call(bf16[2,4,64,192]{3,2,1,0:T(8,128)(2,1)S(1)} %get-tuple-element.22.own.refs_0_, bf16[2,4,64,192]{3,2,1,0:T(8,128)(2,1)S(1)} %collective-permute-done.neighbour.refs_1_, bf16[416,128]{1,0:T(8,128)(2,1)S(1)} %collective-permute-done.3.refs_2_, ...), custom_call_target="tpu_custom_call" | custom-call | flops 127401984 | bytes 4194304 | tf_op jit(solution)/shard_map/edge_rows_own/pallas_call | solution.py:442
  13.1 0.0 collective-permute-done.2.refs_2_.refs_1_
  13.1 0.0 copy-done
  13.1 2.2 %safe_rows.1 = (bf16[2,6,80,128]{3,2,1,0:T(8,128)(2,1)S(1)}, bf16[2,7,80,128]{3,2,1,0:T(8,128)(2,1)S(1)}, bf16[1,6,80,128]{3,2,1,0:T(8,128)(2,1)S(1)}, bf16[3,3,...) custom-call(bf16[2,4,64,192]{3,2,1,0:T(8,128)(2,1)S(1)} %get-tuple-element.22, ...), custom_call_target="tpu_custom_call" | custom-call | flops 509607936 | bytes 4194304 | tf_op jit(solution)/shard_map/safe_rows/pallas_call | solution.py:442
  15.3 0.0 collective-permute-done.1.refs_0_
  15.3 2.2 %edge_rows.1 = (bf16[2,6,80,128]{3,2,1,0:T(8,128)(2,1)S(1)}, bf16[2,7,80,128]{3,2,1,0:T(8,128)(2,1)S(1)}, bf16[1,6,80,128]{3,2,1,0:T(8,128)(2,1)S(1)}, bf16[2,6,64,128]{3,2,1,0:T(8,128)(2,1)S(1)}) custom-call(bf16[416,128]{1,0:T(8,128)(2,1)S(1)} %collective-permute-done.1.refs_0_, ...), custom_call_target="tpu_custom_call", output_to_operand_aliasing={{0}: (3, {}), {1}: (4, {}), {2}: (5, {})} | custom-call | flops 509607936 | bytes 4194304 | tf_op jit(solution)/shard_map/edge_rows/pallas_call | solution.py:442
  17.5 0.0 copy-start.1
  17.5 4.3 %collective-permute-start.4 = (bf16[2,6,64,128]{3,2,1,0:T(8,128)(2,1)S(1)}, bf16[2,6,64,128]{3,2,1,0:T(8,128)(2,1)S(1)}, u32[]{:S(2)}, u32[]{:S(2)}) collective-permute-start(bf16[2,6,64,128]{3,2,1,0:T(8,128)(2,1)S(1)} %get-tuple-element.34), channel_id=1, source_target_pairs={{0,4},{2,6},{4,8},{6,10},{8,12},{10,14},{1,5},{3,7},{5,9},{7,11},{... | collective-permute-start | bytes 589832 | tf_op jit(solution)/shard_map/ppermute | solution.py:26
  21.8 1.2 %second_layer.1.own = f32[2,4,64,192]{3,2,1,0:T(8,128)S(1)} custom-call(bf16[2,6,80,128]{3,2,1,0:T(8,128)(2,1)S(1)} %get-tuple-element.35.h_lo, bf16[2,7,80,128]{3,2,1,0:T(8,128)(2,1)S(1)} %get-tuple-element.36.h_pairs, bf16[1,6,80,128]{3,2,1,0:T(8,128)(2,1)S(1)} %get-tuple-element.37.h_stacked, ...), custom_call_target="tpu_custom_call" | custom-call | flops 509607936 | bytes 4194304 | tf_op jit(solution)/shard_map/second_layer/pallas_call | solution.py:442
  23.1 2.0 %collective-permute-done.4.partial = bf16[2,6,64,128]{3,2,1,0:T(8,128)(2,1)S(1)} collective-permute-done((bf16[2,6,64,128]{3,2,1,0:T(8,128)(2,1)S(1)}, bf16[2,6,64,128]{3,2,1,0:T(8,128)(2,1)S(1)}, u32[]{:S(2)}, u32[]{:S(2)}) %collective-permute-start.4) | collective-permute-done | bytes 196640 | tf_op jit(solution)/shard_map/ppermute | solution.py:26
  25.1 0.0 copy-done.1
  25.1 1.0 %finish.1 = bf16[2,4,64,192]{3,2,1,0:T(8,128)(2,1)} custom-call(bf16[2,6,64,128]{3,2,1,0:T(8,128)(2,1)S(1)} %collective-permute-done.4.partial, f32[2,4,64,192]{3,2,1,0:T(8,128)S(1)} %second_layer.1.own, f32[1,192]{1,0:T(1,128)S(1)} %bitcast.4), custom_call_target="tpu_custom_call" | custom-call | bytes 4194304 | tf_op jit(solution)/shard_map/finish/pallas_call | solution.py:442
Async XLA Ops:
  0.0 2.0 %collective-permute-start = (bf16[2,4,64,192]{3,2,1,0:T(8,128)(2,1)}, bf16[2,4,64,192]{3,2,1,0:T(8,128)(2,1)S(1)}, u32[]{:S(2)}, u32[]{:S(2)}) collective-permute-start(bf16[2,4,64,192]{3,2,1,0:T(8,128)(2,1)} %own_far.1), channel_id=1, source_target_pairs={{0,1},{1,0},{2,3},{3,2},{4,5},{5,4},{6,7},{7,6},{8,9},{9,8},{10,11... | collective-permute-start | bytes 589832 | tf_op jit(solution)/shard_map/ppermute | solution.py:19
  2.2 11.0 %copy-start = (f32[192]{0:T(256)S(1)}, f32[192]{0:T(256)}, u32[]{:S(2)}) copy-start(f32[192]{0:T(256)} %param.7) | copy-start | bytes 2308
  2.2 10.9 %collective-permute-start.2 = (bf16[800,128]{1,0:T(8,128)(2,1)S(1)}, bf16[800,128]{1,0:T(8,128)(2,1)S(1)}, u32[]{:S(2)}, u32[]{:S(2)}) collective-permute-start(bf16[800,128]{1,0:T(8,128)(2,1)S(1)} %get-tuple-element.24), channel_id=1, source_target_pairs={{0,4},{2,6},{4,8},{6,10},{8,12},{10,14},{1,5},{3,7},{5,9},{7,11},{... | collective-permute-start | bytes 614408 | tf_op jit(solution)/shard_map/ppermute | solution.py:26
  6.8 5.0 %collective-permute-start.3 = (bf16[416,128]{1,0:T(8,128)(2,1)S(1)}, bf16[416,128]{1,0:T(8,128)(2,1)S(1)}, u32[]{:S(2)}, u32[]{:S(2)}) collective-permute-start(bf16[416,128]{1,0:T(8,128)(2,1)S(1)} %get-tuple-element.23), channel_id=1, source_target_pairs={{0,2},{2,0},{1,3},{3,1},{4,6},{6,4},{5,7},{7,5},{8,10},{10,8},{9,1... | collective-permute-start | bytes 319496 | tf_op jit(solution)/shard_map/ppermute | solution.py:489
  8.4 6.9 %collective-permute-start.1 = (bf16[416,128]{1,0:T(8,128)(2,1)S(1)}, bf16[416,128]{1,0:T(8,128)(2,1)S(1)}, u32[]{:S(2)}, u32[]{:S(2)}) collective-permute-start(bf16[416,128]{1,0:T(8,128)(2,1)S(1)} %get-tuple-element.23), channel_id=1, source_target_pairs={{0,6},{2,4},{4,10},{6,8},{8,14},{10,12},{1,7},{3,5},{5,11},{7,9},{... | collective-permute-start | bytes 319496 | tf_op jit(solution)/shard_map/ppermute | solution.py:26
  17.5 7.5 %copy-start.1 = (f32[192]{0:T(256)S(1)}, f32[192]{0:T(256)}, u32[]{:S(2)}) copy-start(f32[192]{0:T(256)} %param.9) | copy-start | bytes 2308
  17.5 7.5 %collective-permute-start.4 = (bf16[2,6,64,128]{3,2,1,0:T(8,128)(2,1)S(1)}, bf16[2,6,64,128]{3,2,1,0:T(8,128)(2,1)S(1)}, u32[]{:S(2)}, u32[]{:S(2)}) collective-permute-start(bf16[2,6,64,128]{3,2,1,0:T(8,128)(2,1)S(1)} %get-tuple-element.34), channel_id=1, source_target_pairs={{0,4},{2,6},{4,8},{6,10},{8,12},{10,14},{1,5},{3,7},{5,9},{7,11},{... | collective-permute-start | bytes 589832 | tf_op jit(solution)/shard_map/ppermute | solution.py:26

commit v14 on v13

--- a/solution.py
+++ b/solution.py
@@ -281,21 +281,30 @@
     return [(t, 0), (t + 1, 1), (t + 2, 2)]
 
 
-def partial_sums(frames, hidden, w2, rows, cols, partial):
+def safe_sums(strips, rows):
+    if strips == 2:
+        strip = lax.axis_index("strip")
+        return (HALO * strip, rows - HALO), ((1 - strip) * (rows - HALO), HALO)
+    return (0, 0), (0, rows)
+
+
+def partial_sums(frames, hidden, w2, start, count, cols, partial):
     width, last = cols + TILE, frames - 1
+    rows = partial.shape[1] * 2 // 3
     for t, taps in enumerate(([(last - 1, 0), (last, 1)], [(last, 0)])):
-        products = convolve(taps, w2, columns(taps, *hidden, 0, rows))
-        for r in range(rows):
+        products = convolve(taps, w2, columns(taps, *hidden, start, count))
+        for r in range(count):
             y = join(products, r * width, width)[:cols].astype(jnp.bfloat16)
             rest = y.shape[-1] - LANES
-            partial[t, r] = y[:, :LANES]
+            partial[t, start + r] = y[:, :LANES]
             half = slice((r % 2) * rest, (r % 2 + 1) * rest)
-            partial[t, rows + r // 2, :, half] = y[:, LANES:]
+            partial[t, rows + start // 2 + r // 2, :, half] = y[:, LANES:]
 
 
 def safe_kernel(strips, *refs):
     *refs, lo, pairs, stacked, arrived = refs
-    own, neighbour, block, plane, middle, last, gains, w2_far, h_lo, h_pairs, h_stacked, *w2 = refs
+    own, neighbour, block, plane, middle, last, gains, w2_far, h_lo, h_pairs, h_stacked, partial, w2_first, w2_middle, w2_last = refs
+    w2 = [w2_first, w2_middle, w2_last]
     copies = [pltpu.make_async_copy(w2_far.at[a], w2[a], arrived.at[a]) for a in range(3)]
     for copy in copies:
         copy.start()
@@ -335,12 +344,15 @@
             fill(h_lo, h_pairs, h_stacked, t, start + r, slice(0, width), h[:, :LANES], h[:, LANES:])
     for copy in copies:
         copy.wait()
+    (start, count), _ = safe_sums(strips, rows)
+    if count:
+        partial_sums(frames, (h_lo, h_pairs, h_stacked), w2, start, count, cols, partial)
 
 
 def edge_kernel(strips, rows, cols, *refs):
     *refs, near_lo, near_pairs, near_stacked = refs
     *refs, h_lo, h_pairs, h_stacked, partial = refs
-    *edges, block, edge_sums, safe_lo, safe_pairs, safe_stacked, plane, middle, gains, w2_first, w2_middle = refs
+    *edges, block, edge_sums, _, _, _, _, plane, middle, gains, w2_first, w2_middle = refs
     frames, channels = edge_sums.shape[1], edge_sums.shape[-1]
     width, rest = cols + TILE, channels - LANES
     strip = lax.axis_index("strip")
@@ -397,7 +409,8 @@
         for t, row, h in found:
             fill(h_lo, h_pairs, h_stacked, t, row, slice(0, width), h[:, :LANES], h[:, LANES:])
 
-    partial_sums(frames, (h_lo, h_pairs, h_stacked), [w2_first, w2_middle], rows, cols, partial)
+    _, (start, count) = safe_sums(strips, rows)
+    partial_sums(frames, (h_lo, h_pairs, h_stacked), [w2_first, w2_middle], start, count, cols, partial)
 
 
 def second_kernel(frames, rows, cols, h_lo, h_pairs, h_stacked, *refs):
@@ -505,7 +518,7 @@
         functools.partial(safe_kernel, strips),
         "safe_rows",
         [own_in, neighbour, before, plane, middle, last, gain_first, weight_second],
-        h_shapes + [plane_shape] * 3,
+        h_shapes + [partial_shape] + [plane_shape] * 3,
         block_scratch(HALO + frames, rows + 2 * HALO, width),
         semaphores=3,
         flops=flops,
@@ -518,7 +531,7 @@
         h_shapes + [partial_shape],
         block_scratch(HALO, 2 * HALO, width),
         flops=flops,
-        alias={len(before_edges) + 2 + k: k for k in range(3)},
+        alias={len(before_edges) + 2 + k: k for k in range(4)},
     )
     sent = forward(partial)
     own = call(

time: 26.3 us -> 27.2 us (1.034)
  Pallas kernels: 9.52 us -> 10.4 us
  waiting for transfers between devices: 2 us -> 2.56 us
  starting transfers between devices: 14.4 us -> 13.9 us
    pallas_call x7, Pallas kernels: 9.52 us -> 10.4 us  [call(): pl.pallas_call(kernel, out_shape=outs, in_specs=in_specs, out_specs=(away...]
    ppermute x3, waiting for transfers between devices: 2 us -> 2.56 us  [forward(): return lax.ppermute(x, ('frame', 'strip'), pairs)]
    ppermute x3, starting transfers between devices: 12.4 us -> 11.8 us  [forward(): return lax.ppermute(x, ('frame', 'strip'), pairs)]
  transfers between devices with their start and end apart: 5 -> 5, of which waited for: 1 -> 1; matrix products, arithmetic and copies ran while one was open for 0% -> 0% of each run, Pallas kernels for 24% -> 28%
where the time goes in v14:
time: 27.2 us; the launch traced here: 27 us
  starting transfers between devices  13.9 us (51%)
  Pallas kernels  10.4 us (38%)
  waiting for transfers between devices  2.56 us (9%)
    ppermute x3, starting transfers between devices, forward(): return lax.ppermute(x, ('frame', 'strip'), pairs)  11.8 us
    pallas_call x7, Pallas kernels, call(): pl.pallas_call(kernel, out_shape=outs, in_specs=in_specs, out_specs=(away...  10.4 us
    ppermute x3, waiting for transfers between devices, forward(): return lax.ppermute(x, ('frame', 'strip'), pairs)  2.56 us
    ppermute x1, starting transfers between devices, shards(): lax.ppermute(edge, 'strip', way)  1.56 us
  transfers between devices with their start and end apart: 5, of which 1 were waited for; matrix products, arithmetic and copies ran while one was open for 0% of the time, Pallas kernels for 28%

profile of v14, /device:TPU:0, one launch (start us, length us, event | category | flops | bytes accessed | tf_op | source)
XLA Modules:
  0.0 27.0 jit_solution(16250414110639298733)
XLA Ops:
  0.0 0.5 %collective-permute-start = (bf16[2,4,64,192]{3,2,1,0:T(8,128)(2,1)}, bf16[2,4,64,192]{3,2,1,0:T(8,128)(2,1)S(1)}, u32[]{:S(2)}, u32[]{:S(2)}) collective-permute-start(bf16[2,4,64,192]{3,2,1,0:T(8,128)(2,1)} %own_far.1), channel_id=1, source_target_pairs={{0,1},{1,0},{2,3},{3,2},{4,5},{5,4},{6,7},{7,6},{8,9},{9,8},{10,11... | collective-permute-start | bytes 589832 | tf_op jit(solution)/shard_map/ppermute | solution.py:19
  0.5 1.5 %stage.1 = (bf16[2,4,64,192]{3,2,1,0:T(8,128)(2,1)S(1)}, bf16[3,3,192,192]{3,2,1,0:T(8,128)(2,1)S(1)}, bf16[3,3,192,192]{3,2,1,0:T(8,128)(2,1)S(1)}) custom-call(bf16[2,4,64,192]{3,2,1,0:T(8,128)(2,1)} %own_far.1, bf16[3,3,3,192,192]{4,3,2,1,0:T(8,128)(2,1)} %refs_5_.1), custom_call_target="tpu_custom_call" | custom-call | bytes 4194304 | tf_op jit(solution)/shard_map/stage/pallas_call | solution.py:455
  2.0 0.0 collective-permute-done.neighbour.refs_1_
  2.0 0.1 pack.1
  2.2 0.0 copy-start
  2.2 4.7 %collective-permute-start.2 = (bf16[800,128]{1,0:T(8,128)(2,1)S(1)}, bf16[800,128]{1,0:T(8,128)(2,1)S(1)}, u32[]{:S(2)}, u32[]{:S(2)}) collective-permute-start(bf16[800,128]{1,0:T(8,128)(2,1)S(1)} %get-tuple-element.25), channel_id=1, source_target_pairs={{0,4},{2,6},{4,8},{6,10},{8,12},{10,14},{1,5},{3,7},{5,9},{7,11},{... | collective-permute-start | bytes 614408 | tf_op jit(solution)/shard_map/ppermute | solution.py:26
  6.8 1.6 %collective-permute-start.3 = (bf16[416,128]{1,0:T(8,128)(2,1)S(1)}, bf16[416,128]{1,0:T(8,128)(2,1)S(1)}, u32[]{:S(2)}, u32[]{:S(2)}) collective-permute-start(bf16[416,128]{1,0:T(8,128)(2,1)S(1)} %get-tuple-element.24), channel_id=1, source_target_pairs={{0,2},{2,0},{1,3},{3,1},{4,6},{6,4},{5,7},{7,5},{8,10},{10,8},{9,1... | collective-permute-start | bytes 319496 | tf_op jit(solution)/shard_map/ppermute | solution.py:502
  8.4 3.4 %collective-permute-start.1 = (bf16[416,128]{1,0:T(8,128)(2,1)S(1)}, bf16[416,128]{1,0:T(8,128)(2,1)S(1)}, u32[]{:S(2)}, u32[]{:S(2)}) collective-permute-start(bf16[416,128]{1,0:T(8,128)(2,1)S(1)} %get-tuple-element.24), channel_id=1, source_target_pairs={{0,6},{2,4},{4,10},{6,8},{8,14},{10,12},{1,7},{3,5},{5,11},{7,9},{... | collective-permute-start | bytes 319496 | tf_op jit(solution)/shard_map/ppermute | solution.py:26
  11.8 0.0 collective-permute-done.3.refs_2_
  11.9 1.2 %edge_rows_own.1 = (f32[1,2,2,80,192]{4,3,2,1,0:T(8,128)S(1)}, bf16[3,3,192,192]{3,2,1,0:T(8,128)(2,1)S(1)}) custom-call(bf16[2,4,64,192]{3,2,1,0:T(8,128)(2,1)S(1)} %get-tuple-element.23.own.refs_0_, bf16[2,4,64,192]{3,2,1,0:T(8,128)(2,1)S(1)} %collective-permute-done.neighbour.refs_1_, bf16[416,128]{1,0:T(8,128)(2,1)S(1)} %collective-permute-done.3.refs_2_, ...), custom_call_target="tpu_custom_call" | custom-call | flops 127401984 | bytes 4194304 | tf_op jit(solution)/shard_map/edge_rows_own/pallas_call | solution.py:455
  13.1 0.0 collective-permute-done.2.refs_2_.refs_1_
  13.1 0.0 copy-done
  13.1 3.6 %safe_rows.1 = (bf16[2,6,80,128]{3,2,1,0:T(8,128)(2,1)S(1)}, bf16[2,7,80,128]{3,2,1,0:T(8,128)(2,1)S(1)}, bf16[1,6,80,128]{3,2,1,0:T(8,128)(2,1)S(1)}, bf16[2,6,...) custom-call(bf16[2,4,64,192]{3,2,1,0:T(8,128)(2,1)S(1)} %get-tuple-e, ...), custom_call_target="tpu_custom_call" | custom-call | flops 509607936 | bytes 4194304 | tf_op jit(solution)/shard_map/safe_rows/pallas_call | solution.py:455
  16.8 0.0 collective-permute-done.1.refs_0_
  16.8 1.7 %edge_rows.1 = (bf16[2,6,80,128]{3,2,1,0:T(8,128)(2,1)S(1)}, bf16[2,7,80,128]{3,2,1,0:T(8,128)(2,1)S(1)}, bf16[1,6,80,128]{3,2,1,0:T(8,128)(2,1)S(1)}, bf16[2,6,64,128]{3,2,1,0:T(8,128)(2,1)S(1)}) custom-call(bf16[416,128]{1,0:T(8,128)(2,1)S(1)} %collective-permute-done.1.refs_0_, ...), custom_call_target="tpu_custom_call", output_to_operand_aliasing={{0}: (3, {}), {1}: (4, {}), {2}: (5, {}), {3}: (6, {})} | custom-call | flops 509607936 | bytes 4194304 | tf_op jit(solution)/shard_map/edge_rows/pallas_call | solution.py:455
  18.4 0.0 copy-start.1
  18.5 3.7 %collective-permute-start.4 = (bf16[2,6,64,128]{3,2,1,0:T(8,128)(2,1)S(1)}, bf16[2,6,64,128]{3,2,1,0:T(8,128)(2,1)S(1)}, u32[]{:S(2)}, u32[]{:S(2)}) collective-permute-start(bf16[2,6,64,128]{3,2,1,0:T(8,128)(2,1)S(1)} %get-tuple-element.36), channel_id=1, source_target_pairs={{0,4},{2,6},{4,8},{6,10},{8,12},{10,14},{1,5},{3,7},{5,9},{7,11},{... | collective-permute-start | bytes 589832 | tf_op jit(solution)/shard_map/ppermute | solution.py:26
  22.2 1.2 %second_layer.1.own = f32[2,4,64,192]{3,2,1,0:T(8,128)S(1)} custom-call(bf16[2,6,80,128]{3,2,1,0:T(8,128)(2,1)S(1)} %get-tuple-element.37.h_lo, bf16[2,7,80,128]{3,2,1,0:T(8,128)(2,1)S(1)} %get-tuple-element.38.h_pairs, bf16[1,6,80,128]{3,2,1,0:T(8,128)(2,1)S(1)} %get-tuple-element.39.h_stacked, ...), custom_call_target="tpu_custom_call" | custom-call | flops 509607936 | bytes 4194304 | tf_op jit(solution)/shard_map/second_layer/pallas_call | solution.py:455
  23.4 2.6 %collective-permute-done.4.partial = bf16[2,6,64,128]{3,2,1,0:T(8,128)(2,1)S(1)} collective-permute-done((bf16[2,6,64,128]{3,2,1,0:T(8,128)(2,1)S(1)}, bf16[2,6,64,128]{3,2,1,0:T(8,128)(2,1)S(1)}, u32[]{:S(2)}, u32[]{:S(2)}) %collective-permute-start.4) | collective-permute-done | bytes 196640 | tf_op jit(solution)/shard_map/ppermute | solution.py:26
  26.0 0.0 copy-done.1
  26.0 1.0 %finish.1 = bf16[2,4,64,192]{3,2,1,0:T(8,128)(2,1)} custom-call(bf16[2,6,64,128]{3,2,1,0:T(8,128)(2,1)S(1)} %collective-permute-done.4.partial, f32[2,4,64,192]{3,2,1,0:T(8,128)S(1)} %second_layer.1.own, f32[1,192]{1,0:T(1,128)S(1)} %bitcast.4), custom_call_target="tpu_custom_call" | custom-call | bytes 4194304 | tf_op jit(solution)/shard_map/finish/pallas_call | solution.py:455
Async XLA Ops:
  0.0 2.0 %collective-permute-start = (bf16[2,4,64,192]{3,2,1,0:T(8,128)(2,1)}, bf16[2,4,64,192]{3,2,1,0:T(8,128)(2,1)S(1)}, u32[]{:S(2)}, u32[]{:S(2)}) collective-permute-start(bf16[2,4,64,192]{3,2,1,0:T(8,128)(2,1)} %own_far.1), channel_id=1, source_target_pairs={{0,1},{1,0},{2,3},{3,2},{4,5},{5,4},{6,7},{7,6},{8,9},{9,8},{10,11... | collective-permute-start | bytes 589832 | tf_op jit(solution)/shard_map/ppermute | solution.py:19
  2.2 11.0 %copy-start = (f32[192]{0:T(256)S(1)}, f32[192]{0:T(256)}, u32[]{:S(2)}) copy-start(f32[192]{0:T(256)} %param.7) | copy-start | bytes 2308
  2.2 10.9 %collective-permute-start.2 = (bf16[800,128]{1,0:T(8,128)(2,1)S(1)}, bf16[800,128]{1,0:T(8,128)(2,1)S(1)}, u32[]{:S(2)}, u32[]{:S(2)}) collective-permute-start(bf16[800,128]{1,0:T(8,128)(2,1)S(1)} %get-tuple-element.25), channel_id=1, source_target_pairs={{0,4},{2,6},{4,8},{6,10},{8,12},{10,14},{1,5},{3,7},{5,9},{7,11},{... | collective-permute-start | bytes 614408 | tf_op jit(solution)/shard_map/ppermute | solution.py:26
  6.8 5.0 %collective-permute-start.3 = (bf16[416,128]{1,0:T(8,128)(2,1)S(1)}, bf16[416,128]{1,0:T(8,128)(2,1)S(1)}, u32[]{:S(2)}, u32[]{:S(2)}) collective-permute-start(bf16[416,128]{1,0:T(8,128)(2,1)S(1)} %get-tuple-element.24), channel_id=1, source_target_pairs={{0,2},{2,0},{1,3},{3,1},{4,6},{6,4},{5,7},{7,5},{8,10},{10,8},{9,1... | collective-permute-start | bytes 319496 | tf_op jit(solution)/shard_map/ppermute | solution.py:502
  8.4 8.4 %collective-permute-start.1 = (bf16[416,128]{1,0:T(8,128)(2,1)S(1)}, bf16[416,128]{1,0:T(8,128)(2,1)S(1)}, u32[]{:S(2)}, u32[]{:S(2)}) collective-permute-start(bf16[416,128]{1,0:T(8,128)(2,1)S(1)} %get-tuple-element.24), channel_id=1, source_target_pairs={{0,6},{2,4},{4,10},{6,8},{8,14},{10,12},{1,7},{3,5},{5,11},{7,9},{... | collective-permute-start | bytes 319496 | tf_op jit(solution)/shard_map/ppermute | solution.py:26
  18.4 7.5 %copy-start.1 = (f32[192]{0:T(256)S(1)}, f32[192]{0:T(256)}, u32[]{:S(2)}) copy-start(f32[192]{0:T(256)} %param.9) | copy-start | bytes 2308
  18.5 7.5 %collective-permute-start.4 = (bf16[2,6,64,128]{3,2,1,0:T(8,128)(2,1)S(1)}, bf16[2,6,64,128]{3,2,1,0:T(8,128)(2,1)S(1)}, u32[]{:S(2)}, u32[]{:S(2)}) collective-permute-start(bf16[2,6,64,128]{3,2,1,0:T(8,128)(2,1)S(1)} %get-tuple-element.36), channel_id=1, source_target_pairs={{0,4},{2,6},{4,8},{6,10},{8,12},{10,14},{1,5},{3,7},{5,9},{7,11},{... | collective-permute-start | bytes 589832 | tf_op jit(solution)/shard_map/ppermute | solution.py:26

commit v15 on v13

--- a/solution.py
+++ b/solution.py
@@ -36,7 +36,8 @@
         self.high = frames * rows * cols
         self.beside = self.high + frames * (rows // 2) * cols
         self.tiles = -(-frames * rows * HALO // TILE)
-        self.shape = (self.beside + 2 * self.tiles * TILE, LANES)
+        self.shared = frames * rows * HALO <= TILE // 2
+        self.shape = (self.beside + (1 if self.shared else 2) * self.tiles * TILE, LANES)
 
     def low_at(self, f, r):
         return slice((f * self.rows + r) * self.cols, (f * self.rows + r + 1) * self.cols)
@@ -68,6 +69,12 @@
                 moved = pltpu.roll(tile_of(f, r).astype(jnp.float32), lax.rem(place + HALO * slab, TILE), 0)
                 moved = jnp.where((at >= place) & (at < place + HALO), moved, 0.0)
                 sums[tile] = moved if sums[tile] is None else sums[tile] + moved
+        if self.shared:
+            low, high = sums[0][:, :LANES], sums[0][:, LANES:]
+            high = jnp.concatenate([high, jnp.zeros((TILE, LANES - rest), jnp.float32)], axis=-1)
+            both = jnp.where(at < TILE // 2, low, pltpu.roll(high, TILE // 2, 0))
+            out[self.beside_at(0, 0), :] = both.astype(jnp.bfloat16)
+            return
         for tile, cells_beside in enumerate(sums):
             cells_beside = cells_beside.astype(jnp.bfloat16)
             out[self.beside_at(tile, 0), :] = cells_beside[:, :LANES]
@@ -78,16 +85,17 @@
         return ref[self.low_at(f, r), :], ref[self.high_at(f, r), half]
 
     def read_beside(self, ref, f, r, rest):
-        return beside_from(ref, self.beside, (f * self.rows + r) * HALO, rest)
-
-
-def beside_from(ref, start, cell, rest):
+        return beside_from(ref, self.beside, (f * self.rows + r) * HALO, rest, self.shared)
+
+
+def beside_from(ref, start, cell, rest, shared=False):
     slab = lax.axis_index("slab")
     parts = []
     for high, lanes in ((0, LANES), (1, rest)):
-        at = start + (2 * (cell // TILE) + high) * TILE
+        at = start if shared else start + (2 * (cell // TILE) + high) * TILE
+        below = TILE // 2 if shared and high else 0
         cells = ref[pl.ds(pl.multiple_of(at, TILE), TILE), :].astype(jnp.float32)
-        cells = pltpu.roll(cells, lax.rem(2 * TILE - cell % TILE - HALO * slab, TILE), 0)
+        cells = pltpu.roll(cells, lax.rem(2 * TILE - cell % TILE - below - HALO * slab, TILE), 0)
         parts.append(only_beside(cells).astype(jnp.bfloat16)[:, :lanes])
     return parts
 

time: 26.3 us -> 26.5 us (level)
  no operation moved by 1% of the time
where the time goes in v15:
time: 26.5 us; the launch traced here: 26.3 us
  starting transfers between devices  14.2 us (54%)
  Pallas kernels  9.7 us (37%)
  waiting for transfers between devices  2.26 us (9%)
    ppermute x3, starting transfers between devices, forward(): return lax.ppermute(x, ('frame', 'strip'), pairs)  12.2 us
    pallas_call x7, Pallas kernels, call(): pl.pallas_call(kernel, out_shape=outs, in_specs=in_specs, out_specs=(away...  9.7 us
    ppermute x3, waiting for transfers between devices, forward(): return lax.ppermute(x, ('frame', 'strip'), pairs)  2.26 us
    ppermute x1, starting transfers between devices, shards(): lax.ppermute(edge, 'strip', way)  1.56 us
  transfers between devices with their start and end apart: 5, of which 1 were waited for; matrix products, arithmetic and copies ran while one was open for 0% of the time, Pallas kernels for 24%

profile of v15, /device:TPU:0, one launch (start us, length us, event | category | flops | bytes accessed | tf_op | source)
XLA Modules:
  0.0 26.3 jit_solution(15691870574441176746)
XLA Ops:
  0.0 0.5 %collective-permute-start = (bf16[2,4,64,192]{3,2,1,0:T(8,128)(2,1)}, bf16[2,4,64,192]{3,2,1,0:T(8,128)(2,1)S(1)}, u32[]{:S(2)}, u32[]{:S(2)}) collective-permute-start(bf16[2,4,64,192]{3,2,1,0:T(8,128)(2,1)} %own_far.1), channel_id=1, source_target_pairs={{0,1},{1,0},{2,3},{3,2},{4,5},{5,4},{6,7},{7,6},{8,9},{9,8},{10,11... | collective-permute-start | bytes 589832 | tf_op jit(solution)/shard_map/ppermute | solution.py:19
  0.5 1.5 %stage.1 = (bf16[2,4,64,192]{3,2,1,0:T(8,128)(2,1)S(1)}, bf16[3,3,192,192]{3,2,1,0:T(8,128)(2,1)S(1)}, bf16[3,3,192,192]{3,2,1,0:T(8,128)(2,1)S(1)}) custom-call(bf16[2,4,64,192]{3,2,1,0:T(8,128)(2,1)} %own_far.1, bf16[3,3,3,192,192]{4,3,2,1,0:T(8,128)(2,1)} %refs_5_.1), custom_call_target="tpu_custom_call" | custom-call | bytes 4194304 | tf_op jit(solution)/shard_map/stage/pallas_call | solution.py:450
  2.0 0.0 collective-permute-done.neighbour.refs_1_
  2.0 0.1 pack.1
  2.2 0.0 copy-start
  2.2 4.7 %collective-permute-start.2 = (bf16[800,128]{1,0:T(8,128)(2,1)S(1)}, bf16[800,128]{1,0:T(8,128)(2,1)S(1)}, u32[]{:S(2)}, u32[]{:S(2)}) collective-permute-start(bf16[800,128]{1,0:T(8,128)(2,1)S(1)} %get-tuple-element.24), channel_id=1, source_target_pairs={{0,4},{2,6},{4,8},{6,10},{8,12},{10,14},{1,5},{3,7},{5,9},{7,11},{... | collective-permute-start | bytes 614408 | tf_op jit(solution)/shard_map/ppermute | solution.py:26
  6.8 1.6 %collective-permute-start.3 = (bf16[400,128]{1,0:T(8,128)(2,1)S(1)}, bf16[400,128]{1,0:T(8,128)(2,1)S(1)}, u32[]{:S(2)}, u32[]{:S(2)}) collective-permute-start(bf16[400,128]{1,0:T(8,128)(2,1)S(1)} %get-tuple-element.23), channel_id=1, source_target_pairs={{0,2},{2,0},{1,3},{3,1},{4,6},{6,4},{5,7},{7,5},{8,10},{10,8},{9,1... | collective-permute-start | bytes 307208 | tf_op jit(solution)/shard_map/ppermute | solution.py:497
  8.4 3.4 %collective-permute-start.1 = (bf16[400,128]{1,0:T(8,128)(2,1)S(1)}, bf16[400,128]{1,0:T(8,128)(2,1)S(1)}, u32[]{:S(2)}, u32[]{:S(2)}) collective-permute-start(bf16[400,128]{1,0:T(8,128)(2,1)S(1)} %get-tuple-element.23), channel_id=1, source_target_pairs={{0,6},{2,4},{4,10},{6,8},{8,14},{10,12},{1,7},{3,5},{5,11},{7,9},{... | collective-permute-start | bytes 307208 | tf_op jit(solution)/shard_map/ppermute | solution.py:26
  11.8 0.0 collective-permute-done.3.refs_2_
  11.9 1.4 %edge_rows_own.1 = (f32[1,2,2,80,192]{4,3,2,1,0:T(8,128)S(1)}, bf16[3,3,192,192]{3,2,1,0:T(8,128)(2,1)S(1)}) custom-call(bf16[2,4,64,192]{3,2,1,0:T(8,128)(2,1)S(1)} %get-tuple-element.22.own.refs_0_, bf16[2,4,64,192]{3,2,1,0:T(8,128)(2,1)S(1)} %collective-permute-done.neighbour.refs_1_, bf16[400,128]{1,0:T(8,128)(2,1)S(1)} %collective-permute-done.3.refs_2_, ...), custom_call_target="tpu_custom_call" | custom-call | flops 127401984 | bytes 4194304 | tf_op jit(solution)/shard_map/edge_rows_own/pallas_call | solution.py:450
  13.3 0.0 collective-permute-done.2.refs_2_.refs_1_
  13.3 0.0 copy-done
  13.3 2.2 %safe_rows.1 = (bf16[2,6,80,128]{3,2,1,0:T(8,128)(2,1)S(1)}, bf16[2,7,80,128]{3,2,1,0:T(8,128)(2,1)S(1)}, bf16[1,6,80,128]{3,2,1,0:T(8,128)(2,1)S(1)}, bf16[3,3,...) custom-call(bf16[2,4,64,192]{3,2,1,0:T(8,128)(2,1)S(1)} %get-tuple-element.22, ...), custom_call_target="tpu_custom_call" | custom-call | flops 509607936 | bytes 4194304 | tf_op jit(solution)/shard_map/safe_rows/pallas_call | solution.py:450
  15.5 0.0 collective-permute-done.1.refs_0_
  15.5 2.2 %edge_rows.1 = (bf16[2,6,80,128]{3,2,1,0:T(8,128)(2,1)S(1)}, bf16[2,7,80,128]{3,2,1,0:T(8,128)(2,1)S(1)}, bf16[1,6,80,128]{3,2,1,0:T(8,128)(2,1)S(1)}, bf16[2,6,64,128]{3,2,1,0:T(8,128)(2,1)S(1)}) custom-call(bf16[400,128]{1,0:T(8,128)(2,1)S(1)} %collective-permute-done.1.refs_0_, ...), custom_call_target="tpu_custom_call", output_to_operand_aliasing={{0}: (3, {}), {1}: (4, {}), {2}: (5, {})} | custom-call | flops 509607936 | bytes 4194304 | tf_op jit(solution)/shard_map/edge_rows/pallas_call | solution.py:450
  17.7 0.0 copy-start.1
  17.7 4.1 %collective-permute-start.4 = (bf16[2,6,64,128]{3,2,1,0:T(8,128)(2,1)S(1)}, bf16[2,6,64,128]{3,2,1,0:T(8,128)(2,1)S(1)}, u32[]{:S(2)}, u32[]{:S(2)}) collective-permute-start(bf16[2,6,64,128]{3,2,1,0:T(8,128)(2,1)S(1)} %get-tuple-element.34), channel_id=1, source_target_pairs={{0,4},{2,6},{4,8},{6,10},{8,12},{10,14},{1,5},{3,7},{5,9},{7,11},{... | collective-permute-start | bytes 589832 | tf_op jit(solution)/shard_map/ppermute | solution.py:26
  21.8 1.2 %second_layer.1.own = f32[2,4,64,192]{3,2,1,0:T(8,128)S(1)} custom-call(bf16[2,6,80,128]{3,2,1,0:T(8,128)(2,1)S(1)} %get-tuple-element.35.h_lo, bf16[2,7,80,128]{3,2,1,0:T(8,128)(2,1)S(1)} %get-tuple-element.36.h_pairs, bf16[1,6,80,128]{3,2,1,0:T(8,128)(2,1)S(1)} %get-tuple-element.37.h_stacked, ...), custom_call_target="tpu_custom_call" | custom-call | flops 509607936 | bytes 4194304 | tf_op jit(solution)/shard_map/second_layer/pallas_call | solution.py:450
  23.0 2.3 %collective-permute-done.4.partial = bf16[2,6,64,128]{3,2,1,0:T(8,128)(2,1)S(1)} collective-permute-done((bf16[2,6,64,128]{3,2,1,0:T(8,128)(2,1)S(1)}, bf16[2,6,64,128]{3,2,1,0:T(8,128)(2,1)S(1)}, u32[]{:S(2)}, u32[]{:S(2)}) %collective-permute-start.4) | collective-permute-done | bytes 196640 | tf_op jit(solution)/shard_map/ppermute | solution.py:26
  25.3 0.0 copy-done.1
  25.3 1.0 %finish.1 = bf16[2,4,64,192]{3,2,1,0:T(8,128)(2,1)} custom-call(bf16[2,6,64,128]{3,2,1,0:T(8,128)(2,1)S(1)} %collective-permute-done.4.partial, f32[2,4,64,192]{3,2,1,0:T(8,128)S(1)} %second_layer.1.own, f32[1,192]{1,0:T(1,128)S(1)} %bitcast.4), custom_call_target="tpu_custom_call" | custom-call | bytes 4194304 | tf_op jit(solution)/shard_map/finish/pallas_call | solution.py:450
Async XLA Ops:
  0.0 2.0 %collective-permute-start = (bf16[2,4,64,192]{3,2,1,0:T(8,128)(2,1)}, bf16[2,4,64,192]{3,2,1,0:T(8,128)(2,1)S(1)}, u32[]{:S(2)}, u32[]{:S(2)}) collective-permute-start(bf16[2,4,64,192]{3,2,1,0:T(8,128)(2,1)} %own_far.1), channel_id=1, source_target_pairs={{0,1},{1,0},{2,3},{3,2},{4,5},{5,4},{6,7},{7,6},{8,9},{9,8},{10,11... | collective-permute-start | bytes 589832 | tf_op jit(solution)/shard_map/ppermute | solution.py:19
  2.2 11.2 %copy-start = (f32[192]{0:T(256)S(1)}, f32[192]{0:T(256)}, u32[]{:S(2)}) copy-start(f32[192]{0:T(256)} %param.7) | copy-start | bytes 2308
  2.2 11.1 %collective-permute-start.2 = (bf16[800,128]{1,0:T(8,128)(2,1)S(1)}, bf16[800,128]{1,0:T(8,128)(2,1)S(1)}, u32[]{:S(2)}, u32[]{:S(2)}) collective-permute-start(bf16[800,128]{1,0:T(8,128)(2,1)S(1)} %get-tuple-element.24), channel_id=1, source_target_pairs={{0,4},{2,6},{4,8},{6,10},{8,12},{10,14},{1,5},{3,7},{5,9},{7,11},{... | collective-permute-start | bytes 614408 | tf_op jit(solution)/shard_map/ppermute | solution.py:26
  6.8 5.0 %collective-permute-start.3 = (bf16[400,128]{1,0:T(8,128)(2,1)S(1)}, bf16[400,128]{1,0:T(8,128)(2,1)S(1)}, u32[]{:S(2)}, u32[]{:S(2)}) collective-permute-start(bf16[400,128]{1,0:T(8,128)(2,1)S(1)} %get-tuple-element.23), channel_id=1, source_target_pairs={{0,2},{2,0},{1,3},{3,1},{4,6},{6,4},{5,7},{7,5},{8,10},{10,8},{9,1... | collective-permute-start | bytes 307208 | tf_op jit(solution)/shard_map/ppermute | solution.py:497
  8.4 7.1 %collective-permute-start.1 = (bf16[400,128]{1,0:T(8,128)(2,1)S(1)}, bf16[400,128]{1,0:T(8,128)(2,1)S(1)}, u32[]{:S(2)}, u32[]{:S(2)}) collective-permute-start(bf16[400,128]{1,0:T(8,128)(2,1)S(1)} %get-tuple-element.23), channel_id=1, source_target_pairs={{0,6},{2,4},{4,10},{6,8},{8,14},{10,12},{1,7},{3,5},{5,11},{7,9},{... | collective-permute-start | bytes 307208 | tf_op jit(solution)/shard_map/ppermute | solution.py:26
  17.7 7.5 %copy-start.1 = (f32[192]{0:T(256)S(1)}, f32[192]{0:T(256)}, u32[]{:S(2)}) copy-start(f32[192]{0:T(256)} %param.9) | copy-start | bytes 2308
  17.7 7.5 %collective-permute-start.4 = (bf16[2,6,64,128]{3,2,1,0:T(8,128)(2,1)S(1)}, bf16[2,6,64,128]{3,2,1,0:T(8,128)(2,1)S(1)}, u32[]{:S(2)}, u32[]{:S(2)}) collective-permute-start(bf16[2,6,64,128]{3,2,1,0:T(8,128)(2,1)S(1)} %get-tuple-element.34), channel_id=1, source_target_pairs={{0,4},{2,6},{4,8},{6,10},{8,12},{10,14},{1,5},{3,7},{5,9},{7,11},{... | collective-permute-start | bytes 589832 | tf_op jit(solution)/shard_map/ppermute | solution.py:26

commit v16 on v15

--- a/solution.py
+++ b/solution.py
@@ -159,7 +159,8 @@
 def activate(y, gains):
     mean_square = jnp.sum(y * y, axis=-1, keepdims=True) * (1.0 / y.shape[-1])
     v = y * lax.rsqrt(mean_square + EPS) * gains
-    return v / (1.0 + jnp.exp(-v))
+    half = 0.5 * v
+    return half + half * jnp.tanh(half)
 
 
 def clear(buffers):

time: 26.5 us -> 26.5 us (level)
  no operation moved by 1% of the time
where the time goes in v16:
time: 26.5 us; the launch traced here: 26.2 us
  starting transfers between devices  14.1 us (53%)
  Pallas kernels  9.66 us (36%)
  waiting for transfers between devices  2.31 us (9%)
    ppermute x3, starting transfers between devices, forward(): return lax.ppermute(x, ('frame', 'strip'), pairs)  12.1 us
    pallas_call x7, Pallas kernels, call(): pl.pallas_call(kernel, out_shape=outs, in_specs=in_specs, out_specs=(away...  9.66 us
    ppermute x3, waiting for transfers between devices, forward(): return lax.ppermute(x, ('frame', 'strip'), pairs)  2.3 us
    ppermute x1, starting transfers between devices, shards(): lax.ppermute(edge, 'strip', way)  1.56 us
  transfers between devices with their start and end apart: 5, of which 1 were waited for; matrix products, arithmetic and copies ran while one was open for 0% of the time, Pallas kernels for 24%

profile of v16, /device:TPU:0, one launch (start us, length us, event | category | flops | bytes accessed | tf_op | source)
XLA Modules:
  0.0 26.2 jit_solution(12721063694757779238)
XLA Ops:
  0.0 0.5 %collective-permute-start = (bf16[2,4,64,192]{3,2,1,0:T(8,128)(2,1)}, bf16[2,4,64,192]{3,2,1,0:T(8,128)(2,1)S(1)}, u32[]{:S(2)}, u32[]{:S(2)}) collective-permute-start(bf16[2,4,64,192]{3,2,1,0:T(8,128)(2,1)} %own_far.1), channel_id=1, source_target_pairs={{0,1},{1,0},{2,3},{3,2},{4,5},{5,4},{6,7},{7,6},{8,9},{9,8},{10,11... | collective-permute-start | bytes 589832 | tf_op jit(solution)/shard_map/ppermute | solution.py:19
  0.5 1.5 %stage.1 = (bf16[2,4,64,192]{3,2,1,0:T(8,128)(2,1)S(1)}, bf16[3,3,192,192]{3,2,1,0:T(8,128)(2,1)S(1)}, bf16[3,3,192,192]{3,2,1,0:T(8,128)(2,1)S(1)}) custom-call(bf16[2,4,64,192]{3,2,1,0:T(8,128)(2,1)} %own_far.1, bf16[3,3,3,192,192]{4,3,2,1,0:T(8,128)(2,1)} %refs_5_.1), custom_call_target="tpu_custom_call" | custom-call | bytes 4194304 | tf_op jit(solution)/shard_map/stage/pallas_call | solution.py:451
  2.0 0.0 collective-permute-done.neighbour.refs_1_
  2.0 0.1 pack.1
  2.2 0.0 copy-start
  2.2 4.7 %collective-permute-start.2 = (bf16[800,128]{1,0:T(8,128)(2,1)S(1)}, bf16[800,128]{1,0:T(8,128)(2,1)S(1)}, u32[]{:S(2)}, u32[]{:S(2)}) collective-permute-start(bf16[800,128]{1,0:T(8,128)(2,1)S(1)} %get-tuple-element.24), channel_id=1, source_target_pairs={{0,4},{2,6},{4,8},{6,10},{8,12},{10,14},{1,5},{3,7},{5,9},{7,11},{... | collective-permute-start | bytes 614408 | tf_op jit(solution)/shard_map/ppermute | solution.py:26
  6.8 1.6 %collective-permute-start.3 = (bf16[400,128]{1,0:T(8,128)(2,1)S(1)}, bf16[400,128]{1,0:T(8,128)(2,1)S(1)}, u32[]{:S(2)}, u32[]{:S(2)}) collective-permute-start(bf16[400,128]{1,0:T(8,128)(2,1)S(1)} %get-tuple-element.23), channel_id=1, source_target_pairs={{0,2},{2,0},{1,3},{3,1},{4,6},{6,4},{5,7},{7,5},{8,10},{10,8},{9,1... | collective-permute-start | bytes 307208 | tf_op jit(solution)/shard_map/ppermute | solution.py:498
  8.4 3.4 %collective-permute-start.1 = (bf16[400,128]{1,0:T(8,128)(2,1)S(1)}, bf16[400,128]{1,0:T(8,128)(2,1)S(1)}, u32[]{:S(2)}, u32[]{:S(2)}) collective-permute-start(bf16[400,128]{1,0:T(8,128)(2,1)S(1)} %get-tuple-element.23), channel_id=1, source_target_pairs={{0,6},{2,4},{4,10},{6,8},{8,14},{10,12},{1,7},{3,5},{5,11},{7,9},{... | collective-permute-start | bytes 307208 | tf_op jit(solution)/shard_map/ppermute | solution.py:26
  11.8 0.0 collective-permute-done.3.refs_2_
  11.9 1.4 %edge_rows_own.1 = (f32[1,2,2,80,192]{4,3,2,1,0:T(8,128)S(1)}, bf16[3,3,192,192]{3,2,1,0:T(8,128)(2,1)S(1)}) custom-call(bf16[2,4,64,192]{3,2,1,0:T(8,128)(2,1)S(1)} %get-tuple-element.22.own.refs_0_, bf16[2,4,64,192]{3,2,1,0:T(8,128)(2,1)S(1)} %collective-permute-done.neighbour.refs_1_, bf16[400,128]{1,0:T(8,128)(2,1)S(1)} %collective-permute-done.3.refs_2_, ...), custom_call_target="tpu_custom_call" | custom-call | flops 127401984 | bytes 4194304 | tf_op jit(solution)/shard_map/edge_rows_own/pallas_call | solution.py:451
  13.3 0.0 collective-permute-done.2.refs_2_.refs_1_
  13.3 0.0 copy-done
  13.3 2.2 %safe_rows.1 = (bf16[2,6,80,128]{3,2,1,0:T(8,128)(2,1)S(1)}, bf16[2,7,80,128]{3,2,1,0:T(8,128)(2,1)S(1)}, bf16[1,6,80,128]{3,2,1,0:T(8,128)(2,1)S(1)}, bf16[3,3,...) custom-call(bf16[2,4,64,192]{3,2,1,0:T(8,128)(2,1)S(1)} %get-tuple-element.22, ...), custom_call_target="tpu_custom_call" | custom-call | flops 509607936 | bytes 4194304 | tf_op jit(solution)/shard_map/safe_rows/pallas_call | solution.py:451
  15.5 0.0 collective-permute-done.1.refs_0_
  15.5 2.2 %edge_rows.1 = (bf16[2,6,80,128]{3,2,1,0:T(8,128)(2,1)S(1)}, bf16[2,7,80,128]{3,2,1,0:T(8,128)(2,1)S(1)}, bf16[1,6,80,128]{3,2,1,0:T(8,128)(2,1)S(1)}, bf16[2,6,64,128]{3,2,1,0:T(8,128)(2,1)S(1)}) custom-call(bf16[400,128]{1,0:T(8,128)(2,1)S(1)} %collective-permute-done.1.refs_0_, ...), custom_call_target="tpu_custom_call", output_to_operand_aliasing={{0}: (3, {}), {1}: (4, {}), {2}: (5, {})} | custom-call | flops 509607936 | bytes 4194304 | tf_op jit(solution)/shard_map/edge_rows/pallas_call | solution.py:451
  17.7 0.0 copy-start.1
  17.7 4.0 %collective-permute-start.4 = (bf16[2,6,64,128]{3,2,1,0:T(8,128)(2,1)S(1)}, bf16[2,6,64,128]{3,2,1,0:T(8,128)(2,1)S(1)}, u32[]{:S(2)}, u32[]{:S(2)}) collective-permute-start(bf16[2,6,64,128]{3,2,1,0:T(8,128)(2,1)S(1)} %get-tuple-element.34), channel_id=1, source_target_pairs={{0,4},{2,6},{4,8},{6,10},{8,12},{10,14},{1,5},{3,7},{5,9},{7,11},{... | collective-permute-start | bytes 589832 | tf_op jit(solution)/shard_map/ppermute | solution.py:26
  21.8 1.2 %second_layer.1.own = f32[2,4,64,192]{3,2,1,0:T(8,128)S(1)} custom-call(bf16[2,6,80,128]{3,2,1,0:T(8,128)(2,1)S(1)} %get-tuple-element.35.h_lo, bf16[2,7,80,128]{3,2,1,0:T(8,128)(2,1)S(1)} %get-tuple-element.36.h_pairs, bf16[1,6,80,128]{3,2,1,0:T(8,128)(2,1)S(1)} %get-tuple-element.37.h_stacked, ...), custom_call_target="tpu_custom_call" | custom-call | flops 509607936 | bytes 4194304 | tf_op jit(solution)/shard_map/second_layer/pallas_call | solution.py:451
  23.0 2.3 %collective-permute-done.4.partial = bf16[2,6,64,128]{3,2,1,0:T(8,128)(2,1)S(1)} collective-permute-done((bf16[2,6,64,128]{3,2,1,0:T(8,128)(2,1)S(1)}, bf16[2,6,64,128]{3,2,1,0:T(8,128)(2,1)S(1)}, u32[]{:S(2)}, u32[]{:S(2)}) %collective-permute-start.4) | collective-permute-done | bytes 196640 | tf_op jit(solution)/shard_map/ppermute | solution.py:26
  25.3 0.0 copy-done.1
  25.3 0.9 %finish.1 = bf16[2,4,64,192]{3,2,1,0:T(8,128)(2,1)} custom-call(bf16[2,6,64,128]{3,2,1,0:T(8,128)(2,1)S(1)} %collective-permute-done.4.partial, f32[2,4,64,192]{3,2,1,0:T(8,128)S(1)} %second_layer.1.own, f32[1,192]{1,0:T(1,128)S(1)} %bitcast.4), custom_call_target="tpu_custom_call" | custom-call | bytes 4194304 | tf_op jit(solution)/shard_map/finish/pallas_call | solution.py:451
Async XLA Ops:
  0.0 2.0 %collective-permute-start = (bf16[2,4,64,192]{3,2,1,0:T(8,128)(2,1)}, bf16[2,4,64,192]{3,2,1,0:T(8,128)(2,1)S(1)}, u32[]{:S(2)}, u32[]{:S(2)}) collective-permute-start(bf16[2,4,64,192]{3,2,1,0:T(8,128)(2,1)} %own_far.1), channel_id=1, source_target_pairs={{0,1},{1,0},{2,3},{3,2},{4,5},{5,4},{6,7},{7,6},{8,9},{9,8},{10,11... | collective-permute-start | bytes 589832 | tf_op jit(solution)/shard_map/ppermute | solution.py:19
  2.2 11.2 %copy-start = (f32[192]{0:T(256)S(1)}, f32[192]{0:T(256)}, u32[]{:S(2)}) copy-start(f32[192]{0:T(256)} %param.7) | copy-start | bytes 2308
  2.2 11.1 %collective-permute-start.2 = (bf16[800,128]{1,0:T(8,128)(2,1)S(1)}, bf16[800,128]{1,0:T(8,128)(2,1)S(1)}, u32[]{:S(2)}, u32[]{:S(2)}) collective-permute-start(bf16[800,128]{1,0:T(8,128)(2,1)S(1)} %get-tuple-element.24), channel_id=1, source_target_pairs={{0,4},{2,6},{4,8},{6,10},{8,12},{10,14},{1,5},{3,7},{5,9},{7,11},{... | collective-permute-start | bytes 614408 | tf_op jit(solution)/shard_map/ppermute | solution.py:26
  6.8 5.0 %collective-permute-start.3 = (bf16[400,128]{1,0:T(8,128)(2,1)S(1)}, bf16[400,128]{1,0:T(8,128)(2,1)S(1)}, u32[]{:S(2)}, u32[]{:S(2)}) collective-permute-start(bf16[400,128]{1,0:T(8,128)(2,1)S(1)} %get-tuple-element.23), channel_id=1, source_target_pairs={{0,2},{2,0},{1,3},{3,1},{4,6},{6,4},{5,7},{7,5},{8,10},{10,8},{9,1... | collective-permute-start | bytes 307208 | tf_op jit(solution)/shard_map/ppermute | solution.py:498
  8.4 7.1 %collective-permute-start.1 = (bf16[400,128]{1,0:T(8,128)(2,1)S(1)}, bf16[400,128]{1,0:T(8,128)(2,1)S(1)}, u32[]{:S(2)}, u32[]{:S(2)}) collective-permute-start(bf16[400,128]{1,0:T(8,128)(2,1)S(1)} %get-tuple-element.23), channel_id=1, source_target_pairs={{0,6},{2,4},{4,10},{6,8},{8,14},{10,12},{1,7},{3,5},{5,11},{7,9},{... | collective-permute-start | bytes 307208 | tf_op jit(solution)/shard_map/ppermute | solution.py:26
  17.7 7.5 %copy-start.1 = (f32[192]{0:T(256)S(1)}, f32[192]{0:T(256)}, u32[]{:S(2)}) copy-start(f32[192]{0:T(256)} %param.9) | copy-start | bytes 2308
  17.7 7.5 %collective-permute-start.4 = (bf16[2,6,64,128]{3,2,1,0:T(8,128)(2,1)S(1)}, bf16[2,6,64,128]{3,2,1,0:T(8,128)(2,1)S(1)}, u32[]{:S(2)}, u32[]{:S(2)}) collective-permute-start(bf16[2,6,64,128]{3,2,1,0:T(8,128)(2,1)S(1)} %get-tuple-element.34), channel_id=1, source_target_pairs={{0,4},{2,6},{4,8},{6,10},{8,12},{10,14},{1,5},{3,7},{5,9},{7,11},{... | collective-permute-start | bytes 589832 | tf_op jit(solution)/shard_map/ppermute | solution.py:26

commit v17 on v15

--- a/solution.py
+++ b/solution.py
@@ -431,10 +431,10 @@
             sent = [jnp.concatenate([partial[t, r], halves[r]], axis=-1) for r in range(rows)]
             y = y + jnp.stack(sent).astype(jnp.float32)
         sums.append(y.reshape(rows * cols, channels))
-    results = [activate(y, gain).astype(jnp.bfloat16) for y in sums]
     copies = [pltpu.make_async_copy(out.at[t], out_far.at[t], left.at[t]) for t in range(frames)]
     for t in range(frames):
-        out[t] = results[t].reshape(rows, cols, channels)
+        result = activate(sums[t], gain).astype(jnp.bfloat16)
+        out[t] = result.reshape(rows, cols, channels)
         copies[t].start()
     for copy in copies:
         copy.wait()

time: 26.5 us -> 26.5 us (level)
  no operation moved by 1% of the time
where the time goes in v17:
time: 26.5 us; the launch traced here: 26.3 us
  starting transfers between devices  14.2 us (54%)
  Pallas kernels  9.7 us (37%)
  waiting for transfers between devices  2.26 us (9%)
    ppermute x3, starting transfers between devices, forward(): return lax.ppermute(x, ('frame', 'strip'), pairs)  12.2 us
    pallas_call x7, Pallas kernels, call(): pl.pallas_call(kernel, out_shape=outs, in_specs=in_specs, out_specs=(away...  9.7 us
    ppermute x3, waiting for transfers between devices, forward(): return lax.ppermute(x, ('frame', 'strip'), pairs)  2.26 us
    ppermute x1, starting transfers between devices, shards(): lax.ppermute(edge, 'strip', way)  1.56 us
  transfers between devices with their start and end apart: 5, of which 1 were waited for; matrix products, arithmetic and copies ran while one was open for 0% of the time, Pallas kernels for 24%

profile of v17, /device:TPU:0, one launch (start us, length us, event | category | flops | bytes accessed | tf_op | source)
XLA Modules:
  0.0 26.3 jit_solution(15691870574441176746)
XLA Ops:
  0.0 0.5 %collective-permute-start = (bf16[2,4,64,192]{3,2,1,0:T(8,128)(2,1)}, bf16[2,4,64,192]{3,2,1,0:T(8,128)(2,1)S(1)}, u32[]{:S(2)}, u32[]{:S(2)}) collective-permute-start(bf16[2,4,64,192]{3,2,1,0:T(8,128)(2,1)} %own_far.1), channel_id=1, source_target_pairs={{0,1},{1,0},{2,3},{3,2},{4,5},{5,4},{6,7},{7,6},{8,9},{9,8},{10,11... | collective-permute-start | bytes 589832 | tf_op jit(solution)/shard_map/ppermute | solution.py:19
  0.5 1.5 %stage.1 = (bf16[2,4,64,192]{3,2,1,0:T(8,128)(2,1)S(1)}, bf16[3,3,192,192]{3,2,1,0:T(8,128)(2,1)S(1)}, bf16[3,3,192,192]{3,2,1,0:T(8,128)(2,1)S(1)}) custom-call(bf16[2,4,64,192]{3,2,1,0:T(8,128)(2,1)} %own_far.1, bf16[3,3,3,192,192]{4,3,2,1,0:T(8,128)(2,1)} %refs_5_.1), custom_call_target="tpu_custom_call" | custom-call | bytes 4194304 | tf_op jit(solution)/shard_map/stage/pallas_call | solution.py:450
  2.0 0.0 collective-permute-done.neighbour.refs_1_
  2.0 0.1 pack.1
  2.2 0.0 copy-start
  2.2 4.7 %collective-permute-start.2 = (bf16[800,128]{1,0:T(8,128)(2,1)S(1)}, bf16[800,128]{1,0:T(8,128)(2,1)S(1)}, u32[]{:S(2)}, u32[]{:S(2)}) collective-permute-start(bf16[800,128]{1,0:T(8,128)(2,1)S(1)} %get-tuple-element.24), channel_id=1, source_target_pairs={{0,4},{2,6},{4,8},{6,10},{8,12},{10,14},{1,5},{3,7},{5,9},{7,11},{... | collective-permute-start | bytes 614408 | tf_op jit(solution)/shard_map/ppermute | solution.py:26
  6.8 1.6 %collective-permute-start.3 = (bf16[400,128]{1,0:T(8,128)(2,1)S(1)}, bf16[400,128]{1,0:T(8,128)(2,1)S(1)}, u32[]{:S(2)}, u32[]{:S(2)}) collective-permute-start(bf16[400,128]{1,0:T(8,128)(2,1)S(1)} %get-tuple-element.23), channel_id=1, source_target_pairs={{0,2},{2,0},{1,3},{3,1},{4,6},{6,4},{5,7},{7,5},{8,10},{10,8},{9,1... | collective-permute-start | bytes 307208 | tf_op jit(solution)/shard_map/ppermute | solution.py:497
  8.4 3.4 %collective-permute-start.1 = (bf16[400,128]{1,0:T(8,128)(2,1)S(1)}, bf16[400,128]{1,0:T(8,128)(2,1)S(1)}, u32[]{:S(2)}, u32[]{:S(2)}) collective-permute-start(bf16[400,128]{1,0:T(8,128)(2,1)S(1)} %get-tuple-element.23), channel_id=1, source_target_pairs={{0,6},{2,4},{4,10},{6,8},{8,14},{10,12},{1,7},{3,5},{5,11},{7,9},{... | collective-permute-start | bytes 307208 | tf_op jit(solution)/shard_map/ppermute | solution.py:26
  11.8 0.0 collective-permute-done.3.refs_2_
  11.9 1.4 %edge_rows_own.1 = (f32[1,2,2,80,192]{4,3,2,1,0:T(8,128)S(1)}, bf16[3,3,192,192]{3,2,1,0:T(8,128)(2,1)S(1)}) custom-call(bf16[2,4,64,192]{3,2,1,0:T(8,128)(2,1)S(1)} %get-tuple-element.22.own.refs_0_, bf16[2,4,64,192]{3,2,1,0:T(8,128)(2,1)S(1)} %collective-permute-done.neighbour.refs_1_, bf16[400,128]{1,0:T(8,128)(2,1)S(1)} %collective-permute-done.3.refs_2_, ...), custom_call_target="tpu_custom_call" | custom-call | flops 127401984 | bytes 4194304 | tf_op jit(solution)/shard_map/edge_rows_own/pallas_call | solution.py:450
  13.3 0.0 collective-permute-done.2.refs_2_.refs_1_
  13.3 0.0 copy-done
  13.3 2.2 %safe_rows.1 = (bf16[2,6,80,128]{3,2,1,0:T(8,128)(2,1)S(1)}, bf16[2,7,80,128]{3,2,1,0:T(8,128)(2,1)S(1)}, bf16[1,6,80,128]{3,2,1,0:T(8,128)(2,1)S(1)}, bf16[3,3,...) custom-call(bf16[2,4,64,192]{3,2,1,0:T(8,128)(2,1)S(1)} %get-tuple-element.22, ...), custom_call_target="tpu_custom_call" | custom-call | flops 509607936 | bytes 4194304 | tf_op jit(solution)/shard_map/safe_rows/pallas_call | solution.py:450
  15.5 0.0 collective-permute-done.1.refs_0_
  15.5 2.2 %edge_rows.1 = (bf16[2,6,80,128]{3,2,1,0:T(8,128)(2,1)S(1)}, bf16[2,7,80,128]{3,2,1,0:T(8,128)(2,1)S(1)}, bf16[1,6,80,128]{3,2,1,0:T(8,128)(2,1)S(1)}, bf16[2,6,64,128]{3,2,1,0:T(8,128)(2,1)S(1)}) custom-call(bf16[400,128]{1,0:T(8,128)(2,1)S(1)} %collective-permute-done.1.refs_0_, ...), custom_call_target="tpu_custom_call", output_to_operand_aliasing={{0}: (3, {}), {1}: (4, {}), {2}: (5, {})} | custom-call | flops 509607936 | bytes 4194304 | tf_op jit(solution)/shard_map/edge_rows/pallas_call | solution.py:450
  17.7 0.0 copy-start.1
  17.7 4.1 %collective-permute-start.4 = (bf16[2,6,64,128]{3,2,1,0:T(8,128)(2,1)S(1)}, bf16[2,6,64,128]{3,2,1,0:T(8,128)(2,1)S(1)}, u32[]{:S(2)}, u32[]{:S(2)}) collective-permute-start(bf16[2,6,64,128]{3,2,1,0:T(8,128)(2,1)S(1)} %get-tuple-element.34), channel_id=1, source_target_pairs={{0,4},{2,6},{4,8},{6,10},{8,12},{10,14},{1,5},{3,7},{5,9},{7,11},{... | collective-permute-start | bytes 589832 | tf_op jit(solution)/shard_map/ppermute | solution.py:26
  21.8 1.2 %second_layer.1.own = f32[2,4,64,192]{3,2,1,0:T(8,128)S(1)} custom-call(bf16[2,6,80,128]{3,2,1,0:T(8,128)(2,1)S(1)} %get-tuple-element.35.h_lo, bf16[2,7,80,128]{3,2,1,0:T(8,128)(2,1)S(1)} %get-tuple-element.36.h_pairs, bf16[1,6,80,128]{3,2,1,0:T(8,128)(2,1)S(1)} %get-tuple-element.37.h_stacked, ...), custom_call_target="tpu_custom_call" | custom-call | flops 509607936 | bytes 4194304 | tf_op jit(solution)/shard_map/second_layer/pallas_call | solution.py:450
  23.0 2.3 %collective-permute-done.4.partial = bf16[2,6,64,128]{3,2,1,0:T(8,128)(2,1)S(1)} collective-permute-done((bf16[2,6,64,128]{3,2,1,0:T(8,128)(2,1)S(1)}, bf16[2,6,64,128]{3,2,1,0:T(8,128)(2,1)S(1)}, u32[]{:S(2)}, u32[]{:S(2)}) %collective-permute-start.4) | collective-permute-done | bytes 196640 | tf_op jit(solution)/shard_map/ppermute | solution.py:26
  25.3 0.0 copy-done.1
  25.3 1.0 %finish.1 = bf16[2,4,64,192]{3,2,1,0:T(8,128)(2,1)} custom-call(bf16[2,6,64,128]{3,2,1,0:T(8,128)(2,1)S(1)} %collective-permute-done.4.partial, f32[2,4,64,192]{3,2,1,0:T(8,128)S(1)} %second_layer.1.own, f32[1,192]{1,0:T(1,128)S(1)} %bitcast.4), custom_call_target="tpu_custom_call" | custom-call | bytes 4194304 | tf_op jit(solution)/shard_map/finish/pallas_call | solution.py:450
Async XLA Ops:
  0.0 2.0 %collective-permute-start = (bf16[2,4,64,192]{3,2,1,0:T(8,128)(2,1)}, bf16[2,4,64,192]{3,2,1,0:T(8,128)(2,1)S(1)}, u32[]{:S(2)}, u32[]{:S(2)}) collective-permute-start(bf16[2,4,64,192]{3,2,1,0:T(8,128)(2,1)} %own_far.1), channel_id=1, source_target_pairs={{0,1},{1,0},{2,3},{3,2},{4,5},{5,4},{6,7},{7,6},{8,9},{9,8},{10,11... | collective-permute-start | bytes 589832 | tf_op jit(solution)/shard_map/ppermute | solution.py:19
  2.2 11.2 %copy-start = (f32[192]{0:T(256)S(1)}, f32[192]{0:T(256)}, u32[]{:S(2)}) copy-start(f32[192]{0:T(256)} %param.7) | copy-start | bytes 2308
  2.2 11.1 %collective-permute-start.2 = (bf16[800,128]{1,0:T(8,128)(2,1)S(1)}, bf16[800,128]{1,0:T(8,128)(2,1)S(1)}, u32[]{:S(2)}, u32[]{:S(2)}) collective-permute-start(bf16[800,128]{1,0:T(8,128)(2,1)S(1)} %get-tuple-element.24), channel_id=1, source_target_pairs={{0,4},{2,6},{4,8},{6,10},{8,12},{10,14},{1,5},{3,7},{5,9},{7,11},{... | collective-permute-start | bytes 614408 | tf_op jit(solution)/shard_map/ppermute | solution.py:26
  6.8 5.0 %collective-permute-start.3 = (bf16[400,128]{1,0:T(8,128)(2,1)S(1)}, bf16[400,128]{1,0:T(8,128)(2,1)S(1)}, u32[]{:S(2)}, u32[]{:S(2)}) collective-permute-start(bf16[400,128]{1,0:T(8,128)(2,1)S(1)} %get-tuple-element.23), channel_id=1, source_target_pairs={{0,2},{2,0},{1,3},{3,1},{4,6},{6,4},{5,7},{7,5},{8,10},{10,8},{9,1... | collective-permute-start | bytes 307208 | tf_op jit(solution)/shard_map/ppermute | solution.py:497
  8.4 7.1 %collective-permute-start.1 = (bf16[400,128]{1,0:T(8,128)(2,1)S(1)}, bf16[400,128]{1,0:T(8,128)(2,1)S(1)}, u32[]{:S(2)}, u32[]{:S(2)}) collective-permute-start(bf16[400,128]{1,0:T(8,128)(2,1)S(1)} %get-tuple-element.23), channel_id=1, source_target_pairs={{0,6},{2,4},{4,10},{6,8},{8,14},{10,12},{1,7},{3,5},{5,11},{7,9},{... | collective-permute-start | bytes 307208 | tf_op jit(solution)/shard_map/ppermute | solution.py:26
  17.7 7.5 %copy-start.1 = (f32[192]{0:T(256)S(1)}, f32[192]{0:T(256)}, u32[]{:S(2)}) copy-start(f32[192]{0:T(256)} %param.9) | copy-start | bytes 2308
  17.7 7.5 %collective-permute-start.4 = (bf16[2,6,64,128]{3,2,1,0:T(8,128)(2,1)S(1)}, bf16[2,6,64,128]{3,2,1,0:T(8,128)(2,1)S(1)}, u32[]{:S(2)}, u32[]{:S(2)}) collective-permute-start(bf16[2,6,64,128]{3,2,1,0:T(8,128)(2,1)S(1)} %get-tuple-element.34), channel_id=1, source_target_pairs={{0,4},{2,6},{4,8},{6,10},{8,12},{10,14},{1,5},{3,7},{5,9},{7,11},{... | collective-permute-start | bytes 589832 | tf_op jit(solution)/shard_map/ppermute | solution.py:26
